TPU v7x, 32 devices: a whole 2x2x4 slice. The times are simulated.
32 devices in a mesh: grp: 8 (over z, x), fsdp: 4 (over y, core).
Axes of the slice: x: 2, y: 2, z: 4, core: 2. Of those that a mesh axis runs over, the one named last changes fastest.
Arguments:
- patches: bfloat16 [48, 4, 16384], P(None, None, ('grp', 'fsdp')), may hold values from -6 to 6
- patch_counts: int32 [8], P('grp'), may hold values from 682 to 2048, as said below
- var_present: int32 [8, 48], P('grp'), may hold values from 0 to 1, as said below
- item_dataset: int32 [8], P('grp'), may hold values from 0 to 5
- var_ids: int32 [6, 48], replicated, may hold values from 0 to 47, each once within a row
- patch_weight: bfloat16 [48, 4, 1024], P('fsdp'), may hold values from -3 to 3
- var_embed: bfloat16 [48, 1024], P('fsdp'), may hold values from -6 to 6
- agg_query: bfloat16 [1024], replicated, may hold values from -6 to 6
- query_weight: bfloat16 [1024, 1024], P('fsdp'), may hold values from -0.1875 to 0.1875
- key_weight: bfloat16 [1024, 1024], P('fsdp'), may hold values from -0.1875 to 0.1875
- value_weight: bfloat16 [1024, 1024], P('fsdp'), may hold values from -0.1875 to 0.1875
- agg_proj: bfloat16 [1024, 1024], P('fsdp'), may hold values from -0.375 to 0.375
- agg_bias: float32 [1024], replicated, may hold values from -2 to 2
- norm1_gain: float32 [1024], replicated, may hold values from 0.1 to 1.9
- norm1_shift: float32 [1024], replicated, may hold values from -2 to 2
- qkv_weight: bfloat16 [1024, 3072], P('fsdp'), may hold values from -0.1875 to 0.1875
- proj_weight: bfloat16 [1024, 1024], P('fsdp'), may hold values from -4 to 4
- proj_bias: float32 [1024], replicated, may hold values from -2 to 2
- norm2_gain: float32 [1024], replicated, may hold values from 0.1 to 1.9
- norm2_shift: float32 [1024], replicated, may hold values from -2 to 2
- up_weight: bfloat16 [1024, 4096], P(None, 'fsdp'), may hold values from -0.1875 to 0.1875
- up_bias: bfloat16 [4096], P('fsdp'), may hold values from -3 to 3
- down_weight: bfloat16 [4096, 1024], P('fsdp'), may hold values from -0.09375 to 0.09375
- down_bias: float32 [1024], replicated, may hold values from -2 to 2
- out_grad: bfloat16 [16384, 1024], P(('grp', 'fsdp')), may hold values from -6 to 6
Outputs:
- output: bfloat16 [16384, 1024], P(('grp', 'fsdp'))
- patches_grad: float32 [48, 4, 16384], P(None, None, ('grp', 'fsdp'))
- patch_weight_grad: float32 [48, 4, 1024], P('fsdp')
- var_embed_grad: float32 [48, 1024], P('fsdp')
- agg_query_grad: float32 [1024], P('fsdp')
- query_weight_grad: float32 [1024, 1024], P('fsdp')
- key_weight_grad: float32 [1024, 1024], P('fsdp')
- value_weight_grad: float32 [1024, 1024], P('fsdp')
- agg_proj_grad: float32 [1024, 1024], P('fsdp')
- agg_bias_grad: float32 [1024], P('fsdp')
- norm1_gain_grad: float32 [1024], P('fsdp')
- norm1_shift_grad: float32 [1024], P('fsdp')
- qkv_weight_grad: float32 [1024, 3072], P('fsdp')
- proj_weight_grad: float32 [1024, 1024], P('fsdp')
- proj_bias_grad: float32 [1024], P('fsdp')
- norm2_gain_grad: float32 [1024], P('fsdp')
- norm2_shift_grad: float32 [1024], P('fsdp')
- up_weight_grad: float32 [1024, 4096], P(None, 'fsdp')
- up_bias_grad: float32 [4096], P('fsdp')
- down_weight_grad: float32 [4096, 1024], P('fsdp')
- down_bias_grad: float32 [1024], P('fsdp')
Inputs may be any that keep to these rules, and one draw needn't show every extreme that they name: Rows of a group's item at positions from patch_counts[g] on are padding; group g's count lies within 128 below 682 + 1366 * g // 7, and never under 2048 // 3; the first group has exactly 682 valid rows and the last group a full item. `var_present`: each item has 30 to 48 present variables; in every draw one item has all and one has exactly 30. `var_ids`: each dataset's row is a permutation of the 48 variables.
All inputs are finite; a program needn't handle non-finite values.
Results may differ from a plain program's by a relative error of at most 0.019.
Values may be sent and summed in bfloat16 or wider, within the bound.
A program may use at most 512 MiB of HBM per device.

v0:
```python
import jax
import jax.numpy as jnp
from jax import lax
from jax.sharding import PartitionSpec as P

HEADS = 16
VTOT = 48
PIX = 4


exact_mode = lax.Precision.HIGHEST
masked_out = -1e30
head_group = 4


def layer_norm(values_in, gain_vec, shift_vec):
    row_mean = jnp.mean(values_in, axis=-1, keepdims=True)
    centred = values_in - row_mean
    spread = jnp.mean(centred * centred, axis=-1, keepdims=True)
    return centred * lax.rsqrt(spread + 1e-05) * gain_vec + shift_vec


def gelu_exact(values_in):
    return jax.nn.gelu(values_in, approximate=False)


def product(left_side, right_side):
    return jnp.dot(left_side, right_side, preferred_element_type=jnp.float32)


def left_product(left_side, right_side):
    return lax.dot_general(
        left_side, right_side, (((0,), (0,)), ((), ())), preferred_element_type=jnp.float32
    )


def right_product(left_side, right_side):
    return lax.dot_general(
        left_side, right_side, (((1,), (1,)), ((), ())), preferred_element_type=jnp.float32
    )


def column_sums(values_in):
    return jnp.sum(values_in.astype(jnp.float32), axis=0)


def block_logits(query_part, key_part, key_valid, score_scale):
    raw_scores = jnp.einsum(
        "qhe,khe->hqk", query_part, key_part, preferred_element_type=jnp.float32
    )
    return jnp.where(key_valid[None, None, :], raw_scores * score_scale, masked_out)


def on_device(
    patches,
    patch_counts,
    var_present,
    item_dataset,
    var_ids,
    patch_weight,
    var_embed,
    agg_query,
    query_weight,
    key_weight,
    value_weight,
    agg_proj,
    agg_bias,
    norm1_gain,
    norm1_shift,
    qkv_weight,
    proj_weight,
    proj_bias,
    norm2_gain,
    norm2_shift,
    up_weight,
    up_bias,
    down_weight,
    down_bias,
    out_grad,
):
    row_count = patches.shape[2]
    shard_count = lax.axis_size("fsdp")
    group_count = lax.axis_size("grp")
    length = row_count * shard_count
    model_width = proj_weight.shape[1]
    head_dim = model_width // HEADS
    score_scale = head_dim ** (-0.5)
    block_width = head_group * head_dim
    counts = patch_counts.astype(jnp.float32)
    count_total = lax.psum(counts, "grp")
    item_count = patch_counts[0]
    first_row = lax.axis_index("fsdp") * row_count
    own_valid = first_row + jnp.arange(row_count, dtype=jnp.int32) < item_count
    key_valid = jnp.arange(length, dtype=jnp.int32) < item_count
    present = var_present[0] > 0
    slot_vars = lax.dynamic_index_in_dim(var_ids, item_dataset[0], 0, keepdims=False)
    selector = (slot_vars[:, None] == jnp.arange(VTOT, dtype=jnp.int32)[None, :]).astype(
        jnp.bfloat16
    )
    full_patch, full_embed, full_query_w, full_key_w, full_value_w, full_proj = (
        lax.all_gather(patch_weight, "fsdp", axis=0, tiled=True),
        lax.all_gather(var_embed, "fsdp", axis=0, tiled=True),
        lax.all_gather(query_weight, "fsdp", axis=0, tiled=True),
        lax.all_gather(key_weight, "fsdp", axis=0, tiled=True),
        lax.all_gather(value_weight, "fsdp", axis=0, tiled=True),
        lax.all_gather(agg_proj, "fsdp", axis=0, tiled=True),
    )
    stacked = jnp.concatenate([full_patch.reshape(VTOT, PIX * model_width), full_embed], axis=1)
    var_table = product(selector, stacked).astype(jnp.bfloat16).reshape(VTOT, PIX + 1, model_width)
    query_vec = product(agg_query[None, :], full_query_w)[0].astype(jnp.bfloat16)
    key_heads = full_key_w.reshape(model_width, HEADS, head_dim)
    key_query = (
        jnp.einsum(
            "dhj,hj->dh",
            key_heads,
            query_vec.reshape(HEADS, head_dim),
            preferred_element_type=jnp.float32,
        )
        * score_scale
    ).astype(jnp.bfloat16)
    extended = jnp.concatenate(
        [patches.astype(jnp.float32), jnp.ones((VTOT, 1, row_count), jnp.float32)], axis=1
    )
    coeffs = jnp.einsum("vkd,dh->vkh", var_table, key_query, preferred_element_type=jnp.float32)
    var_scores = jnp.einsum("vkp,vkh->vhp", extended, coeffs, precision=exact_mode)
    var_scores = jnp.where(present[:, None, None], var_scores, masked_out)
    var_weights = jax.nn.softmax(var_scores, axis=0)
    mixed_terms = (var_weights[:, None, :, :] * extended[:, :, None, :]).astype(jnp.bfloat16)
    pooled = jnp.einsum(
        "vkhp,vkd->hpd", mixed_terms, var_table, preferred_element_type=jnp.float32
    ).astype(jnp.bfloat16)
    value_heads = full_value_w.reshape(model_width, HEADS, head_dim)
    agg_heads = jnp.einsum("hpd,dhj->phj", pooled, value_heads, preferred_element_type=jnp.float32)
    agg_heads = agg_heads.reshape(row_count, model_width).astype(jnp.bfloat16)
    embedded = product(agg_heads, full_proj) + agg_bias
    full_qkv, full_out, up_full, down_full, up_bias_full = (
        lax.all_gather(qkv_weight, "fsdp", axis=0, tiled=True),
        lax.all_gather(proj_weight, "fsdp", axis=0, tiled=True),
        lax.all_gather(up_weight, "fsdp", axis=1, tiled=True),
        lax.all_gather(down_weight, "fsdp", axis=0, tiled=True),
        lax.all_gather(up_bias, "fsdp", axis=0, tiled=True),
    )
    normed1 = layer_norm(embedded, norm1_gain, norm1_shift).astype(jnp.bfloat16)
    qkv_rows = product(normed1, full_qkv).astype(jnp.bfloat16)
    kv_all = lax.all_gather(qkv_rows[:, model_width:], "fsdp", axis=0, tiled=True)
    log_totals = []
    contexts = []
    for block_index in range(HEADS // head_group):
        start_col = block_index * block_width
        query_part = qkv_rows[:, start_col : start_col + block_width].reshape(
            row_count, head_group, head_dim
        )
        key_part = kv_all[:, start_col : start_col + block_width].reshape(
            length, head_group, head_dim
        )
        value_part = kv_all[
            :, model_width + start_col : model_width + start_col + block_width
        ].reshape(length, head_group, head_dim)
        logits = block_logits(query_part, key_part, key_valid, score_scale)
        row_max = jnp.max(logits, axis=-1, keepdims=True)
        exp_terms = jnp.exp(logits - row_max)
        row_total = jnp.sum(exp_terms, axis=-1, keepdims=True)
        attn_probs = exp_terms / row_total
        log_totals.append(row_max + jnp.log(row_total))
        context_part = jnp.einsum(
            "hqk,khe->qhe",
            attn_probs.astype(jnp.bfloat16),
            value_part,
            preferred_element_type=jnp.float32,
        )
        contexts.append(context_part.reshape(row_count, block_width))
    context = jnp.concatenate(contexts, axis=1).astype(jnp.bfloat16)
    middle = embedded + (product(context, full_out) + proj_bias)
    normed2 = layer_norm(middle, norm2_gain, norm2_shift).astype(jnp.bfloat16)
    pre_act = product(normed2, up_full) + up_bias_full.astype(jnp.float32)
    gelu_out = gelu_exact(pre_act).astype(jnp.bfloat16)
    down_part = product(gelu_out, down_full)
    output = (middle + down_part + down_bias).astype(jnp.bfloat16)
    upstream = out_grad.astype(jnp.float32) * own_valid[:, None].astype(jnp.float32)
    down_grad = upstream.astype(jnp.bfloat16)
    down_bias_grad = column_sums(down_grad)
    down_weight_grad = left_product(gelu_out, down_grad)
    act_grad = right_product(down_grad, down_full)
    gelu_value, gelu_pull = jax.vjp(gelu_exact, pre_act)
    pre_grad = gelu_pull(act_grad)[0].astype(jnp.bfloat16)
    up_weight_grad = left_product(normed2, pre_grad)
    up_bias_grad = column_sums(pre_grad)
    normed2_part = right_product(pre_grad, up_full)
    norm2_value, norm2_pull = jax.vjp(layer_norm, middle, norm2_gain, norm2_shift)
    middle_part, norm2_gain_grad, norm2_shift_grad = norm2_pull(normed2_part)
    middle_grad = upstream + middle_part
    attended_grad = middle_grad.astype(jnp.bfloat16)
    proj_weight_grad = left_product(context, attended_grad)
    proj_bias_grad = column_sums(attended_grad)
    context_grad = right_product(attended_grad, full_out).astype(jnp.bfloat16)
    query_grads = []
    key_grads = []
    value_grads = []
    for block_index in range(HEADS // head_group):
        start_col = block_index * block_width
        query_part = qkv_rows[:, start_col : start_col + block_width].reshape(
            row_count, head_group, head_dim
        )
        key_part = kv_all[:, start_col : start_col + block_width].reshape(
            length, head_group, head_dim
        )
        value_part = kv_all[
            :, model_width + start_col : model_width + start_col + block_width
        ].reshape(length, head_group, head_dim)
        logits = block_logits(query_part, key_part, key_valid, score_scale)
        attn_probs = jnp.exp(logits - log_totals[block_index])
        context_part_grad = context_grad[:, start_col : start_col + block_width].reshape(
            row_count, head_group, head_dim
        )
        probs_grad = jnp.einsum(
            "qhe,khe->hqk", context_part_grad, value_part, preferred_element_type=jnp.float32
        )
        logit_grad = attn_probs * (
            probs_grad - jnp.sum(attn_probs * probs_grad, axis=-1, keepdims=True)
        )
        raw_grad = (logit_grad * score_scale).astype(jnp.bfloat16)
        query_grads.append(
            jnp.einsum(
                "hqk,khe->qhe", raw_grad, key_part, preferred_element_type=jnp.float32
            ).reshape(row_count, block_width)
        )
        key_grads.append(
            jnp.einsum(
                "hqk,qhe->khe", raw_grad, query_part, preferred_element_type=jnp.float32
            ).reshape(length, block_width)
        )
        value_grads.append(
            jnp.einsum(
                "hqk,qhe->khe",
                attn_probs.astype(jnp.bfloat16),
                context_part_grad,
                preferred_element_type=jnp.float32,
            ).reshape(length, block_width)
        )
    kv_grad_part = jnp.concatenate(key_grads + value_grads, axis=1)
    kv_grad = lax.psum_scatter(
        kv_grad_part.astype(jnp.bfloat16), "fsdp", scatter_dimension=0, tiled=True
    ).astype(jnp.float32)
    qkv_grad = jnp.concatenate([jnp.concatenate(query_grads, axis=1), kv_grad], axis=1).astype(
        jnp.bfloat16
    )
    qkv_weight_grad = left_product(normed1, qkv_grad)
    normed1_grad = right_product(qkv_grad, full_qkv)
    norm1_value, norm1_pull = jax.vjp(layer_norm, embedded, norm1_gain, norm1_shift)
    embedded_part, norm1_gain_grad, norm1_shift_grad = norm1_pull(normed1_grad)
    embedded_grad = (middle_grad + embedded_part).astype(jnp.bfloat16)
    agg_bias_grad = column_sums(embedded_grad)
    agg_proj_grad = left_product(agg_heads, embedded_grad)
    heads_grad = (
        right_product(embedded_grad, full_proj)
        .astype(jnp.bfloat16)
        .reshape(row_count, HEADS, head_dim)
    )
    value_weight_grad = jnp.einsum(
        "hpd,phj->dhj", pooled, heads_grad, preferred_element_type=jnp.float32
    ).reshape(model_width, model_width)
    pooled_grad = jnp.einsum(
        "phj,dhj->hpd", heads_grad, value_heads, preferred_element_type=jnp.float32
    ).astype(jnp.bfloat16)
    mixed_grad = jnp.einsum(
        "hpd,vkd->vkhp", pooled_grad, var_table, preferred_element_type=jnp.float32
    )
    table_grad = jnp.einsum(
        "vkhp,hpd->vkd", mixed_terms, pooled_grad, preferred_element_type=jnp.float32
    )
    weights_grad = jnp.sum(mixed_grad * extended[:, :, None, :], axis=1)
    scores_grad = var_weights * (
        weights_grad - jnp.sum(var_weights * weights_grad, axis=0, keepdims=True)
    )
    coeffs_grad = jnp.einsum("vhp,vkp->vkh", scores_grad, extended, precision=exact_mode)
    extended_grad = jnp.sum(mixed_grad * var_weights[:, None, :, :], axis=2) + jnp.einsum(
        "vhp,vkh->vkp", scores_grad, coeffs, precision=exact_mode
    )
    table_grad = table_grad + jnp.einsum(
        "vkh,dh->vkd", coeffs_grad, key_query.astype(jnp.float32), precision=exact_mode
    )
    key_query_grad = jnp.einsum(
        "vkh,vkd->dh", coeffs_grad, var_table.astype(jnp.float32), precision=exact_mode
    ).astype(jnp.bfloat16)
    key_weight_grad = (
        key_query_grad.astype(jnp.float32)[:, :, None]
        * query_vec.astype(jnp.float32).reshape(1, HEADS, head_dim)
        * score_scale
    ).reshape(model_width, model_width)
    query_grad = (
        (
            jnp.einsum("dhj,dh->hj", key_heads, key_query_grad, preferred_element_type=jnp.float32)
            * score_scale
        )
        .reshape(model_width)
        .astype(jnp.bfloat16)
    )
    query_weight_grad = (
        agg_query.astype(jnp.float32)[:, None] * query_grad.astype(jnp.float32)[None, :]
    )
    agg_query_grad = product(full_query_w, query_grad)
    var_grads = jnp.dot(
        selector.astype(jnp.float32).T,
        table_grad.reshape(VTOT, (PIX + 1) * model_width),
        precision=exact_mode,
    )
    patch_weight_grad = var_grads[:, : PIX * model_width].reshape(VTOT, PIX, model_width)
    var_embed_grad = var_grads[:, PIX * model_width :]
    patches_part = extended_grad[:, :PIX, :]
    shards = (
        lax.psum_scatter(
            patch_weight_grad.astype(jnp.bfloat16), "fsdp", scatter_dimension=0, tiled=True
        ).astype(jnp.float32),
        lax.psum_scatter(
            var_embed_grad.astype(jnp.bfloat16), "fsdp", scatter_dimension=0, tiled=True
        ).astype(jnp.float32),
        lax.psum_scatter(
            agg_query_grad.astype(jnp.bfloat16), "fsdp", scatter_dimension=0, tiled=True
        ).astype(jnp.float32),
        lax.psum_scatter(
            query_weight_grad.astype(jnp.bfloat16), "fsdp", scatter_dimension=0, tiled=True
        ).astype(jnp.float32),
        lax.psum_scatter(
            key_weight_grad.astype(jnp.bfloat16), "fsdp", scatter_dimension=0, tiled=True
        ).astype(jnp.float32),
        lax.psum_scatter(
            value_weight_grad.astype(jnp.bfloat16), "fsdp", scatter_dimension=0, tiled=True
        ).astype(jnp.float32),
        lax.psum_scatter(
            agg_proj_grad.astype(jnp.bfloat16), "fsdp", scatter_dimension=0, tiled=True
        ).astype(jnp.float32),
        lax.psum_scatter(
            agg_bias_grad.astype(jnp.bfloat16), "fsdp", scatter_dimension=0, tiled=True
        ).astype(jnp.float32),
        lax.psum_scatter(
            norm1_gain_grad.astype(jnp.bfloat16), "fsdp", scatter_dimension=0, tiled=True
        ).astype(jnp.float32),
        lax.psum_scatter(
            norm1_shift_grad.astype(jnp.bfloat16), "fsdp", scatter_dimension=0, tiled=True
        ).astype(jnp.float32),
        lax.psum_scatter(
            qkv_weight_grad.astype(jnp.bfloat16), "fsdp", scatter_dimension=0, tiled=True
        ).astype(jnp.float32),
        lax.psum_scatter(
            proj_weight_grad.astype(jnp.bfloat16), "fsdp", scatter_dimension=0, tiled=True
        ).astype(jnp.float32),
        lax.psum_scatter(
            proj_bias_grad.astype(jnp.bfloat16), "fsdp", scatter_dimension=0, tiled=True
        ).astype(jnp.float32),
        lax.psum_scatter(
            norm2_gain_grad.astype(jnp.bfloat16), "fsdp", scatter_dimension=0, tiled=True
        ).astype(jnp.float32),
        lax.psum_scatter(
            norm2_shift_grad.astype(jnp.bfloat16), "fsdp", scatter_dimension=0, tiled=True
        ).astype(jnp.float32),
        lax.psum_scatter(
            up_weight_grad.astype(jnp.bfloat16), "fsdp", scatter_dimension=1, tiled=True
        ).astype(jnp.float32),
        lax.psum_scatter(
            up_bias_grad.astype(jnp.bfloat16), "fsdp", scatter_dimension=0, tiled=True
        ).astype(jnp.float32),
        lax.psum_scatter(
            down_weight_grad.astype(jnp.bfloat16), "fsdp", scatter_dimension=0, tiled=True
        ).astype(jnp.float32),
        lax.psum_scatter(
            down_bias_grad.astype(jnp.bfloat16), "fsdp", scatter_dimension=0, tiled=True
        ).astype(jnp.float32),
    )
    count_share = counts[0] / count_total[0]
    summed = lax.psum(
        (
            shards[0] * count_share,
            shards[1] * count_share,
            shards[2] * count_share,
            shards[3] * count_share,
            shards[4] * count_share,
            shards[5] * count_share,
            shards[6] * count_share,
            shards[7] * count_share,
            shards[8] * count_share,
            shards[9] * count_share,
            shards[10] * count_share,
            shards[11] * count_share,
            shards[12] * count_share,
            shards[13] * count_share,
            shards[14] * count_share,
            shards[15] * count_share,
            shards[16] * count_share,
            shards[17] * count_share,
            shards[18] * count_share,
        ),
        "grp",
    )
    input_scale = group_count * count_share
    patches_grad = patches_part * input_scale
    return (
        output,
        patches_grad,
        summed[0],
        summed[1],
        summed[2],
        summed[3],
        summed[4],
        summed[5],
        summed[6],
        summed[7],
        summed[8],
        summed[9],
        summed[10],
        summed[11],
        summed[12],
        summed[13],
        summed[14],
        summed[15],
        summed[16],
        summed[17],
        summed[18],
    )


def solution(mesh):
    return jax.shard_map(
        on_device,
        mesh=mesh,
        in_specs=(
            P(None, None, ("grp", "fsdp")),
            P("grp"),
            P("grp", None),
            P("grp"),
            P(),
            P("fsdp", None, None),
            P("fsdp", None),
            P(),
            P("fsdp", None),
            P("fsdp", None),
            P("fsdp", None),
            P("fsdp", None),
            P(),
            P(),
            P(),
            P("fsdp", None),
            P("fsdp", None),
            P(),
            P(),
            P(),
            P(None, "fsdp"),
            P("fsdp"),
            P("fsdp", None),
            P(),
            P(("grp", "fsdp"), None),
        ),
        out_specs=(
            P(("grp", "fsdp"), None),
            P(None, None, ("grp", "fsdp")),
            P("fsdp", None, None),
            P("fsdp", None),
            P("fsdp"),
            P("fsdp", None),
            P("fsdp", None),
            P("fsdp", None),
            P("fsdp", None),
            P("fsdp"),
            P("fsdp"),
            P("fsdp"),
            P("fsdp", None),
            P("fsdp", None),
            P("fsdp"),
            P("fsdp"),
            P("fsdp"),
            P(None, "fsdp"),
            P("fsdp"),
            P("fsdp", None),
            P("fsdp"),
        ),
        check_vma=False,
    )
```

profile of v0, /device:TPU:0, one launch (start us, length us, event | category | flops | bytes accessed | tf_op | source)
XLA Modules:
  0.0 1630.1 jit_solution(3442856087907749235)
XLA Ops:
  21.1 9.5 all_gather.36
  39.7 22.3 %all-gather.13.cloned.1.call-done = bf16[1024,1024]{0,1:T(8,128)(2,1)} async-done(((bf16[256,1024]{0,1:T(8,128)(2,1)}), bf16[1024,1024]{0,1:T(8,128)(2,1)}) %all-gather.13.cloned.1.call-update) | async-done | bytes 2097168 | tf_op jit(solution)/shard_map/all_gather | solution.py:104
  70.8 15.4 all-gather.15.cloned.1.call-done
  89.3 10.1 bitcast_convert_fusion
  99.4 8.9 convolution_convert_fusion.10
  114.5 43.6 %all-gather.19.cloned.1.call-done = bf16[1024,3072]{1,0:T(8,128)(2,1)} async-done(((bf16[256,3072]{1,0:T(8,128)(2,1)}), bf16[1024,3072]{1,0:T(8,128)(2,1)}) %all-gather.19.cloned.1.call-update) | async-done | bytes 6291472 | tf_op jit(solution)/shard_map/all_gather | solution.py:137
  180.8 45.8 %all-gather.21.cloned.1.call-done = bf16[2048,2048]{1,0:T(8,128)(2,1)} async-done(((bf16[512,2048]{1,0:T(8,128)(2,1)}), bf16[2048,2048]{1,0:T(8,128)(2,1)}) %all-gather.21.cloned.1.call-update) | async-done | bytes 8388624 | tf_op jit(solution)/shard_map/all_gather | solution.py:145
  246.1 8.2 fusion.307
  256.8 10.0 fusion.17
  266.8 23.2 %fusion.13 = (f32[4,512]{1,0:T(4,128)S(1)}, f32[4,512]{1,0:T(4,128)S(1)}, f32[4,512]{1,0:T(4,128)S(1)}, f32[4,512]{1,0:T(4,128)S(1)}, f32[4,512,2048]{2,1,0:T(8,128)}) fusion(f32[4,512,2048]{2,1,0:T(8,128)} %get-tuple-element.102, f32[4,512]{1,0:T(4,128)S(1)} %get-tuple-element.101, pred[2048]{0:T(1024)(128)(4,1)S(1)} %iota_compare_fusion.3, ...), kind=kOutput, calls=%fused_computation.37 | convolution fusion | flops 591388672 | bytes 68462592 | tf_op jit(solution)/shard_map/qhe,khe->hqk/dot_general | solution.py:48
  290.0 15.2 fusion.14
  305.2 8.7 fusion.179
  319.4 10.7 fusion.181
  331.5 9.1 fusion.180
  345.9 28.3 %multiply_convert_fusion.4 = (bf16[512,4096]{1,0:T(8,128)(2,1)}, f32[512,4096]{1,0:T(8,128)}, f32[512,4096]{1,0:T(8,128)}) fusion(f32[4096]{0:T(1024)S(1)} %copy-done.89, bf16[1024,4096]{1,0:T(8,128)(2,1)} %all-gather.25.cloned.1.call-done, f32[512,1024]{1,0:T(8,128)} %copy-done.15, f32[1024]{0:T(1024)S(1)} %copy-done.111, f32[1024]{0:T(1024)S(1)} %copy-done.100, ...), kind=kOutput, calls=%fused_computation.69 | convolution fusion | flops 4436000768 | bytes 31485952 | tf_op jit(solution)/shard_map/dot_general | solution.py:28
  374.2 14.3 fusion.304
  388.5 10.0 multiply_reduce_fusion.6
  410.6 9.2 fusion.309
  419.8 9.0 fusion.147
  449.9 8.9 fusion.153
  458.8 8.2 fusion.312
  471.7 24.6 %fusion.159 = bf16[4,64,2048]{2,1,0:T(8,128)(2,1)} fusion(bf16[512,4,64]{0,2,1:T(8,128)(2,1)S(1)} %bitcast.246, f32[4,512,2048]{2,1,0:T(8,128)} %fusion.312, f32[4,512,2048]{2,1,0:T(8,128)} %copy-done.2, f32[4,512]{1,0:T(4,128)S(1)} %get-tuple-element.111, pred[2048]{0:T(1024)(128)(4,1)S(1)} %iota_compare_fusion.3), kind=kOutput, calls=%fused_computation.143 | convolution fusion | flops 583536640 | bytes 34875392 | tf_op jit(solution)/shard_map/hqk,qhe->khe/dot_general | solution.py:228
  496.3 24.8 %fusion.162 = bf16[4,64,2048]{2,1,0:T(8,128)(2,1)} fusion(bf16[512,4,64]{0,2,1:T(8,128)(2,1)S(1)} %bitcast.242, f32[4,512,2048]{2,1,0:T(8,128)} %fusion.311, f32[4,512,2048]{2,1,0:T(8,128)} %fusion.307, f32[4,512]{1,0:T(4,128)S(1)} %get-tuple-element.112, pred[2048]{0:T(1024)(128)(4,1)S(1)} %iota_compare_fusion.3), kind=kOutput, calls=%fused_computation.144 | convolution fusion | flops 583536640 | bytes 34875392 | tf_op jit(solution)/shard_map/hqk,qhe->khe/dot_general | solution.py:228
  521.1 24.6 %fusion.165 = bf16[4,64,2048]{2,1,0:T(8,128)(2,1)} fusion(bf16[512,4,64]{0,2,1:T(8,128)(2,1)S(1)} %bitcast.270, f32[4,512,2048]{2,1,0:T(8,128)} %fusion.310, f32[4,512,2048]{2,1,0:T(8,128)} %get-tuple-element.103, f32[4,512]{1,0:T(4,128)S(1)} %get-tuple-element.113, pred[2048]{0:T(1024)(128)(4,1)S(1)} %iota_compare_fusion.3), kind=kOutput, calls=%fused_computation.145 | convolution fusion | flops 583536640 | bytes 34875392 | tf_op jit(solution)/shard_map/hqk,qhe->khe/dot_general | solution.py:228
  545.7 24.6 %fusion.168 = bf16[4,64,2048]{2,1,0:T(8,128)(2,1)} fusion(bf16[512,4,64]{0,2,1:T(8,128)(2,1)S(1)} %bitcast.244, f32[4,512,2048]{2,1,0:T(8,128)} %fusion.309, f32[4,512,2048]{2,1,0:T(8,128)} %get-tuple-element.102, f32[4,512]{1,0:T(4,128)S(1)} %get-tuple-element.114, pred[2048]{0:T(1024)(128)(4,1)S(1)} %iota_compare_fusion.3), kind=kOutput, calls=%fused_computation.146 | convolution fusion | flops 583536640 | bytes 34875392 | tf_op jit(solution)/shard_map/hqk,qhe->khe/dot_general | solution.py:228
  586.7 9.8 convolution_convert_fusion.2
  597.9 9.4 convolution_convert_fusion.1
  608.7 29.8 %fusion.191 = bf16[4,64,512]{2,1,0:T(8,128)(2,1)S(1)} fusion(bf16[2048,4,64]{0,2,1:T(8,128)(2,1)S(1)} %bitcast.227, f32[4,512,2048]{2,1,0:T(8,128)} %fusion.309, f32[4,512,2048]{2,1,0:T(8,128)} %get-tuple-element.102, f32[4,512]{1,0:T(4,128)S(1)} %get-tuple-element.114, pred[2048]{0:T(1024)(128)(4,1)S(1)} %iota_compare_fusion.3), kind=kOutput, calls=%fused_computation.185 | convolution fusion | flops 583143424 | bytes 34875392 | tf_op jit(solution)/shard_map/hqk,khe->qhe/dot_general | solution.py:223
  639.2 28.0 %fusion.188 = bf16[4,64,512]{2,1,0:T(8,128)(2,1)S(1)} fusion(bf16[2048,4,64]{0,2,1:T(8,128)(2,1)S(1)} %bitcast.258, f32[4,512,2048]{2,1,0:T(8,128)} %fusion.310, f32[4,512,2048]{2,1,0:T(8,128)} %get-tuple-element.103, f32[4,512]{1,0:T(4,128)S(1)} %get-tuple-element.113, pred[2048]{0:T(1024)(128)(4,1)S(1)} %iota_compare_fusion.3), kind=kOutput, calls=%fused_computation.184 | convolution fusion | flops 583143424 | bytes 34875392 | tf_op jit(solution)/shard_map/hqk,khe->qhe/dot_general | solution.py:223
  668.0 29.5 %fusion.185 = bf16[4,64,512]{2,1,0:T(8,128)(2,1)S(1)} fusion(bf16[2048,4,64]{0,2,1:T(8,128)(2,1)S(1)} %bitcast.225, f32[4,512,2048]{2,1,0:T(8,128)} %fusion.311, f32[4,512,2048]{2,1,0:T(8,128)} %fusion.307, f32[4,512]{1,0:T(4,128)S(1)} %get-tuple-element.112, pred[2048]{0:T(1024)(128)(4,1)S(1)} %iota_compare_fusion.3), kind=kOutput, calls=%fused_computation.183 | convolution fusion | flops 583143424 | bytes 34875392 | tf_op jit(solution)/shard_map/hqk,khe->qhe/dot_general | solution.py:223
  698.3 27.7 %fusion.182 = bf16[4,64,512]{2,1,0:T(8,128)(2,1)S(1)} fusion(bf16[2048,4,64]{0,2,1:T(8,128)(2,1)S(1)} %bitcast.223, f32[4,512,2048]{2,1,0:T(8,128)} %fusion.312, f32[4,512,2048]{2,1,0:T(8,128)} %copy-done.2, f32[4,512]{1,0:T(4,128)S(1)} %get-tuple-element.111, pred[2048]{0:T(1024)(128)(4,1)S(1)} %iota_compare_fusion.3), kind=kOutput, calls=%fused_computation.182 | convolution fusion | flops 583143424 | bytes 34875392 | tf_op jit(solution)/shard_map/hqk,khe->qhe/dot_general | solution.py:223
  745.1 8.2 convolution_convert_fusion
  753.4 10.8 multiply_reduce_fusion.4
  768.2 10.2 fusion.175
  781.8 10.5 convolution_convert_fusion.9
  818.7 9.0 convolution_convert_fusion.5
  827.8 22.3 %psum.140 = f32[1]{0:T(128)} all-reduce(f32[1]{0:T(128)S(6)} %convert_element_type.315), channel_id=1, replica_groups=mesh['grp'=8,'fsdp'=4] {'grp'}, use_global_device_ids=true, to_apply=%region_26.27 | all-reduce | flops 1 | bytes 8 | tf_op jit(solution)/shard_map/psum | solution.py:90
  862.6 11.0 all-reduce.19.cloned.1.call-done
  875.2 32.3 %reduce-scatter.18.cloned.1.call-done = bf16[256,1024]{1,0:T(8,128)(2,1)} async-done(((bf16[1024,1024]{1,0:T(8,128)(2,1)}), bf16[256,1024]{1,0:T(8,128)(2,1)}) %reduce-scatter.18.cloned.1.call-update) | async-done | bytes 524304 | tf_op jit(solution)/shard_map/reduce_scatter | solution.py:326
  909.7 31.7 %reduce-scatter.20.cloned.1.call-done = bf16[256,1024]{1,0:T(8,128)(2,1)} async-done(((bf16[1024,1024]{1,0:T(8,128)(2,1)}), bf16[256,1024]{1,0:T(8,128)(2,1)}) %reduce-scatter.20.cloned.1.call-update) | async-done | bytes 524304 | tf_op jit(solution)/shard_map/reduce_scatter | solution.py:329
  943.6 31.8 %reduce-scatter.14.cloned.1.call-done = bf16[256,1024]{1,0:T(8,128)(2,1)} async-done(((bf16[1024,1024]{1,0:T(8,128)(2,1)}), bf16[256,1024]{1,0:T(8,128)(2,1)}) %reduce-scatter.14.cloned.1.call-update) | async-done | bytes 524304 | tf_op jit(solution)/shard_map/reduce_scatter | solution.py:320
  977.5 31.7 %reduce-scatter.16.cloned.1.call-done = bf16[256,1024]{1,0:T(8,128)(2,1)} async-done(((bf16[1024,1024]{1,0:T(8,128)(2,1)}), bf16[256,1024]{1,0:T(8,128)(2,1)}) %reduce-scatter.16.cloned.1.call-update) | async-done | bytes 524304 | tf_op jit(solution)/shard_map/reduce_scatter | solution.py:323
  1011.4 59.0 %reduce-scatter.22.cloned.1.call-done = bf16[256,3072]{1,0:T(8,128)(2,1)} async-done(((bf16[1024,3072]{1,0:T(8,128)(2,1)}), bf16[256,3072]{1,0:T(8,128)(2,1)}) %reduce-scatter.22.cloned.1.call-update) | async-done | bytes 1572880 | tf_op jit(solution)/shard_map/reduce_scatter | solution.py:341
  1075.9 10.7 add_convert_fusion.2
  1090.6 8.6 fusion
  1100.6 12.6 all-reduce.15
  1118.5 42.4 %all-reduce.13 = (f32[12,1024]{1,0:T(8,128)}, f32[256]{0:T(256)}, f32[256]{0:T(256)}, f32[256]{0:T(256)}, f32[256]{0:T(256)}, /*index=5*/f32[256]{0:T(256)}, f32...) all-reduce(f32[12,1024]{1,0:T(8,128)S(1)} %convert_multiply_fusion., ...), channel_id=1, replica_groups=mesh['grp'=8,'fsdp'=4] {'grp'}, use_global_device_ids=true, to_apply=%region_30.31 | all-reduce | flops 15360 | bytes 122880 | tf_op jit(solution)/shard_map/psum | solution.py:370
  1161.0 444.0 %all-reduce.21.cloned.1.call-done = (f32[12,4,1024]{2,1,0:T(4,128)}, f32[256,1024]{1,0:T(8,128)}, f32[256,1024]{1,0:T(8,128)}, f32[256,1024]{1,0:T(8,128)}, f32[...) async-done(((f32[12,4,1024]{2,1,0:T(4,128)}, f32[256,1024]{1,0:T(8,128)}, ...) | async-done | bytes 16973840 | tf_op jit(solution)/shard_map/psum | solution.py:370
  (453 shorter events, 261.1 us)
Async XLA Ops:
  7.2 25.0 %copy-start.115 = (s32[1,48]{1,0:T(1,128)S(1)}, s32[1,48]{1,0:T(1,128)}, u32[]{:S(2)}) copy-start(s32[1,48]{1,0:T(1,128)} %param.27) | copy-start | bytes 580
  7.2 29.8 %all-gather.11.cloned.1.call-start = ((), (), s32[]{:S(2)}) async-start(), calls=%async_computation.9 | async-start | bytes 2621440 | tf_op jit(solution)/shard_map/all_gather | solution.py:103
  8.0 54.1 %all-gather.13.cloned.1.call-start = ((), (), s32[]{:S(2)}) async-start(), calls=%async_computation.10 | async-start | bytes 2621440 | tf_op jit(solution)/shard_map/all_gather | solution.py:104
  10.1 76.2 %all-gather.15.cloned.1.call-start = ((), (), s32[]{:S(2)}) async-start(), calls=%async_computation.11 | async-start | bytes 2621440 | tf_op jit(solution)/shard_map/all_gather | solution.py:105
  10.8 99.5 %all-gather.17.cloned.1.call-start = ((), (), s32[]{:S(2)}) async-start(), calls=%async_computation.12 | async-start | bytes 2621440 | tf_op jit(solution)/shard_map/all_gather | solution.py:106
  11.4 146.7 %all-gather.19.cloned.1.call-start = ((), (), s32[]{:S(2)}) async-start(), calls=%async_computation.13 | async-start | bytes 7864320 | tf_op jit(solution)/shard_map/all_gather | solution.py:137
  12.0 214.6 %all-gather.21.cloned.1.call-start = ((), (), s32[]{:S(2)}) async-start(), calls=%async_computation.14 | async-start | bytes 10485760 | tf_op jit(solution)/shard_map/all_gather | solution.py:145
  31.6 39.2 %copy-start.17 = (bf16[48,5120]{1,0:T(8,128)(2,1)}, bf16[48,5120]{1,0:T(8,128)(2,1)S(1)}, u32[]{:S(2)}) copy-start(bf16[48,5120]{1,0:T(8,128)(2,1)S(1)} %convolution_convert_fusion.4) | copy-start | bytes 1474564
  32.1 57.2 %copy-start.65 = (bf16[48,5,1024]{2,1,0:T(8,128)(2,1)}, bf16[48,5,1024]{2,1,0:T(8,128)(2,1)S(1)}, u32[]{:S(2)}) copy-start(bf16[48,5,1024]{2,1,0:T(8,128)(2,1)S(1)} %reshape.356) | copy-start | bytes 1474564
  32.2 38.6 %copy-start.18 = (bf16[48,5,512]{2,0,1:T(8,128)(2,1)}, bf16[48,5,512]{2,0,1:T(8,128)(2,1)S(1)}, u32[]{:S(2)}) copy-start(bf16[48,5,512]{2,0,1:T(8,128)(2,1)S(1)} %get-tuple-element.93) | copy-start | bytes 737284
  32.2 57.1 %copy-start.68 = (f32[48,5,512]{2,0,1:T(8,128)}, f32[48,5,512]{2,0,1:T(8,128)S(1)}, u32[]{:S(2)}) copy-start(f32[48,5,512]{2,0,1:T(8,128)S(1)} %get-tuple-element.94) | copy-start | bytes 1474564
  99.4 58.7 %copy-start.97 = (f32[1024]{0:T(1024)S(1)}, f32[1024]{0:T(1024)}, u32[]{:S(2)}) copy-start(f32[1024]{0:T(1024)} %param.38) | copy-start | bytes 12292
  99.4 58.7 %copy-start.112 = (f32[1024]{0:T(1024)S(1)}, f32[1024]{0:T(1024)}, u32[]{:S(2)}) copy-start(f32[1024]{0:T(1024)} %param.39) | copy-start | bytes 12292
  108.3 56.6 %copy-start.53 = (bf16[16,512,64]{1,2,0:T(8,128)(2,1)}, bf16[16,512,64]{1,2,0:T(8,128)(2,1)S(1)}, u32[]{:S(2)}) copy-start(bf16[16,512,64]{1,2,0:T(8,128)(2,1)S(1)} %convolution_convert_fusion.10) | copy-start | bytes 3145732
  113.3 51.7 %copy-start.7 = (f32[512,1024]{1,0:T(8,128)}, f32[512,1024]{1,0:T(8,128)S(1)}, u32[]{:S(2)}) copy-start(f32[512,1024]{1,0:T(8,128)S(1)} %get-tuple-element.100) | copy-start | bytes 6291460
  113.3 51.6 %copy-start.85 = (f32[512]{0:T(512)}, f32[512]{0:T(512)S(1)}, u32[]{:S(2)}) copy-start(f32[512]{0:T(512)S(1)} %broadcast_multiply_fusion.1) | copy-start | bytes 6148
  114.5 50.4 %copy-start.93 = (f32[512]{0:T(512)}, f32[512]{0:T(512)S(1)}, u32[]{:S(2)}) copy-start(f32[512]{0:T(512)S(1)} %fusion.220) | copy-start | bytes 6148
  168.1 172.5 %all-gather.23.cloned.1.call-start = ((), (), s32[]{:S(2)}) async-start(), calls=%async_computation.15 | async-start | bytes 2621440 | tf_op jit(solution)/shard_map/all_gather | solution.py:138
  168.9 177.0 %all-gather.25.cloned.1.call-start = ((), (), s32[]{:S(2)}) async-start(), calls=%async_computation.16 | async-start | bytes 10485760 | tf_op jit(solution)/shard_map/all_gather | solution.py:139
  169.6 204.6 %all-gather.27.cloned.1.call-start = ((), (), s32[]{:S(2)}) async-start(), calls=%async_computation.17 | async-start | bytes 10485760 | tf_op jit(solution)/shard_map/all_gather | solution.py:140
  170.4 556.3 %reduce-scatter.12.cloned.1.call-start = ((), (), s32[]{:S(2)}) async-start(), calls=%async_computation.18 | async-start | bytes 10485760 | tf_op jit(solution)/shard_map/reduce_scatter | solution.py:241
  179.0 67.1 %copy-start.44 = (bf16[512,256]{0,1:T(8,128)(2,1)}, bf16[512,256]{0,1:T(8,128)(2,1)S(1)}, u32[]{:S(2)}) copy-start(bf16[512,256]{0,1:T(8,128)(2,1)S(1)} %copy.177) | copy-start | bytes 786436
  180.8 75.9 %copy-start.46 = (bf16[512,256]{0,1:T(8,128)(2,1)}, bf16[512,256]{0,1:T(8,128)(2,1)S(1)}, u32[]{:S(2)}) copy-start(bf16[512,256]{0,1:T(8,128)(2,1)S(1)} %copy.171) | copy-start | bytes 786436
  256.7 57.2 %copy-start.2 = (f32[4,512,2048]{2,1,0:T(8,128)}, f32[4,512,2048]{2,1,0:T(8,128)S(1)}, u32[]{:S(2)}) copy-start(f32[4,512,2048]{2,1,0:T(8,128)S(1)} %fusion.308) | copy-start | bytes 50331652
  345.9 28.4 %copy-start.82 = (f32[512]{0:T(512)S(1)}, f32[512]{0:T(512)}, u32[]{:S(2)}) copy-start(f32[512]{0:T(512)} %fusion.219) | copy-start | bytes 6148
  545.7 31.8 %copy-start.61 = (bf16[4,64,2048]{2,1,0:T(8,128)(2,1)S(1)}, bf16[4,64,2048]{2,1,0:T(8,128)(2,1)}, u32[]{:S(2)}) copy-start(bf16[4,64,2048]{2,1,0:T(8,128)(2,1)} %fusion.159) | copy-start | bytes 3145732
  582.8 269.2 %reduce-scatter.24.cloned.1.call-start = ((), (), s32[]{:S(2)}) async-start(), calls=%async_computation.24 | async-start | bytes 2621440 | tf_op jit(solution)/shard_map/reduce_scatter | solution.py:344
  586.6 267.5 %reduce-scatter.26.cloned.1.call-start = ((), (), s32[]{:S(2)}) async-start(), calls=%async_computation.25 | async-start | bytes 10485760 | tf_op jit(solution)/shard_map/reduce_scatter | solution.py:356
  596.5 261.8 %reduce-scatter.28.cloned.1.call-start = ((), (), s32[]{:S(2)}) async-start(), calls=%async_computation.26 | async-start | bytes 10485760 | tf_op jit(solution)/shard_map/reduce_scatter | solution.py:362
  607.4 31.8 %copy-start.55 = (bf16[2048,256]{0,1:T(8,128)(2,1)S(1)}, bf16[2048,256]{0,1:T(8,128)(2,1)}, u32[]{:S(2)}) copy-start(bf16[2048,256]{0,1:T(8,128)(2,1)} %copy.175) | copy-start | bytes 3145732
  607.4 266.2 %all-reduce.19.cloned.1.call-start = ((), (), s32[]{:S(2)}) async-start(), calls=%async_computation.27 | async-start | bytes 786432
  639.2 28.8 %copy-start.23 = (bf16[2048,256]{0,1:T(8,128)(2,1)S(1)}, bf16[2048,256]{0,1:T(8,128)(2,1)}, u32[]{:S(2)}) copy-start(bf16[2048,256]{0,1:T(8,128)(2,1)} %copy-done.22) | copy-start | bytes 3145732
  668.0 30.3 %copy-start.21 = (bf16[2048,256]{0,1:T(8,128)(2,1)S(1)}, bf16[2048,256]{0,1:T(8,128)(2,1)}, u32[]{:S(2)}) copy-start(bf16[2048,256]{0,1:T(8,128)(2,1)} %copy-done.20) | copy-start | bytes 3145732
  698.3 31.5 %copy-start.9 = (f32[512,1024]{1,0:T(8,128)S(1)}, f32[512,1024]{1,0:T(8,128)}, u32[]{:S(2)}) copy-start(f32[512,1024]{1,0:T(8,128)} %copy-done.7) | copy-start | bytes 6291460
  698.3 31.5 %copy-start.81 = (f32[1024]{0:T(1024)S(1)}, f32[1024]{0:T(1024)}, u32[]{:S(2)}) copy-start(f32[1024]{0:T(1024)} %param.37) | copy-start | bytes 12292
  698.3 31.5 %copy-start.86 = (f32[512]{0:T(512)S(1)}, f32[512]{0:T(512)}, u32[]{:S(2)}) copy-start(f32[512]{0:T(512)} %copy-done.85) | copy-start | bytes 6148
  698.3 31.5 %copy-start.94 = (f32[512]{0:T(512)S(1)}, f32[512]{0:T(512)}, u32[]{:S(2)}) copy-start(f32[512]{0:T(512)} %copy-done.93) | copy-start | bytes 6148
  698.3 31.5 %copy-start.98 = (f32[1024]{0:T(1024)S(1)}, f32[1024]{0:T(1024)}, u32[]{:S(2)}) copy-start(f32[1024]{0:T(1024)} %param.38) | copy-start | bytes 12292
  781.7 125.9 %reduce-scatter.18.cloned.1.call-start = ((), (), s32[]{:S(2)}) async-start(), calls=%async_computation.21 | async-start | bytes 2621440 | tf_op jit(solution)/shard_map/reduce_scatter | solution.py:326
  796.3 145.1 %reduce-scatter.20.cloned.1.call-start = ((), (), s32[]{:S(2)}) async-start(), calls=%async_computation.22 | async-start | bytes 2621440 | tf_op jit(solution)/shard_map/reduce_scatter | solution.py:329
  800.6 174.8 %reduce-scatter.14.cloned.1.call-start = ((), (), s32[]{:S(2)}) async-start(), calls=%async_computation.19 | async-start | bytes 2621440 | tf_op jit(solution)/shard_map/reduce_scatter | solution.py:320
  806.0 203.2 %reduce-scatter.16.cloned.1.call-start = ((), (), s32[]{:S(2)}) async-start(), calls=%async_computation.20 | async-start | bytes 2621440 | tf_op jit(solution)/shard_map/reduce_scatter | solution.py:323
  818.6 32.1 %copy-start.108 = (u32[32]{0:T(128)S(1)}, u32[32]{0:T(128)}, u32[]{:S(2)}) copy-start(u32[32]{0:T(128)} %constant.117) | copy-start | bytes 388
  818.7 251.7 %reduce-scatter.22.cloned.1.call-start = ((), (), s32[]{:S(2)}) async-start(), calls=%async_computation.23 | async-start | bytes 7864320 | tf_op jit(solution)/shard_map/reduce_scatter | solution.py:341
  827.7 777.2 %all-reduce.21.cloned.1.call-start = ((), (), s32[]{:S(2)}) async-start(), calls=%async_computation.28 | async-start | bytes 33947648 | tf_op jit(solution)/shard_map/psum | solution.py:370
  1075.8 38.5 %copy-start.43 = (f32[48,5,16]{2,1,0:T(8,128)S(1)}, f32[48,5,16]{2,1,0:T(8,128)}, u32[]{:S(2)}) copy-start(f32[48,5,16]{2,1,0:T(8,128)} %copy-done.42) | copy-start | bytes 46084
  1075.8 38.5 %copy-start.72 = (f32[16,512]{1,0:T(8,128)S(1)}, f32[16,512]{1,0:T(8,128)}, u32[]{:S(2)}) copy-start(f32[16,512]{1,0:T(8,128)} %copy-done.71) | copy-start | bytes 98308
  1099.2 19.1 %collective-permute-start = (bf16[12,1024]{1,0:T(8,128)(2,1)S(1)}, bf16[12,1024]{1,0:T(8,128)(2,1)S(1)}, u32[]{:S(2)}, u32[]{:S(2)}) collective-permute-start(bf16[12,1024]{1,0:T(8,128)(2,1)S(1)} %slice.115), channel_id=1, source_target_pairs={{0,1},{1,2},{2,3},{4,5},{5,6},{6,7},{8,9},{9,10},{10,11},{12,13},{... | collective-permute-start | bytes 73736
  (100 other events, 980.2 us)
Sparse Core Ops, SparseCore 0:
  9.6 27.3 all-gather.10
  39.2 22.8 all-gather.12
  63.6 22.5 all-gather.14
  87.6 22.5 all-gather.16
  111.7 46.3 all-gather.18
  168.3 58.2 all-gather.20
  228.1 22.5 all-gather.22
  252.3 58.2 all-gather.24
  312.2 58.2 all-gather.26
  583.0 72.3 reduce-scatter.11
  658.0 31.4 reduce-scatter.23
  691.9 71.7 reduce-scatter.25
  766.4 71.6 reduce-scatter.27
  841.0 32.6 all-reduce.18
  876.1 31.3 reduce-scatter.17
  910.0 31.4 reduce-scatter.19
  944.0 31.3 reduce-scatter.13
  977.8 31.4 reduce-scatter.15
  1011.9 58.3 reduce-scatter.21
  1078.3 526.6 all-reduce.20
where the time goes:
time: 1640 us; the launch traced here: 1630 us
  waiting for transfers between devices  780 us (48%)
  matrix products  552 us (34%)
  local copies, waits for them, and re-layouts  112 us (7%)
  blocking collectives  107 us (7%)
  other arithmetic  56.3 us (3%)
  between operations  20.9 us (1%)
    psum x1, waiting for transfers between devices, on_device(): lax.psum((shards[0] * count_share, shards[1] * count_share, shards[2] * c...  444 us
    dot_general x4, matrix products, on_device(): jnp.einsum('hqk,khe->qhe', raw_grad, key_part, preferred_element_type=jnp...  115 us
    dot_general x4, matrix products, on_device(): jnp.einsum('hqk,qhe->khe', raw_grad, query_part, preferred_element_type=j...  98.6 us
    reduce_scatter x1, waiting for transfers between devices, on_device(): lax.psum_scatter(qkv_weight_grad.astype(jnp.bfloat16), 'fsdp', scatter_di...  59 us
    dot_general x8, matrix products, product(): return jnp.dot(left_side, right_side, preferred_element_type=jnp.float32)  56.7 us
    unnamed x280, local copies, waits for them, and re-layouts  51.5 us
    all_gather x1, waiting for transfers between devices, on_device(): lax.all_gather(qkv_rows[:, model_width:], 'fsdp', axis=0, tiled=True)  45.8 us
    dot_general x4, matrix products, block_logits(): jnp.einsum('qhe,khe->hqk', query_part, key_part, preferred_element_type=j...  43.8 us
  transfers between devices with their start and end apart: 21, of which 13 were waited for; matrix products, arithmetic and copies ran while one was open for 29% of the time, Pallas kernels for 0%

commit v1 on v0

v1 whole, which is shorter than its diff:
```python
import functools

import jax
import jax.numpy as jnp
from jax import lax
from jax.experimental import pallas as pl
from jax.experimental.pallas import tpu as pltpu
from jax.sharding import PartitionSpec as P

HEADS = 16
VTOT = 48
PIX = 4

exact_mode = lax.Precision.HIGHEST
masked_out = -1e30
VMEM_LIMIT = 56 * 1024 * 1024


def swap(value, axis, bit):
    size = lax.axis_size(axis)
    return lax.ppermute(value, axis, [(i, i ^ bit) for i in range(size)])


def has_bit(axis, bit):
    return (lax.axis_index(axis) // bit) % 2 == 1


def merge(mine, other, axis, bit):
    return jnp.where(
        has_bit(axis, bit),
        jnp.concatenate([other, mine], axis=0),
        jnp.concatenate([mine, other], axis=0),
    )


def product(left_side, right_side):
    return jnp.dot(left_side, right_side, preferred_element_type=jnp.float32)


def left_product(left_side, right_side):
    return lax.dot_general(
        left_side, right_side, (((0,), (0,)), ((), ())), preferred_element_type=jnp.float32
    )


def right_product(left_side, right_side):
    return lax.dot_general(
        left_side, right_side, (((1,), (1,)), ((), ())), preferred_element_type=jnp.float32
    )


def column_sums(values_in):
    return jnp.sum(values_in.astype(jnp.float32), axis=0)


def gather_far_half(own):
    rows = own.shape[0]
    half = rows // 2
    which = lax.axis_index("grp") % 2
    sent = lax.dynamic_slice_in_dim(own, which * half, half, 0)
    got = swap(sent, "fsdp", 2)
    rest = swap(got, "grp", 1)
    return merge(got, rest, "grp", 1)


def gather_far_eighth(own):
    rows = own.shape[0]
    part = rows // 8
    which = lax.axis_index("grp") % 8
    sent = lax.dynamic_slice_in_dim(own, which * part, part, 0)
    got = swap(sent, "fsdp", 2)[None]
    for bit in (2, 4):
        got = merge(got, swap(got, "grp", bit), "grp", bit)
    rest = swap(got, "grp", 1)
    odd = has_bit("grp", 1)
    both = jnp.where(odd, jnp.stack([rest, got], axis=1), jnp.stack([got, rest], axis=1))
    return both.reshape(own.shape)


def four_shards(own, far):
    return [own, swap(own, "fsdp", 1), far, swap(far, "fsdp", 1)]


def in_order(shards, axis=0):
    me = lax.axis_index("fsdp")
    size = shards[0].shape[axis]
    shape = list(shards[0].shape)
    shape[axis] = size * len(shards)
    whole = jnp.zeros(shape, shards[0].dtype)
    for j, shard in enumerate(shards):
        whole = lax.dynamic_update_slice_in_dim(whole, shard, (me ^ j) * size, axis)
    return whole


def reduce_gradient(quarter, share):
    def low(value):
        return value.astype(jnp.bfloat16)

    sent = jnp.stack([low(quarter(1) * share), low(quarter(3) * share)])
    got = swap(sent, "fsdp", 1)
    far = swap(low(quarter(2) * share + got[1].astype(jnp.float32)), "fsdp", 2)
    held = low(quarter(0) * share + got[0].astype(jnp.float32) + far.astype(jnp.float32))
    return reduce_groups(held)


def group_bits():
    bits = []
    bit = 1
    while bit < lax.axis_size("grp"):
        bits.append(bit)
        bit *= 2
    return bits


def halve(held, axis, bit):
    half = held.shape[0] // 2
    upper = has_bit(axis, bit).astype(jnp.int32)
    keep = lax.dynamic_slice_in_dim(held, upper * half, half, 0)
    give = lax.dynamic_slice_in_dim(held, (1 - upper) * half, half, 0)
    got = swap(give, axis, bit)
    return (keep.astype(jnp.float32) + got.astype(jnp.float32)).astype(held.dtype)


def reduce_groups(held):
    bits = group_bits()
    for bit in bits:
        held = halve(held, "grp", bit)
    for bit in reversed(bits):
        held = merge(held, swap(held, "grp", bit), "grp", bit)
    return held.astype(jnp.float32)


def slot_softmax(patch_ref, coeff_ref, mask_ref):
    scores = coeff_ref[0, PIX] + mask_ref[...]
    for k in range(PIX):
        scores = scores + patch_ref[k].astype(jnp.float32) * coeff_ref[0, k]
    top = jnp.max(scores, axis=0, keepdims=True)
    terms = jnp.exp(scores - top)
    return terms / jnp.sum(terms, axis=0, keepdims=True)


def mixed_of(patch_ref, weights):
    parts = [
        (weights * patch_ref[k].astype(jnp.float32)).astype(jnp.bfloat16) for k in range(PIX)
    ]
    parts.append(weights.astype(jnp.bfloat16))
    return jnp.concatenate(parts, axis=0)


def aggregate_kernel(patch_ref, coeff_ref, mask_ref, table_ref, out_ref):
    weights = slot_softmax(patch_ref, coeff_ref, mask_ref)
    mixed = mixed_of(patch_ref, weights)
    out_ref[...] = jnp.dot(
        table_ref[...], mixed, preferred_element_type=jnp.float32
    ).astype(jnp.bfloat16)


def aggregate(patch_rows, coeff_heads, slot_mask, table_values):
    rows = patch_rows.shape[2]
    width = table_values.shape[0]
    head_dim = width // HEADS
    slots = slot_mask.shape[0]
    return pl.pallas_call(
        aggregate_kernel,
        grid=(HEADS,),
        in_specs=[
            pl.BlockSpec((PIX, slots, rows), lambda h: (0, 0, 0)),
            pl.BlockSpec((1, PIX + 1, slots, 1), lambda h: (h, 0, 0, 0)),
            pl.BlockSpec((slots, 1), lambda h: (0, 0)),
            pl.BlockSpec((head_dim, (PIX + 1) * slots), lambda h: (h, 0)),
        ],
        out_specs=pl.BlockSpec((head_dim, rows), lambda h: (h, 0)),
        out_shape=jax.ShapeDtypeStruct((width, rows), jnp.bfloat16),
        compiler_params=pltpu.CompilerParams(vmem_limit_bytes=VMEM_LIMIT),
        cost_estimate=pl.CostEstimate(
            flops=2 * (PIX + 1) * slots * rows * width * 4,
            bytes_accessed=4 * width * rows,
            transcendentals=HEADS * slots * rows,
        ),
        name="aggregate",
    )(patch_rows, coeff_heads, slot_mask, table_values)


def aggregate_back_kernel(
    patch_ref, coeff_ref, mask_ref, table_ref, heads_ref, scale_ref, table_grad_ref, coeff_grad_ref, patch_grad_ref
):
    head = pl.program_id(0)
    slots = mask_ref.shape[0]
    weights = slot_softmax(patch_ref, coeff_ref, mask_ref)
    mixed = mixed_of(patch_ref, weights)
    heads_grad = heads_ref[...]
    table_grad_ref[...] = lax.dot_general(
        heads_grad, mixed, (((1,), (1,)), ((), ())), preferred_element_type=jnp.float32
    )
    mixed_grad = lax.dot_general(
        table_ref[...], heads_grad, (((0,), (0,)), ((), ())), preferred_element_type=jnp.float32
    )
    parts = [mixed_grad[k * slots : (k + 1) * slots] for k in range(PIX + 1)]
    values = [patch_ref[k].astype(jnp.float32) for k in range(PIX)]
    weights_grad = parts[PIX]
    for k in range(PIX):
        weights_grad = weights_grad + parts[k] * values[k]
    mean_grad = jnp.sum(weights * weights_grad, axis=0, keepdims=True)
    scores_grad = weights * (weights_grad - mean_grad)
    for k in range(PIX):
        coeff_grad_ref[0, k] = jnp.sum(scores_grad * values[k], axis=1, keepdims=True)
    coeff_grad_ref[0, PIX] = jnp.sum(scores_grad, axis=1, keepdims=True)

    @pl.when(head == 0)
    def _():
        patch_grad_ref[...] = jnp.zeros_like(patch_grad_ref)

    scale = scale_ref[0]
    for k in range(PIX):
        patch_grad_ref[k] += scale * (parts[k] * weights + scores_grad * coeff_ref[0, k])


def aggregate_back(patch_rows, coeff_heads, slot_mask, table_values, heads_grad, scale):
    rows = patch_rows.shape[2]
    width = table_values.shape[0]
    head_dim = width // HEADS
    slots = slot_mask.shape[0]
    return pl.pallas_call(
        aggregate_back_kernel,
        grid=(HEADS,),
        in_specs=[
            pl.BlockSpec((PIX, slots, rows), lambda h: (0, 0, 0)),
            pl.BlockSpec((1, PIX + 1, slots, 1), lambda h: (h, 0, 0, 0)),
            pl.BlockSpec((slots, 1), lambda h: (0, 0)),
            pl.BlockSpec((head_dim, (PIX + 1) * slots), lambda h: (h, 0)),
            pl.BlockSpec((head_dim, rows), lambda h: (h, 0)),
            pl.BlockSpec(memory_space=pltpu.SMEM),
        ],
        out_specs=[
            pl.BlockSpec((head_dim, (PIX + 1) * slots), lambda h: (h, 0)),
            pl.BlockSpec((1, PIX + 1, slots, 1), lambda h: (h, 0, 0, 0)),
            pl.BlockSpec((PIX, slots, rows), lambda h: (0, 0, 0)),
        ],
        out_shape=[
            jax.ShapeDtypeStruct((width, (PIX + 1) * slots), jnp.float32),
            jax.ShapeDtypeStruct((HEADS, PIX + 1, slots, 1), jnp.float32),
            jax.ShapeDtypeStruct((PIX, slots, rows), jnp.float32),
        ],
        compiler_params=pltpu.CompilerParams(vmem_limit_bytes=VMEM_LIMIT),
        cost_estimate=pl.CostEstimate(
            flops=4 * (PIX + 1) * slots * rows * width * 4,
            bytes_accessed=8 * width * rows,
            transcendentals=HEADS * slots * rows,
        ),
        name="aggregate_back",
    )(patch_rows, coeff_heads, slot_mask, table_values, heads_grad, scale)


def lane_half(rows, pair, head_dim):
    lane = lax.broadcasted_iota(jnp.int32, (rows, 2 * head_dim), 1)
    return (lane // head_dim) == pair


def attend_kernel(shards, head_dim, first, last, *refs):
    valid_ref, q_ref = refs[:2]
    keys = refs[2 : 2 + shards]
    values = refs[2 + shards : 2 + 2 * shards]
    rest = refs[2 + 2 * shards :]
    if not first:
        old_sum_ref, old_top_ref, old_total_ref = rest[:3]
        rest = rest[3:]
    rows = q_ref.shape[0]
    tile = min(rows, 256)
    scale = head_dim ** (-0.5)
    for start in range(0, rows, tile):
        block = q_ref[start : start + tile, :] * jnp.asarray(scale, jnp.bfloat16)
        sums, tops, totals = [], [], []
        for pair in range(2):
            side = lane_half(tile, pair, head_dim)
            query = jnp.where(side, block, jnp.zeros_like(block))
            logits = []
            for j in range(shards):
                raw = lax.dot_general(
                    query, keys[j][...], (((1,), (1,)), ((), ())), preferred_element_type=jnp.float32
                )
                place = lax.broadcasted_iota(jnp.int32, (1, raw.shape[1]), 1)
                logits.append(jnp.where(place < valid_ref[j], raw, masked_out))
            top = functools.reduce(
                jnp.maximum, [jnp.max(part, axis=1, keepdims=True) for part in logits]
            )
            total = 0.0
            weighted = 0.0
            for j in range(shards):
                terms = jnp.exp(logits[j] - top)
                total = total + jnp.sum(terms, axis=1, keepdims=True)
                weighted = weighted + jnp.dot(
                    terms.astype(jnp.bfloat16), values[j][...], preferred_element_type=jnp.float32
                )
            sums.append(weighted)
            tops.append(top)
            totals.append(total)
        side = lane_half(tile, 0, head_dim)
        weighted = jnp.where(side, sums[0], sums[1])
        top = jnp.where(side, tops[0], tops[1])
        total = jnp.where(side, totals[0], totals[1])
        at = slice(start, start + tile)
        if not first:
            old_top = old_top_ref[at, :]
            new_top = jnp.maximum(top, old_top)
            mine = jnp.exp(top - new_top)
            others = jnp.exp(old_top - new_top)
            weighted = weighted * mine + old_sum_ref[at, :] * others
            total = total * mine + old_total_ref[at, :] * others
            top = new_top
        if last:
            rest[0][at, :] = (weighted / total).astype(jnp.bfloat16)
            rest[1][at, :] = top + jnp.log(total)
        else:
            rest[0][at, :] = weighted
            rest[1][at, :] = top
            rest[2][at, :] = total


def attend(queries, key_values, valid, width, old=None, last=False):
    rows = queries.shape[0]
    head_dim = width // HEADS
    lanes = 2 * head_dim
    shards = len(key_values)
    whole = pl.BlockSpec((rows, lanes), lambda i: (0, i))

    def at(array, offset):
        start = offset // lanes
        return pl.BlockSpec((array.shape[0], lanes), lambda i: (0, start + i))

    in_specs = [pl.BlockSpec(memory_space=pltpu.SMEM), whole]
    in_specs += [at(array, k) for array, k, v in key_values]
    in_specs += [at(array, v) for array, k, v in key_values]
    operands = [valid, queries]
    operands += [array for array, k, v in key_values] * 2
    if old is not None:
        in_specs += [whole] * 3
        operands += list(old)
    wide = jax.ShapeDtypeStruct((rows, width), jnp.float32)
    if last:
        out_shape = [jax.ShapeDtypeStruct((rows, width), jnp.bfloat16), wide]
    else:
        out_shape = [wide] * 3
    length = sum(array.shape[0] for array, k, v in key_values)
    return pl.pallas_call(
        functools.partial(attend_kernel, shards, head_dim, old is None, last),
        grid=(HEADS // 2,),
        in_specs=in_specs,
        out_specs=[whole] * len(out_shape),
        out_shape=out_shape,
        compiler_params=pltpu.CompilerParams(vmem_limit_bytes=VMEM_LIMIT),
        cost_estimate=pl.CostEstimate(
            flops=4 * rows * length * width * 4,
            bytes_accessed=4 * length * width,
            transcendentals=HEADS * rows * length,
        ),
        name="attend",
    )(*operands)


def attend_back_kernel(shards, head_dim, first, *refs):
    valid_ref, q_ref, grad_ref, out_ref, log_ref = refs[:5]
    keys = refs[5 : 5 + shards]
    values = refs[5 + shards : 5 + 2 * shards]
    rest = refs[5 + 2 * shards :]
    old_ref = None
    if not first:
        old_ref, rest = rest[0], rest[1:]
    q_grad_ref = rest[0]
    k_grads = rest[1 : 1 + shards]
    v_grads = rest[1 + shards : 1 + 2 * shards]
    rows = q_ref.shape[0]
    lanes = 2 * head_dim
    scale = head_dim ** (-0.5)
    query = q_ref[...]
    grad = grad_ref[...]
    log_rows = jnp.transpose(log_ref[...])
    dots = jnp.transpose(grad.astype(jnp.float32) * out_ref[...].astype(jnp.float32))
    q_grad = jnp.zeros((rows, lanes), jnp.float32)
    k_sums = [0.0] * shards
    v_sums = [0.0] * shards
    for pair in range(2):
        side = lane_half(rows, pair, head_dim)
        here = slice(pair * head_dim, (pair + 1) * head_dim)
        log_row = log_rows[pair * head_dim : pair * head_dim + 1, :]
        dot_row = jnp.sum(dots[here, :], axis=0, keepdims=True)
        one_query = jnp.where(side, query, jnp.zeros_like(query))
        one_grad = jnp.where(side, grad, jnp.zeros_like(grad))
        scaled = one_query * jnp.asarray(scale, jnp.bfloat16)
        for j in range(shards):
            key = keys[j][...]
            one_key = jnp.where(lane_half(key.shape[0], pair, head_dim), key, jnp.zeros_like(key))
            raw = lax.dot_general(
                key, scaled, (((1,), (1,)), ((), ())), preferred_element_type=jnp.float32
            )
            place = lax.broadcasted_iota(jnp.int32, raw.shape, 0)
            probs = jnp.exp(jnp.where(place < valid_ref[j], raw - log_row, masked_out))
            probs_grad = lax.dot_general(
                values[j][...], one_grad, (((1,), (1,)), ((), ())), preferred_element_type=jnp.float32
            )
            raw_grad = (probs * (probs_grad - dot_row)).astype(jnp.bfloat16)
            v_sums[j] = v_sums[j] + jnp.dot(
                probs.astype(jnp.bfloat16), one_grad, preferred_element_type=jnp.float32
            )
            k_sums[j] = k_sums[j] + jnp.dot(raw_grad, scaled, preferred_element_type=jnp.float32)
            q_grad = q_grad + lax.dot_general(
                raw_grad, one_key, (((0,), (0,)), ((), ())), preferred_element_type=jnp.float32
            )
    q_grad = q_grad * scale
    if old_ref is not None:
        q_grad = q_grad + old_ref[...]
    q_grad_ref[...] = q_grad.astype(q_grad_ref.dtype)
    for j in range(shards):
        k_grads[j][...] = k_sums[j].astype(jnp.bfloat16)
        v_grads[j][...] = v_sums[j].astype(jnp.bfloat16)


def attend_back(queries, grad, out, logs, key_values, valid, old=None, last=False):
    rows, width = grad.shape
    head_dim = width // HEADS
    lanes = 2 * head_dim
    shards = len(key_values)
    whole = pl.BlockSpec((rows, lanes), lambda i: (0, i))

    def at(array, offset):
        start = offset // lanes
        return pl.BlockSpec((array.shape[0], lanes), lambda i: (0, start + i))

    in_specs = [pl.BlockSpec(memory_space=pltpu.SMEM), whole, whole, whole, whole]
    in_specs += [at(array, k) for array, k, v in key_values]
    in_specs += [at(array, v) for array, k, v in key_values]
    operands = [valid, queries, grad, out, logs]
    operands += [array for array, k, v in key_values] * 2
    if old is not None:
        in_specs.append(whole)
        operands.append(old)
    out_shape = [jax.ShapeDtypeStruct((rows, width), jnp.bfloat16 if last else jnp.float32)]
    out_shape += [
        jax.ShapeDtypeStruct((array.shape[0], width), jnp.bfloat16) for array, k, v in key_values
    ] * 2
    length = sum(array.shape[0] for array, k, v in key_values)
    result = pl.pallas_call(
        functools.partial(attend_back_kernel, shards, head_dim, old is None),
        grid=(HEADS // 2,),
        in_specs=in_specs,
        out_specs=[whole]
        + [
            pl.BlockSpec((array.shape[0], lanes), lambda i: (0, i)) for array, k, v in key_values
        ]
        * 2,
        out_shape=out_shape,
        compiler_params=pltpu.CompilerParams(vmem_limit_bytes=VMEM_LIMIT),
        cost_estimate=pl.CostEstimate(
            flops=10 * rows * length * width * 4,
            bytes_accessed=8 * length * width,
            transcendentals=HEADS * rows * length,
        ),
        name="attend_back",
    )(*operands)
    return result[0], result[1 : 1 + shards], result[1 + shards :]


def normalise(values_in):
    row_mean = jnp.mean(values_in, axis=-1, keepdims=True)
    centred = values_in - row_mean
    spread = jnp.mean(centred * centred, axis=-1, keepdims=True)
    inverse = lax.rsqrt(spread + 1e-05)
    return centred * inverse, inverse


def norm_back(grad, xhat, inverse, gain_vec):
    scaled = grad * gain_vec
    first = jnp.mean(scaled, axis=-1, keepdims=True)
    second = jnp.mean(scaled * xhat, axis=-1, keepdims=True)
    return (scaled - first - xhat * second) * inverse


def on_device(
    patches,
    patch_counts,
    var_present,
    item_dataset,
    var_ids,
    patch_weight,
    var_embed,
    agg_query,
    query_weight,
    key_weight,
    value_weight,
    agg_proj,
    agg_bias,
    norm1_gain,
    norm1_shift,
    qkv_weight,
    proj_weight,
    proj_bias,
    norm2_gain,
    norm2_shift,
    up_weight,
    up_bias,
    down_weight,
    down_bias,
    out_grad,
):
    low = jnp.bfloat16
    wide = jnp.float32
    rows = patches.shape[2]
    me = lax.axis_index("fsdp")
    group_count = lax.axis_size("grp")
    width = proj_weight.shape[1]
    head_dim = width // HEADS
    own_width = width // 4
    own_vars = patch_weight.shape[0]
    score_scale = head_dim ** (-0.5)

    counts = patch_counts.astype(wide)
    count_total = counts
    for bit in group_bits():
        count_total = count_total + swap(count_total, "grp", bit)
    count_share = counts[0] / count_total[0]
    item_count = patch_counts[0]
    own_valid = me * rows + jnp.arange(rows, dtype=jnp.int32) < item_count
    shard_valid = jnp.clip(
        item_count - (me ^ jnp.arange(4, dtype=jnp.int32)) * rows, 0, rows
    ).astype(jnp.int32)

    present = var_present[0] > 0
    slot_vars = lax.dynamic_index_in_dim(var_ids, item_dataset[0], 0, keepdims=False)
    selector = slot_vars[:, None] == jnp.arange(VTOT, dtype=jnp.int32)[None, :]
    own_rows = jnp.concatenate(
        [
            patch_weight.reshape(own_vars * PIX, width),
            var_embed,
            up_bias[None, :],
        ],
        axis=0,
    )
    near_rows = swap(own_rows, "fsdp", 1)
    far_rows = swap(jnp.stack([own_rows, near_rows]), "fsdp", 2)
    row_sets = [own_rows, near_rows, far_rows[0], far_rows[1]]
    table_parts = []
    for part in row_sets:
        pixels = part[: own_vars * PIX].reshape(own_vars, PIX, width)
        embeds = part[own_vars * PIX : own_vars * (PIX + 1)][:, None, :]
        table_parts.append(jnp.concatenate([pixels, embeds], axis=1).transpose(1, 0, 2))
    stacked = in_order(table_parts, axis=1)
    stacked_rows = stacked.reshape((PIX + 1) * VTOT, width)
    up_biases = [part[own_vars * (PIX + 1)].astype(wide) for part in row_sets]

    own_query = lax.dynamic_slice_in_dim(agg_query, me * own_width, own_width, 0)
    query_sum = product(own_query[None, :], query_weight)
    query_sum = query_sum + swap(query_sum, "fsdp", 1)
    query_sum = query_sum + swap(query_sum, "fsdp", 2)
    query_vec = query_sum[0].astype(low)
    own_key_query = (
        jnp.einsum(
            "dhj,hj->hd",
            key_weight.reshape(own_width, HEADS, head_dim),
            query_vec.reshape(HEADS, head_dim),
            preferred_element_type=wide,
        )
        * score_scale
    ).astype(low)
    near_key_query = swap(own_key_query, "fsdp", 1)
    far_key_query = swap(jnp.stack([own_key_query, near_key_query]), "fsdp", 2)
    key_query = in_order(
        [own_key_query, near_key_query, far_key_query[0], far_key_query[1]], axis=1
    )
    coeffs_by_var = right_product(key_query, stacked_rows).reshape(HEADS, PIX + 1, VTOT)
    coeff_heads = jnp.einsum(
        "hku,su->hks", coeffs_by_var, selector.astype(wide), precision=exact_mode
    )[..., None]

    value_shards = four_shards(value_weight, gather_far_half(value_weight))
    full_value = in_order(value_shards)
    table_by_var = left_product(full_value, stacked_rows.T).astype(low)
    table_values = (
        jnp.einsum(
            "hku,su->hks",
            table_by_var.reshape(width, PIX + 1, VTOT),
            selector.astype(low),
            preferred_element_type=wide,
        )
        .astype(low)
        .reshape(width, (PIX + 1) * VTOT)
    )
    own_table = lax.dynamic_slice_in_dim(stacked_rows, me * own_width, own_width, 1)
    key_table = product(own_table, key_weight)
    key_table = key_table + swap(key_table.astype(low), "fsdp", 1).astype(wide)
    key_table = key_table + swap(key_table.astype(low), "fsdp", 2).astype(wide)

    agg_proj_shards = four_shards(agg_proj, gather_far_half(agg_proj))
    full_agg_proj = in_order(agg_proj_shards)
    qkv_shards = four_shards(qkv_weight, gather_far_half(qkv_weight))
    full_qkv = in_order(qkv_shards)
    proj_shards = four_shards(proj_weight, gather_far_half(proj_weight))
    full_proj = in_order(proj_shards)
    up_shards = four_shards(up_weight, gather_far_eighth(up_weight))
    down_shards = four_shards(down_weight, gather_far_eighth(down_weight))

    patch_rows = patches.transpose(1, 0, 2)
    slot_mask = jnp.where(present, 0.0, masked_out).astype(wide)[:, None]
    heads_t = aggregate(patch_rows, coeff_heads, slot_mask, table_values)
    embedded = left_product(heads_t, full_agg_proj) + agg_bias
    xhat1, inverse1 = normalise(embedded)
    normed1 = (xhat1 * norm1_gain + norm1_shift).astype(low)
    qkv_rows = product(normed1, full_qkv).astype(low)
    kv_own = qkv_rows[:, width:]
    kv_near = swap(kv_own, "fsdp", 1)
    kv_far = swap(kv_own, "fsdp", 2)
    kv_last = swap(kv_far, "fsdp", 1)
    near_set = [(qkv_rows, width, 2 * width), (kv_near, 0, width)]
    far_set = [(kv_far, 0, width), (kv_last, 0, width)]
    partial_out = attend(qkv_rows, near_set, shard_valid[:2], width)
    context, logs = attend(qkv_rows, far_set, shard_valid[2:], width, old=partial_out, last=True)
    middle = embedded + (product(context, full_proj) + proj_bias)
    xhat2, inverse2 = normalise(middle)
    normed2 = (xhat2 * norm2_gain + norm2_shift).astype(low)
    gelu_parts = []
    slope_parts = []
    down_sum = 0.0
    for j in range(4):
        pre_act = product(normed2, up_shards[j]) + up_biases[j]
        cdf = 0.5 * (1.0 + lax.erf(pre_act * 0.7071067811865476))
        density = jnp.exp(-0.5 * pre_act * pre_act) * 0.3989422804014327
        gelu_parts.append((pre_act * cdf).astype(low))
        slope_parts.append(cdf + pre_act * density)
        down_sum = down_sum + product(gelu_parts[j], down_shards[j])
    output = (middle + down_sum + down_bias).astype(low)

    upstream = out_grad.astype(wide) * own_valid[:, None].astype(wide)
    down_grad = upstream.astype(low)
    down_bias_grad = column_sums(down_grad)
    down_weight_grad = reduce_gradient(
        lambda j: left_product(gelu_parts[j], down_grad), count_share
    )
    pre_grads = []
    up_bias_parts = []
    normed2_grad = 0.0
    for j in range(4):
        act_grad = right_product(down_grad, down_shards[j])
        pre_grads.append((act_grad * slope_parts[j]).astype(low))
        up_bias_parts.append(column_sums(pre_grads[j])[None, :])
        normed2_grad = normed2_grad + right_product(pre_grads[j], up_shards[j])
    up_bias_grad = in_order(up_bias_parts)
    up_weight_grad = reduce_gradient(lambda j: left_product(normed2, pre_grads[j]), count_share)
    norm2_gain_grad = jnp.sum(normed2_grad * xhat2, axis=0)
    norm2_shift_grad = jnp.sum(normed2_grad, axis=0)
    middle_grad = upstream + norm_back(normed2_grad, xhat2, inverse2, norm2_gain)
    attended_grad = middle_grad.astype(low)
    proj_bias_grad = column_sums(attended_grad)

    def columns(array, j):
        return lax.dynamic_slice_in_dim(array, (me ^ j) * own_width, own_width, 1)

    proj_weight_grad = reduce_gradient(
        lambda j: left_product(columns(context, j), attended_grad), count_share
    )
    context_grad = right_product(attended_grad, full_proj).astype(low)

    q_part, far_k, far_v = attend_back(
        qkv_rows, context_grad, context, logs, far_set, shard_valid[2:]
    )
    far_kv = [jnp.concatenate([far_k[i], far_v[i]], axis=1) for i in range(2)]
    far_got = swap(far_kv[1], "fsdp", 1)
    far_sum = (far_kv[0].astype(wide) + far_got.astype(wide)).astype(low)
    from_far = swap(far_sum, "fsdp", 2)
    q_grad, near_k, near_v = attend_back(
        qkv_rows, context_grad, context, logs, near_set, shard_valid[:2], old=q_part, last=True
    )
    near_kv = [jnp.concatenate([near_k[i], near_v[i]], axis=1) for i in range(2)]
    near_got = swap(near_kv[1], "fsdp", 1)
    kv_grad = (near_kv[0].astype(wide) + near_got.astype(wide) + from_far.astype(wide)).astype(low)
    qkv_grad = jnp.concatenate([q_grad, kv_grad], axis=1)
    normed1_grad = right_product(qkv_grad, full_qkv)
    norm1_gain_grad = jnp.sum(normed1_grad * xhat1, axis=0)
    norm1_shift_grad = jnp.sum(normed1_grad, axis=0)
    embedded_grad = (middle_grad + norm_back(normed1_grad, xhat1, inverse1, norm1_gain)).astype(low)
    agg_bias_grad = column_sums(embedded_grad)
    qkv_weight_grad = reduce_gradient(
        lambda j: left_product(columns(normed1, j), qkv_grad), count_share
    )

    def head_rows(j):
        return lax.dynamic_slice_in_dim(heads_t, (me ^ j) * own_width, own_width, 0)

    agg_proj_grad = reduce_gradient(lambda j: product(head_rows(j), embedded_grad), count_share)
    heads_grad = right_product(full_agg_proj, embedded_grad).astype(low)
    input_scale = (group_count * count_share)[None]
    table_grad, coeff_grad, patch_grad = aggregate_back(
        patch_rows, coeff_heads, slot_mask, table_values, heads_grad, input_scale
    )
    patches_grad = patch_grad.transpose(1, 0, 2)

    table_sum = jnp.einsum(
        "hks,su->kuh",
        table_grad.reshape(width, PIX + 1, VTOT),
        selector.astype(wide),
        precision=exact_mode,
    ).reshape((PIX + 1) * VTOT, width)
    coeff_sum = jnp.einsum(
        "hks,su->hku", coeff_grad[..., 0], selector.astype(wide), precision=exact_mode
    ).reshape(-1)
    coeff_rows = -(-coeff_sum.shape[0] // width)
    coeff_flat = jnp.pad(coeff_sum, (0, coeff_rows * width - coeff_sum.shape[0]))
    vectors = [
        agg_bias_grad,
        norm1_gain_grad,
        norm1_shift_grad,
        proj_bias_grad,
        norm2_gain_grad,
        norm2_shift_grad,
        down_bias_grad,
    ]
    pieces = [table_sum, coeff_flat.reshape(coeff_rows, width), jnp.stack(vectors), up_bias_grad]
    bundle = jnp.concatenate(pieces, axis=0) * count_share
    used = bundle.shape[0]
    step = 4 * group_count
    bundle = jnp.pad(bundle, ((0, -used % step), (0, 0)))
    for bit in (1, 2):
        bundle = halve(bundle, "fsdp", bit)
    bits = group_bits()
    for bit in bits:
        bundle = halve(bundle, "grp", bit)
    for bit in reversed(bits):
        bundle = merge(bundle, swap(bundle, "grp", bit), "grp", bit)
    for bit in (2, 1):
        bundle = merge(bundle, swap(bundle, "fsdp", bit), "fsdp", bit)
    table_total = bundle[: table_sum.shape[0]]
    at = table_sum.shape[0]
    coeff_total = bundle[at : at + coeff_rows].reshape(-1)[: coeff_sum.shape[0]]
    coeff_total = coeff_total.reshape(HEADS, (PIX + 1) * VTOT)
    at += coeff_rows
    vector_total = bundle[at : at + len(vectors)]
    at += len(vectors)
    up_bias_total = lax.dynamic_slice_in_dim(bundle, at + me, 1, 0)[0]
    vector_own = lax.dynamic_slice_in_dim(vector_total, me * own_width, own_width, 1)

    value_weight_grad = left_product(own_table, table_total.astype(low))
    key_query_grad = jnp.dot(coeff_total, own_table.astype(wide), precision=exact_mode)
    key_weight_grad = (
        key_query_grad.T[:, :, None]
        * query_vec.astype(wide).reshape(1, HEADS, head_dim)
        * score_scale
    ).reshape(own_width, width)
    query_grad = (
        jnp.einsum(
            "hx,xhj->hj",
            coeff_total,
            key_table.reshape((PIX + 1) * VTOT, HEADS, head_dim),
            precision=exact_mode,
        ).reshape(width)
        * score_scale
    )
    query_weight_grad = own_query.astype(wide)[:, None] * query_grad[None, :]
    agg_query_grad = jnp.dot(
        query_weight.astype(wide), query_grad, precision=exact_mode
    )
    own_totals = lax.dynamic_slice_in_dim(
        table_total.reshape(PIX + 1, VTOT, width), me * own_vars, own_vars, 1
    ).reshape((PIX + 1) * own_vars, width)
    own_coeffs = lax.dynamic_slice_in_dim(
        coeff_total.reshape(HEADS, PIX + 1, VTOT), me * own_vars, own_vars, 2
    ).reshape(HEADS, (PIX + 1) * own_vars)
    var_grads = right_product(own_totals.astype(low), full_value) + lax.dot_general(
        own_coeffs, key_query.astype(wide), (((0,), (0,)), ((), ())), precision=exact_mode
    )
    var_grads = var_grads.reshape(PIX + 1, own_vars, width)
    patch_weight_grad = var_grads[:PIX].transpose(1, 0, 2)
    var_embed_grad = var_grads[PIX]
    return (
        output,
        patches_grad,
        patch_weight_grad,
        var_embed_grad,
        agg_query_grad,
        query_weight_grad,
        key_weight_grad,
        value_weight_grad,
        agg_proj_grad,
        vector_own[0],
        vector_own[1],
        vector_own[2],
        qkv_weight_grad,
        proj_weight_grad,
        vector_own[3],
        vector_own[4],
        vector_own[5],
        up_weight_grad,
        up_bias_total,
        down_weight_grad,
        vector_own[6],
    )


def solution(mesh):
    shard = P("fsdp")
    shard_rows = P("fsdp", None)
    return jax.shard_map(
        on_device,
        mesh=mesh,
        in_specs=(
            P(None, None, ("grp", "fsdp")),
            P("grp"),
            P("grp", None),
            P("grp"),
            P(),
            P("fsdp", None, None),
            shard_rows,
            P(),
            shard_rows,
            shard_rows,
            shard_rows,
            shard_rows,
            P(),
            P(),
            P(),
            shard_rows,
            shard_rows,
            P(),
            P(),
            P(),
            P(None, "fsdp"),
            shard,
            shard_rows,
            P(),
            P(("grp", "fsdp"), None),
        ),
        out_specs=(
            P(("grp", "fsdp"), None),
            P(None, None, ("grp", "fsdp")),
            P("fsdp", None, None),
            shard_rows,
            shard,
            shard_rows,
            shard_rows,
            shard_rows,
            shard_rows,
            shard,
            shard,
            shard,
            shard_rows,
            shard_rows,
            shard,
            shard,
            shard,
            P(None, "fsdp"),
            shard,
            shard_rows,
            shard,
        ),
        check_vma=False,
    )
```

time: 1640 us -> 913 us (0.56)
  matrix products: 552 us -> 130 us
  waiting for transfers between devices: 780 us -> 383 us
  Pallas kernels: 0 us -> 123 us
  blocking collectives: 107 us -> 0 us
  starting transfers between devices: 2.1 us -> 97 us
  local copies, waits for them, and re-layouts: 112 us -> 77.1 us
  other arithmetic: 56.3 us -> 85.4 us
    psum x1 -> x0, waiting for transfers between devices: 444 us -> none  [on_device(): lax.psum((shards[0] * count_share, shards[1] * count_share, shards[2] * c...]
    dot_general x39 -> x9, matrix products: 423 us -> 5.96 us  [the longest x1 1.21 us: on_device(): jnp.einsum('dhj,hj->hd', key_weight.reshape(own_width, HEADS, head_dim),...]
    ppermute x0 -> x95, waiting for transfers between devices: none -> 383 us  [swap(): return lax.ppermute(value, axis, [(i, i ^ bit) for i in range(size)])]
    reduce_scatter x9 -> x0, waiting for transfers between devices: 187 us -> none  [the longest x1 59 us: on_device(): lax.psum_scatter(qkv_weight_grad.astype(jnp.bfloat16), 'fsdp', scatter_di...]
    all_gather x9 -> x0, waiting for transfers between devices: 134 us -> none  [the longest x1 45.8 us: on_device(): lax.all_gather(qkv_rows[:, model_width:], 'fsdp', axis=0, tiled=True)]
    pallas_call x0 -> x6, Pallas kernels: none -> 123 us  [the longest x2 59.1 us: attend_back(): pl.pallas_call(functools.partial(attend_back_kernel, shards, head_dim, ol...]
    ppermute x0 -> x95, starting transfers between devices: none -> 97 us  [swap(): return lax.ppermute(value, axis, [(i, i ^ bit) for i in range(size)])]
    psum x2 -> x0, blocking collectives: 64.7 us -> none  [the longest x1 42.4 us: on_device(): lax.psum((shards[0] * count_share, shards[1] * count_share, shards[2] * c...]
  transfers between devices with their start and end apart: 21 -> 95, of which waited for: 13 -> 40; matrix products, arithmetic and copies ran while one was open for 29% -> 28% of each run, Pallas kernels for 0% -> 10%
where the time goes in v1:
time: 913 us; the launch traced here: 901 us
  waiting for transfers between devices  383 us (42%)
  matrix products  130 us (14%)
  Pallas kernels  123 us (13%)
  starting transfers between devices  97 us (11%)
  other arithmetic  85.4 us (9%)
  local copies, waits for them, and re-layouts  77.1 us (8%)
    ppermute x95, waiting for transfers between devices, swap(): return lax.ppermute(value, axis, [(i, i ^ bit) for i in range(size)])  383 us
    ppermute x95, starting transfers between devices, swap(): return lax.ppermute(value, axis, [(i, i ^ bit) for i in range(size)])  97 us
    pallas_call x2, Pallas kernels, attend_back(): pl.pallas_call(functools.partial(attend_back_kernel, shards, head_dim, ol...  59.1 us
    dot_general x13, matrix products, right_product(): lax.dot_general(left_side, right_side, (((1,), (1,)), ((), ())), preferre...  45.2 us
    dot_general x16, matrix products, product(): return jnp.dot(left_side, right_side, preferred_element_type=jnp.float32)  41.7 us
    pallas_call x2, Pallas kernels, attend(): pl.pallas_call(functools.partial(attend_kernel, shards, head_dim, old is...  37.8 us
    dot_general x19, matrix products, left_product(): lax.dot_general(left_side, right_side, (((0,), (0,)), ((), ())), preferre...  36.7 us
    dynamic_update_slice x23, local copies, waits for them, and re-layouts, in_order(): whole = lax.dynamic_update_slice_in_dim(whole, shard, (me ^ j) * size, axis)  22.8 us
  transfers between devices with their start and end apart: 95, of which 40 were waited for; matrix products, arithmetic and copies ran while one was open for 28% of the time, Pallas kernels for 10%

profile of v1, /device:TPU:0, one launch (start us, length us, event | category | flops | bytes accessed | tf_op | source)
XLA Modules:
  0.0 901.1 jit_solution(8150036334310460329)
XLA Ops:
  55.3 4.7 collective-permute-done.5
  83.6 3.7 collective-permute-done.15
  97.5 7.2 collective-permute-done.16
  104.7 3.7 constant_dynamic-update-slice_fusion.5
  108.5 11.5 %aggregate.1 = bf16[1024,512]{1,0:T(8,128)(2,1)} custom-call(bf16[4,48,512]{2,1,0:T(8,128)(2,1)} %bitcast.290, f32[16,5,48,1]{3,2,1,0:T(8,128)} %copy.67.coeff_ref, f32[48,1]{1,0:T(8,128)} %copy.68.mask_ref, bf16[1024,240]{1,0:T(8,128)(2,1)} %copy.69.table_ref), custom_call_target="tpu_custom_call" | custom-call | flops 1006632960 | bytes 2097152 | tf_op jit(solution)/shard_map/aggregate/pallas_call | solution.py:163
  129.6 6.6 convolution_convert_fusion.refs_1_.refs_2_.refs_4_.refs_5_.refs_7_
  144.4 4.0 collective-permute-start.42
  154.4 37.3 %collective-permute-done.31 = bf16[128,1024]{1,0:T(8,128)(2,1)} collective-permute-done((bf16[128,1024]{1,0:T(8,128)(2,1)}, bf16[128,1024]{1,0:T(8,128)(2,1)}, u32[]{:S(2)}, u32[]{:S(2)}) %collective-permute-start.31) | collective-permute-done | bytes 262176 | tf_op jit(solution)/shard_map/ppermute | solution.py:21
  198.7 3.7 collective-permute-done.32
  209.5 23.5 %collective-permute-done.29 = bf16[2,128,1024]{2,1,0:T(8,128)(2,1)S(1)} collective-permute-done((bf16[2,128,1024]{2,1,0:T(8,128)(2,1)S(1)}, bf16[2,128,1024]{2,1,0:T(8,128)(2,1)S(1)}, u32[]{:S(2)}, u32[]{:S(2)}) %collective-permute-start.29) | collective-permute-done | bytes 524320 | tf_op jit(solution)/shard_map/ppermute | solution.py:21
  234.2 7.9 collective-permute-done.33
  250.0 9.1 %collective-permute-done.54 = bf16[240,1024]{1,0:T(8,128)(2,1)S(1)} collective-permute-done((bf16[240,1024]{1,0:T(8,128)(2,1)S(1)}, bf16[240,1024]{1,0:T(8,128)(2,1)S(1)}, u32[]{:S(2)}, u32[]{:S(2)}) %collective-permute-start.54) | collective-permute-done | bytes 491552 | tf_op jit(solution)/shard_map/ppermute | solution.py:21
  262.8 25.2 %collective-permute-done.34 = bf16[4,128,1024]{2,1,0:T(8,128)(2,1)} collective-permute-done((bf16[4,128,1024]{2,1,0:T(8,128)(2,1)}, bf16[4,128,1024]{2,1,0:T(8,128)(2,1)}, u32[]{:S(2)}, u32[]{:S(2)}) %collective-permute-start.34) | collective-permute-done | bytes 1048608 | tf_op jit(solution)/shard_map/ppermute | solution.py:21
  296.2 18.3 %attend.2 = (f32[512,1024]{1,0:T(8,128)}, f32[512,1024]{1,0:T(8,128)}, f32[512,1024]{1,0:T(8,128)}) custom-call(s32[2]{0:T(128)} %get-tuple-element.138.refs_0_, bf16[512,3072]{1,0:T(8,128)(2,1)} %copy-done.26, bf16[512,3072]{1,0:T(8,128)(2,1)} %copy-done.26, bf16[512,2048]{1,0:T(8,128)(2,1)} %collective-permute-done.20.refs_3_.refs_5_.refs_6_.refs_8_, ...), custom_call_target="tpu_custom_call" | custom-call | flops 8589934592 | bytes 4194304 | tf_op jit(solution)/shard_map/attend/pallas_call | solution.py:344
  314.5 19.5 %attend.3 = (bf16[512,1024]{1,0:T(8,128)(2,1)}, f32[512,1024]{1,0:T(8,128)}) custom-call(s32[2]{0:T(128)} %get-tuple-element.139.refs_0_, bf16[512,3072]{1,0:T(8,128)(2,1)} %copy-done.26, bf16[512,2048]{1,0:T(8,128)(2,1)} %collective-permute-done.18.refs_2_.refs_4_.refs_5_.refs_7_, bf16[512,2048]{1,0:T(8,128)(2,1)} %collective-permute-done.19.refs_3_.refs_5_.refs_6_.refs_8_, ...), custom_call_target="tpu_custom_call" | custom-call | flops 8589934592 | bytes 4194304 | tf_op jit(solution)/shard_map/attend/pallas_call | solution.py:344
  341.9 4.3 convert_reduce_fusion.1
  360.7 4.8 multiply_convert_fusion.6
  365.5 3.8 convert_reduce_fusion.2
  372.6 4.0 convert_reduce_fusion
  376.7 4.2 multiply_reduce_fusion
  383.0 3.9 convolution_convert_fusion.2.refs_2_
  391.2 4.2 fusion.147
  398.0 29.4 %attend_back.2 = (f32[512,1024]{1,0:T(8,128)}, bf16[512,1024]{1,0:T(8,128)(2,1)}, bf16[512,1024]{1,0:T(8,128)(2,1)}, bf16[512,1024]{1,0:T(8,128)(2,1)}, bf16[512,1024]{1,0:T(8,128)(2,1)}) custom-call(s32[2]{0:T(128)} %get-tuple-element.139.refs_0_, bf16[512,3072]{1,0:T(8,128)(2,1)} %copy-done.26, bf16[512,1024]{1,0:T(8,128)(2,1)} %convolution_convert_fusion.2.refs_2_, ...), custom_call_target="tpu_custom_call" | custom-call | flops 21474836480 | bytes 8388608 | tf_op jit(solution)/shard_map/attend_back/pallas_call | solution.py:441
  431.0 29.7 %attend_back.3 = (bf16[512,1024]{1,0:T(8,128)(2,1)}, bf16[512,1024]{1,0:T(8,128)(2,1)}, bf16[512,1024]{1,0:T(8,128)(2,1)}, bf16[512,1024]{1,0:T(8,128)(2,1)}, bf16[512,1024]{1,0:T(8,128)(2,1)}) custom-call(s32[2]{0:T(128)} %get-tuple-element.138.refs_0_, bf16[512,3072]{1,0:T(8,128)(2,1)} %copy-done.26, bf16[512,1024]{1,0:T(8,128)(2,1)} %convolution_convert_fusion.2.refs_2_, ...), custom_call_target="tpu_custom_call" | custom-call | flops 21474836480 | bytes 8388608 | tf_op jit(solution)/shard_map/attend_back/pallas_call | solution.py:441
  475.1 4.3 add_convert_fusion.5
  480.9 3.8 add_convert_fusion.1
  489.9 4.8 collective-permute-done.72
  508.4 30.4 %collective-permute-done.39 = bf16[512,2048]{1,0:T(8,128)(2,1)} collective-permute-done((bf16[512,2048]{1,0:T(8,128)(2,1)}, bf16[512,2048]{1,0:T(8,128)(2,1)}, u32[]{:S(2)}, u32[]{:S(2)}) %collective-permute-start.39) | collective-permute-done | bytes 2097184 | tf_op jit(solution)/shard_map/ppermute | solution.py:21
  538.8 4.1 add_convert_fusion
  543.0 7.5 multiply_reduce_fusion.1
  551.4 4.2 convolution_convert_fusion.1.heads_ref
  555.6 14.1 %aggregate_back.1 = (f32[1024,240]{1,0:T(8,128)}, f32[16,5,48,1]{3,2,1,0:T(8,128)}, f32[4,48,512]{2,1,0:T(8,128)}) custom-call(bf16[4,48,512]{2,1,0:T(8,128)(2,1)} %bitcast.291, f32[16,5,48,1]{3,2,1,0:T(8,128)} %copy.67.coeff_ref, f32[48,1]{1,0:T(8,128)} %copy.68.mask_ref, bf16[1024,240]{1,0:T(8,128)(2,1)} %copy.69.table_ref, ...), custom_call_target="tpu_custom_call" | custom-call | flops 2013265920 | bytes 4194304 | tf_op jit(solution)/shard_map/aggregate_back/pallas_call | solution.py:223
  583.7 7.0 collective-permute-done.44
  624.8 4.3 fusion.3
  644.5 33.5 %collective-permute-done.80 = bf16[1024,1024]{1,0:T(8,128)(2,1)} collective-permute-done((bf16[1024,1024]{1,0:T(8,128)(2,1)}, bf16[1024,1024]{1,0:T(8,128)(2,1)}, u32[]{:S(2)}, u32[]{:S(2)}) %collective-permute-start.80) | collective-permute-done | bytes 2097184 | tf_op jit(solution)/shard_map/ppermute | solution.py:21
  678.0 4.8 fusion.5
  688.4 34.5 %collective-permute-done.88 = bf16[1024,1024]{1,0:T(8,128)(2,1)} collective-permute-done((bf16[1024,1024]{1,0:T(8,128)(2,1)}, bf16[1024,1024]{1,0:T(8,128)(2,1)}, u32[]{:S(2)}, u32[]{:S(2)}) %collective-permute-start.88) | collective-permute-done | bytes 2097184 | tf_op jit(solution)/shard_map/ppermute | solution.py:21
  728.7 24.0 %collective-permute-done.64 = bf16[256,3072]{1,0:T(8,128)(2,1)S(1)} collective-permute-done((bf16[256,3072]{1,0:T(8,128)(2,1)S(1)}, bf16[256,3072]{1,0:T(8,128)(2,1)S(1)}, u32[]{:S(2)}, u32[]{:S(2)}) %collective-permute-start.64) | collective-permute-done | bytes 1572896 | tf_op jit(solution)/shard_map/ppermute | solution.py:21
  761.0 10.8 %collective-permute-done.65 = bf16[128,3072]{1,0:T(8,128)(2,1)S(1)} collective-permute-done((bf16[128,3072]{1,0:T(8,128)(2,1)S(1)}, bf16[128,3072]{1,0:T(8,128)(2,1)S(1)}, u32[]{:S(2)}, u32[]{:S(2)}) %collective-permute-start.65) | collective-permute-done | bytes 786464 | tf_op jit(solution)/shard_map/ppermute | solution.py:21
  779.7 9.5 %collective-permute-done.66 = bf16[64,3072]{1,0:T(8,128)(2,1)S(1)} collective-permute-done((bf16[64,3072]{1,0:T(8,128)(2,1)S(1)}, bf16[64,3072]{1,0:T(8,128)(2,1)S(1)}, u32[]{:S(2)}, u32[]{:S(2)}) %collective-permute-start.66) | collective-permute-done | bytes 393248 | tf_op jit(solution)/shard_map/ppermute | solution.py:21
  789.5 13.8 %collective-permute-done.91 = bf16[128,1024]{1,0:T(8,128)(2,1)S(1)} collective-permute-done((bf16[128,1024]{1,0:T(8,128)(2,1)S(1)}, bf16[128,1024]{1,0:T(8,128)(2,1)S(1)}, u32[]{:S(2)}, u32[]{:S(2)}) %collective-permute-start.91) | collective-permute-done | bytes 262176 | tf_op jit(solution)/shard_map/ppermute | solution.py:21
  803.5 6.2 collective-permute-done.84
  809.8 4.7 collective-permute-start.85
  814.5 3.7 collective-permute-done.67
  830.3 5.5 collective-permute-start.69
  838.2 8.6 collective-permute-done.93
  848.4 4.1 collective-permute-done.61
  857.1 33.1 %collective-permute-done.62 = bf16[128,1024]{1,0:T(8,128)(2,1)S(1)} collective-permute-done((bf16[128,1024]{1,0:T(8,128)(2,1)S(1)}, bf16[128,1024]{1,0:T(8,128)(2,1)S(1)}, u32[]{:S(2)}, u32[]{:S(2)}) %collective-permute-start.62) | collective-permute-done | bytes 262176 | tf_op jit(solution)/shard_map/ppermute | solution.py:21
  (581 shorter events, 339.0 us)
Async XLA Ops:
  3.9 41.9 %collective-permute-start.4 = (bf16[61,1024]{1,0:T(8,128)(2,1)}, bf16[61,1024]{1,0:T(8,128)(2,1)S(1)}, u32[]{:S(2)}, u32[]{:S(2)}) collective-permute-start(bf16[61,1024]{1,0:T(8,128)(2,1)} %pad_maximum_fusion.9), channel_id=1, source_target_pairs={{0,1},{1,0},{2,3},{3,2},{4,5},{5,4},{6,7},{7,6},{8,9},{9,8},{10,11... | collective-permute-start | bytes 374792 | tf_op jit(solution)/shard_map/ppermute | solution.py:21
  5.9 22.9 %collective-permute-start = (f32[1,1024]{1,0:T(1,128)S(1)}, f32[1,1024]{1,0:T(1,128)S(1)}, u32[]{:S(2)}, u32[]{:S(2)}) collective-permute-start(f32[1,1024]{1,0:T(1,128)S(1)} %fusion.143), channel_id=1, source_target_pairs={{0,1},{1,0},{2,3},{3,2},{4,5},{5,4},{6,7},{7,6},{8,9},{9,8},{10,11... | collective-permute-start | bytes 12296 | tf_op jit(solution)/shard_map/ppermute | solution.py:21
  5.9 65.8 %collective-permute-start.6 = (bf16[256,1024]{1,0:T(8,128)(2,1)}, bf16[256,1024]{1,0:T(8,128)(2,1)}, u32[]{:S(2)}, u32[]{:S(2)}) collective-permute-start(bf16[256,1024]{1,0:T(8,128)(2,1)} %param.35), channel_id=1, source_target_pairs={{0,1},{1,0},{2,3},{3,2},{4,5},{5,4},{6,7},{7,6},{8,9},{9,8},{10,11... | collective-permute-start | bytes 1572872 | tf_op jit(solution)/shard_map/ppermute | solution.py:21
  6.4 72.5 %collective-permute-start.10 = (bf16[256,1024]{1,0:T(8,128)(2,1)}, bf16[256,1024]{1,0:T(8,128)(2,1)}, u32[]{:S(2)}, u32[]{:S(2)}) collective-permute-start(bf16[256,1024]{1,0:T(8,128)(2,1)} %param.36), channel_id=1, source_target_pairs={{0,1},{1,0},{2,3},{3,2},{4,5},{5,4},{6,7},{7,6},{8,9},{9,8},{10,11... | collective-permute-start | bytes 1572872 | tf_op jit(solution)/shard_map/ppermute | solution.py:21
  6.4 88.4 %collective-permute-start.14 = (bf16[256,3072]{1,0:T(8,128)(2,1)}, bf16[256,3072]{1,0:T(8,128)(2,1)}, u32[]{:S(2)}, u32[]{:S(2)}) collective-permute-start(bf16[256,3072]{1,0:T(8,128)(2,1)} %param.40), channel_id=1, source_target_pairs={{0,1},{1,0},{2,3},{3,2},{4,5},{5,4},{6,7},{7,6},{8,9},{9,8},{10,11... | collective-permute-start | bytes 4718600 | tf_op jit(solution)/shard_map/ppermute | solution.py:21
  78.9 126.1 %collective-permute-start.21 = (bf16[256,1024]{1,0:T(8,128)(2,1)}, bf16[256,1024]{1,0:T(8,128)(2,1)}, u32[]{:S(2)}, u32[]{:S(2)}) collective-permute-start(bf16[256,1024]{1,0:T(8,128)(2,1)} %param.41), channel_id=1, source_target_pairs={{0,1},{1,0},{2,3},{3,2},{4,5},{5,4},{6,7},{7,6},{8,9},{9,8},{10,11... | collective-permute-start | bytes 1572872 | tf_op jit(solution)/shard_map/ppermute | solution.py:21
  81.2 112.1 %collective-permute-start.22 = (bf16[128,1024]{1,0:T(8,128)(2,1)}, bf16[128,1024]{1,0:T(8,128)(2,1)}, u32[]{:S(2)}, u32[]{:S(2)}) collective-permute-start(bf16[128,1024]{1,0:T(8,128)(2,1)} %constant_dynamic-slice_fusion.24), channel_id=1, source_target_pairs={{0,2},{1,3},{2,0},{3,1},{4,6},{5,7},{6,4},{7,5},{8,10},{9,11},{10,... | collective-permute-start | bytes 786440 | tf_op jit(solution)/shard_map/ppermute | solution.py:21
  87.4 65.4 %collective-permute-start.27 = (bf16[128,1024]{1,0:T(8,128)(2,1)}, bf16[128,1024]{1,0:T(8,128)(2,1)S(1)}, u32[]{:S(2)}, u32[]{:S(2)}) collective-permute-start(bf16[128,1024]{1,0:T(8,128)(2,1)} %constant_dynamic-slice_fusion.23), channel_id=1, source_target_pairs={{0,2},{1,3},{2,0},{3,1},{4,6},{5,7},{6,4},{7,5},{8,10},{9,11},{10,... | collective-permute-start | bytes 786440 | tf_op jit(solution)/shard_map/ppermute | solution.py:21
  94.8 25.2 %collective-permute-start.13 = (bf16[256,1024]{1,0:T(8,128)(2,1)}, bf16[256,1024]{1,0:T(8,128)(2,1)S(1)}, u32[]{:S(2)}, u32[]{:S(2)}) collective-permute-start(bf16[256,1024]{1,0:T(8,128)(2,1)} %get-tuple-element.119), channel_id=1, source_target_pairs={{0,1},{1,0},{2,3},{3,2},{4,5},{5,4},{6,7},{7,6},{8,9},{9,8},{10,11... | collective-permute-start | bytes 1572872 | tf_op jit(solution)/shard_map/ppermute | solution.py:21
  108.5 19.7 %collective-permute-start.17 = (bf16[256,3072]{1,0:T(8,128)(2,1)S(1)}, bf16[256,3072]{1,0:T(8,128)(2,1)S(1)}, u32[]{:S(2)}, u32[]{:S(2)}) collective-permute-start(bf16[256,3072]{1,0:T(8,128)(2,1)S(1)} %get-tuple-element.117), channel_id=1, source_target_pairs={{0,1},{1,0},{2,3},{3,2},{4,5},{5,4},{6,7},{7,6},{8,9},{9,8},{10,11... | collective-permute-start | bytes 4718600 | tf_op jit(solution)/shard_map/ppermute | solution.py:21
  138.6 106.7 %collective-permute-start.18 = (bf16[512,2048]{1,0:T(8,128)(2,1)}, bf16[512,2048]{1,0:T(8,128)(2,1)}, u32[]{:S(2)}, u32[]{:S(2)}) collective-permute-start(bf16[512,2048]{1,0:T(8,128)(2,1)} %slice.177), channel_id=1, source_target_pairs={{0,2},{1,3},{2,0},{3,1},{4,6},{5,7},{6,4},{7,5},{8,10},{9,11},{10,... | collective-permute-start | bytes 6291464 | tf_op jit(solution)/shard_map/ppermute | solution.py:21
  149.0 42.7 %collective-permute-start.31 = (bf16[128,1024]{1,0:T(8,128)(2,1)}, bf16[128,1024]{1,0:T(8,128)(2,1)}, u32[]{:S(2)}, u32[]{:S(2)}) collective-permute-start(bf16[128,1024]{1,0:T(8,128)(2,1)} %constant_dynamic-slice_fusion.22), channel_id=1, source_target_pairs={{0,2},{1,3},{2,0},{3,1},{4,6},{5,7},{6,4},{7,5},{8,10},{9,11},{10,... | collective-permute-start | bytes 786440 | tf_op jit(solution)/shard_map/ppermute | solution.py:21
  152.7 42.4 %collective-permute-start.28 = (bf16[1,128,1024]{2,1,0:T(8,128)(2,1)S(1)}, bf16[1,128,1024]{2,1,0:T(8,128)(2,1)S(1)}, u32[]{:S(2)}, u32[]{:S(2)}) collective-permute-start(bf16[1,128,1024]{2,1,0:T(8,128)(2,1)S(1)} %bitcast.286), channel_id=1, source_target_pairs={{0,8},{4,12},{8,0},{12,4},{16,24},{20,28},{24,16},{28,20},{1,9},{5... | collective-permute-start | bytes 786440 | tf_op jit(solution)/shard_map/ppermute | solution.py:21
  195.3 37.8 %collective-permute-start.29 = (bf16[2,128,1024]{2,1,0:T(8,128)(2,1)S(1)}, bf16[2,128,1024]{2,1,0:T(8,128)(2,1)S(1)}, u32[]{:S(2)}, u32[]{:S(2)}) collective-permute-start(bf16[2,128,1024]{2,1,0:T(8,128)(2,1)S(1)} %maximum_select_fusion.16), channel_id=1, source_target_pairs={{0,16},{4,20},{8,24},{12,28},{16,0},{20,4},{24,8},{28,12},{1,17},{... | collective-permute-start | bytes 1572872 | tf_op jit(solution)/shard_map/ppermute | solution.py:21
  203.5 38.5 %collective-permute-start.33 = (bf16[2,128,1024]{2,1,0:T(8,128)(2,1)S(1)}, bf16[2,128,1024]{2,1,0:T(8,128)(2,1)S(1)}, u32[]{:S(2)}, u32[]{:S(2)}) collective-permute-start(bf16[2,128,1024]{2,1,0:T(8,128)(2,1)S(1)} %maximum_select_fusion.17), channel_id=1, source_target_pairs={{0,16},{4,20},{8,24},{12,28},{16,0},{20,4},{24,8},{28,12},{1,17},{... | collective-permute-start | bytes 1572872 | tf_op jit(solution)/shard_map/ppermute | solution.py:21
  205.0 91.2 %collective-permute-start.20 = (bf16[512,2048]{1,0:T(8,128)(2,1)}, bf16[512,2048]{1,0:T(8,128)(2,1)}, u32[]{:S(2)}, u32[]{:S(2)}) collective-permute-start(bf16[512,2048]{1,0:T(8,128)(2,1)} %slice.177), channel_id=1, source_target_pairs={{0,1},{1,0},{2,3},{3,2},{4,5},{5,4},{6,7},{7,6},{8,9},{9,8},{10,11... | collective-permute-start | bytes 6291464 | tf_op jit(solution)/shard_map/ppermute | solution.py:21
  205.1 39.6 %collective-permute-start.53 = (bf16[240,1024]{1,0:T(8,128)(2,1)S(1)}, bf16[240,1024]{1,0:T(8,128)(2,1)S(1)}, u32[]{:S(2)}, u32[]{:S(2)}) collective-permute-start(bf16[240,1024]{1,0:T(8,128)(2,1)S(1)} %get-tuple-element.160), channel_id=1, source_target_pairs={{0,1},{1,0},{2,3},{3,2},{4,5},{5,4},{6,7},{7,6},{8,9},{9,8},{10,11... | collective-permute-start | bytes 1474568 | tf_op jit(solution)/shard_map/ppermute | solution.py:21
  242.1 50.2 %collective-permute-start.30 = (bf16[4,128,1024]{2,1,0:T(8,128)(2,1)}, bf16[4,128,1024]{2,1,0:T(8,128)(2,1)}, u32[]{:S(2)}, u32[]{:S(2)}) collective-permute-start(bf16[4,128,1024]{2,1,0:T(8,128)(2,1)} %maximum_select_fusion.6), channel_id=1, source_target_pairs={{0,4},{4,0},{8,12},{12,8},{16,20},{20,16},{24,28},{28,24},{1,5},{5... | collective-permute-start | bytes 3145736 | tf_op jit(solution)/shard_map/ppermute | solution.py:21
  244.6 43.3 %collective-permute-start.34 = (bf16[4,128,1024]{2,1,0:T(8,128)(2,1)}, bf16[4,128,1024]{2,1,0:T(8,128)(2,1)}, u32[]{:S(2)}, u32[]{:S(2)}) collective-permute-start(bf16[4,128,1024]{2,1,0:T(8,128)(2,1)} %maximum_select_fusion.7), channel_id=1, source_target_pairs={{0,4},{4,0},{8,12},{12,8},{16,20},{20,16},{24,28},{28,24},{1,5},{5... | collective-permute-start | bytes 3145736 | tf_op jit(solution)/shard_map/ppermute | solution.py:21
  245.2 69.2 %collective-permute-start.19 = (bf16[512,2048]{1,0:T(8,128)(2,1)}, bf16[512,2048]{1,0:T(8,128)(2,1)}, u32[]{:S(2)}, u32[]{:S(2)}) collective-permute-start(bf16[512,2048]{1,0:T(8,128)(2,1)} %collective-permute-done.18.refs_2_.refs_4_.refs_5_.refs_7_), channel_id=1, source_target_pairs={{0,1},{1,0},{2,3},{3,2},{4,5},{5,4},{6,7},{7,6},{8,9},{9,8},{10,11... | collective-permute-start | bytes 6291464 | tf_op jit(solution)/shard_map/ppermute | solution.py:21
  259.1 101.6 %collective-permute-start.25 = (bf16[1024,1024]{1,0:T(8,128)(2,1)}, bf16[1024,1024]{1,0:T(8,128)(2,1)}, u32[]{:S(2)}, u32[]{:S(2)}) collective-permute-start(bf16[1024,1024]{1,0:T(8,128)(2,1)} %param.45), channel_id=1, source_target_pairs={{0,1},{1,0},{2,3},{3,2},{4,5},{5,4},{6,7},{7,6},{8,9},{9,8},{10,11... | collective-permute-start | bytes 6291464 | tf_op jit(solution)/shard_map/ppermute | solution.py:21
  287.9 77.5 %collective-permute-start.26 = (bf16[1024,1024]{1,0:T(8,128)(2,1)}, bf16[1024,1024]{1,0:T(8,128)(2,1)}, u32[]{:S(2)}, u32[]{:S(2)}) collective-permute-start(bf16[1024,1024]{1,0:T(8,128)(2,1)} %param.47), channel_id=1, source_target_pairs={{0,1},{1,0},{2,3},{3,2},{4,5},{5,4},{6,7},{7,6},{8,9},{9,8},{10,11... | collective-permute-start | bytes 6291464 | tf_op jit(solution)/shard_map/ppermute | solution.py:21
  292.3 80.3 %collective-permute-start.36 = (bf16[1024,1024]{1,0:T(8,128)(2,1)}, bf16[1024,1024]{1,0:T(8,128)(2,1)}, u32[]{:S(2)}, u32[]{:S(2)}) collective-permute-start(bf16[1024,1024]{1,0:T(8,128)(2,1)} %bitcast.40), channel_id=1, source_target_pairs={{0,1},{1,0},{2,3},{3,2},{4,5},{5,4},{6,7},{7,6},{8,9},{9,8},{10,11... | collective-permute-start | bytes 6291464 | tf_op jit(solution)/shard_map/ppermute | solution.py:21
  296.2 61.7 %collective-permute-start.35 = (bf16[1024,1024]{1,0:T(8,128)(2,1)}, bf16[1024,1024]{1,0:T(8,128)(2,1)}, u32[]{:S(2)}, u32[]{:S(2)}) collective-permute-start(bf16[1024,1024]{1,0:T(8,128)(2,1)} %bitcast.34), channel_id=1, source_target_pairs={{0,1},{1,0},{2,3},{3,2},{4,5},{5,4},{6,7},{7,6},{8,9},{9,8},{10,11... | collective-permute-start | bytes 6291464 | tf_op jit(solution)/shard_map/ppermute | solution.py:21
  430.5 49.8 %collective-permute-start.38 = (bf16[512,2048]{1,0:T(8,128)(2,1)}, bf16[512,2048]{1,0:T(8,128)(2,1)}, u32[]{:S(2)}, u32[]{:S(2)}) collective-permute-start(bf16[512,2048]{1,0:T(8,128)(2,1)} %pad_maximum_fusion.5), channel_id=1, source_target_pairs={{0,1},{1,0},{2,3},{3,2},{4,5},{5,4},{6,7},{7,6},{8,9},{9,8},{10,11... | collective-permute-start | bytes 6291464 | tf_op jit(solution)/shard_map/ppermute | solution.py:21
  463.8 44.6 %collective-permute-start.37 = (bf16[512,2048]{1,0:T(8,128)(2,1)}, bf16[512,2048]{1,0:T(8,128)(2,1)}, u32[]{:S(2)}, u32[]{:S(2)}) collective-permute-start(bf16[512,2048]{1,0:T(8,128)(2,1)} %pad_maximum_fusion.4), channel_id=1, source_target_pairs={{0,1},{1,0},{2,3},{3,2},{4,5},{5,4},{6,7},{7,6},{8,9},{9,8},{10,11... | collective-permute-start | bytes 6291464 | tf_op jit(solution)/shard_map/ppermute | solution.py:21
  484.7 54.1 %collective-permute-start.39 = (bf16[512,2048]{1,0:T(8,128)(2,1)}, bf16[512,2048]{1,0:T(8,128)(2,1)}, u32[]{:S(2)}, u32[]{:S(2)}) collective-permute-start(bf16[512,2048]{1,0:T(8,128)(2,1)} %add_convert_fusion.1), channel_id=1, source_target_pairs={{0,2},{1,3},{2,0},{3,1},{4,6},{5,7},{6,4},{7,5},{8,10},{9,11},{10,... | collective-permute-start | bytes 6291464 | tf_op jit(solution)/shard_map/ppermute | solution.py:21
  504.3 120.4 %collective-permute-start.79 = (bf16[2,1024,1024]{2,1,0:T(8,128)(2,1)}, bf16[2,1024,1024]{2,1,0:T(8,128)(2,1)}, u32[]{:S(2)}, u32[]{:S(2)}) collective-permute-start(bf16[2,1024,1024]{2,1,0:T(8,128)(2,1)} %pad_maximum_fusion), channel_id=1, source_target_pairs={{0,1},{1,0},{2,3},{3,2},{4,5},{5,4},{6,7},{7,6},{8,9},{9,8},{10,11... | collective-permute-start | bytes 12582920 | tf_op jit(solution)/shard_map/ppermute | solution.py:21
  507.0 68.3 %collective-permute-start.75 = (bf16[32,1024]{1,0:T(8,128)(2,1)S(1)}, bf16[32,1024]{1,0:T(8,128)(2,1)S(1)}, u32[]{:S(2)}, u32[]{:S(2)}) collective-permute-start(bf16[32,1024]{1,0:T(8,128)(2,1)S(1)} %constant_dynamic-slice_fusion.8), channel_id=1, source_target_pairs={{0,16},{4,20},{8,24},{12,28},{16,0},{20,4},{24,8},{28,12},{1,17},{... | collective-permute-start | bytes 196616 | tf_op jit(solution)/shard_map/ppermute | solution.py:21
  578.6 53.3 %collective-permute-start.87 = (bf16[2,1024,1024]{2,1,0:T(8,128)(2,1)S(1)}, bf16[2,1024,1024]{2,1,0:T(8,128)(2,1)S(1)}, u32[]{:S(2)}, u32[]{:S(2)}) collective-permute-start(bf16[2,1024,1024]{2,1,0:T(8,128)(2,1)S(1)} %pad_maximum_fusion.1), channel_id=1, source_target_pairs={{0,1},{1,0},{2,3},{3,2},{4,5},{5,4},{6,7},{7,6},{8,9},{9,8},{10,11... | collective-permute-start | bytes 12582920 | tf_op jit(solution)/shard_map/ppermute | solution.py:21
  620.3 62.5 %collective-permute-start.63 = (bf16[2,256,3072]{2,1,0:T(8,128)(2,1)}, bf16[2,256,3072]{2,1,0:T(8,128)(2,1)}, u32[]{:S(2)}, u32[]{:S(2)}) collective-permute-start(bf16[2,256,3072]{2,1,0:T(8,128)(2,1)} %pad_maximum_fusion.3), channel_id=1, source_target_pairs={{0,1},{1,0},{2,3},{3,2},{4,5},{5,4},{6,7},{7,6},{8,9},{9,8},{10,11... | collective-permute-start | bytes 9437192 | tf_op jit(solution)/shard_map/ppermute | solution.py:21
  629.1 48.9 %collective-permute-start.80 = (bf16[1024,1024]{1,0:T(8,128)(2,1)}, bf16[1024,1024]{1,0:T(8,128)(2,1)}, u32[]{:S(2)}, u32[]{:S(2)}) collective-permute-start(bf16[1024,1024]{1,0:T(8,128)(2,1)} %fusion.3), channel_id=1, source_target_pairs={{0,2},{1,3},{2,0},{3,1},{4,6},{5,7},{6,4},{7,5},{8,10},{9,11},{10,... | collective-permute-start | bytes 6291464 | tf_op jit(solution)/shard_map/ppermute | solution.py:21
  635.7 87.2 %collective-permute-start.88 = (bf16[1024,1024]{1,0:T(8,128)(2,1)}, bf16[1024,1024]{1,0:T(8,128)(2,1)}, u32[]{:S(2)}, u32[]{:S(2)}) collective-permute-start(bf16[1024,1024]{1,0:T(8,128)(2,1)} %fusion), channel_id=1, source_target_pairs={{0,2},{1,3},{2,0},{3,1},{4,6},{5,7},{6,4},{7,5},{8,10},{9,11},{10,... | collective-permute-start | bytes 6291464 | tf_op jit(solution)/shard_map/ppermute | solution.py:21
  637.2 200.0 %collective-permute-start.60 = (bf16[32,1024]{1,0:T(8,128)(2,1)S(1)}, bf16[32,1024]{1,0:T(8,128)(2,1)}, u32[]{:S(2)}, u32[]{:S(2)}) collective-permute-start(bf16[32,1024]{1,0:T(8,128)(2,1)S(1)} %add_convert_fusion.20), channel_id=1, source_target_pairs={{0,16},{4,20},{8,24},{12,28},{16,0},{20,4},{24,8},{28,12},{1,17},{... | collective-permute-start | bytes 196616 | tf_op jit(solution)/shard_map/ppermute | solution.py:21
  685.6 67.1 %collective-permute-start.64 = (bf16[256,3072]{1,0:T(8,128)(2,1)S(1)}, bf16[256,3072]{1,0:T(8,128)(2,1)S(1)}, u32[]{:S(2)}, u32[]{:S(2)}) collective-permute-start(bf16[256,3072]{1,0:T(8,128)(2,1)S(1)} %fusion.12), channel_id=1, source_target_pairs={{0,2},{1,3},{2,0},{3,1},{4,6},{5,7},{6,4},{7,5},{8,10},{9,11},{10,... | collective-permute-start | bytes 4718600 | tf_op jit(solution)/shard_map/ppermute | solution.py:21
  686.1 41.1 %collective-permute-start.81 = (bf16[512,1024]{1,0:T(8,128)(2,1)S(1)}, bf16[512,1024]{1,0:T(8,128)(2,1)S(1)}, u32[]{:S(2)}, u32[]{:S(2)}) collective-permute-start(bf16[512,1024]{1,0:T(8,128)(2,1)S(1)} %constant_dynamic-slice_fusion.7), channel_id=1, source_target_pairs={{0,4},{4,0},{8,12},{12,8},{16,20},{20,16},{24,28},{28,24},{1,5},{5... | collective-permute-start | bytes 3145736 | tf_op jit(solution)/shard_map/ppermute | solution.py:21
  725.9 31.2 %collective-permute-start.89 = (bf16[512,1024]{1,0:T(8,128)(2,1)S(1)}, bf16[512,1024]{1,0:T(8,128)(2,1)S(1)}, u32[]{:S(2)}, u32[]{:S(2)}) collective-permute-start(bf16[512,1024]{1,0:T(8,128)(2,1)S(1)} %constant_dynamic-slice_fusion.3), channel_id=1, source_target_pairs={{0,4},{4,0},{8,12},{12,8},{16,20},{20,16},{24,28},{28,24},{1,5},{5... | collective-permute-start | bytes 3145736 | tf_op jit(solution)/shard_map/ppermute | solution.py:21
  727.6 31.1 %collective-permute-start.82 = (bf16[256,1024]{1,0:T(8,128)(2,1)S(1)}, bf16[256,1024]{1,0:T(8,128)(2,1)S(1)}, u32[]{:S(2)}, u32[]{:S(2)}) collective-permute-start(bf16[256,1024]{1,0:T(8,128)(2,1)S(1)} %constant_dynamic-slice_fusion.6), channel_id=1, source_target_pairs={{0,8},{4,12},{8,0},{12,4},{16,24},{20,28},{24,16},{28,20},{1,9},{5... | collective-permute-start | bytes 1572872 | tf_op jit(solution)/shard_map/ppermute | solution.py:21
  776.6 26.8 %collective-permute-start.91 = (bf16[128,1024]{1,0:T(8,128)(2,1)S(1)}, bf16[128,1024]{1,0:T(8,128)(2,1)S(1)}, u32[]{:S(2)}, u32[]{:S(2)}) collective-permute-start(bf16[128,1024]{1,0:T(8,128)(2,1)S(1)} %constant_dynamic-slice_fusion.1), channel_id=1, source_target_pairs={{0,16},{4,20},{8,24},{12,28},{16,0},{20,4},{24,8},{28,12},{1,17},{... | collective-permute-start | bytes 786440 | tf_op jit(solution)/shard_map/ppermute | solution.py:21
  776.8 32.9 %collective-permute-start.84 = (bf16[128,1024]{1,0:T(8,128)(2,1)S(1)}, bf16[128,1024]{1,0:T(8,128)(2,1)S(1)}, u32[]{:S(2)}, u32[]{:S(2)}) collective-permute-start(bf16[128,1024]{1,0:T(8,128)(2,1)S(1)} %add_convert_fusion.13), channel_id=1, source_target_pairs={{0,16},{4,20},{8,24},{12,28},{16,0},{20,4},{24,8},{28,12},{1,17},{... | collective-permute-start | bytes 786440 | tf_op jit(solution)/shard_map/ppermute | solution.py:21
  789.3 28.9 %collective-permute-start.67 = (bf16[32,3072]{1,0:T(8,128)(2,1)S(1)}, bf16[32,3072]{1,0:T(8,128)(2,1)S(1)}, u32[]{:S(2)}, u32[]{:S(2)}) collective-permute-start(bf16[32,3072]{1,0:T(8,128)(2,1)S(1)} %constant_dynamic-slice_fusion.11), channel_id=1, source_target_pairs={{0,16},{4,20},{8,24},{12,28},{16,0},{20,4},{24,8},{28,12},{1,17},{... | collective-permute-start | bytes 589832 | tf_op jit(solution)/shard_map/ppermute | solution.py:21
  809.8 26.1 %collective-permute-start.85 = (bf16[256,1024]{1,0:T(8,128)(2,1)S(1)}, bf16[256,1024]{1,0:T(8,128)(2,1)S(1)}, u32[]{:S(2)}, u32[]{:S(2)}) collective-permute-start(bf16[256,1024]{1,0:T(8,128)(2,1)S(1)} %maximum_select_fusion.21), channel_id=1, source_target_pairs={{0,8},{4,12},{8,0},{12,4},{16,24},{20,28},{24,16},{28,20},{1,9},{5... | collective-permute-start | bytes 1572872 | tf_op jit(solution)/shard_map/ppermute | solution.py:21
  822.6 24.2 %collective-permute-start.93 = (bf16[256,1024]{1,0:T(8,128)(2,1)S(1)}, bf16[256,1024]{1,0:T(8,128)(2,1)S(1)}, u32[]{:S(2)}, u32[]{:S(2)}) collective-permute-start(bf16[256,1024]{1,0:T(8,128)(2,1)S(1)} %maximum_select_fusion.22), channel_id=1, source_target_pairs={{0,8},{4,12},{8,0},{12,4},{16,24},{20,28},{24,16},{28,20},{1,9},{5... | collective-permute-start | bytes 1572872 | tf_op jit(solution)/shard_map/ppermute | solution.py:21
  830.3 25.5 %collective-permute-start.69 = (bf16[64,3072]{1,0:T(8,128)(2,1)S(1)}, bf16[64,3072]{1,0:T(8,128)(2,1)S(1)}, u32[]{:S(2)}, u32[]{:S(2)}) collective-permute-start(bf16[64,3072]{1,0:T(8,128)(2,1)S(1)} %maximum_select_fusion.23), channel_id=1, source_target_pairs={{0,8},{4,12},{8,0},{12,4},{16,24},{20,28},{24,16},{28,20},{1,9},{5... | collective-permute-start | bytes 1179656 | tf_op jit(solution)/shard_map/ppermute | solution.py:21
  836.4 55.0 %collective-permute-start.86 = (bf16[512,1024]{1,0:T(8,128)(2,1)S(1)}, bf16[512,1024]{1,0:T(8,128)(2,1)S(1)}, u32[]{:S(2)}, u32[]{:S(2)}) collective-permute-start(bf16[512,1024]{1,0:T(8,128)(2,1)S(1)} %maximum_select_fusion.10), channel_id=1, source_target_pairs={{0,4},{4,0},{8,12},{12,8},{16,20},{20,16},{24,28},{28,24},{1,5},{5... | collective-permute-start | bytes 3145736 | tf_op jit(solution)/shard_map/ppermute | solution.py:21
  847.3 47.0 %collective-permute-start.94 = (bf16[512,1024]{1,0:T(8,128)(2,1)S(1)}, bf16[512,1024]{1,0:T(8,128)(2,1)S(1)}, u32[]{:S(2)}, u32[]{:S(2)}) collective-permute-start(bf16[512,1024]{1,0:T(8,128)(2,1)S(1)} %maximum_select_fusion.11), channel_id=1, source_target_pairs={{0,4},{4,0},{8,12},{12,8},{16,20},{20,16},{24,28},{28,24},{1,5},{5... | collective-permute-start | bytes 3145736 | tf_op jit(solution)/shard_map/ppermute | solution.py:21
  852.6 37.7 %collective-permute-start.62 = (bf16[128,1024]{1,0:T(8,128)(2,1)S(1)}, bf16[128,1024]{1,0:T(8,128)(2,1)S(1)}, u32[]{:S(2)}, u32[]{:S(2)}) collective-permute-start(bf16[128,1024]{1,0:T(8,128)(2,1)S(1)} %maximum_select_fusion.25), channel_id=1, source_target_pairs={{0,4},{4,0},{8,12},{12,8},{16,20},{20,16},{24,28},{28,24},{1,5},{5... | collective-permute-start | bytes 786440 | tf_op jit(solution)/shard_map/ppermute | solution.py:21
  856.0 42.7 %collective-permute-start.70 = (bf16[128,3072]{1,0:T(8,128)(2,1)S(1)}, bf16[128,3072]{1,0:T(8,128)(2,1)S(1)}, u32[]{:S(2)}, u32[]{:S(2)}) collective-permute-start(bf16[128,3072]{1,0:T(8,128)(2,1)S(1)} %maximum_select_fusion.12), channel_id=1, source_target_pairs={{0,4},{4,0},{8,12},{12,8},{16,20},{20,16},{24,28},{28,24},{1,5},{5... | collective-permute-start | bytes 2359304 | tf_op jit(solution)/shard_map/ppermute | solution.py:21
  (129 other events, 1524.6 us)

commit v2 on v1

--- a/solution.py
+++ b/solution.py
@@ -61,20 +61,6 @@
     got = swap(sent, "fsdp", 2)
     rest = swap(got, "grp", 1)
     return merge(got, rest, "grp", 1)
-
-
-def gather_far_eighth(own):
-    rows = own.shape[0]
-    part = rows // 8
-    which = lax.axis_index("grp") % 8
-    sent = lax.dynamic_slice_in_dim(own, which * part, part, 0)
-    got = swap(sent, "fsdp", 2)[None]
-    for bit in (2, 4):
-        got = merge(got, swap(got, "grp", bit), "grp", bit)
-    rest = swap(got, "grp", 1)
-    odd = has_bit("grp", 1)
-    both = jnp.where(odd, jnp.stack([rest, got], axis=1), jnp.stack([got, rest], axis=1))
-    return both.reshape(own.shape)
 
 
 def four_shards(own, far):
@@ -92,17 +78,6 @@
     return whole
 
 
-def reduce_gradient(quarter, share):
-    def low(value):
-        return value.astype(jnp.bfloat16)
-
-    sent = jnp.stack([low(quarter(1) * share), low(quarter(3) * share)])
-    got = swap(sent, "fsdp", 1)
-    far = swap(low(quarter(2) * share + got[1].astype(jnp.float32)), "fsdp", 2)
-    held = low(quarter(0) * share + got[0].astype(jnp.float32) + far.astype(jnp.float32))
-    return reduce_groups(held)
-
-
 def group_bits():
     bits = []
     bit = 1
@@ -110,24 +85,6 @@
         bits.append(bit)
         bit *= 2
     return bits
-
-
-def halve(held, axis, bit):
-    half = held.shape[0] // 2
-    upper = has_bit(axis, bit).astype(jnp.int32)
-    keep = lax.dynamic_slice_in_dim(held, upper * half, half, 0)
-    give = lax.dynamic_slice_in_dim(held, (1 - upper) * half, half, 0)
-    got = swap(give, axis, bit)
-    return (keep.astype(jnp.float32) + got.astype(jnp.float32)).astype(held.dtype)
-
-
-def reduce_groups(held):
-    bits = group_bits()
-    for bit in bits:
-        held = halve(held, "grp", bit)
-    for bit in reversed(bits):
-        held = merge(held, swap(held, "grp", bit), "grp", bit)
-    return held.astype(jnp.float32)
 
 
 def slot_softmax(patch_ref, coeff_ref, mask_ref):
@@ -459,6 +416,314 @@
     return result[0], result[1 : 1 + shards], result[1 + shards :]
 
 
+def feed_kernel(
+    first_ref, second_ref, grad_ref, up_ref, down_ref, bias_ref, rows_ref, gelu_ref, pre_ref, out_ref, back_ref, bias_grad_ref
+):
+    tile = first_ref.shape[0]
+    entry = jnp.concatenate([first_ref[...], second_ref[...]], axis=0)
+    grad = jnp.concatenate([grad_ref[0], grad_ref[1]], axis=0)
+    pre_act = jnp.dot(entry, up_ref[...], preferred_element_type=jnp.float32) + bias_ref[...]
+    cdf = 0.5 * (1.0 + lax.erf(pre_act * 0.7071067811865476))
+    density = jnp.exp(-0.5 * pre_act * pre_act) * 0.3989422804014327
+    gelu = (pre_act * cdf).astype(jnp.bfloat16)
+    act_grad = lax.dot_general(
+        grad, down_ref[...], (((1,), (1,)), ((), ())), preferred_element_type=jnp.float32
+    )
+    pre_grad = (act_grad * (cdf + pre_act * density)).astype(jnp.bfloat16)
+    out = jnp.dot(gelu, down_ref[...], preferred_element_type=jnp.float32).astype(jnp.bfloat16)
+    back = lax.dot_general(
+        pre_grad, up_ref[...], (((1,), (1,)), ((), ())), preferred_element_type=jnp.float32
+    ).astype(jnp.bfloat16)
+
+    @pl.when(pl.program_id(0) == 0)
+    def _():
+        bias_grad_ref[...] = jnp.zeros_like(bias_grad_ref)
+
+    bias_grad_ref[...] += jnp.sum(pre_grad.astype(jnp.float32), axis=0, keepdims=True)
+    for ref, value in (
+        (rows_ref, entry),
+        (gelu_ref, gelu),
+        (pre_ref, pre_grad),
+        (out_ref, out),
+        (back_ref, back),
+    ):
+        ref[0] = value[:tile]
+        ref[1] = value[tile:]
+
+
+def feed(first, second, grads, up, down, bias):
+    rows, width = first.shape
+    hidden = up.shape[1]
+    tile = min(rows, 128)
+    one = pl.BlockSpec((tile, width), lambda i: (i, 0))
+    pair = pl.BlockSpec((2, tile, width), lambda i: (0, i, 0))
+    pair_hidden = pl.BlockSpec((2, tile, hidden), lambda i: (0, i, 0))
+
+    def fixed(shape):
+        return pl.BlockSpec(shape, lambda i: (0, 0))
+
+    out = jax.ShapeDtypeStruct((2, rows, width), jnp.bfloat16)
+    out_hidden = jax.ShapeDtypeStruct((2, rows, hidden), jnp.bfloat16)
+    return pl.pallas_call(
+        feed_kernel,
+        grid=(rows // tile,),
+        in_specs=[
+            one,
+            one,
+            pair,
+            fixed(up.shape),
+            fixed(down.shape),
+            fixed((1, hidden)),
+        ],
+        out_specs=[pair, pair_hidden, pair_hidden, pair, pair, fixed((1, hidden))],
+        out_shape=[
+            out,
+            out_hidden,
+            out_hidden,
+            out,
+            out,
+            jax.ShapeDtypeStruct((1, hidden), jnp.float32),
+        ],
+        compiler_params=pltpu.CompilerParams(vmem_limit_bytes=VMEM_LIMIT),
+        cost_estimate=pl.CostEstimate(
+            flops=16 * rows * width * hidden * 2,
+            bytes_accessed=16 * rows * width,
+            transcendentals=4 * rows * hidden,
+        ),
+        name="feed",
+    )(first, second, grads, up, down, bias)
+
+
+def flip(index, bit):
+    bit_set = (index // bit) % 2
+    return index + bit - 2 * bit * bit_set, bit_set
+
+
+def total_kernel(group_size, widths, share_ref, *refs):
+    pairs = [(refs[2 * i], refs[2 * i + 1]) for i in range(3)]
+    bundle_ref = refs[6]
+    outs = refs[7:10]
+    bundle_out = refs[10]
+    send1, recv1, own1, send2, recv2, hold, halves, done, full, send_sem, recv_sem = refs[11:]
+    me = lax.axis_index("fsdp")
+    group = lax.axis_index("grp")
+    core_partner, core = flip(me, 1)
+    far_partner, far = flip(me, 2)
+    quarter = own1.shape[2]
+    wide = jnp.float32
+    low = jnp.bfloat16
+
+    steps = []
+    size, bit, offset = quarter, 1, 0
+    while bit < group_size:
+        partner, bit_set = flip(group, bit)
+        halving = size >= 64
+        steps.append((partner, bit_set, halving, size, offset))
+        if halving:
+            size = size // 2
+            offset = offset + bit_set * size
+        bit *= 2
+    halvings = [i for i, step in enumerate(steps) if step[2]]
+
+    barrier = pltpu.get_barrier_semaphore()
+    partners = [{"fsdp": core_partner}, {"fsdp": far_partner}]
+    partners += [{"grp": step[0]} for step in steps]
+    for partner in partners:
+        pl.semaphore_signal(
+            barrier, inc=1, device_id=partner, device_id_type=pl.DeviceIdType.MESH
+        )
+    pl.semaphore_wait(barrier, len(partners))
+
+    chunks = [(None, None, None, 0, bundle_ref.shape[1])]
+    for (left, right), out in zip(pairs, outs):
+        for start in range(0, right.shape[1], widths):
+            chunks.append((left, right, out, start, widths))
+
+    def copy(stage, c, src, dst, device):
+        return pltpu.make_async_remote_copy(
+            src_ref=src,
+            dst_ref=dst,
+            send_sem=send_sem.at[stage, c],
+            recv_sem=recv_sem.at[stage, c],
+            device_id=device,
+            device_id_type=pl.DeviceIdType.MESH,
+        )
+
+    def span(start, size):
+        return pl.ds(pl.multiple_of(start, 16), size)
+
+    def columns(c):
+        return pl.ds(0, chunks[c][4])
+
+    def core_copy(c):
+        cols = columns(c)
+        return copy(
+            0, c, send1.at[c, :, :, cols], recv1.at[c, :, :, cols], {"fsdp": core_partner}
+        )
+
+    def far_copy(c):
+        cols = columns(c)
+        return copy(1, c, send2.at[c, :, cols], recv2.at[c, :, cols], {"fsdp": far_partner})
+
+    def step_copy(i, c):
+        partner, bit_set, halving, size, offset = steps[i]
+        cols = columns(c)
+        if halving:
+            size = size // 2
+            offset = offset + (1 - bit_set) * size
+        src = hold.at[c, span(offset, size), cols]
+        dst = halves[i].at[c, :, cols]
+        return copy(2 + i, c, src, dst, {"grp": partner})
+
+    def back_copy(i, c):
+        partner, bit_set, halving, size, offset = steps[i]
+        size = size // 2
+        offset = offset + bit_set * size
+        at = done.at[c, span(offset, size), columns(c)]
+        return copy(2 + len(steps) + i, c, at, at, {"grp": partner})
+
+    def begin(c):
+        left, right, out, start, width = chunks[c]
+        cols = columns(c)
+
+        def part(q):
+            rows = span(q * quarter, quarter)
+            if left is None:
+                return bundle_ref[rows, :]
+            value = jnp.dot(
+                left[rows, :], right[:, start : start + width], preferred_element_type=wide
+            )
+            return (value * share_ref[0]).astype(low)
+
+        for y in range(2):
+            send1[c, y, :, cols] = part(2 * y + 1 - core)
+        core_copy(c).start()
+        for y in range(2):
+            own1[c, y, :, cols] = part(2 * y + core)
+
+    def after_core(c):
+        cols = columns(c)
+        core_copy(c).wait()
+        value = own1[c, 1 - far, :, cols].astype(wide) + recv1[c, 1 - far, :, cols].astype(wide)
+        send2[c, :, cols] = value.astype(low)
+        far_copy(c).start()
+
+    def after_far(c):
+        cols = columns(c)
+        far_copy(c).wait()
+        value = own1[c, far, :, cols].astype(wide) + recv1[c, far, :, cols].astype(wide)
+        hold[c, :, cols] = (value + recv2[c, :, cols].astype(wide)).astype(low)
+        step_copy(0, c).start()
+
+    def after_step(i, c):
+        cols = columns(c)
+        step_copy(i, c).wait()
+        partner, bit_set, halving, size, offset = steps[i]
+        if halving:
+            size = size // 2
+            offset = offset + bit_set * size
+        at = span(offset, size)
+        value = hold[c, at, cols].astype(wide) + halves[i][c, :, cols].astype(wide)
+        if i + 1 < len(steps):
+            hold[c, at, cols] = value.astype(low)
+            step_copy(i + 1, c).start()
+        else:
+            done[c, at, cols] = value.astype(low)
+            back_copy(halvings[-1], c).start()
+
+    def after_back(k, c):
+        back_copy(halvings[k], c).wait()
+        if k > 0:
+            back_copy(halvings[k - 1], c).start()
+        else:
+            left, right, out, start, width = chunks[c]
+            if out is None:
+                full[me] = done[c, :, columns(c)]
+                bundle_core().start()
+            else:
+                out[:, start : start + width] = done[c].astype(wide)
+
+    last = 2 + 2 * len(steps)
+
+    def bundle_core():
+        return copy(last, 0, full.at[me], full.at[me], {"fsdp": core_partner})
+
+    def bundle_far():
+        at = full.at[pl.ds(me - core, 2)]
+        return copy(last, 1, at, at, {"fsdp": far_partner})
+
+    def finish_core(c):
+        bundle_core().wait()
+        bundle_far().start()
+
+    def finish_far(c):
+        bundle_far().wait()
+        for q in range(4):
+            bundle_out[q * quarter : (q + 1) * quarter, :] = full[q].astype(wide)
+
+    stages = [begin, after_core, after_far]
+    stages += [functools.partial(after_step, i) for i in range(len(steps))]
+    stages += [functools.partial(after_back, k) for k in reversed(range(len(halvings)))]
+    order = [1, 0] + list(range(2, len(stages)))
+    extra = [finish_core, finish_far]
+    for t in range(len(chunks) + len(stages) - 1):
+        for s in order:
+            if 0 <= t - s < len(chunks):
+                stages[s](t - s)
+        if 0 <= t - len(stages) < len(extra):
+            extra[t - len(stages)](0)
+
+
+def total(group_size, share, qkv_pair, agg_pair, proj_pair, bundle):
+    pairs = [qkv_pair, agg_pair, proj_pair]
+    width = qkv_pair[0].shape[0]
+    quarter = width // 4
+    widths = 512
+    count = 1 + sum(right.shape[1] // widths for left, right in pairs)
+    steps = 0
+    halves = []
+    size = quarter
+    while 2**steps < group_size:
+        if size >= 64:
+            size //= 2
+        halves.append(pltpu.VMEM((count, size, widths), jnp.bfloat16))
+        steps += 1
+    low = jnp.bfloat16
+    whole = pl.BlockSpec(memory_space=pltpu.VMEM)
+    scratch = [
+        pltpu.VMEM((count, 2, quarter, widths), low),
+        pltpu.VMEM((count, 2, quarter, widths), low),
+        pltpu.VMEM((count, 2, quarter, widths), low),
+        pltpu.VMEM((count, quarter, widths), low),
+        pltpu.VMEM((count, quarter, widths), low),
+        pltpu.VMEM((count, quarter, widths), low),
+        halves,
+        pltpu.VMEM((count, quarter, widths), low),
+        pltpu.VMEM((4, quarter, bundle.shape[1]), low),
+        pltpu.SemaphoreType.DMA((3 + 2 * steps, count)),
+        pltpu.SemaphoreType.DMA((3 + 2 * steps, count)),
+    ]
+    return pl.pallas_call(
+        functools.partial(total_kernel, group_size, widths),
+        in_specs=[pl.BlockSpec(memory_space=pltpu.SMEM)] + [whole] * 7,
+        out_specs=[whole] * 4,
+        out_shape=[
+            jax.ShapeDtypeStruct((quarter, right.shape[1]), jnp.float32) for left, right in pairs
+        ]
+        + [jax.ShapeDtypeStruct(bundle.shape, jnp.float32)],
+        scratch_shapes=scratch,
+        compiler_params=pltpu.CompilerParams(
+            collective_id=0, has_side_effects=True, vmem_limit_bytes=VMEM_LIMIT
+        ),
+        cost_estimate=pl.CostEstimate(
+            flops=sum(2 * left.size * right.shape[1] for left, right in pairs),
+            bytes_accessed=200_000_000,
+            transcendentals=0,
+        ),
+        name="total",
+    )(share, *[array for pair in pairs for array in pair], bundle)
+
+
 def normalise(values_in):
     row_mean = jnp.mean(values_in, axis=-1, keepdims=True)
     centred = values_in - row_mean
@@ -530,7 +795,6 @@
         [
             patch_weight.reshape(own_vars * PIX, width),
             var_embed,
-            up_bias[None, :],
         ],
         axis=0,
     )
@@ -544,7 +808,6 @@
         table_parts.append(jnp.concatenate([pixels, embeds], axis=1).transpose(1, 0, 2))
     stacked = in_order(table_parts, axis=1)
     stacked_rows = stacked.reshape((PIX + 1) * VTOT, width)
-    up_biases = [part[own_vars * (PIX + 1)].astype(wide) for part in row_sets]
 
     own_query = lax.dynamic_slice_in_dim(agg_query, me * own_width, own_width, 0)
     query_sum = product(own_query[None, :], query_weight)
@@ -594,8 +857,13 @@
     full_qkv = in_order(qkv_shards)
     proj_shards = four_shards(proj_weight, gather_far_half(proj_weight))
     full_proj = in_order(proj_shards)
-    up_shards = four_shards(up_weight, gather_far_eighth(up_weight))
-    down_shards = four_shards(down_weight, gather_far_eighth(down_weight))
+    upstream = out_grad.astype(wide) * own_valid[:, None].astype(wide)
+    down_grad = upstream.astype(low)
+    near_down_grad = swap(down_grad, "fsdp", 1)
+    far_down_grad = swap(down_grad, "fsdp", 2)
+    last_down_grad = swap(far_down_grad, "fsdp", 1)
+    near_grads = jnp.stack([down_grad, near_down_grad])
+    far_grads = jnp.stack([far_down_grad, last_down_grad])
 
     patch_rows = patches.transpose(1, 0, 2)
     slot_mask = jnp.where(present, 0.0, masked_out).astype(wide)[:, None]
@@ -615,46 +883,42 @@
     middle = embedded + (product(context, full_proj) + proj_bias)
     xhat2, inverse2 = normalise(middle)
     normed2 = (xhat2 * norm2_gain + norm2_shift).astype(low)
-    gelu_parts = []
-    slope_parts = []
-    down_sum = 0.0
-    for j in range(4):
-        pre_act = product(normed2, up_shards[j]) + up_biases[j]
-        cdf = 0.5 * (1.0 + lax.erf(pre_act * 0.7071067811865476))
-        density = jnp.exp(-0.5 * pre_act * pre_act) * 0.3989422804014327
-        gelu_parts.append((pre_act * cdf).astype(low))
-        slope_parts.append(cdf + pre_act * density)
-        down_sum = down_sum + product(gelu_parts[j], down_shards[j])
+    near_normed2 = swap(normed2, "fsdp", 1)
+    far_normed2 = swap(normed2, "fsdp", 2)
+    last_normed2 = swap(far_normed2, "fsdp", 1)
+    bias_row = up_bias.astype(wide)[None, :]
+    near = feed(normed2, near_normed2, near_grads, up_weight, down_weight, bias_row)
+    far = feed(far_normed2, last_normed2, far_grads, up_weight, down_weight, bias_row)
+    far_got = swap(far[4][1], "fsdp", 1)
+    far_sum = (far[4][0].astype(wide) + far_got.astype(wide)).astype(low)
+    far_back = swap(far_sum, "fsdp", 2)
+    near_back = swap(near[4][1], "fsdp", 1)
+
+    def both_left(left, right):
+        def one(i):
+            return left_product(
+                left[i].reshape(-1, left[i].shape[2]), right[i].reshape(-1, right[i].shape[2])
+            )
+
+        return ((one(0) + one(1)) * count_share).astype(low)
+
+    down_weight_part = both_left([near[1], far[1]], [near_grads, far_grads])
+    up_weight_part = both_left([near[0], far[0]], [near[2], far[2]])
+    down_weight_grad = lax.psum(down_weight_part, "grp").astype(wide)
+    up_weight_grad = lax.psum(up_weight_part, "grp").astype(wide)
+    up_bias_grad = near[5] + far[5]
+    down_bias_grad = column_sums(down_grad)
+    normed2_grad = near[4][0].astype(wide) + near_back.astype(wide) + far_back.astype(wide)
+    out_got = swap(jnp.stack([near[3][1], far[3][1]]), "fsdp", 1)
+    out_far = swap((far[3][0].astype(wide) + out_got[1].astype(wide)).astype(low), "fsdp", 2)
+    down_sum = near[3][0].astype(wide) + out_got[0].astype(wide) + out_far.astype(wide)
     output = (middle + down_sum + down_bias).astype(low)
-
-    upstream = out_grad.astype(wide) * own_valid[:, None].astype(wide)
-    down_grad = upstream.astype(low)
-    down_bias_grad = column_sums(down_grad)
-    down_weight_grad = reduce_gradient(
-        lambda j: left_product(gelu_parts[j], down_grad), count_share
-    )
-    pre_grads = []
-    up_bias_parts = []
-    normed2_grad = 0.0
-    for j in range(4):
-        act_grad = right_product(down_grad, down_shards[j])
-        pre_grads.append((act_grad * slope_parts[j]).astype(low))
-        up_bias_parts.append(column_sums(pre_grads[j])[None, :])
-        normed2_grad = normed2_grad + right_product(pre_grads[j], up_shards[j])
-    up_bias_grad = in_order(up_bias_parts)
-    up_weight_grad = reduce_gradient(lambda j: left_product(normed2, pre_grads[j]), count_share)
     norm2_gain_grad = jnp.sum(normed2_grad * xhat2, axis=0)
     norm2_shift_grad = jnp.sum(normed2_grad, axis=0)
     middle_grad = upstream + norm_back(normed2_grad, xhat2, inverse2, norm2_gain)
     attended_grad = middle_grad.astype(low)
     proj_bias_grad = column_sums(attended_grad)
 
-    def columns(array, j):
-        return lax.dynamic_slice_in_dim(array, (me ^ j) * own_width, own_width, 1)
-
-    proj_weight_grad = reduce_gradient(
-        lambda j: left_product(columns(context, j), attended_grad), count_share
-    )
     context_grad = right_product(attended_grad, full_proj).astype(low)
 
     q_part, far_k, far_v = attend_back(
@@ -676,14 +940,6 @@
     norm1_shift_grad = jnp.sum(normed1_grad, axis=0)
     embedded_grad = (middle_grad + norm_back(normed1_grad, xhat1, inverse1, norm1_gain)).astype(low)
     agg_bias_grad = column_sums(embedded_grad)
-    qkv_weight_grad = reduce_gradient(
-        lambda j: left_product(columns(normed1, j), qkv_grad), count_share
-    )
-
-    def head_rows(j):
-        return lax.dynamic_slice_in_dim(heads_t, (me ^ j) * own_width, own_width, 0)
-
-    agg_proj_grad = reduce_gradient(lambda j: product(head_rows(j), embedded_grad), count_share)
     heads_grad = right_product(full_agg_proj, embedded_grad).astype(low)
     input_scale = (group_count * count_share)[None]
     table_grad, coeff_grad, patch_grad = aggregate_back(
@@ -711,20 +967,20 @@
         norm2_shift_grad,
         down_bias_grad,
     ]
-    pieces = [table_sum, coeff_flat.reshape(coeff_rows, width), jnp.stack(vectors), up_bias_grad]
+    up_bias_rows = lax.dynamic_update_slice_in_dim(jnp.zeros((4, width), wide), up_bias_grad, me, 0)
+    pieces = [table_sum, coeff_flat.reshape(coeff_rows, width), jnp.stack(vectors), up_bias_rows]
     bundle = jnp.concatenate(pieces, axis=0) * count_share
-    used = bundle.shape[0]
-    step = 4 * group_count
-    bundle = jnp.pad(bundle, ((0, -used % step), (0, 0)))
-    for bit in (1, 2):
-        bundle = halve(bundle, "fsdp", bit)
-    bits = group_bits()
-    for bit in bits:
-        bundle = halve(bundle, "grp", bit)
-    for bit in reversed(bits):
-        bundle = merge(bundle, swap(bundle, "grp", bit), "grp", bit)
-    for bit in (2, 1):
-        bundle = merge(bundle, swap(bundle, "fsdp", bit), "fsdp", bit)
+    bundle = jnp.pad(bundle, ((0, -bundle.shape[0] % 128), (0, 0))).astype(low)
+    bundle_shape = bundle.shape
+    qkv_weight_grad, agg_proj_grad, proj_weight_grad, bundle = total(
+        group_count,
+        count_share[None],
+        (normed1.T, qkv_grad),
+        (heads_t, embedded_grad),
+        (context.T, attended_grad),
+        bundle.reshape(width, -1),
+    )
+    bundle = bundle.reshape(bundle_shape)
     table_total = bundle[: table_sum.shape[0]]
     at = table_sum.shape[0]
     coeff_total = bundle[at : at + coeff_rows].reshape(-1)[: coeff_sum.shape[0]]

time: 913 us -> 693 us (0.76)
  waiting for transfers between devices: 383 us -> 183 us
  Pallas kernels: 123 us -> 256 us
  matrix products: 130 us -> 50.4 us
  starting transfers between devices: 97 us -> 30.7 us
  other arithmetic: 85.4 us -> 61.2 us
  between operations: 6.29 us -> 18.9 us
  local copies, waits for them, and re-layouts: 77.1 us -> 88 us
    ppermute x95 -> x44, waiting for transfers between devices: 383 us -> 183 us  [swap(): return lax.ppermute(value, axis, [(i, i ^ bit) for i in range(size)])]
    pallas_call x0 -> x3, Pallas kernels: none -> 133 us  [the longest x1 103 us: total(): pl.pallas_call(functools.partial(total_kernel, group_size, widths), in_sp...]
    ppermute x95 -> x44, starting transfers between devices: 97 us -> 30.7 us  [swap(): return lax.ppermute(value, axis, [(i, i ^ bit) for i in range(size)])]
    dot_general x13 -> x5, matrix products: 45.2 us -> 13.5 us  [right_product(): lax.dot_general(left_side, right_side, (((1,), (1,)), ((), ())), preferre...]
    dot_general x16 -> x4, matrix products: 41.7 us -> 11.4 us  [product(): return jnp.dot(left_side, right_side, preferred_element_type=jnp.float32)]
    dot_general x19 -> x7, matrix products: 36.7 us -> 19 us  [left_product(): lax.dot_general(left_side, right_side, (((0,), (0,)), ((), ())), preferre...]
    select_n x23 -> x0, other arithmetic: 15.5 us -> none  [the longest x21 9.43 us: merge(): jnp.where(has_bit(axis, bit), jnp.concatenate([other, mine], axis=0), jnp...]
    convert_element_type x25 -> x4, other arithmetic: 21.5 us -> 9.46 us  [the longest x1 4.22 us: on_device(): up_weight_grad = lax.psum(up_weight_part, 'grp').astype(wide)]
  transfers between devices with their start and end apart: 95 -> 45, of which waited for: 40 -> 17; matrix products, arithmetic and copies ran while one was open for 28% -> 19% of each run, Pallas kernels for 10% -> 20%
where the time goes in v2:
time: 693 us; the launch traced here: 688 us
  Pallas kernels  256 us (37%)
  waiting for transfers between devices  183 us (26%)
  local copies, waits for them, and re-layouts  88 us (13%)
  other arithmetic  61.2 us (9%)
  matrix products  50.4 us (7%)
  starting transfers between devices  30.7 us (4%)
  between operations  18.9 us (3%)
    ppermute x44, waiting for transfers between devices, swap(): return lax.ppermute(value, axis, [(i, i ^ bit) for i in range(size)])  183 us
    pallas_call x1, Pallas kernels, total(): pl.pallas_call(functools.partial(total_kernel, group_size, widths), in_sp...  103 us
    pallas_call x2, Pallas kernels, attend_back(): pl.pallas_call(functools.partial(attend_back_kernel, shards, head_dim, ol...  58.9 us
    pallas_call x2, Pallas kernels, attend(): pl.pallas_call(functools.partial(attend_kernel, shards, head_dim, old is...  38.5 us
    ppermute x44, starting transfers between devices, swap(): return lax.ppermute(value, axis, [(i, i ^ bit) for i in range(size)])  30.7 us
    pallas_call x2, Pallas kernels, feed(): pl.pallas_call(feed_kernel, grid=(rows // tile,), in_specs=[one, one, pai...  30.3 us
    dynamic_update_slice x19, local copies, waits for them, and re-layouts, in_order(): whole = lax.dynamic_update_slice_in_dim(whole, shard, (me ^ j) * size, axis)  22.9 us
    dot_general x7, matrix products, left_product(): lax.dot_general(left_side, right_side, (((0,), (0,)), ((), ())), preferre...  19 us
  transfers between devices with their start and end apart: 45, of which 17 were waited for; matrix products, arithmetic and copies ran while one was open for 19% of the time, Pallas kernels for 20%

profile of v2, /device:TPU:0, one launch (start us, length us, event | category | flops | bytes accessed | tf_op | source)
XLA Modules:
  0.0 688.1 jit_solution(8912740606290509941)
XLA Ops:
  9.4 2.6 collective-permute-start.7
  19.6 3.4 broadcast_in_dim.78
  36.1 2.3 dynamic_update_slice.79
  38.5 3.7 collective-permute-done.3
  48.2 9.2 %collective-permute-done.5 = bf16[2,60,1024]{2,1,0:T(8,128)(2,1)} collective-permute-done((bf16[2,60,1024]{2,1,0:T(8,128)(2,1)}, bf16[2,60,1024]{2,1,0:T(8,128)(2,1)}, u32[]{:S(2)}, u32[]{:S(2)}) %collective-permute-start.5) | collective-permute-done | bytes 245792 | tf_op jit(solution)/shard_map/ppermute | solution.py:21
  69.9 2.6 collective-permute-done.15
  81.5 3.4 constant_dynamic-update-slice_fusion.6
  84.9 6.5 collective-permute-done.16
  91.4 4.4 constant_dynamic-update-slice_fusion.5
  97.9 11.5 %aggregate.1.refs_2_ = bf16[1024,512]{1,0:T(8,128)(2,1)} custom-call(bf16[4,48,512]{2,1,0:T(8,128)(2,1)} %bitcast.205, f32[16,5,48,1]{3,2,1,0:T(8,128)} %copy.73.coeff_ref, f32[48,1]{1,0:T(8,128)} %copy.74.mask_ref, bf16[1024,240]{1,0:T(8,128)(2,1)} %copy.75.table_ref), custom_call_target="tpu_custom_call" | custom-call | flops 1006632960 | bytes 2097152 | tf_op jit(solution)/shard_map/aggregate/pallas_call | solution.py:120
  111.3 3.3 add_reduce_fusion
  115.1 2.7 constant_dynamic-update-slice_fusion.4
  117.7 6.7 convolution_convert_fusion.refs_1_.refs_2_.refs_4_.refs_5_.refs_7_
  130.1 45.4 %collective-permute-done.18.refs_2_.refs_4_.refs_5_.refs_7_ = bf16[512,2048]{1,0:T(8,128)(2,1)} collective-permute-done((bf16[512,2048]{1,0:T(8,128)(2,1)}, bf16[512,2048]{1,0:T(8,128)(2,1)}, u32[]{:S(2)}, u32[]{:S(2)}) %collective-permute-start.18) | collective-permute-done | bytes 2097184 | tf_op jit(solution)/shard_map/ppermute | solution.py:21
  183.0 5.9 collective-permute-done.23
  191.4 12.0 %collective-permute-done.29 = bf16[512,1024]{1,0:T(8,128)(2,1)} collective-permute-done((bf16[512,1024]{1,0:T(8,128)(2,1)S(1)}, bf16[512,1024]{1,0:T(8,128)(2,1)}, u32[]{:S(2)}, u32[]{:S(2)}) %collective-permute-start.29) | collective-permute-done | bytes 1048608 | tf_op jit(solution)/shard_map/ppermute | solution.py:21
  203.5 19.0 %attend.2 = (f32[512,1024]{1,0:T(8,128)}, f32[512,1024]{1,0:T(8,128)}, f32[512,1024]{1,0:T(8,128)}) custom-call(s32[2]{0:T(128)} %get-tuple-element.175.refs_0_, bf16[512,3072]{1,0:T(8,128)(2,1)} %copy-done.27, bf16[512,3072]{1,0:T(8,128)(2,1)} %copy-done.27, bf16[512,2048]{1,0:T(8,128)(2,1)} %collective-permute-done.20.refs_3_.refs_5_.refs_6_.refs_8_, ...), custom_call_target="tpu_custom_call" | custom-call | flops 8589934592 | bytes 4194304 | tf_op jit(solution)/shard_map/attend/pallas_call | solution.py:301
  222.5 19.5 %attend.3 = (bf16[512,1024]{1,0:T(8,128)(2,1)}, f32[512,1024]{1,0:T(8,128)}) custom-call(s32[2]{0:T(128)} %get-tuple-element.176.refs_0_, bf16[512,3072]{1,0:T(8,128)(2,1)} %copy-done.27, bf16[512,2048]{1,0:T(8,128)(2,1)} %collective-permute-done.18.refs_2_.refs_4_.refs_5_.refs_7_, bf16[512,2048]{1,0:T(8,128)(2,1)} %collective-permute-done.19.refs_3_.refs_5_.refs_6_.refs_8_, ...), custom_call_target="tpu_custom_call" | custom-call | flops 8589934592 | bytes 4194304 | tf_op jit(solution)/shard_map/attend/pallas_call | solution.py:301
  242.0 3.3 fusion.53
  252.3 2.9 collective-permute-start.40
  256.6 3.9 collective-permute-start.41
  263.5 3.1 pad_maximum_fusion.2.grad_ref
  266.6 5.7 collective-permute-done.27.first_ref
  273.3 14.9 %feed.2 = (bf16[2,512,1024]{2,1,0:T(8,128)(2,1)}, bf16[2,512,1024]{2,1,0:T(8,128)(2,1)}, bf16[2,512,1024]{2,1,0:T(8,128)(2,1)}, bf16[2,512,1024]{2,1,0:T(8,128)(...) custom-call(bf16[512,1024]{1,0:T(8,128)(2,1)} %copy-done.33, bf16[512,1024]{1,0:T(8,128)(2,1)} %copy-done.69, ...), custom_call_target="tpu_custom_call" | custom-call | flops 17179869184 | bytes 8388608 | tf_op jit(solution)/shard_map/feed/pallas_call | solution.py:467
  291.7 15.4 %feed.3 = (bf16[2,512,1024]{2,1,0:T(8,128)(2,1)}, bf16[2,512,1024]{2,1,0:T(8,128)(2,1)}, bf16[2,512,1024]{2,1,0:T(8,128)(2,1)}, bf16[2,512,1024]{2,1,0:T(8,128)(...) custom-call(bf16[512,1024]{1,0:T(8,128)(2,1)} %collective-permute-done.27.first_ref, ...), custom_call_target="tpu_custom_call" | custom-call | flops 17179869184 | bytes 8388608 | tf_op jit(solution)/shard_map/feed/pallas_call | solution.py:467
  310.9 2.4 fusion.43
  313.3 2.4 fusion.60
  318.3 3.7 fusion.3
  324.8 5.3 fusion.1
  330.2 13.3 %collective-permute-done.35 = bf16[512,1024]{1,0:T(8,128)(2,1)} collective-permute-done((bf16[512,1024]{1,0:T(8,128)(2,1)}, bf16[512,1024]{1,0:T(8,128)(2,1)}, u32[]{:S(2)}, u32[]{:S(2)}) %collective-permute-start.35) | collective-permute-done | bytes 1048608 | tf_op jit(solution)/shard_map/ppermute | solution.py:21
  343.4 3.7 multiply_reduce_fusion
  347.2 17.8 %collective-permute-done.32 = bf16[512,1024]{1,0:T(8,128)(2,1)} collective-permute-done((bf16[512,1024]{1,0:T(8,128)(2,1)}, bf16[512,1024]{1,0:T(8,128)(2,1)}, u32[]{:S(2)}, u32[]{:S(2)}) %collective-permute-start.32) | collective-permute-done | bytes 1048608 | tf_op jit(solution)/shard_map/ppermute | solution.py:21
  365.0 5.1 convert_reduce_fusion.1
  372.3 29.3 %attend_back.2 = (f32[512,1024]{1,0:T(8,128)}, bf16[512,1024]{1,0:T(8,128)(2,1)}, bf16[512,1024]{1,0:T(8,128)(2,1)}, bf16[512,1024]{1,0:T(8,128)(2,1)}, bf16[512,1024]{1,0:T(8,128)(2,1)}) custom-call(s32[2]{0:T(128)} %get-tuple-element.176.refs_0_, bf16[512,3072]{1,0:T(8,128)(2,1)} %copy-done.27, bf16[512,1024]{1,0:T(8,128)(2,1)} %convolution_convert_fusion.2.refs_2_, ...), custom_call_target="tpu_custom_call" | custom-call | flops 21474836480 | bytes 8388608 | tf_op jit(solution)/shard_map/attend_back/pallas_call | solution.py:398
  403.5 29.6 %attend_back.3 = (bf16[512,1024]{1,0:T(8,128)(2,1)}, bf16[512,1024]{1,0:T(8,128)(2,1)}, bf16[512,1024]{1,0:T(8,128)(2,1)}, bf16[512,1024]{1,0:T(8,128)(2,1)}, bf16[512,1024]{1,0:T(8,128)(2,1)}) custom-call(s32[2]{0:T(128)} %get-tuple-element.175.refs_0_, bf16[512,3072]{1,0:T(8,128)(2,1)} %copy-done.27, bf16[512,1024]{1,0:T(8,128)(2,1)} %convolution_convert_fusion.2.refs_2_, ...), custom_call_target="tpu_custom_call" | custom-call | flops 21474836480 | bytes 8388608 | tf_op jit(solution)/shard_map/attend_back/pallas_call | solution.py:398
  433.1 3.3 pad_maximum_fusion.4
  445.2 52.3 %collective-permute-done.43 = bf16[240,1024]{1,0:T(8,128)(2,1)} collective-permute-done((bf16[240,1024]{1,0:T(8,128)(2,1)}, bf16[240,1024]{1,0:T(8,128)(2,1)}, u32[]{:S(2)}, u32[]{:S(2)}) %collective-permute-start.43) | collective-permute-done | bytes 491552 | tf_op jit(solution)/shard_map/ppermute | solution.py:21
  497.5 2.5 convert_add_fusion.2
  500.0 2.5 copy.85
  505.2 4.2 convert_element_type.261
  509.4 2.5 convert_element_type.263
  511.9 3.5 add_convert_fusion
  515.5 5.9 fusion.44
  526.0 4.2 convolution_convert_fusion.1.heads_ref
  530.2 14.1 %aggregate_back.1 = (f32[1024,240]{1,0:T(8,128)}, f32[16,5,48,1]{3,2,1,0:T(8,128)}, f32[4,48,512]{2,1,0:T(8,128)}) custom-call(bf16[4,48,512]{2,1,0:T(8,128)(2,1)} %bitcast.206, f32[16,5,48,1]{3,2,1,0:T(8,128)} %copy.73.coeff_ref, f32[48,1]{1,0:T(8,128)} %copy.74.mask_ref, bf16[1024,240]{1,0:T(8,128)(2,1)} %copy.75.table_ref, ...), custom_call_target="tpu_custom_call" | custom-call | flops 2013265920 | bytes 4194304 | tf_op jit(solution)/shard_map/aggregate_back/pallas_call | solution.py:180
  552.3 102.7 %total.1 = (f32[256,3072]{1,0:T(8,128)}, f32[256,1024]{1,0:T(8,128)}, f32[256,1024]{1,0:T(8,128)}, f32[1024,256]{1,0:T(8,128)}) custom-call(f32[1]{0:T(128)} %div.43.share_ref, bf16[1024,512]{1,0:T(8,128)(2,1)} %copy.84.refs_0_, bf16[512,3072]{1,0:T(8,128)(2,1)} %pad_maximum_fusion.refs_1_, bf16[1024,512]{1,0:T(8,128)(2,1)} %aggregate.1.refs_2_, ...), custom_call_target="tpu_custom_call" | custom-call | flops 5368709120 | bytes 200000000 | tf_op jit(solution)/shard_map/total/pallas_call | solution.py:706
  657.2 2.3 fusion.58
  675.6 2.3 copy.141
  (383 shorter events, 140.8 us)
Async XLA Ops:
  7.2 497.9 %all-reduce.5.cloned.1.call-start = ((), (), s32[]{:S(2)}) async-start(), calls=%async_computation | async-start | bytes 8388608 | tf_op jit(solution)/shard_map/psum | solution.py:908
  7.3 58.3 %collective-permute-start.6 = (bf16[256,1024]{1,0:T(8,128)(2,1)}, bf16[256,1024]{1,0:T(8,128)(2,1)}, u32[]{:S(2)}, u32[]{:S(2)}) collective-permute-start(bf16[256,1024]{1,0:T(8,128)(2,1)} %param.35), channel_id=1, source_target_pairs={{0,1},{1,0},{2,3},{3,2},{4,5},{5,4},{6,7},{7,6},{8,9},{9,8},{10,11... | collective-permute-start | bytes 1572872 | tf_op jit(solution)/shard_map/ppermute | solution.py:21
  9.4 38.7 %collective-permute-start.7 = (bf16[128,1024]{1,0:T(8,128)(2,1)}, bf16[128,1024]{1,0:T(8,128)(2,1)}, u32[]{:S(2)}, u32[]{:S(2)}) collective-permute-start(bf16[128,1024]{1,0:T(8,128)(2,1)} %constant_dynamic-slice_fusion.6), channel_id=1, source_target_pairs={{0,2},{1,3},{2,0},{3,1},{4,6},{5,7},{6,4},{7,5},{8,10},{9,11},{10,... | collective-permute-start | bytes 786440 | tf_op jit(solution)/shard_map/ppermute | solution.py:21
  14.9 27.3 %collective-permute-start.4 = (bf16[60,1024]{1,0:T(8,128)(2,1)}, bf16[60,1024]{1,0:T(8,128)(2,1)S(1)}, u32[]{:S(2)}, u32[]{:S(2)}) collective-permute-start(bf16[60,1024]{1,0:T(8,128)(2,1)} %constant_dynamic-update-slice_fusion.18), channel_id=1, source_target_pairs={{0,1},{1,0},{2,3},{3,2},{4,5},{5,4},{6,7},{7,6},{8,9},{9,8},{10,11... | collective-permute-start | bytes 368648 | tf_op jit(solution)/shard_map/ppermute | solution.py:21
  16.6 10.7 %collective-permute-start = (f32[1,1024]{1,0:T(1,128)S(1)}, f32[1,1024]{1,0:T(1,128)S(1)}, u32[]{:S(2)}, u32[]{:S(2)}) collective-permute-start(f32[1,1024]{1,0:T(1,128)S(1)} %fusion.55), channel_id=1, source_target_pairs={{0,1},{1,0},{2,3},{3,2},{4,5},{5,4},{6,7},{7,6},{8,9},{9,8},{10,11... | collective-permute-start | bytes 12296 | tf_op jit(solution)/shard_map/ppermute | solution.py:21
  17.0 64.5 %collective-permute-start.14 = (bf16[256,3072]{1,0:T(8,128)(2,1)}, bf16[256,3072]{1,0:T(8,128)(2,1)}, u32[]{:S(2)}, u32[]{:S(2)}) collective-permute-start(bf16[256,3072]{1,0:T(8,128)(2,1)} %param.40), channel_id=1, source_target_pairs={{0,1},{1,0},{2,3},{3,2},{4,5},{5,4},{6,7},{7,6},{8,9},{9,8},{10,11... | collective-permute-start | bytes 4718600 | tf_op jit(solution)/shard_map/ppermute | solution.py:21
  27.4 3.7 collective-permute-start.1
  32.9 5.5 collective-permute-start.2
  33.7 62.8 %copy-start.59 = (s32[48]{0:T(128)}, s32[48]{0:T(128)S(1)}, u32[]{:S(2)}) copy-start(s32[48]{0:T(128)S(1)} %fusion.42) | copy-start | bytes 580
  38.4 3.8 collective-permute-start.3
  42.2 23.2 %collective-permute-start.11 = (bf16[128,1024]{1,0:T(8,128)(2,1)}, bf16[128,1024]{1,0:T(8,128)(2,1)}, u32[]{:S(2)}, u32[]{:S(2)}) collective-permute-start(bf16[128,1024]{1,0:T(8,128)(2,1)} %constant_dynamic-slice_fusion.5), channel_id=1, source_target_pairs={{0,2},{1,3},{2,0},{3,1},{4,6},{5,7},{6,4},{7,5},{8,10},{9,11},{10,... | collective-permute-start | bytes 786440 | tf_op jit(solution)/shard_map/ppermute | solution.py:21
  44.0 13.4 %collective-permute-start.5 = (bf16[2,60,1024]{2,1,0:T(8,128)(2,1)}, bf16[2,60,1024]{2,1,0:T(8,128)(2,1)}, u32[]{:S(2)}, u32[]{:S(2)}) collective-permute-start(bf16[2,60,1024]{2,1,0:T(8,128)(2,1)} %pad_maximum_fusion.6), channel_id=1, source_target_pairs={{0,2},{1,3},{2,0},{3,1},{4,6},{5,7},{6,4},{7,5},{8,10},{9,11},{10,... | collective-permute-start | bytes 737288 | tf_op jit(solution)/shard_map/ppermute | solution.py:21
  48.2 24.4 %collective-permute-start.15 = (bf16[128,3072]{1,0:T(8,128)(2,1)}, bf16[128,3072]{1,0:T(8,128)(2,1)}, u32[]{:S(2)}, u32[]{:S(2)}) collective-permute-start(bf16[128,3072]{1,0:T(8,128)(2,1)} %constant_dynamic-slice_fusion.4), channel_id=1, source_target_pairs={{0,2},{1,3},{2,0},{3,1},{4,6},{5,7},{6,4},{7,5},{8,10},{9,11},{10,... | collective-permute-start | bytes 2359304 | tf_op jit(solution)/shard_map/ppermute | solution.py:21
  57.4 9.8 %collective-permute-start.8 = (bf16[128,1024]{1,0:T(8,128)(2,1)}, bf16[128,1024]{1,0:T(8,128)(2,1)}, u32[]{:S(2)}, u32[]{:S(2)}) collective-permute-start(bf16[128,1024]{1,0:T(8,128)(2,1)} %collective-permute-done.7), channel_id=1, source_target_pairs={{0,4},{4,0},{8,12},{12,8},{16,20},{20,16},{24,28},{28,24},{1,5},{5... | collective-permute-start | bytes 786440 | tf_op jit(solution)/shard_map/ppermute | solution.py:21
  65.5 10.8 %collective-permute-start.10 = (bf16[256,1024]{1,0:T(8,128)(2,1)}, bf16[256,1024]{1,0:T(8,128)(2,1)}, u32[]{:S(2)}, u32[]{:S(2)}) collective-permute-start(bf16[256,1024]{1,0:T(8,128)(2,1)} %param.36), channel_id=1, source_target_pairs={{0,1},{1,0},{2,3},{3,2},{4,5},{5,4},{6,7},{7,6},{8,9},{9,8},{10,11... | collective-permute-start | bytes 1572872 | tf_op jit(solution)/shard_map/ppermute | solution.py:21
  65.5 12.6 %collective-permute-start.12 = (bf16[128,1024]{1,0:T(8,128)(2,1)}, bf16[128,1024]{1,0:T(8,128)(2,1)S(1)}, u32[]{:S(2)}, u32[]{:S(2)}) collective-permute-start(bf16[128,1024]{1,0:T(8,128)(2,1)} %collective-permute-done.11), channel_id=1, source_target_pairs={{0,4},{4,0},{8,12},{12,8},{16,20},{20,16},{24,28},{28,24},{1,5},{5... | collective-permute-start | bytes 786440 | tf_op jit(solution)/shard_map/ppermute | solution.py:21
  69.5 10.9 %collective-permute-start.9 = (bf16[256,1024]{1,0:T(8,128)(2,1)}, bf16[256,1024]{1,0:T(8,128)(2,1)}, u32[]{:S(2)}, u32[]{:S(2)}) collective-permute-start(bf16[256,1024]{1,0:T(8,128)(2,1)} %get-tuple-element.157), channel_id=1, source_target_pairs={{0,1},{1,0},{2,3},{3,2},{4,5},{5,4},{6,7},{7,6},{8,9},{9,8},{10,11... | collective-permute-start | bytes 1572872 | tf_op jit(solution)/shard_map/ppermute | solution.py:21
  72.6 18.9 %collective-permute-start.16 = (bf16[128,3072]{1,0:T(8,128)(2,1)}, bf16[128,3072]{1,0:T(8,128)(2,1)}, u32[]{:S(2)}, u32[]{:S(2)}) collective-permute-start(bf16[128,3072]{1,0:T(8,128)(2,1)} %collective-permute-done.15), channel_id=1, source_target_pairs={{0,4},{4,0},{8,12},{12,8},{16,20},{20,16},{24,28},{28,24},{1,5},{5... | collective-permute-start | bytes 2359304 | tf_op jit(solution)/shard_map/ppermute | solution.py:21
  80.3 29.1 %collective-permute-start.13 = (bf16[256,1024]{1,0:T(8,128)(2,1)}, bf16[256,1024]{1,0:T(8,128)(2,1)}, u32[]{:S(2)}, u32[]{:S(2)}) collective-permute-start(bf16[256,1024]{1,0:T(8,128)(2,1)} %get-tuple-element.155), channel_id=1, source_target_pairs={{0,1},{1,0},{2,3},{3,2},{4,5},{5,4},{6,7},{7,6},{8,9},{9,8},{10,11... | collective-permute-start | bytes 1572872 | tf_op jit(solution)/shard_map/ppermute | solution.py:21
  95.8 19.2 %collective-permute-start.17 = (bf16[256,3072]{1,0:T(8,128)(2,1)}, bf16[256,3072]{1,0:T(8,128)(2,1)}, u32[]{:S(2)}, u32[]{:S(2)}) collective-permute-start(bf16[256,3072]{1,0:T(8,128)(2,1)} %get-tuple-element.153), channel_id=1, source_target_pairs={{0,1},{1,0},{2,3},{3,2},{4,5},{5,4},{6,7},{7,6},{8,9},{9,8},{10,11... | collective-permute-start | bytes 4718600 | tf_op jit(solution)/shard_map/ppermute | solution.py:21
  126.8 48.7 %collective-permute-start.18 = (bf16[512,2048]{1,0:T(8,128)(2,1)}, bf16[512,2048]{1,0:T(8,128)(2,1)}, u32[]{:S(2)}, u32[]{:S(2)}) collective-permute-start(bf16[512,2048]{1,0:T(8,128)(2,1)} %slice.166), channel_id=1, source_target_pairs={{0,2},{1,3},{2,0},{3,1},{4,6},{5,7},{6,4},{7,5},{8,10},{9,11},{10,... | collective-permute-start | bytes 6291464 | tf_op jit(solution)/shard_map/ppermute | solution.py:21
  128.1 75.4 %collective-permute-start.20 = (bf16[512,2048]{1,0:T(8,128)(2,1)}, bf16[512,2048]{1,0:T(8,128)(2,1)}, u32[]{:S(2)}, u32[]{:S(2)}) collective-permute-start(bf16[512,2048]{1,0:T(8,128)(2,1)} %slice.166), channel_id=1, source_target_pairs={{0,1},{1,0},{2,3},{3,2},{4,5},{5,4},{6,7},{7,6},{8,9},{9,8},{10,11... | collective-permute-start | bytes 6291464 | tf_op jit(solution)/shard_map/ppermute | solution.py:21
  128.3 53.6 %collective-permute-start.21 = (bf16[256,1024]{1,0:T(8,128)(2,1)S(1)}, bf16[256,1024]{1,0:T(8,128)(2,1)}, u32[]{:S(2)}, u32[]{:S(2)}) collective-permute-start(bf16[256,1024]{1,0:T(8,128)(2,1)S(1)} %copy-done.30), channel_id=1, source_target_pairs={{0,1},{1,0},{2,3},{3,2},{4,5},{5,4},{6,7},{7,6},{8,9},{9,8},{10,11... | collective-permute-start | bytes 1572872 | tf_op jit(solution)/shard_map/ppermute | solution.py:21
  128.6 52.2 %collective-permute-start.22 = (bf16[128,1024]{1,0:T(8,128)(2,1)S(1)}, bf16[128,1024]{1,0:T(8,128)(2,1)}, u32[]{:S(2)}, u32[]{:S(2)}) collective-permute-start(bf16[128,1024]{1,0:T(8,128)(2,1)S(1)} %constant_dynamic-slice_fusion.3), channel_id=1, source_target_pairs={{0,2},{1,3},{2,0},{3,1},{4,6},{5,7},{6,4},{7,5},{8,10},{9,11},{10,... | collective-permute-start | bytes 786440 | tf_op jit(solution)/shard_map/ppermute | solution.py:21
  175.6 46.9 %collective-permute-start.19 = (bf16[512,2048]{1,0:T(8,128)(2,1)}, bf16[512,2048]{1,0:T(8,128)(2,1)}, u32[]{:S(2)}, u32[]{:S(2)}) collective-permute-start(bf16[512,2048]{1,0:T(8,128)(2,1)} %collective-permute-done.18.refs_2_.refs_4_.refs_5_.refs_7_), channel_id=1, source_target_pairs={{0,1},{1,0},{2,3},{3,2},{4,5},{5,4},{6,7},{7,6},{8,9},{9,8},{10,11... | collective-permute-start | bytes 6291464 | tf_op jit(solution)/shard_map/ppermute | solution.py:21
  177.7 25.7 %collective-permute-start.29 = (bf16[512,1024]{1,0:T(8,128)(2,1)S(1)}, bf16[512,1024]{1,0:T(8,128)(2,1)}, u32[]{:S(2)}, u32[]{:S(2)}) collective-permute-start(bf16[512,1024]{1,0:T(8,128)(2,1)S(1)} %get-tuple-element.144), channel_id=1, source_target_pairs={{0,2},{1,3},{2,0},{3,1},{4,6},{5,7},{6,4},{7,5},{8,10},{9,11},{10,... | collective-permute-start | bytes 3145736 | tf_op jit(solution)/shard_map/ppermute | solution.py:21
  180.8 8.1 %collective-permute-start.23 = (bf16[128,1024]{1,0:T(8,128)(2,1)}, bf16[128,1024]{1,0:T(8,128)(2,1)S(1)}, u32[]{:S(2)}, u32[]{:S(2)}) collective-permute-start(bf16[128,1024]{1,0:T(8,128)(2,1)} %collective-permute-done.22), channel_id=1, source_target_pairs={{0,4},{4,0},{8,12},{12,8},{16,20},{20,16},{24,28},{28,24},{1,5},{5... | collective-permute-start | bytes 786440 | tf_op jit(solution)/shard_map/ppermute | solution.py:21
  190.2 13.2 %collective-permute-start.24 = (bf16[256,1024]{1,0:T(8,128)(2,1)S(1)}, bf16[256,1024]{1,0:T(8,128)(2,1)S(1)}, u32[]{:S(2)}, u32[]{:S(2)}) collective-permute-start(bf16[256,1024]{1,0:T(8,128)(2,1)S(1)} %get-tuple-element.151), channel_id=1, source_target_pairs={{0,1},{1,0},{2,3},{3,2},{4,5},{5,4},{6,7},{7,6},{8,9},{9,8},{10,11... | collective-permute-start | bytes 1572872 | tf_op jit(solution)/shard_map/ppermute | solution.py:21
  190.3 71.5 %collective-permute-start.26 = (bf16[512,1024]{1,0:T(8,128)(2,1)S(1)}, bf16[512,1024]{1,0:T(8,128)(2,1)S(1)}, u32[]{:S(2)}, u32[]{:S(2)}) collective-permute-start(bf16[512,1024]{1,0:T(8,128)(2,1)S(1)} %get-tuple-element.144), channel_id=1, source_target_pairs={{0,1},{1,0},{2,3},{3,2},{4,5},{5,4},{6,7},{7,6},{8,9},{9,8},{10,11... | collective-permute-start | bytes 3145736 | tf_op jit(solution)/shard_map/ppermute | solution.py:21
  203.4 60.1 %collective-permute-start.30 = (bf16[512,1024]{1,0:T(8,128)(2,1)}, bf16[512,1024]{1,0:T(8,128)(2,1)}, u32[]{:S(2)}, u32[]{:S(2)}) collective-permute-start(bf16[512,1024]{1,0:T(8,128)(2,1)} %collective-permute-done.29), channel_id=1, source_target_pairs={{0,1},{1,0},{2,3},{3,2},{4,5},{5,4},{6,7},{7,6},{8,9},{9,8},{10,11... | collective-permute-start | bytes 3145736 | tf_op jit(solution)/shard_map/ppermute | solution.py:21
  246.7 25.7 %collective-permute-start.27 = (bf16[512,1024]{1,0:T(8,128)(2,1)S(1)}, bf16[512,1024]{1,0:T(8,128)(2,1)}, u32[]{:S(2)}, u32[]{:S(2)}) collective-permute-start(bf16[512,1024]{1,0:T(8,128)(2,1)S(1)} %add_convert_fusion.4.first_ref), channel_id=1, source_target_pairs={{0,2},{1,3},{2,0},{3,1},{4,6},{5,7},{6,4},{7,5},{8,10},{9,11},{10,... | collective-permute-start | bytes 3145736 | tf_op jit(solution)/shard_map/ppermute | solution.py:21
  247.9 24.5 %collective-permute-start.25 = (bf16[512,1024]{1,0:T(8,128)(2,1)S(1)}, bf16[512,1024]{1,0:T(8,128)(2,1)S(1)}, u32[]{:S(2)}, u32[]{:S(2)}) collective-permute-start(bf16[512,1024]{1,0:T(8,128)(2,1)S(1)} %add_convert_fusion.4.first_ref), channel_id=1, source_target_pairs={{0,1},{1,0},{2,3},{3,2},{4,5},{5,4},{6,7},{7,6},{8,9},{9,8},{10,11... | collective-permute-start | bytes 3145736 | tf_op jit(solution)/shard_map/ppermute | solution.py:21
  248.1 3.6 collective-permute-start.39
  252.3 3.7 collective-permute-start.40
  256.6 4.6 collective-permute-start.41
  272.3 19.4 %collective-permute-start.28 = (bf16[512,1024]{1,0:T(8,128)(2,1)}, bf16[512,1024]{1,0:T(8,128)(2,1)}, u32[]{:S(2)}, u32[]{:S(2)}) collective-permute-start(bf16[512,1024]{1,0:T(8,128)(2,1)} %collective-permute-done.27.first_ref), channel_id=1, source_target_pairs={{0,1},{1,0},{2,3},{3,2},{4,5},{5,4},{6,7},{7,6},{8,9},{9,8},{10,11... | collective-permute-start | bytes 3145736 | tf_op jit(solution)/shard_map/ppermute | solution.py:21
  291.2 39.0 %collective-permute-start.33 = (bf16[512,1024]{1,0:T(8,128)(2,1)}, bf16[512,1024]{1,0:T(8,128)(2,1)}, u32[]{:S(2)}, u32[]{:S(2)}) collective-permute-start(bf16[512,1024]{1,0:T(8,128)(2,1)} %slice_bitcast_fusion.1), channel_id=1, source_target_pairs={{0,1},{1,0},{2,3},{3,2},{4,5},{5,4},{6,7},{7,6},{8,9},{9,8},{10,11... | collective-permute-start | bytes 3145736 | tf_op jit(solution)/shard_map/ppermute | solution.py:21
  308.6 13.5 %collective-permute-start.31 = (bf16[2,512,1024]{2,1,0:T(8,128)(2,1)S(1)}, bf16[2,512,1024]{2,1,0:T(8,128)(2,1)S(1)}, u32[]{:S(2)}, u32[]{:S(2)}) collective-permute-start(bf16[2,512,1024]{2,1,0:T(8,128)(2,1)S(1)} %pad_maximum_fusion.3), channel_id=1, source_target_pairs={{0,1},{1,0},{2,3},{3,2},{4,5},{5,4},{6,7},{7,6},{8,9},{9,8},{10,11... | collective-permute-start | bytes 6291464 | tf_op jit(solution)/shard_map/ppermute | solution.py:21
  310.0 5.7 collective-permute-start.34
  317.1 26.3 %collective-permute-start.35 = (bf16[512,1024]{1,0:T(8,128)(2,1)}, bf16[512,1024]{1,0:T(8,128)(2,1)}, u32[]{:S(2)}, u32[]{:S(2)}) collective-permute-start(bf16[512,1024]{1,0:T(8,128)(2,1)} %fusion.4), channel_id=1, source_target_pairs={{0,2},{1,3},{2,0},{3,1},{4,6},{5,7},{6,4},{7,5},{8,10},{9,11},{10,... | collective-permute-start | bytes 3145736 | tf_op jit(solution)/shard_map/ppermute | solution.py:21
  323.7 41.3 %collective-permute-start.32 = (bf16[512,1024]{1,0:T(8,128)(2,1)}, bf16[512,1024]{1,0:T(8,128)(2,1)}, u32[]{:S(2)}, u32[]{:S(2)}) collective-permute-start(bf16[512,1024]{1,0:T(8,128)(2,1)} %fusion.10), channel_id=1, source_target_pairs={{0,2},{1,3},{2,0},{3,1},{4,6},{5,7},{6,4},{7,5},{8,10},{9,11},{10,... | collective-permute-start | bytes 3145736 | tf_op jit(solution)/shard_map/ppermute | solution.py:21
  330.1 34.9 %copy-start.2 = (f32[512,1024]{1,0:T(8,128)S(1)}, f32[512,1024]{1,0:T(8,128)}, u32[]{:S(2)}) copy-start(f32[512,1024]{1,0:T(8,128)} %copy-done.1) | copy-start | bytes 6291460
  330.1 34.8 %copy-start.8 = (bf16[2,512,1024]{2,1,0:T(8,128)(2,1)S(1)}, bf16[2,512,1024]{2,1,0:T(8,128)(2,1)}, u32[]{:S(2)}) copy-start(bf16[2,512,1024]{2,1,0:T(8,128)(2,1)} %get-tuple-element.61) | copy-start | bytes 6291460
  403.4 33.4 %collective-permute-start.37 = (bf16[512,2048]{1,0:T(8,128)(2,1)S(1)}, bf16[512,2048]{1,0:T(8,128)(2,1)S(1)}, u32[]{:S(2)}, u32[]{:S(2)}) collective-permute-start(bf16[512,2048]{1,0:T(8,128)(2,1)S(1)} %pad_maximum_fusion.5), channel_id=1, source_target_pairs={{0,1},{1,0},{2,3},{3,2},{4,5},{5,4},{6,7},{7,6},{8,9},{9,8},{10,11... | collective-permute-start | bytes 6291464 | tf_op jit(solution)/shard_map/ppermute | solution.py:21
  436.4 75.5 %collective-permute-start.36 = (bf16[512,2048]{1,0:T(8,128)(2,1)}, bf16[512,2048]{1,0:T(8,128)(2,1)}, u32[]{:S(2)}, u32[]{:S(2)}) collective-permute-start(bf16[512,2048]{1,0:T(8,128)(2,1)} %pad_maximum_fusion.4), channel_id=1, source_target_pairs={{0,1},{1,0},{2,3},{3,2},{4,5},{5,4},{6,7},{7,6},{8,9},{9,8},{10,11... | collective-permute-start | bytes 6291464 | tf_op jit(solution)/shard_map/ppermute | solution.py:21
  439.1 72.8 %collective-permute-start.38 = (bf16[512,2048]{1,0:T(8,128)(2,1)}, bf16[512,2048]{1,0:T(8,128)(2,1)}, u32[]{:S(2)}, u32[]{:S(2)}) collective-permute-start(bf16[512,2048]{1,0:T(8,128)(2,1)} %add_convert_fusion.1), channel_id=1, source_target_pairs={{0,2},{1,3},{2,0},{3,1},{4,6},{5,7},{6,4},{7,5},{8,10},{9,11},{10,... | collective-permute-start | bytes 6291464 | tf_op jit(solution)/shard_map/ppermute | solution.py:21
  441.5 1.9 collective-permute-start.42
  444.3 53.1 %collective-permute-start.43 = (bf16[240,1024]{1,0:T(8,128)(2,1)}, bf16[240,1024]{1,0:T(8,128)(2,1)}, u32[]{:S(2)}, u32[]{:S(2)}) collective-permute-start(bf16[240,1024]{1,0:T(8,128)(2,1)} %fusion.12), channel_id=1, source_target_pairs={{0,2},{1,3},{2,0},{3,1},{4,6},{5,7},{6,4},{7,5},{8,10},{9,11},{10,... | collective-permute-start | bytes 1474568 | tf_op jit(solution)/shard_map/ppermute | solution.py:21
  (75 other events, 434.1 us)
Sparse Core Ops, SparseCore 0:
  330.2 156.4 all-reduce.4

commit v3 on v2

--- a/solution.py
+++ b/solution.py
@@ -208,212 +208,336 @@
     )(patch_rows, coeff_heads, slot_mask, table_values, heads_grad, scale)
 
 
+def flip(index, bit):
+    bit_set = (index // bit) % 2
+    return index + bit - 2 * bit * bit_set, bit_set
+
+
+def meet(partners):
+    barrier = pltpu.get_barrier_semaphore()
+    for partner in partners:
+        pl.semaphore_signal(
+            barrier, inc=1, device_id=partner, device_id_type=pl.DeviceIdType.MESH
+        )
+    pl.semaphore_wait(barrier, len(partners))
+
+
 def lane_half(rows, pair, head_dim):
     lane = lax.broadcasted_iota(jnp.int32, (rows, 2 * head_dim), 1)
     return (lane // head_dim) == pair
 
 
-def attend_kernel(shards, head_dim, first, last, *refs):
-    valid_ref, q_ref = refs[:2]
-    keys = refs[2 : 2 + shards]
-    values = refs[2 + shards : 2 + 2 * shards]
-    rest = refs[2 + 2 * shards :]
-    if not first:
-        old_sum_ref, old_top_ref, old_total_ref = rest[:3]
-        rest = rest[3:]
-    rows = q_ref.shape[0]
+def attend_kernel(
+    head_dim, valid_ref, rows_ref, weight_ref, q_ref, kv_ref, out_ref, log_ref, sum_s, top_s, total_s, send_sem, recv_sem
+):
+    me = lax.axis_index("fsdp")
+    near = {"fsdp": flip(me, 1)[0]}
+    far = {"fsdp": flip(me, 2)[0]}
+    wide = jnp.float32
+    low = jnp.bfloat16
+    rows, width = rows_ref.shape
+    lanes = 2 * head_dim
+    pairs = width // lanes
+    scale = head_dim ** (-0.5)
+    meet([near, far])
+
+    def copy(kind, i, source, target, device):
+        return pltpu.make_async_remote_copy(
+            src_ref=kv_ref.at[source, i],
+            dst_ref=kv_ref.at[target, i],
+            send_sem=send_sem.at[kind, i],
+            recv_sem=recv_sem.at[kind, i],
+            device_id=device,
+            device_id_type=pl.DeviceIdType.MESH,
+        )
+
+    def near_copy(i):
+        return copy(0, i, 0, 1, near)
+
+    def far_copy(i):
+        return copy(1, i, 0, 2, far)
+
+    def last_copy(i):
+        return copy(2, i, 2, 3, near)
+
+    entry = rows_ref[...]
+    for g in range(pairs // 2):
+        for part in range(2):
+            start = (part + 1) * width + g * 2 * lanes
+            value = jnp.dot(
+                entry, weight_ref[:, start : start + 2 * lanes], preferred_element_type=wide
+            ).astype(low)
+            kv_ref[0, 2 * g, part] = value[:, :lanes]
+            kv_ref[0, 2 * g + 1, part] = value[:, lanes:]
+        for i in (2 * g, 2 * g + 1):
+            far_copy(i).start()
+            near_copy(i).start()
+    for g in range(pairs // 2):
+        start = g * 2 * lanes
+        value = jnp.dot(
+            entry, weight_ref[:, start : start + 2 * lanes], preferred_element_type=wide
+        ).astype(low)
+        value = value * jnp.asarray(scale, low)
+        q_ref[2 * g] = value[:, :lanes]
+        q_ref[2 * g + 1] = value[:, lanes:]
+
     tile = min(rows, 256)
-    scale = head_dim ** (-0.5)
-    for start in range(0, rows, tile):
-        block = q_ref[start : start + tile, :] * jnp.asarray(scale, jnp.bfloat16)
-        sums, tops, totals = [], [], []
-        for pair in range(2):
-            side = lane_half(tile, pair, head_dim)
-            query = jnp.where(side, block, jnp.zeros_like(block))
-            logits = []
-            for j in range(shards):
-                raw = lax.dot_general(
-                    query, keys[j][...], (((1,), (1,)), ((), ())), preferred_element_type=jnp.float32
+
+    def attend(i, shards, first):
+        for start in range(0, rows, tile):
+            at = slice(start, start + tile)
+            block = q_ref[i, at, :]
+            sums, tops, totals = [], [], []
+            for pair in range(2):
+                query = jnp.where(lane_half(tile, pair, head_dim), block, jnp.zeros_like(block))
+                logits = []
+                for j in shards:
+                    raw = lax.dot_general(
+                        query, kv_ref[j, i, 0], (((1,), (1,)), ((), ())), preferred_element_type=wide
+                    )
+                    place = lax.broadcasted_iota(jnp.int32, (1, rows), 1)
+                    logits.append(jnp.where(place < valid_ref[j], raw, masked_out))
+                top = functools.reduce(
+                    jnp.maximum, [jnp.max(part, axis=1, keepdims=True) for part in logits]
                 )
-                place = lax.broadcasted_iota(jnp.int32, (1, raw.shape[1]), 1)
-                logits.append(jnp.where(place < valid_ref[j], raw, masked_out))
-            top = functools.reduce(
-                jnp.maximum, [jnp.max(part, axis=1, keepdims=True) for part in logits]
-            )
-            total = 0.0
-            weighted = 0.0
-            for j in range(shards):
-                terms = jnp.exp(logits[j] - top)
-                total = total + jnp.sum(terms, axis=1, keepdims=True)
-                weighted = weighted + jnp.dot(
-                    terms.astype(jnp.bfloat16), values[j][...], preferred_element_type=jnp.float32
-                )
-            sums.append(weighted)
-            tops.append(top)
-            totals.append(total)
-        side = lane_half(tile, 0, head_dim)
-        weighted = jnp.where(side, sums[0], sums[1])
-        top = jnp.where(side, tops[0], tops[1])
-        total = jnp.where(side, totals[0], totals[1])
-        at = slice(start, start + tile)
-        if not first:
-            old_top = old_top_ref[at, :]
-            new_top = jnp.maximum(top, old_top)
-            mine = jnp.exp(top - new_top)
-            others = jnp.exp(old_top - new_top)
-            weighted = weighted * mine + old_sum_ref[at, :] * others
-            total = total * mine + old_total_ref[at, :] * others
-            top = new_top
-        if last:
-            rest[0][at, :] = (weighted / total).astype(jnp.bfloat16)
-            rest[1][at, :] = top + jnp.log(total)
-        else:
-            rest[0][at, :] = weighted
-            rest[1][at, :] = top
-            rest[2][at, :] = total
-
-
-def attend(queries, key_values, valid, width, old=None, last=False):
-    rows = queries.shape[0]
+                sum_now, total_now = 0.0, 0.0
+                for j, part in zip(shards, logits):
+                    terms = jnp.exp(part - top)
+                    total_now = total_now + jnp.sum(terms, axis=1, keepdims=True)
+                    sum_now = sum_now + jnp.dot(
+                        terms.astype(low), kv_ref[j, i, 1], preferred_element_type=wide
+                    )
+                sums.append(sum_now)
+                tops.append(top)
+                totals.append(total_now)
+            side = lane_half(tile, 0, head_dim)
+            sum_now = jnp.where(side, sums[0], sums[1])
+            top = jnp.where(side, tops[0], tops[1])
+            total_now = jnp.where(side, totals[0], totals[1])
+            if not first:
+                old_top = top_s[at, :]
+                new_top = jnp.maximum(top, old_top)
+                mine = jnp.exp(top - new_top)
+                others = jnp.exp(old_top - new_top)
+                sum_now = sum_now * mine + sum_s[at, :] * others
+                total_now = total_now * mine + total_s[at, :] * others
+                top = new_top
+            sum_s[at, :] = sum_now
+            top_s[at, :] = top
+            total_s[at, :] = total_now
+
+    def one_pair(i, carry):
+        near_copy(i).wait_recv()
+        attend(i, (0, 1), True)
+        far_copy(i).wait_recv()
+        last_copy(i).start()
+        attend(i, (2,), False)
+        last_copy(i).wait_recv()
+        attend(i, (3,), False)
+        out_ref[i] = (sum_s[...] / total_s[...]).astype(low)
+        log_ref[i] = top_s[...] + jnp.log(total_s[...])
+        return carry
+
+    lax.fori_loop(0, pairs, one_pair, 0)
+
+    def end(i, carry):
+        near_copy(i).wait_send()
+        far_copy(i).wait_send()
+        last_copy(i).wait_send()
+        return carry
+
+    lax.fori_loop(0, pairs, end, 0)
+
+
+def attend(rows_in, weight, valid):
+    rows, width = rows_in.shape
     head_dim = width // HEADS
     lanes = 2 * head_dim
-    shards = len(key_values)
-    whole = pl.BlockSpec((rows, lanes), lambda i: (0, i))
-
-    def at(array, offset):
-        start = offset // lanes
-        return pl.BlockSpec((array.shape[0], lanes), lambda i: (0, start + i))
-
-    in_specs = [pl.BlockSpec(memory_space=pltpu.SMEM), whole]
-    in_specs += [at(array, k) for array, k, v in key_values]
-    in_specs += [at(array, v) for array, k, v in key_values]
-    operands = [valid, queries]
-    operands += [array for array, k, v in key_values] * 2
-    if old is not None:
-        in_specs += [whole] * 3
-        operands += list(old)
-    wide = jax.ShapeDtypeStruct((rows, width), jnp.float32)
-    if last:
-        out_shape = [jax.ShapeDtypeStruct((rows, width), jnp.bfloat16), wide]
-    else:
-        out_shape = [wide] * 3
-    length = sum(array.shape[0] for array, k, v in key_values)
+    pairs = HEADS // 2
+    whole = pl.BlockSpec(memory_space=pltpu.VMEM)
+    low = jnp.bfloat16
+    wide = jnp.float32
     return pl.pallas_call(
-        functools.partial(attend_kernel, shards, head_dim, old is None, last),
-        grid=(HEADS // 2,),
-        in_specs=in_specs,
-        out_specs=[whole] * len(out_shape),
-        out_shape=out_shape,
-        compiler_params=pltpu.CompilerParams(vmem_limit_bytes=VMEM_LIMIT),
+        functools.partial(attend_kernel, head_dim),
+        in_specs=[pl.BlockSpec(memory_space=pltpu.SMEM), whole, whole],
+        out_specs=[whole] * 4,
+        out_shape=[
+            jax.ShapeDtypeStruct((pairs, rows, lanes), low),
+            jax.ShapeDtypeStruct((4, pairs, 2, rows, lanes), low),
+            jax.ShapeDtypeStruct((pairs, rows, lanes), low),
+            jax.ShapeDtypeStruct((pairs, rows, lanes), wide),
+        ],
+        scratch_shapes=[
+            pltpu.VMEM((rows, lanes), wide),
+            pltpu.VMEM((rows, lanes), wide),
+            pltpu.VMEM((rows, lanes), wide),
+            pltpu.SemaphoreType.DMA((3, pairs)),
+            pltpu.SemaphoreType.DMA((3, pairs)),
+        ],
+        compiler_params=pltpu.CompilerParams(
+            collective_id=1, has_side_effects=True, vmem_limit_bytes=VMEM_LIMIT
+        ),
         cost_estimate=pl.CostEstimate(
-            flops=4 * rows * length * width * 4,
-            bytes_accessed=4 * length * width,
-            transcendentals=HEADS * rows * length,
+            flops=64 * rows * rows * width, bytes_accessed=100_000_000, transcendentals=0
         ),
         name="attend",
-    )(*operands)
-
-
-def attend_back_kernel(shards, head_dim, first, *refs):
-    valid_ref, q_ref, grad_ref, out_ref, log_ref = refs[:5]
-    keys = refs[5 : 5 + shards]
-    values = refs[5 + shards : 5 + 2 * shards]
-    rest = refs[5 + 2 * shards :]
-    old_ref = None
-    if not first:
-        old_ref, rest = rest[0], rest[1:]
-    q_grad_ref = rest[0]
-    k_grads = rest[1 : 1 + shards]
-    v_grads = rest[1 + shards : 1 + 2 * shards]
-    rows = q_ref.shape[0]
-    lanes = 2 * head_dim
+    )(valid, rows_in, weight)
+
+
+def attend_back_kernel(
+    head_dim, valid_ref, q_ref, kv_ref, grad_ref, out_ref, log_ref, *refs
+):
+    result_ref, q_sum, own_s, far_s, last_s, near_s, got_far, got_last, got_near, log_rows, dot_rows = refs[:11]
+    send_sem, recv_sem = refs[11:]
+    me = lax.axis_index("fsdp")
+    near = {"fsdp": flip(me, 1)[0]}
+    far = {"fsdp": flip(me, 2)[0]}
+    wide = jnp.float32
+    low = jnp.bfloat16
+    pairs, rows, lanes = q_ref.shape
+    width = pairs * lanes
     scale = head_dim ** (-0.5)
-    query = q_ref[...]
-    grad = grad_ref[...]
-    log_rows = jnp.transpose(log_ref[...])
-    dots = jnp.transpose(grad.astype(jnp.float32) * out_ref[...].astype(jnp.float32))
-    q_grad = jnp.zeros((rows, lanes), jnp.float32)
-    k_sums = [0.0] * shards
-    v_sums = [0.0] * shards
-    for pair in range(2):
-        side = lane_half(rows, pair, head_dim)
-        here = slice(pair * head_dim, (pair + 1) * head_dim)
-        log_row = log_rows[pair * head_dim : pair * head_dim + 1, :]
-        dot_row = jnp.sum(dots[here, :], axis=0, keepdims=True)
-        one_query = jnp.where(side, query, jnp.zeros_like(query))
-        one_grad = jnp.where(side, grad, jnp.zeros_like(grad))
-        scaled = one_query * jnp.asarray(scale, jnp.bfloat16)
-        for j in range(shards):
-            key = keys[j][...]
-            one_key = jnp.where(lane_half(key.shape[0], pair, head_dim), key, jnp.zeros_like(key))
-            raw = lax.dot_general(
-                key, scaled, (((1,), (1,)), ((), ())), preferred_element_type=jnp.float32
-            )
-            place = lax.broadcasted_iota(jnp.int32, raw.shape, 0)
-            probs = jnp.exp(jnp.where(place < valid_ref[j], raw - log_row, masked_out))
-            probs_grad = lax.dot_general(
-                values[j][...], one_grad, (((1,), (1,)), ((), ())), preferred_element_type=jnp.float32
-            )
-            raw_grad = (probs * (probs_grad - dot_row)).astype(jnp.bfloat16)
-            v_sums[j] = v_sums[j] + jnp.dot(
-                probs.astype(jnp.bfloat16), one_grad, preferred_element_type=jnp.float32
-            )
-            k_sums[j] = k_sums[j] + jnp.dot(raw_grad, scaled, preferred_element_type=jnp.float32)
-            q_grad = q_grad + lax.dot_general(
-                raw_grad, one_key, (((0,), (0,)), ((), ())), preferred_element_type=jnp.float32
-            )
-    q_grad = q_grad * scale
-    if old_ref is not None:
-        q_grad = q_grad + old_ref[...]
-    q_grad_ref[...] = q_grad.astype(q_grad_ref.dtype)
-    for j in range(shards):
-        k_grads[j][...] = k_sums[j].astype(jnp.bfloat16)
-        v_grads[j][...] = v_sums[j].astype(jnp.bfloat16)
-
-
-def attend_back(queries, grad, out, logs, key_values, valid, old=None, last=False):
-    rows, width = grad.shape
-    head_dim = width // HEADS
-    lanes = 2 * head_dim
-    shards = len(key_values)
-    whole = pl.BlockSpec((rows, lanes), lambda i: (0, i))
-
-    def at(array, offset):
-        start = offset // lanes
-        return pl.BlockSpec((array.shape[0], lanes), lambda i: (0, start + i))
-
-    in_specs = [pl.BlockSpec(memory_space=pltpu.SMEM), whole, whole, whole, whole]
-    in_specs += [at(array, k) for array, k, v in key_values]
-    in_specs += [at(array, v) for array, k, v in key_values]
-    operands = [valid, queries, grad, out, logs]
-    operands += [array for array, k, v in key_values] * 2
-    if old is not None:
-        in_specs.append(whole)
-        operands.append(old)
-    out_shape = [jax.ShapeDtypeStruct((rows, width), jnp.bfloat16 if last else jnp.float32)]
-    out_shape += [
-        jax.ShapeDtypeStruct((array.shape[0], width), jnp.bfloat16) for array, k, v in key_values
-    ] * 2
-    length = sum(array.shape[0] for array, k, v in key_values)
-    result = pl.pallas_call(
-        functools.partial(attend_back_kernel, shards, head_dim, old is None),
-        grid=(HEADS // 2,),
-        in_specs=in_specs,
-        out_specs=[whole]
-        + [
-            pl.BlockSpec((array.shape[0], lanes), lambda i: (0, i)) for array, k, v in key_values
-        ]
-        * 2,
-        out_shape=out_shape,
-        compiler_params=pltpu.CompilerParams(vmem_limit_bytes=VMEM_LIMIT),
+    meet([near, far])
+
+    def copy(kind, i, source, target, device):
+        return pltpu.make_async_remote_copy(
+            src_ref=source.at[i],
+            dst_ref=target.at[i],
+            send_sem=send_sem.at[kind, i],
+            recv_sem=recv_sem.at[kind, i],
+            device_id=device,
+            device_id_type=pl.DeviceIdType.MESH,
+        )
+
+    def last_copy(i):
+        return copy(0, i, last_s, got_last, near)
+
+    def near_copy(i):
+        return copy(1, i, near_s, got_near, near)
+
+    def far_copy(i):
+        return copy(2, i, far_s, got_far, far)
+
+    def back(i, shards, targets):
+        query = q_ref[i]
+        grad = grad_ref[i]
+        q_grad = None
+        k_sums = [None, None]
+        v_sums = [None, None]
+
+        def plus(old, new):
+            return new if old is None else old + new
+
+        for pair in range(2):
+            side = lane_half(rows, pair, head_dim)
+            log_row = log_rows[i, pair : pair + 1, :]
+            dot_row = dot_rows[i, pair : pair + 1, :]
+            one_query = jnp.where(side, query, jnp.zeros_like(query))
+            one_grad = jnp.where(side, grad, jnp.zeros_like(grad))
+            for n, j in enumerate(shards):
+                key = kv_ref[j, i, 0]
+                one_key = jnp.where(side, key, jnp.zeros_like(key))
+                raw = lax.dot_general(
+                    key, one_query, (((1,), (1,)), ((), ())), preferred_element_type=wide
+                )
+                place = lax.broadcasted_iota(jnp.int32, raw.shape, 0)
+                probs = jnp.exp(jnp.where(place < valid_ref[j], raw - log_row, masked_out))
+                probs_grad = lax.dot_general(
+                    kv_ref[j, i, 1], one_grad, (((1,), (1,)), ((), ())), preferred_element_type=wide
+                )
+                raw_grad = (probs * (probs_grad - dot_row)).astype(low)
+                v_sums[n] = plus(
+                    v_sums[n], jnp.dot(probs.astype(low), one_grad, preferred_element_type=wide)
+                )
+                k_sums[n] = plus(
+                    k_sums[n], jnp.dot(raw_grad, one_query, preferred_element_type=wide)
+                )
+                q_grad = plus(
+                    q_grad,
+                    lax.dot_general(
+                        raw_grad, one_key, (((0,), (0,)), ((), ())), preferred_element_type=wide
+                    ),
+                )
+        for n, target in enumerate(targets):
+            target[i, 0] = k_sums[n].astype(target.dtype)
+            target[i, 1] = v_sums[n].astype(target.dtype)
+        return q_grad
+
+    def send_far(i):
+        last_copy(i).wait()
+        far_s[i] = (far_s[i].astype(wide) + got_last[i].astype(wide)).astype(low)
+        far_copy(i).start()
+
+    def first_loop(i, carry):
+        log_t = jnp.transpose(log_ref[i])
+        dots = jnp.transpose(grad_ref[i].astype(wide) * out_ref[i].astype(wide))
+        for pair in range(2):
+            here = slice(pair * head_dim, (pair + 1) * head_dim)
+            log_rows[i, pair : pair + 1, :] = log_t[pair * head_dim : pair * head_dim + 1, :]
+            dot_rows[i, pair : pair + 1, :] = jnp.sum(dots[here, :], axis=0, keepdims=True)
+        q_sum[i] = back(i, (3, 2), (last_s, far_s))
+        last_copy(i).start()
+
+        @pl.when(i > 0)
+        def _():
+            send_far(i - 1)
+
+        return carry
+
+    lax.fori_loop(0, pairs, first_loop, 0)
+    send_far(pairs - 1)
+
+    def second_loop(i, carry):
+        q_sum[i] = (q_sum[i] + back(i, (1, 0), (near_s, own_s))) * scale
+        near_copy(i).start()
+        return carry
+
+    lax.fori_loop(0, pairs, second_loop, 0)
+    for i in range(pairs):
+        near_copy(i).wait()
+        far_copy(i).wait()
+        at = slice(i * lanes, (i + 1) * lanes)
+        result_ref[:, at] = q_sum[i].astype(low)
+        for part in range(2):
+            value = own_s[i, part] + got_near[i, part].astype(wide) + got_far[i, part].astype(wide)
+            start = (part + 1) * width + i * lanes
+            result_ref[:, start : start + lanes] = value.astype(low)
+
+
+def attend_back(queries, key_values, grad, out, logs, valid):
+    pairs, rows, lanes = queries.shape
+    head_dim = lanes // 2
+    whole = pl.BlockSpec(memory_space=pltpu.VMEM)
+    low = jnp.bfloat16
+    wide = jnp.float32
+    slab = (pairs, 2, rows, lanes)
+    return pl.pallas_call(
+        functools.partial(attend_back_kernel, head_dim),
+        in_specs=[pl.BlockSpec(memory_space=pltpu.SMEM)] + [whole] * 5,
+        out_specs=whole,
+        out_shape=jax.ShapeDtypeStruct((rows, 3 * pairs * lanes), low),
+        scratch_shapes=[
+            pltpu.VMEM((pairs, rows, lanes), wide),
+            pltpu.VMEM(slab, wide),
+            pltpu.VMEM(slab, low),
+            pltpu.VMEM(slab, low),
+            pltpu.VMEM(slab, low),
+            pltpu.VMEM(slab, low),
+            pltpu.VMEM(slab, low),
+            pltpu.VMEM(slab, low),
+            pltpu.VMEM((pairs, 8, rows), wide),
+            pltpu.VMEM((pairs, 8, rows), wide),
+            pltpu.SemaphoreType.DMA((3, pairs)),
+            pltpu.SemaphoreType.DMA((3, pairs)),
+        ],
+        compiler_params=pltpu.CompilerParams(
+            collective_id=2, has_side_effects=True, vmem_limit_bytes=VMEM_LIMIT
+        ),
         cost_estimate=pl.CostEstimate(
-            flops=10 * rows * length * width * 4,
-            bytes_accessed=8 * length * width,
-            transcendentals=HEADS * rows * length,
+            flops=160 * rows * rows * pairs * lanes, bytes_accessed=100_000_000, transcendentals=0
         ),
         name="attend_back",
-    )(*operands)
-    return result[0], result[1 : 1 + shards], result[1 + shards :]
+    )(valid, queries, key_values, grad, out, logs)
 
 
 def feed_kernel(
@@ -494,11 +618,6 @@
     )(first, second, grads, up, down, bias)
 
 
-def flip(index, bit):
-    bit_set = (index // bit) % 2
-    return index + bit - 2 * bit * bit_set, bit_set
-
-
 def total_kernel(group_size, widths, share_ref, *refs):
     pairs = [(refs[2 * i], refs[2 * i + 1]) for i in range(3)]
     bundle_ref = refs[6]
@@ -525,14 +644,7 @@
         bit *= 2
     halvings = [i for i, step in enumerate(steps) if step[2]]
 
-    barrier = pltpu.get_barrier_semaphore()
-    partners = [{"fsdp": core_partner}, {"fsdp": far_partner}]
-    partners += [{"grp": step[0]} for step in steps]
-    for partner in partners:
-        pl.semaphore_signal(
-            barrier, inc=1, device_id=partner, device_id_type=pl.DeviceIdType.MESH
-        )
-    pl.semaphore_wait(barrier, len(partners))
+    meet([{"fsdp": core_partner}, {"fsdp": far_partner}] + [{"grp": step[0]} for step in steps])
 
     chunks = [(None, None, None, 0, bundle_ref.shape[1])]
     for (left, right), out in zip(pairs, outs):
@@ -871,15 +983,8 @@
     embedded = left_product(heads_t, full_agg_proj) + agg_bias
     xhat1, inverse1 = normalise(embedded)
     normed1 = (xhat1 * norm1_gain + norm1_shift).astype(low)
-    qkv_rows = product(normed1, full_qkv).astype(low)
-    kv_own = qkv_rows[:, width:]
-    kv_near = swap(kv_own, "fsdp", 1)
-    kv_far = swap(kv_own, "fsdp", 2)
-    kv_last = swap(kv_far, "fsdp", 1)
-    near_set = [(qkv_rows, width, 2 * width), (kv_near, 0, width)]
-    far_set = [(kv_far, 0, width), (kv_last, 0, width)]
-    partial_out = attend(qkv_rows, near_set, shard_valid[:2], width)
-    context, logs = attend(qkv_rows, far_set, shard_valid[2:], width, old=partial_out, last=True)
+    queries, key_values, context_pairs, logs = attend(normed1, full_qkv, shard_valid)
+    context = context_pairs.transpose(1, 0, 2).reshape(rows, width)
     middle = embedded + (product(context, full_proj) + proj_bias)
     xhat2, inverse2 = normalise(middle)
     normed2 = (xhat2 * norm2_gain + norm2_shift).astype(low)
@@ -920,21 +1025,8 @@
     proj_bias_grad = column_sums(attended_grad)
 
     context_grad = right_product(attended_grad, full_proj).astype(low)
-
-    q_part, far_k, far_v = attend_back(
-        qkv_rows, context_grad, context, logs, far_set, shard_valid[2:]
-    )
-    far_kv = [jnp.concatenate([far_k[i], far_v[i]], axis=1) for i in range(2)]
-    far_got = swap(far_kv[1], "fsdp", 1)
-    far_sum = (far_kv[0].astype(wide) + far_got.astype(wide)).astype(low)
-    from_far = swap(far_sum, "fsdp", 2)
-    q_grad, near_k, near_v = attend_back(
-        qkv_rows, context_grad, context, logs, near_set, shard_valid[:2], old=q_part, last=True
-    )
-    near_kv = [jnp.concatenate([near_k[i], near_v[i]], axis=1) for i in range(2)]
-    near_got = swap(near_kv[1], "fsdp", 1)
-    kv_grad = (near_kv[0].astype(wide) + near_got.astype(wide) + from_far.astype(wide)).astype(low)
-    qkv_grad = jnp.concatenate([q_grad, kv_grad], axis=1)
+    context_grad = context_grad.reshape(rows, HEADS // 2, 2 * head_dim).transpose(1, 0, 2)
+    qkv_grad = attend_back(queries, key_values, context_grad, context_pairs, logs, shard_valid)
     normed1_grad = right_product(qkv_grad, full_qkv)
     norm1_gain_grad = jnp.sum(normed1_grad * xhat1, axis=0)
     norm1_shift_grad = jnp.sum(normed1_grad, axis=0)

time: 693 us -> 593 us (0.86)
  waiting for transfers between devices: 183 us -> 78.3 us
  Pallas kernels: 256 us -> 282 us
  other arithmetic: 61.2 us -> 49 us
    ppermute x44 -> x38, waiting for transfers between devices: 183 us -> 78.3 us  [swap(): return lax.ppermute(value, axis, [(i, i ^ bit) for i in range(size)])]
    pallas_call x4 -> x2, Pallas kernels: 97.4 us -> 123 us  [the longest x1 63.5 us: attend_back(): pl.pallas_call(functools.partial(attend_back_kernel, head_dim), in_specs=...]
    concatenate x3 -> x0, other arithmetic: 6.95 us -> none  [the longest x1 3.27 us: on_device(): jnp.concatenate([near_k[i], near_v[i]], axis=1)]
    dynamic_update_slice x19 -> x18, local copies, waits for them, and re-layouts: 22.9 us -> 20.8 us  [in_order(): whole = lax.dynamic_update_slice_in_dim(whole, shard, (me ^ j) * size, axis)]
    unnamed x164 -> x148, local copies, waits for them, and re-layouts: 17.9 us -> 19.6 us
    ppermute x44 -> x38, starting transfers between devices: 30.7 us -> 29.9 us  [swap(): return lax.ppermute(value, axis, [(i, i ^ bit) for i in range(size)])]
  transfers between devices with their start and end apart: 45 -> 39, of which waited for: 17 -> 13; matrix products, arithmetic and copies ran while one was open for 19% -> 27% of each run, Pallas kernels for 20% -> 48%
where the time goes in v3:
time: 593 us; the launch traced here: 588 us
  Pallas kernels  282 us (48%)
  local copies, waits for them, and re-layouts  86 us (15%)
  waiting for transfers between devices  78.3 us (13%)
  other arithmetic  49 us (8%)
  matrix products  44 us (7%)
  starting transfers between devices  29.9 us (5%)
  between operations  18.7 us (3%)
    pallas_call x1, Pallas kernels, total(): pl.pallas_call(functools.partial(total_kernel, group_size, widths), in_sp...  103 us
    ppermute x38, waiting for transfers between devices, swap(): return lax.ppermute(value, axis, [(i, i ^ bit) for i in range(size)])  78.3 us
    pallas_call x1, Pallas kernels, attend_back(): pl.pallas_call(functools.partial(attend_back_kernel, head_dim), in_specs=...  63.5 us
    pallas_call x1, Pallas kernels, attend(): pl.pallas_call(functools.partial(attend_kernel, head_dim), in_specs=[pl.B...  59.8 us
    pallas_call x2, Pallas kernels, feed(): pl.pallas_call(feed_kernel, grid=(rows // tile,), in_specs=[one, one, pai...  30.1 us
    ppermute x38, starting transfers between devices, swap(): return lax.ppermute(value, axis, [(i, i ^ bit) for i in range(size)])  29.9 us
    dynamic_update_slice x18, local copies, waits for them, and re-layouts, in_order(): whole = lax.dynamic_update_slice_in_dim(whole, shard, (me ^ j) * size, axis)  20.8 us
    unnamed x148, local copies, waits for them, and re-layouts  19.6 us
  transfers between devices with their start and end apart: 39, of which 13 were waited for; matrix products, arithmetic and copies ran while one was open for 27% of the time, Pallas kernels for 48%

profile of v3, /device:TPU:0, one launch (start us, length us, event | category | flops | bytes accessed | tf_op | source)
XLA Modules:
  0.0 588.2 jit_solution(15515311773561863557)
XLA Ops:
  10.5 4.3 collective-permute-start.33
  20.1 3.5 broadcast_in_dim.78
  38.2 2.3 dynamic_update_slice.79
  41.1 2.9 collective-permute-start.34
  45.5 4.0 collective-permute-start.35
  52.9 3.8 collective-permute-done.3
  60.1 2.1 dynamic_update_slice.80
  62.4 5.8 collective-permute-done.5
  75.7 2.4 collective-permute-start.19
  81.6 2.4 constant_dynamic-update-slice_fusion.9
  85.7 3.2 collective-permute-done.8
  93.6 3.3 collective-permute-done.20
  99.2 5.5 collective-permute-done.15
  108.9 2.7 constant_dynamic-update-slice_fusion.6
  111.5 13.4 %collective-permute-done.16 = bf16[128,3072]{1,0:T(8,128)(2,1)} collective-permute-done((bf16[128,3072]{1,0:T(8,128)(2,1)}, bf16[128,3072]{1,0:T(8,128)(2,1)}, u32[]{:S(2)}, u32[]{:S(2)}) %collective-permute-start.16) | collective-permute-done | bytes 786464 | tf_op jit(solution)/shard_map/ppermute | solution.py:21
  124.9 3.8 constant_dynamic-update-slice_fusion.5
  128.8 11.7 %aggregate.1.refs_2_ = bf16[1024,512]{1,0:T(8,128)(2,1)} custom-call(bf16[4,48,512]{2,1,0:T(8,128)(2,1)} %bitcast.210, f32[16,5,48,1]{3,2,1,0:T(8,128)} %copy.73.coeff_ref, f32[48,1]{1,0:T(8,128)} %copy.74.mask_ref, bf16[1024,240]{1,0:T(8,128)(2,1)} %copy.75.table_ref), custom_call_target="tpu_custom_call" | custom-call | flops 1006632960 | bytes 2097152 | tf_op jit(solution)/shard_map/aggregate/pallas_call | solution.py:120
  145.6 2.7 constant_dynamic-update-slice_fusion.4.weight_ref
  148.3 59.8 %attend.1 = (bf16[8,512,128]{2,1,0:T(8,128)(2,1)}, bf16[4,8,2,512,128]{4,3,2,1,0:T(8,128)(2,1)}, bf16[8,512,128]{2,1,0:T(8,128)(2,1)}, f32[8,512,128]{2,1,0:T(8,128)}) custom-call(s32[4]{0:T(128)} %subtract_clamp_fusion.valid_ref, bf16[512,1024]{1,0:T(8,128)(2,1)} %add_convert_fusion.3.rows_ref, bf16[1024,3072]{1,0:T(8,128)(2,1)} %constant_dynamic-update-slice_fusion.4.weight_ref), custom_call_target="tpu_custom_call" | custom-call | flops 17179869184 | bytes 100000000 | tf_op jit(solution)/shard_map/attend/pallas_call | solution.py:360
  208.1 2.3 copy.76
  210.3 3.3 fusion.50
  218.7 2.3 copy.86.refs_0_
  221.0 3.1 pad_maximum_fusion.grad_ref
  224.1 2.2 convert_add_fusion.2
  226.3 2.5 copy.87
  228.9 3.1 pad_maximum_fusion.1.grad_ref
  231.9 9.8 %collective-permute-done.24.first_ref = bf16[512,1024]{1,0:T(8,128)(2,1)} collective-permute-done((bf16[512,1024]{1,0:T(8,128)(2,1)}, bf16[512,1024]{1,0:T(8,128)(2,1)}, u32[]{:S(2)}, u32[]{:S(2)}) %collective-permute-start.24) | collective-permute-done | bytes 1048608 | tf_op jit(solution)/shard_map/ppermute | solution.py:21
  241.7 15.0 %feed.2 = (bf16[2,512,1024]{2,1,0:T(8,128)(2,1)}, bf16[2,512,1024]{2,1,0:T(8,128)(2,1)}, bf16[2,512,1024]{2,1,0:T(8,128)(2,1)}, bf16[2,512,1024]{2,1,0:T(8,128)(...) custom-call(bf16[512,1024]{1,0:T(8,128)(2,1)} %add_convert_fusion.2.first_ref, ...), custom_call_target="tpu_custom_call" | custom-call | flops 17179869184 | bytes 8388608 | tf_op jit(solution)/shard_map/feed/pallas_call | solution.py:591
  261.2 15.1 %feed.3 = (bf16[2,512,1024]{2,1,0:T(8,128)(2,1)}, bf16[2,512,1024]{2,1,0:T(8,128)(2,1)}, bf16[2,512,1024]{2,1,0:T(8,128)(2,1)}, bf16[2,512,1024]{2,1,0:T(8,128)(...) custom-call(bf16[512,1024]{1,0:T(8,128)(2,1)} %collective-permute-done.24.first_ref, ...), custom_call_target="tpu_custom_call" | custom-call | flops 17179869184 | bytes 8388608 | tf_op jit(solution)/shard_map/feed/pallas_call | solution.py:591
  279.9 4.1 fusion.42
  284.0 2.4 fusion.57
  289.1 3.8 fusion.3
  295.6 5.3 fusion.1
  301.8 12.4 %collective-permute-done.32 = bf16[512,1024]{1,0:T(8,128)(2,1)} collective-permute-done((bf16[512,1024]{1,0:T(8,128)(2,1)}, bf16[512,1024]{1,0:T(8,128)(2,1)}, u32[]{:S(2)}, u32[]{:S(2)}) %collective-permute-start.32) | collective-permute-done | bytes 1048608 | tf_op jit(solution)/shard_map/ppermute | solution.py:21
  314.1 3.7 multiply_reduce_fusion
  317.9 17.8 %collective-permute-done.29 = bf16[512,1024]{1,0:T(8,128)(2,1)} collective-permute-done((bf16[512,1024]{1,0:T(8,128)(2,1)}, bf16[512,1024]{1,0:T(8,128)(2,1)}, u32[]{:S(2)}, u32[]{:S(2)}) %collective-permute-start.29) | collective-permute-done | bytes 1048608 | tf_op jit(solution)/shard_map/ppermute | solution.py:21
  335.7 5.2 convert_reduce_fusion.1
  341.8 3.9 convolution_convert_fusion.1
  345.7 2.3 copy.77
  348.0 2.3 copy.78
  350.2 63.5 %attend_back.1.refs_1_ = bf16[512,3072]{1,0:T(8,128)(2,1)} custom-call(s32[4]{0:T(128)} %subtract_clamp_fusion.valid_ref, bf16[8,512,128]{2,1,0:T(8,128)(2,1)} %get-tuple-element.49.q_ref, bf16[4,8,2,512,128]{4,3,2,1,0:T(8,128)(2,1)} %get-tuple-element.50.kv_ref, bf16[8,512,128]{2,1,0:T(8,128)(2,1)} %bitcast.209, ...), custom_call_target="tpu_custom_call" | custom-call | flops 42949672960 | bytes 100000000 | tf_op jit(solution)/shard_map/attend_back/pallas_call | solution.py:514
  413.8 7.9 %multiply_reduce_fusion.1 = (f32[1024]{0:T(1024)}, f32[512]{0:T(512)S(1)}, f32[512]{0:T(512)S(1)}, f32[1024]{0:T(1024)}, f32[512,1024]{1,0:T(8,128)S(1)}) fusion(f32[512]{0:T(512)S(1)} %add_rsqrt_fusion.1, f32[512]{0:T(512)S(1)} %broadcast_multiply_fusion.7, f32[512,1024]{1,0:T(8,128)S(1)} %get-tuple-element.153, f32[1024]{0:T(1024)S(1)} %copy-done.43, ...), kind=kOutput, calls=%fused_computation.20 | convolution fusion | flops 3226465280 | bytes 13656064 | tf_op jit(solution)/shard_map/dot_general | solution.py:47
  423.3 2.3 convolution_convert_fusion.heads_ref
  425.5 14.1 %aggregate_back.1 = (f32[1024,240]{1,0:T(8,128)}, f32[16,5,48,1]{3,2,1,0:T(8,128)}, f32[4,48,512]{2,1,0:T(8,128)}) custom-call(bf16[4,48,512]{2,1,0:T(8,128)(2,1)} %bitcast.211, f32[16,5,48,1]{3,2,1,0:T(8,128)} %copy.73.coeff_ref, f32[48,1]{1,0:T(8,128)} %copy.74.mask_ref, bf16[1024,240]{1,0:T(8,128)(2,1)} %copy.75.table_ref, ...), custom_call_target="tpu_custom_call" | custom-call | flops 2013265920 | bytes 4194304 | tf_op jit(solution)/shard_map/aggregate_back/pallas_call | solution.py:180
  446.3 103.1 %total.1 = (f32[256,3072]{1,0:T(8,128)}, f32[256,1024]{1,0:T(8,128)}, f32[256,1024]{1,0:T(8,128)}, f32[1024,256]{1,0:T(8,128)}) custom-call(f32[1]{0:T(128)} %div.43.share_ref, bf16[1024,512]{1,0:T(8,128)(2,1)} %copy.86.refs_0_, bf16[512,3072]{1,0:T(8,128)(2,1)} %attend_back.1.refs_1_, bf16[1024,512]{1,0:T(8,128)(2,1)} %aggregate.1.refs_2_, ...), custom_call_target="tpu_custom_call" | custom-call | flops 5368709120 | bytes 200000000 | tf_op jit(solution)/shard_map/total/pallas_call | solution.py:818
  563.1 2.0 copy.92
  569.8 4.2 convert_element_type.228
  574.1 2.6 convert_element_type.230
  (347 shorter events, 108.8 us)
Async XLA Ops:
  7.2 562.6 %all-reduce.5.cloned.1.call-start = ((), (), s32[]{:S(2)}) async-start(), calls=%async_computation | async-start | bytes 8388608 | tf_op jit(solution)/shard_map/psum | solution.py:1013
  7.3 68.4 %collective-permute-start.10 = (bf16[256,1024]{1,0:T(8,128)(2,1)}, bf16[256,1024]{1,0:T(8,128)(2,1)}, u32[]{:S(2)}, u32[]{:S(2)}) collective-permute-start(bf16[256,1024]{1,0:T(8,128)(2,1)} %param.36), channel_id=1, source_target_pairs={{0,1},{1,0},{2,3},{3,2},{4,5},{5,4},{6,7},{7,6},{8,9},{9,8},{10,11... | collective-permute-start | bytes 1572872 | tf_op jit(solution)/shard_map/ppermute | solution.py:21
  7.8 83.9 %collective-permute-start.18 = (bf16[256,1024]{1,0:T(8,128)(2,1)}, bf16[256,1024]{1,0:T(8,128)(2,1)}, u32[]{:S(2)}, u32[]{:S(2)}) collective-permute-start(bf16[256,1024]{1,0:T(8,128)(2,1)} %param.41), channel_id=1, source_target_pairs={{0,1},{1,0},{2,3},{3,2},{4,5},{5,4},{6,7},{7,6},{8,9},{9,8},{10,11... | collective-permute-start | bytes 1572872 | tf_op jit(solution)/shard_map/ppermute | solution.py:21
  7.9 76.7 %collective-permute-start.6 = (bf16[256,1024]{1,0:T(8,128)(2,1)}, bf16[256,1024]{1,0:T(8,128)(2,1)}, u32[]{:S(2)}, u32[]{:S(2)}) collective-permute-start(bf16[256,1024]{1,0:T(8,128)(2,1)} %param.35), channel_id=1, source_target_pairs={{0,1},{1,0},{2,3},{3,2},{4,5},{5,4},{6,7},{7,6},{8,9},{9,8},{10,11... | collective-permute-start | bytes 1572872 | tf_op jit(solution)/shard_map/ppermute | solution.py:21
  9.8 21.6 %collective-permute-start = (f32[1,1024]{1,0:T(1,128)S(1)}, f32[1,1024]{1,0:T(1,128)S(1)}, u32[]{:S(2)}, u32[]{:S(2)}) collective-permute-start(f32[1,1024]{1,0:T(1,128)S(1)} %fusion.52), channel_id=1, source_target_pairs={{0,1},{1,0},{2,3},{3,2},{4,5},{5,4},{6,7},{7,6},{8,9},{9,8},{10,11... | collective-permute-start | bytes 12296 | tf_op jit(solution)/shard_map/ppermute | solution.py:21
  10.5 30.0 %collective-permute-start.33 = (f32[1]{0:T(128)}, f32[1]{0:T(128)}, u32[]{:S(2)}, u32[]{:S(2)}) collective-permute-start(f32[1]{0:T(128)} %convert_element_type.211), channel_id=1, source_target_pairs={{0,4},{4,0},{8,12},{12,8},{16,20},{20,16},{24,28},{28,24},{1,5},{5... | collective-permute-start | bytes 20 | tf_op jit(solution)/shard_map/ppermute | solution.py:21
  31.4 3.7 collective-permute-start.1
  34.4 27.8 %copy-start.44 = (bf16[128,1024]{1,0:T(8,128)(2,1)S(1)}, bf16[128,1024]{1,0:T(8,128)(2,1)}, u32[]{:S(2)}) copy-start(bf16[128,1024]{1,0:T(8,128)(2,1)} %constant_dynamic-slice_fusion.6) | copy-start | bytes 786436
  35.3 16.7 %collective-permute-start.2 = (bf16[16,256]{1,0:T(8,128)(2,1)S(1)}, bf16[16,256]{1,0:T(8,128)(2,1)S(1)}, u32[]{:S(2)}, u32[]{:S(2)}) collective-permute-start(bf16[16,256]{1,0:T(8,128)(2,1)S(1)} %get-tuple-element.137), channel_id=1, source_target_pairs={{0,1},{1,0},{2,3},{3,2},{4,5},{5,4},{6,7},{7,6},{8,9},{9,8},{10,11... | collective-permute-start | bytes 24584 | tf_op jit(solution)/shard_map/ppermute | solution.py:21
  36.1 71.1 %copy-start.52 = (s32[48]{0:T(128)}, s32[48]{0:T(128)S(1)}, u32[]{:S(2)}) copy-start(s32[48]{0:T(128)S(1)} %fusion.41) | copy-start | bytes 580
  41.1 3.7 collective-permute-start.34
  45.5 4.6 collective-permute-start.35
  50.1 12.1 %collective-permute-start.11 = (bf16[128,1024]{1,0:T(8,128)(2,1)S(1)}, bf16[128,1024]{1,0:T(8,128)(2,1)}, u32[]{:S(2)}, u32[]{:S(2)}) collective-permute-start(bf16[128,1024]{1,0:T(8,128)(2,1)S(1)} %copy-done.45), channel_id=1, source_target_pairs={{0,2},{1,3},{2,0},{3,1},{4,6},{5,7},{6,4},{7,5},{8,10},{9,11},{10,... | collective-permute-start | bytes 786440 | tf_op jit(solution)/shard_map/ppermute | solution.py:21
  52.0 4.6 collective-permute-start.3
  56.6 1.3 collective-permute-start.4
  58.8 9.4 %collective-permute-start.5 = (bf16[2,60,1024]{2,1,0:T(8,128)(2,1)}, bf16[2,60,1024]{2,1,0:T(8,128)(2,1)S(1)}, u32[]{:S(2)}, u32[]{:S(2)}) collective-permute-start(bf16[2,60,1024]{2,1,0:T(8,128)(2,1)} %pad_maximum_fusion.3), channel_id=1, source_target_pairs={{0,2},{1,3},{2,0},{3,1},{4,6},{5,7},{6,4},{7,5},{8,10},{9,11},{10,... | collective-permute-start | bytes 737288 | tf_op jit(solution)/shard_map/ppermute | solution.py:21
  62.2 17.8 %collective-permute-start.7 = (bf16[128,1024]{1,0:T(8,128)(2,1)S(1)}, bf16[128,1024]{1,0:T(8,128)(2,1)}, u32[]{:S(2)}, u32[]{:S(2)}) collective-permute-start(bf16[128,1024]{1,0:T(8,128)(2,1)S(1)} %copy-done.44), channel_id=1, source_target_pairs={{0,2},{1,3},{2,0},{3,1},{4,6},{5,7},{6,4},{7,5},{8,10},{9,11},{10,... | collective-permute-start | bytes 786440 | tf_op jit(solution)/shard_map/ppermute | solution.py:21
  68.2 11.8 %collective-permute-start.12 = (bf16[128,1024]{1,0:T(8,128)(2,1)}, bf16[128,1024]{1,0:T(8,128)(2,1)}, u32[]{:S(2)}, u32[]{:S(2)}) collective-permute-start(bf16[128,1024]{1,0:T(8,128)(2,1)} %collective-permute-done.11), channel_id=1, source_target_pairs={{0,4},{4,0},{8,12},{12,8},{16,20},{20,16},{24,28},{28,24},{1,5},{5... | collective-permute-start | bytes 786440 | tf_op jit(solution)/shard_map/ppermute | solution.py:21
  72.0 33.2 %copy-start.20 = (bf16[5,48,1024]{2,1,0:T(8,128)(2,1)}, bf16[5,48,1024]{2,1,0:T(8,128)(2,1)S(1)}, u32[]{:S(2)}) copy-start(bf16[5,48,1024]{2,1,0:T(8,128)(2,1)S(1)} %dynamic_update_slice.82) | copy-start | bytes 1474564
  73.1 25.1 %copy-start.3 = (f32[240,1024]{1,0:T(8,128)}, f32[240,1024]{1,0:T(8,128)S(1)}, u32[]{:S(2)}) copy-start(f32[240,1024]{1,0:T(8,128)S(1)} %get-tuple-element.158) | copy-start | bytes 2949124
  75.7 8.3 %collective-permute-start.19 = (bf16[128,1024]{1,0:T(8,128)(2,1)S(1)}, bf16[128,1024]{1,0:T(8,128)(2,1)S(1)}, u32[]{:S(2)}, u32[]{:S(2)}) collective-permute-start(bf16[128,1024]{1,0:T(8,128)(2,1)S(1)} %constant_dynamic-slice_fusion.3), channel_id=1, source_target_pairs={{0,2},{1,3},{2,0},{3,1},{4,6},{5,7},{6,4},{7,5},{8,10},{9,11},{10,... | collective-permute-start | bytes 786440 | tf_op jit(solution)/shard_map/ppermute | solution.py:21
  80.0 28.6 %collective-permute-start.14 = (bf16[256,3072]{1,0:T(8,128)(2,1)}, bf16[256,3072]{1,0:T(8,128)(2,1)}, u32[]{:S(2)}, u32[]{:S(2)}) collective-permute-start(bf16[256,3072]{1,0:T(8,128)(2,1)} %param.40), channel_id=1, source_target_pairs={{0,1},{1,0},{2,3},{3,2},{4,5},{5,4},{6,7},{7,6},{8,9},{9,8},{10,11... | collective-permute-start | bytes 4718600 | tf_op jit(solution)/shard_map/ppermute | solution.py:21
  80.0 8.9 %collective-permute-start.8 = (bf16[128,1024]{1,0:T(8,128)(2,1)}, bf16[128,1024]{1,0:T(8,128)(2,1)S(1)}, u32[]{:S(2)}, u32[]{:S(2)}) collective-permute-start(bf16[128,1024]{1,0:T(8,128)(2,1)} %collective-permute-done.7), channel_id=1, source_target_pairs={{0,4},{4,0},{8,12},{12,8},{16,20},{20,16},{24,28},{28,24},{1,5},{5... | collective-permute-start | bytes 786440 | tf_op jit(solution)/shard_map/ppermute | solution.py:21
  84.0 20.7 %collective-permute-start.15 = (bf16[128,3072]{1,0:T(8,128)(2,1)}, bf16[128,3072]{1,0:T(8,128)(2,1)}, u32[]{:S(2)}, u32[]{:S(2)}) collective-permute-start(bf16[128,3072]{1,0:T(8,128)(2,1)} %constant_dynamic-slice_fusion.4), channel_id=1, source_target_pairs={{0,2},{1,3},{2,0},{3,1},{4,6},{5,7},{6,4},{7,5},{8,10},{9,11},{10,... | collective-permute-start | bytes 2359304 | tf_op jit(solution)/shard_map/ppermute | solution.py:21
  84.6 13.5 %collective-permute-start.36 = (bf16[240,1024]{1,0:T(8,128)(2,1)S(1)}, bf16[240,1024]{1,0:T(8,128)(2,1)S(1)}, u32[]{:S(2)}, u32[]{:S(2)}) collective-permute-start(bf16[240,1024]{1,0:T(8,128)(2,1)S(1)} %copy-done.39), channel_id=1, source_target_pairs={{0,1},{1,0},{2,3},{3,2},{4,5},{5,4},{6,7},{7,6},{8,9},{9,8},{10,11... | collective-permute-start | bytes 1474568 | tf_op jit(solution)/shard_map/ppermute | solution.py:21
  88.9 8.0 %collective-permute-start.20 = (bf16[128,1024]{1,0:T(8,128)(2,1)S(1)}, bf16[128,1024]{1,0:T(8,128)(2,1)S(1)}, u32[]{:S(2)}, u32[]{:S(2)}) collective-permute-start(bf16[128,1024]{1,0:T(8,128)(2,1)S(1)} %collective-permute-done.19), channel_id=1, source_target_pairs={{0,4},{4,0},{8,12},{12,8},{16,20},{20,16},{24,28},{28,24},{1,5},{5... | collective-permute-start | bytes 786440 | tf_op jit(solution)/shard_map/ppermute | solution.py:21
  91.7 13.0 %collective-permute-start.9 = (bf16[256,1024]{1,0:T(8,128)(2,1)S(1)}, bf16[256,1024]{1,0:T(8,128)(2,1)S(1)}, u32[]{:S(2)}, u32[]{:S(2)}) collective-permute-start(bf16[256,1024]{1,0:T(8,128)(2,1)S(1)} %get-tuple-element.135), channel_id=1, source_target_pairs={{0,1},{1,0},{2,3},{3,2},{4,5},{5,4},{6,7},{7,6},{8,9},{9,8},{10,11... | collective-permute-start | bytes 1572872 | tf_op jit(solution)/shard_map/ppermute | solution.py:21
  96.9 124.1 %collective-permute-start.23 = (bf16[512,1024]{1,0:T(8,128)(2,1)}, bf16[512,1024]{1,0:T(8,128)(2,1)}, u32[]{:S(2)}, u32[]{:S(2)}) collective-permute-start(bf16[512,1024]{1,0:T(8,128)(2,1)} %get-tuple-element.122), channel_id=1, source_target_pairs={{0,1},{1,0},{2,3},{3,2},{4,5},{5,4},{6,7},{7,6},{8,9},{9,8},{10,11... | collective-permute-start | bytes 3145736 | tf_op jit(solution)/shard_map/ppermute | solution.py:21
  98.1 43.1 %collective-permute-start.26 = (bf16[512,1024]{1,0:T(8,128)(2,1)}, bf16[512,1024]{1,0:T(8,128)(2,1)}, u32[]{:S(2)}, u32[]{:S(2)}) collective-permute-start(bf16[512,1024]{1,0:T(8,128)(2,1)} %get-tuple-element.122), channel_id=1, source_target_pairs={{0,2},{1,3},{2,0},{3,1},{4,6},{5,7},{6,4},{7,5},{8,10},{9,11},{10,... | collective-permute-start | bytes 3145736 | tf_op jit(solution)/shard_map/ppermute | solution.py:21
  104.7 35.8 %collective-permute-start.13 = (bf16[256,1024]{1,0:T(8,128)(2,1)}, bf16[256,1024]{1,0:T(8,128)(2,1)S(1)}, u32[]{:S(2)}, u32[]{:S(2)}) collective-permute-start(bf16[256,1024]{1,0:T(8,128)(2,1)} %get-tuple-element.133), channel_id=1, source_target_pairs={{0,1},{1,0},{2,3},{3,2},{4,5},{5,4},{6,7},{7,6},{8,9},{9,8},{10,11... | collective-permute-start | bytes 1572872 | tf_op jit(solution)/shard_map/ppermute | solution.py:21
  104.7 20.3 %collective-permute-start.16 = (bf16[128,3072]{1,0:T(8,128)(2,1)}, bf16[128,3072]{1,0:T(8,128)(2,1)}, u32[]{:S(2)}, u32[]{:S(2)}) collective-permute-start(bf16[128,3072]{1,0:T(8,128)(2,1)} %collective-permute-done.15), channel_id=1, source_target_pairs={{0,4},{4,0},{8,12},{12,8},{16,20},{20,16},{24,28},{28,24},{1,5},{5... | collective-permute-start | bytes 2359304 | tf_op jit(solution)/shard_map/ppermute | solution.py:21
  108.6 32.6 %collective-permute-start.21 = (bf16[256,1024]{1,0:T(8,128)(2,1)}, bf16[256,1024]{1,0:T(8,128)(2,1)S(1)}, u32[]{:S(2)}, u32[]{:S(2)}) collective-permute-start(bf16[256,1024]{1,0:T(8,128)(2,1)} %get-tuple-element.129), channel_id=1, source_target_pairs={{0,1},{1,0},{2,3},{3,2},{4,5},{5,4},{6,7},{7,6},{8,9},{9,8},{10,11... | collective-permute-start | bytes 1572872 | tf_op jit(solution)/shard_map/ppermute | solution.py:21
  128.8 16.8 %collective-permute-start.17 = (bf16[256,3072]{1,0:T(8,128)(2,1)S(1)}, bf16[256,3072]{1,0:T(8,128)(2,1)}, u32[]{:S(2)}, u32[]{:S(2)}) collective-permute-start(bf16[256,3072]{1,0:T(8,128)(2,1)S(1)} %get-tuple-element.131), channel_id=1, source_target_pairs={{0,1},{1,0},{2,3},{3,2},{4,5},{5,4},{6,7},{7,6},{8,9},{9,8},{10,11... | collective-permute-start | bytes 4718600 | tf_op jit(solution)/shard_map/ppermute | solution.py:21
  140.5 83.7 %collective-permute-start.37 = (bf16[240,1024]{1,0:T(8,128)(2,1)}, bf16[240,1024]{1,0:T(8,128)(2,1)}, u32[]{:S(2)}, u32[]{:S(2)}) collective-permute-start(bf16[240,1024]{1,0:T(8,128)(2,1)} %fusion.12), channel_id=1, source_target_pairs={{0,2},{1,3},{2,0},{3,1},{4,6},{5,7},{6,4},{7,5},{8,10},{9,11},{10,... | collective-permute-start | bytes 1474568 | tf_op jit(solution)/shard_map/ppermute | solution.py:21
  141.2 87.7 %collective-permute-start.27 = (bf16[512,1024]{1,0:T(8,128)(2,1)}, bf16[512,1024]{1,0:T(8,128)(2,1)}, u32[]{:S(2)}, u32[]{:S(2)}) collective-permute-start(bf16[512,1024]{1,0:T(8,128)(2,1)} %collective-permute-done.26), channel_id=1, source_target_pairs={{0,1},{1,0},{2,3},{3,2},{4,5},{5,4},{6,7},{7,6},{8,9},{9,8},{10,11... | collective-permute-start | bytes 3145736 | tf_op jit(solution)/shard_map/ppermute | solution.py:21
  215.8 25.9 %collective-permute-start.22 = (bf16[512,1024]{1,0:T(8,128)(2,1)}, bf16[512,1024]{1,0:T(8,128)(2,1)}, u32[]{:S(2)}, u32[]{:S(2)}) collective-permute-start(bf16[512,1024]{1,0:T(8,128)(2,1)} %add_convert_fusion.2.first_ref), channel_id=1, source_target_pairs={{0,1},{1,0},{2,3},{3,2},{4,5},{5,4},{6,7},{7,6},{8,9},{9,8},{10,11... | collective-permute-start | bytes 3145736 | tf_op jit(solution)/shard_map/ppermute | solution.py:21
  215.9 25.8 %collective-permute-start.24 = (bf16[512,1024]{1,0:T(8,128)(2,1)}, bf16[512,1024]{1,0:T(8,128)(2,1)}, u32[]{:S(2)}, u32[]{:S(2)}) collective-permute-start(bf16[512,1024]{1,0:T(8,128)(2,1)} %add_convert_fusion.2.first_ref), channel_id=1, source_target_pairs={{0,2},{1,3},{2,0},{3,1},{4,6},{5,7},{6,4},{7,5},{8,10},{9,11},{10,... | collective-permute-start | bytes 3145736 | tf_op jit(solution)/shard_map/ppermute | solution.py:21
  241.7 18.5 %collective-permute-start.25 = (bf16[512,1024]{1,0:T(8,128)(2,1)}, bf16[512,1024]{1,0:T(8,128)(2,1)S(1)}, u32[]{:S(2)}, u32[]{:S(2)}) collective-permute-start(bf16[512,1024]{1,0:T(8,128)(2,1)} %collective-permute-done.24.first_ref), channel_id=1, source_target_pairs={{0,1},{1,0},{2,3},{3,2},{4,5},{5,4},{6,7},{7,6},{8,9},{9,8},{10,11... | collective-permute-start | bytes 3145736 | tf_op jit(solution)/shard_map/ppermute | solution.py:21
  259.7 42.1 %collective-permute-start.30 = (bf16[512,1024]{1,0:T(8,128)(2,1)}, bf16[512,1024]{1,0:T(8,128)(2,1)}, u32[]{:S(2)}, u32[]{:S(2)}) collective-permute-start(bf16[512,1024]{1,0:T(8,128)(2,1)} %slice_bitcast_fusion.1), channel_id=1, source_target_pairs={{0,1},{1,0},{2,3},{3,2},{4,5},{5,4},{6,7},{7,6},{8,9},{9,8},{10,11... | collective-permute-start | bytes 3145736 | tf_op jit(solution)/shard_map/ppermute | solution.py:21
  277.8 15.1 %collective-permute-start.28 = (bf16[2,512,1024]{2,1,0:T(8,128)(2,1)S(1)}, bf16[2,512,1024]{2,1,0:T(8,128)(2,1)S(1)}, u32[]{:S(2)}, u32[]{:S(2)}) collective-permute-start(bf16[2,512,1024]{2,1,0:T(8,128)(2,1)S(1)} %pad_maximum_fusion.2), channel_id=1, source_target_pairs={{0,1},{1,0},{2,3},{3,2},{4,5},{5,4},{6,7},{7,6},{8,9},{9,8},{10,11... | collective-permute-start | bytes 6291464 | tf_op jit(solution)/shard_map/ppermute | solution.py:21
  279.2 7.2 %collective-permute-start.31 = (bf16[512,1024]{1,0:T(8,128)(2,1)S(1)}, bf16[512,1024]{1,0:T(8,128)(2,1)S(1)}, u32[]{:S(2)}, u32[]{:S(2)}) collective-permute-start(bf16[512,1024]{1,0:T(8,128)(2,1)S(1)} %slice_bitcast_fusion), channel_id=1, source_target_pairs={{0,1},{1,0},{2,3},{3,2},{4,5},{5,4},{6,7},{7,6},{8,9},{9,8},{10,11... | collective-permute-start | bytes 3145736 | tf_op jit(solution)/shard_map/ppermute | solution.py:21
  287.8 26.3 %collective-permute-start.32 = (bf16[512,1024]{1,0:T(8,128)(2,1)}, bf16[512,1024]{1,0:T(8,128)(2,1)}, u32[]{:S(2)}, u32[]{:S(2)}) collective-permute-start(bf16[512,1024]{1,0:T(8,128)(2,1)} %fusion.4), channel_id=1, source_target_pairs={{0,2},{1,3},{2,0},{3,1},{4,6},{5,7},{6,4},{7,5},{8,10},{9,11},{10,... | collective-permute-start | bytes 3145736 | tf_op jit(solution)/shard_map/ppermute | solution.py:21
  294.6 41.0 %collective-permute-start.29 = (bf16[512,1024]{1,0:T(8,128)(2,1)}, bf16[512,1024]{1,0:T(8,128)(2,1)}, u32[]{:S(2)}, u32[]{:S(2)}) collective-permute-start(bf16[512,1024]{1,0:T(8,128)(2,1)} %fusion.10), channel_id=1, source_target_pairs={{0,2},{1,3},{2,0},{3,1},{4,6},{5,7},{6,4},{7,5},{8,10},{9,11},{10,... | collective-permute-start | bytes 3145736 | tf_op jit(solution)/shard_map/ppermute | solution.py:21
  301.7 33.9 %copy-start.2 = (f32[512,1024]{1,0:T(8,128)S(1)}, f32[512,1024]{1,0:T(8,128)}, u32[]{:S(2)}) copy-start(f32[512,1024]{1,0:T(8,128)} %copy-done.1) | copy-start | bytes 6291460
  301.7 33.9 %copy-start.15 = (bf16[2,512,1024]{2,1,0:T(8,128)(2,1)S(1)}, bf16[2,512,1024]{2,1,0:T(8,128)(2,1)}, u32[]{:S(2)}) copy-start(bf16[2,512,1024]{2,1,0:T(8,128)(2,1)} %get-tuple-element.47) | copy-start | bytes 6291460
  301.7 33.9 %copy-start.19 = (bf16[512,1024]{1,0:T(8,128)(2,1)S(1)}, bf16[512,1024]{1,0:T(8,128)(2,1)}, u32[]{:S(2)}) copy-start(bf16[512,1024]{1,0:T(8,128)(2,1)} %param.49) | copy-start | bytes 3145732
  301.7 33.9 %copy-start.54 = (f32[1024]{0:T(1024)S(1)}, f32[1024]{0:T(1024)}, u32[]{:S(2)}) copy-start(f32[1024]{0:T(1024)} %param.48) | copy-start | bytes 12292
  446.3 104.0 %copy-start.17 = (f32[240,1024]{0,1:T(8,128)S(1)}, f32[240,1024]{0,1:T(8,128)}, u32[]{:S(2)}) copy-start(f32[240,1024]{0,1:T(8,128)} %copy.87) | copy-start | bytes 2949124
  (60 other events, 253.9 us)
Sparse Core Ops, SparseCore 0:
  301.1 156.4 all-reduce.4

commit v4 on v3

--- a/solution.py
+++ b/solution.py
@@ -21,18 +21,6 @@
     return lax.ppermute(value, axis, [(i, i ^ bit) for i in range(size)])
 
 
-def has_bit(axis, bit):
-    return (lax.axis_index(axis) // bit) % 2 == 1
-
-
-def merge(mine, other, axis, bit):
-    return jnp.where(
-        has_bit(axis, bit),
-        jnp.concatenate([other, mine], axis=0),
-        jnp.concatenate([mine, other], axis=0),
-    )
-
-
 def product(left_side, right_side):
     return jnp.dot(left_side, right_side, preferred_element_type=jnp.float32)
 
@@ -51,161 +39,6 @@
 
 def column_sums(values_in):
     return jnp.sum(values_in.astype(jnp.float32), axis=0)
-
-
-def gather_far_half(own):
-    rows = own.shape[0]
-    half = rows // 2
-    which = lax.axis_index("grp") % 2
-    sent = lax.dynamic_slice_in_dim(own, which * half, half, 0)
-    got = swap(sent, "fsdp", 2)
-    rest = swap(got, "grp", 1)
-    return merge(got, rest, "grp", 1)
-
-
-def four_shards(own, far):
-    return [own, swap(own, "fsdp", 1), far, swap(far, "fsdp", 1)]
-
-
-def in_order(shards, axis=0):
-    me = lax.axis_index("fsdp")
-    size = shards[0].shape[axis]
-    shape = list(shards[0].shape)
-    shape[axis] = size * len(shards)
-    whole = jnp.zeros(shape, shards[0].dtype)
-    for j, shard in enumerate(shards):
-        whole = lax.dynamic_update_slice_in_dim(whole, shard, (me ^ j) * size, axis)
-    return whole
-
-
-def group_bits():
-    bits = []
-    bit = 1
-    while bit < lax.axis_size("grp"):
-        bits.append(bit)
-        bit *= 2
-    return bits
-
-
-def slot_softmax(patch_ref, coeff_ref, mask_ref):
-    scores = coeff_ref[0, PIX] + mask_ref[...]
-    for k in range(PIX):
-        scores = scores + patch_ref[k].astype(jnp.float32) * coeff_ref[0, k]
-    top = jnp.max(scores, axis=0, keepdims=True)
-    terms = jnp.exp(scores - top)
-    return terms / jnp.sum(terms, axis=0, keepdims=True)
-
-
-def mixed_of(patch_ref, weights):
-    parts = [
-        (weights * patch_ref[k].astype(jnp.float32)).astype(jnp.bfloat16) for k in range(PIX)
-    ]
-    parts.append(weights.astype(jnp.bfloat16))
-    return jnp.concatenate(parts, axis=0)
-
-
-def aggregate_kernel(patch_ref, coeff_ref, mask_ref, table_ref, out_ref):
-    weights = slot_softmax(patch_ref, coeff_ref, mask_ref)
-    mixed = mixed_of(patch_ref, weights)
-    out_ref[...] = jnp.dot(
-        table_ref[...], mixed, preferred_element_type=jnp.float32
-    ).astype(jnp.bfloat16)
-
-
-def aggregate(patch_rows, coeff_heads, slot_mask, table_values):
-    rows = patch_rows.shape[2]
-    width = table_values.shape[0]
-    head_dim = width // HEADS
-    slots = slot_mask.shape[0]
-    return pl.pallas_call(
-        aggregate_kernel,
-        grid=(HEADS,),
-        in_specs=[
-            pl.BlockSpec((PIX, slots, rows), lambda h: (0, 0, 0)),
-            pl.BlockSpec((1, PIX + 1, slots, 1), lambda h: (h, 0, 0, 0)),
-            pl.BlockSpec((slots, 1), lambda h: (0, 0)),
-            pl.BlockSpec((head_dim, (PIX + 1) * slots), lambda h: (h, 0)),
-        ],
-        out_specs=pl.BlockSpec((head_dim, rows), lambda h: (h, 0)),
-        out_shape=jax.ShapeDtypeStruct((width, rows), jnp.bfloat16),
-        compiler_params=pltpu.CompilerParams(vmem_limit_bytes=VMEM_LIMIT),
-        cost_estimate=pl.CostEstimate(
-            flops=2 * (PIX + 1) * slots * rows * width * 4,
-            bytes_accessed=4 * width * rows,
-            transcendentals=HEADS * slots * rows,
-        ),
-        name="aggregate",
-    )(patch_rows, coeff_heads, slot_mask, table_values)
-
-
-def aggregate_back_kernel(
-    patch_ref, coeff_ref, mask_ref, table_ref, heads_ref, scale_ref, table_grad_ref, coeff_grad_ref, patch_grad_ref
-):
-    head = pl.program_id(0)
-    slots = mask_ref.shape[0]
-    weights = slot_softmax(patch_ref, coeff_ref, mask_ref)
-    mixed = mixed_of(patch_ref, weights)
-    heads_grad = heads_ref[...]
-    table_grad_ref[...] = lax.dot_general(
-        heads_grad, mixed, (((1,), (1,)), ((), ())), preferred_element_type=jnp.float32
-    )
-    mixed_grad = lax.dot_general(
-        table_ref[...], heads_grad, (((0,), (0,)), ((), ())), preferred_element_type=jnp.float32
-    )
-    parts = [mixed_grad[k * slots : (k + 1) * slots] for k in range(PIX + 1)]
-    values = [patch_ref[k].astype(jnp.float32) for k in range(PIX)]
-    weights_grad = parts[PIX]
-    for k in range(PIX):
-        weights_grad = weights_grad + parts[k] * values[k]
-    mean_grad = jnp.sum(weights * weights_grad, axis=0, keepdims=True)
-    scores_grad = weights * (weights_grad - mean_grad)
-    for k in range(PIX):
-        coeff_grad_ref[0, k] = jnp.sum(scores_grad * values[k], axis=1, keepdims=True)
-    coeff_grad_ref[0, PIX] = jnp.sum(scores_grad, axis=1, keepdims=True)
-
-    @pl.when(head == 0)
-    def _():
-        patch_grad_ref[...] = jnp.zeros_like(patch_grad_ref)
-
-    scale = scale_ref[0]
-    for k in range(PIX):
-        patch_grad_ref[k] += scale * (parts[k] * weights + scores_grad * coeff_ref[0, k])
-
-
-def aggregate_back(patch_rows, coeff_heads, slot_mask, table_values, heads_grad, scale):
-    rows = patch_rows.shape[2]
-    width = table_values.shape[0]
-    head_dim = width // HEADS
-    slots = slot_mask.shape[0]
-    return pl.pallas_call(
-        aggregate_back_kernel,
-        grid=(HEADS,),
-        in_specs=[
-            pl.BlockSpec((PIX, slots, rows), lambda h: (0, 0, 0)),
-            pl.BlockSpec((1, PIX + 1, slots, 1), lambda h: (h, 0, 0, 0)),
-            pl.BlockSpec((slots, 1), lambda h: (0, 0)),
-            pl.BlockSpec((head_dim, (PIX + 1) * slots), lambda h: (h, 0)),
-            pl.BlockSpec((head_dim, rows), lambda h: (h, 0)),
-            pl.BlockSpec(memory_space=pltpu.SMEM),
-        ],
-        out_specs=[
-            pl.BlockSpec((head_dim, (PIX + 1) * slots), lambda h: (h, 0)),
-            pl.BlockSpec((1, PIX + 1, slots, 1), lambda h: (h, 0, 0, 0)),
-            pl.BlockSpec((PIX, slots, rows), lambda h: (0, 0, 0)),
-        ],
-        out_shape=[
-            jax.ShapeDtypeStruct((width, (PIX + 1) * slots), jnp.float32),
-            jax.ShapeDtypeStruct((HEADS, PIX + 1, slots, 1), jnp.float32),
-            jax.ShapeDtypeStruct((PIX, slots, rows), jnp.float32),
-        ],
-        compiler_params=pltpu.CompilerParams(vmem_limit_bytes=VMEM_LIMIT),
-        cost_estimate=pl.CostEstimate(
-            flops=4 * (PIX + 1) * slots * rows * width * 4,
-            bytes_accessed=8 * width * rows,
-            transcendentals=HEADS * slots * rows,
-        ),
-        name="aggregate_back",
-    )(patch_rows, coeff_heads, slot_mask, table_values, heads_grad, scale)
 
 
 def flip(index, bit):
@@ -220,6 +53,497 @@
             barrier, inc=1, device_id=partner, device_id_type=pl.DeviceIdType.MESH
         )
     pl.semaphore_wait(barrier, len(partners))
+
+
+def normalise(values_in):
+    row_mean = jnp.mean(values_in, axis=-1, keepdims=True)
+    centred = values_in - row_mean
+    spread = jnp.mean(centred * centred, axis=-1, keepdims=True)
+    inverse = lax.rsqrt(spread + 1e-05)
+    return centred * inverse, inverse
+
+
+def norm_back(grad, xhat, inverse, gain_vec):
+    scaled = grad * gain_vec
+    first = jnp.mean(scaled, axis=-1, keepdims=True)
+    second = jnp.mean(scaled * xhat, axis=-1, keepdims=True)
+    return (scaled - first - xhat * second) * inverse
+
+
+def slot_softmax(patch_ref, columns, mask_ref):
+    scores = columns[PIX] + mask_ref[...]
+    for k in range(PIX):
+        scores = scores + patch_ref[k].astype(jnp.float32) * columns[k]
+    top = jnp.max(scores, axis=0, keepdims=True)
+    terms = jnp.exp(scores - top)
+    return terms / jnp.sum(terms, axis=0, keepdims=True)
+
+
+def mixed_of(patch_ref, weights, rows):
+    parts = [
+        (weights * patch_ref[k].astype(jnp.float32)).astype(jnp.bfloat16) for k in range(PIX)
+    ]
+    parts.append(weights.astype(jnp.bfloat16))
+    used = weights.shape[0] * (PIX + 1)
+    if rows > used:
+        parts.append(jnp.zeros((rows - used, weights.shape[1]), jnp.bfloat16))
+    return jnp.concatenate(parts, axis=0)
+
+
+def head_columns(coeff_ref, head, slots):
+    lane = lax.broadcasted_iota(jnp.int32, (slots, coeff_ref.shape[1]), 1)
+    return [
+        jnp.sum(
+            jnp.where(lane == head, coeff_ref[k * slots : (k + 1) * slots, :], 0.0),
+            axis=1,
+            keepdims=True,
+        )
+        for k in range(PIX + 1)
+    ]
+
+
+def prepare_kernel(group_size, head_dim, *refs):
+    (
+        count_ref, own_query, query_w, key_w, own_table, select_ref, own_value, own_agg,
+        own_qkv, own_proj, own_grad, patch_ref, mask_ref, bias_ref, gain_ref, shift_ref,
+    ) = refs[:16]
+    (
+        count_out, tables, query_out, keys_out, full_value, full_agg, full_qkv, full_proj,
+        near_grad, far_grads, table_out, coeff_out, heads_out, embed_out, norm_out,
+    ) = refs[16:31]
+    query_part, query_got, counts = refs[31:34]
+    whole_value, whole_agg, whole_qkv, whole_proj, grads = refs[34:39]
+    send_sem, recv_sem, small_send, small_recv, local_sem = refs[39:]
+    wide = jnp.float32
+    low = jnp.bfloat16
+    me = lax.axis_index("fsdp")
+    group = lax.axis_index("grp")
+    near_index = flip(me, 1)[0]
+    far_index = flip(me, 2)[0]
+    near = {"fsdp": near_index}
+    far = {"fsdp": far_index}
+    block = own_value.shape[0]
+    heads = keys_out.shape[0]
+    slots = mask_ref.shape[0]
+    rows = own_grad.shape[0]
+    bits = []
+    bit = 1
+    while bit < group_size:
+        bits.append(bit)
+        bit *= 2
+    meet(
+        [near, far, {"fsdp": flip(far_index, 1)[0]}]
+        + [{"grp": flip(group, bit)[0]} for bit in bits]
+    )
+
+    def remote(src, dst, sends, recvs, at, device):
+        return pltpu.make_async_remote_copy(
+            src_ref=src,
+            dst_ref=dst,
+            send_sem=sends.at[at],
+            recv_sem=recvs.at[at],
+            device_id=device,
+            device_id_type=pl.DeviceIdType.MESH,
+        )
+
+    def span(start, size):
+        return pl.ds(pl.multiple_of(start, 16), size)
+
+    width = own_value.shape[1]
+    items = [(own_value, whole_value, 0, width, False), (own_agg, whole_agg, 0, width, False)]
+    for n in range(full_qkv.shape[1] // width):
+        items.append((own_qkv, whole_qkv, n * width, width, True))
+    items.append((own_proj, whole_proj, 0, width, True))
+    x_bit = flip(group, 1)[1]
+    piece = flip(group, 2)[1] + 2 * flip(group, 4)[1] + 4 * x_bit
+    eighth = block // 8
+
+    def weight_copy(n, stage):
+        own, whole, start, size, eighths = items[n]
+        cols = pl.ds(start, size)
+
+        def region(base, offset, count):
+            return whole.at[span(base * block + offset, count), cols]
+
+        if stage == 0:
+            return remote(
+                own.at[:, cols], region(me, 0, block), send_sem, recv_sem, (n, 0), near
+            )
+        if stage == 1:
+            offset, count = (piece * eighth, eighth) if eighths else (x_bit * (block // 2), block // 2)
+            return remote(
+                own.at[span(offset, count), cols],
+                region(me, offset, count),
+                send_sem,
+                recv_sem,
+                (n, 1),
+                far,
+            )
+        if stage == 2:
+            at = region(far_index, piece * eighth, eighth)
+            return remote(at, at, send_sem, recv_sem, (n, 2), {"grp": flip(group, 2)[0]})
+        if stage == 3:
+            at = region(far_index, (piece // 2) * 2 * eighth, 2 * eighth)
+            return remote(at, at, send_sem, recv_sem, (n, 3), {"grp": flip(group, 4)[0]})
+        if stage == 4:
+            at = region(far_index, x_bit * (block // 2), block // 2)
+            return remote(at, at, send_sem, recv_sem, (n, 4), {"grp": flip(group, 1)[0]})
+        at = region(far_index, 0, block)
+        return remote(at, at, send_sem, recv_sem, (n, 5), near)
+
+    def out_copy(n):
+        own, whole, start, size, eighths = items[n]
+        target = [full_value, full_agg, full_qkv, full_proj][min(n, 2) if n + 1 < len(items) else 3]
+        cols = pl.ds(start, size)
+        return pltpu.make_async_copy(whole.at[:, cols], target.at[:, cols], local_sem.at[2 + n])
+
+    grad_parts = 4
+    part_rows = rows // grad_parts
+
+    def grad_near():
+        return remote(own_grad, grads.at[0], small_send, small_recv, 0, near)
+
+    def grad_far(p):
+        at = pl.ds(p * part_rows, part_rows)
+        return remote(
+            own_grad.at[at, :], grads.at[1, at, :], small_send, small_recv, 1 + p, far
+        )
+
+    def grad_last(p):
+        at = pl.ds(p * part_rows, part_rows)
+        return remote(
+            grads.at[1, at, :],
+            grads.at[2, at, :],
+            small_send,
+            small_recv,
+            1 + grad_parts + p,
+            near,
+        )
+
+    def grad_out(n):
+        if n == 0:
+            return pltpu.make_async_copy(grads.at[0], near_grad, local_sem.at[0])
+        return pltpu.make_async_copy(grads.at[pl.ds(1, 2)], far_grads, local_sem.at[1])
+
+    base = 1 + 2 * grad_parts
+
+    def table_copy(kind):
+        if kind == 0:
+            return remote(own_table, tables.at[me], small_send, small_recv, base, near)
+        if kind == 1:
+            return remote(own_table, tables.at[me], small_send, small_recv, base + 1, far)
+        at = tables.at[far_index]
+        return remote(at, at, small_send, small_recv, base + 2, near)
+
+    others = [near, far, {"fsdp": flip(far_index, 1)[0]}]
+
+    def query_copy(kind):
+        return remote(
+            query_part, query_got.at[kind], small_send, small_recv, base + 3 + kind, others[kind]
+        )
+
+    def key_copy(kind):
+        at = keys_out.at[:, pl.ds(pl.multiple_of(me * block, 128), block)]
+        return remote(at, at, small_send, small_recv, base + 6 + kind, others[kind])
+
+    def count_copy(n):
+        partner = {"grp": flip(group, bits[n])[0]}
+        return remote(
+            counts.at[2 * n], counts.at[2 * n + 1], small_send, small_recv, base + 9 + n, partner
+        )
+
+    def count_step(n):
+        count_copy(n).wait()
+        value = counts[2 * n] + counts[2 * n + 1]
+        if n + 1 < len(bits):
+            counts[2 * n + 2] = value
+            count_copy(n + 1).start()
+        else:
+            count_out[...] = value
+
+    def forward(n, stage):
+        weight_copy(n, stage).wait()
+        weight_copy(n, 4 if (stage == 1 and not items[n][4]) else stage + 1).start()
+
+    def keep(n):
+        weight_copy(n, 0).wait()
+        weight_copy(n, 5).wait()
+        out_copy(n).start()
+
+    late = list(range(2, len(items)))
+
+    query_part[...] = jnp.dot(own_query[...], query_w[...], preferred_element_type=wide)[:8]
+    for kind in range(3):
+        query_copy(kind).start()
+    for n in late:
+        weight_copy(n, 1).start()
+    table_copy(1).start()
+    table_copy(0).start()
+    counts[0] = count_ref[...]
+    count_copy(0).start()
+    weight_copy(0, 0).start()
+    weight_copy(1, 0).start()
+    tables[me] = own_table[...]
+    whole_value[span(me * block, block), :] = own_value[...]
+    whole_agg[span(me * block, block), :] = own_agg[...]
+    whole_qkv[span(me * block, block), :] = own_qkv[...]
+    whole_proj[span(me * block, block), :] = own_proj[...]
+    for kind in range(3):
+        query_copy(kind).wait()
+    query = query_part[...] + query_got[0] + query_got[1] + query_got[2]
+    query_out[...] = query
+    lane = lax.broadcasted_iota(jnp.int32, (heads, width), 1)
+    head = lax.broadcasted_iota(jnp.int32, (heads, width), 0)
+    spread = jnp.where(lane // head_dim == head, jnp.broadcast_to(query[:1], (heads, width)), 0.0)
+    own_keys = lax.dot_general(
+        spread.astype(low), key_w[...], (((1,), (1,)), ((), ())), preferred_element_type=wide
+    ) * (head_dim ** (-0.5))
+    keys_out[:, pl.ds(pl.multiple_of(me * block, 128), block)] = own_keys.astype(low)
+    for kind in range(3):
+        key_copy(kind).start()
+    weight_copy(0, 1).start()
+    weight_copy(1, 1).start()
+    for p in range(grad_parts):
+        grad_far(p).start()
+    for n in late:
+        weight_copy(n, 0).start()
+    grad_near().start()
+    for n in late:
+        forward(n, 1)
+    table_copy(0).wait()
+    table_copy(1).wait()
+    table_copy(2).start()
+    for n in late:
+        forward(n, 2)
+    table_copy(2).wait()
+    stacked = tables[...].reshape(select_ref.shape[1], width)
+    table = jnp.dot(select_ref[...], stacked, preferred_element_type=wide).astype(low)
+    for kind in range(3):
+        key_copy(kind).wait()
+    coeff_out[...] = lax.dot_general(
+        table, keys_out[...], (((1,), (1,)), ((), ())), preferred_element_type=wide
+    )
+    forward(0, 1)
+    forward(2, 3)
+    forward(1, 1)
+    forward(0, 4)
+    forward(2, 4)
+    weight_copy(0, 0).wait()
+    weight_copy(0, 5).wait()
+    out_copy(0).start()
+    values = jnp.dot(table, whole_value[...], preferred_element_type=wide)
+    table_out[...] = jnp.transpose(values).astype(low)
+    forward(3, 3)
+
+    def one_head(h, carry):
+        weights = slot_softmax(patch_ref, head_columns(coeff_out, h, slots), mask_ref)
+        mixed = mixed_of(patch_ref, weights, table_out.shape[1])
+        at = pl.ds(pl.multiple_of(h * head_dim, 16), head_dim)
+        heads_out[at, :] = jnp.dot(
+            table_out[at, :], mixed, preferred_element_type=wide
+        ).astype(low)
+        return carry
+
+    half = heads // 2
+    lax.fori_loop(0, half, one_head, 0)
+    forward(1, 4)
+    count_step(0)
+    lax.fori_loop(half, heads, one_head, 0)
+    keep(2)
+    forward(4, 3)
+    forward(3, 4)
+    keep(1)
+    embedded = (
+        lax.dot_general(
+            heads_out[...], whole_agg[...], (((0,), (0,)), ((), ())), preferred_element_type=wide
+        )
+        + bias_ref[...]
+    )
+    embed_out[...] = embedded
+    count_step(1)
+    grad_far(0).wait()
+    grad_last(0).start()
+    xhat, inverse = normalise(embedded)
+    norm_out[...] = (xhat * gain_ref[...] + shift_ref[...]).astype(low)
+    forward(5, 3)
+    forward(4, 4)
+    keep(3)
+    grad_far(1).wait()
+    grad_last(1).start()
+    keep(4)
+    for n in range(2, len(bits)):
+        count_step(n)
+    forward(5, 4)
+    grad_far(2).wait()
+    grad_last(2).start()
+    keep(5)
+    grad_near().wait()
+    grad_out(0).start()
+    grad_far(3).wait()
+    grad_last(3).start()
+    for p in range(grad_parts):
+        grad_last(p).wait()
+    grad_out(1).start()
+    for n in range(len(items)):
+        out_copy(n).wait()
+    for n in range(2):
+        grad_out(n).wait()
+
+
+def prepare(
+    group_size, count_rows, own_query, query_w, key_w, own_table, select, own_value, own_agg,
+    own_qkv, own_proj, own_grad, patch_rows, slot_mask, bias, gain, shift,
+):
+    block, width = own_value.shape
+    head_dim = width // HEADS
+    rows = own_grad.shape[0]
+    slots = slot_mask.shape[0]
+    size = select.shape[0]
+    low = jnp.bfloat16
+    wide = jnp.float32
+    vmem = pl.BlockSpec(memory_space=pltpu.VMEM)
+    hbm = pl.BlockSpec(memory_space=pl.ANY)
+    steps = 0
+    while 2**steps < group_size:
+        steps += 1
+    items = 3 + own_qkv.shape[1] // width
+    small = 1 + 2 * 4 + 9 + steps
+
+    def shape(dims, kind):
+        return jax.ShapeDtypeStruct(dims, kind)
+
+    return pl.pallas_call(
+        functools.partial(prepare_kernel, group_size, head_dim),
+        in_specs=[vmem] * 16,
+        out_specs=[vmem] * 4 + [hbm] * 6 + [vmem] * 5,
+        out_shape=[
+            shape((8, 128), wide),
+            shape((4,) + own_table.shape, low),
+            shape((8, width), wide),
+            shape((HEADS, width), low),
+            shape((4 * block, width), low),
+            shape((4 * block, width), low),
+            shape((4 * block, own_qkv.shape[1]), low),
+            shape((4 * block, width), low),
+            shape((rows, width), low),
+            shape((2, rows, width), low),
+            shape((width, size), low),
+            shape((size, HEADS), wide),
+            shape((width, rows), low),
+            shape((rows, width), wide),
+            shape((rows, width), low),
+        ],
+        scratch_shapes=[
+            pltpu.VMEM((8, width), wide),
+            pltpu.VMEM((3, 8, width), wide),
+            pltpu.VMEM((2 * steps, 8, 128), wide),
+            pltpu.VMEM((4 * block, width), low),
+            pltpu.VMEM((4 * block, width), low),
+            pltpu.VMEM((4 * block, own_qkv.shape[1]), low),
+            pltpu.VMEM((4 * block, width), low),
+            pltpu.VMEM((3, rows, width), low),
+            pltpu.SemaphoreType.DMA((items, 6)),
+            pltpu.SemaphoreType.DMA((items, 6)),
+            pltpu.SemaphoreType.DMA((small,)),
+            pltpu.SemaphoreType.DMA((small,)),
+            pltpu.SemaphoreType.DMA((2 + items,)),
+        ],
+        compiler_params=pltpu.CompilerParams(
+            collective_id=3, has_side_effects=True, vmem_limit_bytes=VMEM_LIMIT
+        ),
+        cost_estimate=pl.CostEstimate(
+            flops=8 * size * rows * width, bytes_accessed=100_000_000, transcendentals=0
+        ),
+        name="prepare",
+    )(
+        count_rows, own_query, query_w, key_w, own_table, select, own_value, own_agg,
+        own_qkv, own_proj, own_grad, patch_rows, slot_mask, bias, gain, shift,
+    )
+
+
+def aggregate_back_kernel(
+    patch_ref, coeff_ref, mask_ref, table_ref, select_ref, heads_ref, scale_ref,
+    sum_ref, coeff_sum_ref, patch_grad_ref, table_s, coeff_s,
+):
+    slots = mask_ref.shape[0]
+    head_dim = table_ref.shape[0] // HEADS
+    size = table_ref.shape[1]
+    wide = jnp.float32
+    low = jnp.bfloat16
+    patch_grad_ref[...] = jnp.zeros_like(patch_grad_ref)
+    coeff_s[...] = jnp.zeros_like(coeff_s)
+    lane = lax.broadcasted_iota(jnp.int32, (slots, HEADS), 1)
+
+    def one_head(h, carry):
+        columns = head_columns(coeff_ref, h, slots)
+        weights = slot_softmax(patch_ref, columns, mask_ref)
+        mixed = mixed_of(patch_ref, weights, size)
+        at = pl.ds(pl.multiple_of(h * head_dim, 16), head_dim)
+        heads_grad = heads_ref[at, :]
+        table_s[at, :] = (
+            lax.dot_general(
+                heads_grad, mixed, (((1,), (1,)), ((), ())), preferred_element_type=wide
+            )
+            * scale_ref[0]
+        ).astype(low)
+        mixed_grad = lax.dot_general(
+            table_ref[at, :], heads_grad, (((0,), (0,)), ((), ())), preferred_element_type=wide
+        )
+        parts = [mixed_grad[k * slots : (k + 1) * slots] for k in range(PIX + 1)]
+        values = [patch_ref[k].astype(wide) for k in range(PIX)]
+        weights_grad = parts[PIX]
+        for k in range(PIX):
+            weights_grad = weights_grad + parts[k] * values[k]
+        mean_grad = jnp.sum(weights * weights_grad, axis=0, keepdims=True)
+        scores_grad = weights * (weights_grad - mean_grad)
+        for k in range(PIX + 1):
+            value = scores_grad * values[k] if k < PIX else scores_grad
+            column = jnp.sum(value, axis=1, keepdims=True)
+            rows = slice(k * slots, (k + 1) * slots)
+            coeff_s[rows, :] = coeff_s[rows, :] + jnp.where(lane == h, column, 0.0)
+        for k in range(PIX):
+            patch_grad_ref[k] += scale_ref[1] * (parts[k] * weights + scores_grad * columns[k])
+        return carry
+
+    lax.fori_loop(0, HEADS, one_head, 0)
+    sum_ref[...] = lax.dot_general(
+        select_ref[...], table_s[...], (((0,), (1,)), ((), ())), preferred_element_type=wide
+    ).astype(low)
+    coeff_sum_ref[...] = scale_ref[0] * lax.dot_general(
+        select_ref[...].astype(wide),
+        coeff_s[...],
+        (((0,), (0,)), ((), ())),
+        preferred_element_type=wide,
+        precision=exact_mode,
+    )
+
+
+def aggregate_back(patch_rows, coeffs, slot_mask, table_values, select, heads_grad, scales):
+    rows = patch_rows.shape[2]
+    width, size = table_values.shape
+    slots = slot_mask.shape[0]
+    vmem = pl.BlockSpec(memory_space=pltpu.VMEM)
+    return pl.pallas_call(
+        aggregate_back_kernel,
+        in_specs=[vmem] * 6 + [pl.BlockSpec(memory_space=pltpu.SMEM)],
+        out_specs=[vmem] * 3,
+        out_shape=[
+            jax.ShapeDtypeStruct((select.shape[1], width), jnp.bfloat16),
+            jax.ShapeDtypeStruct((select.shape[1], HEADS), jnp.float32),
+            jax.ShapeDtypeStruct((PIX, slots, rows), jnp.float32),
+        ],
+        scratch_shapes=[
+            pltpu.VMEM((width, size), jnp.bfloat16),
+            pltpu.VMEM((size, HEADS), jnp.float32),
+        ],
+        compiler_params=pltpu.CompilerParams(vmem_limit_bytes=VMEM_LIMIT),
+        cost_estimate=pl.CostEstimate(
+            flops=16 * size * rows * width,
+            bytes_accessed=8 * width * rows,
+            transcendentals=HEADS * slots * rows,
+        ),
+        name="aggregate_back",
+    )(patch_rows, coeffs, slot_mask, table_values, select, heads_grad, scales)
 
 
 def lane_half(rows, pair, head_dim):
@@ -540,82 +864,222 @@
     )(valid, queries, key_values, grad, out, logs)
 
 
-def feed_kernel(
-    first_ref, second_ref, grad_ref, up_ref, down_ref, bias_ref, rows_ref, gelu_ref, pre_ref, out_ref, back_ref, bias_grad_ref
+def feed_kernel(*refs):
+    (
+        share_ref, context_ref, proj_ref, embed_ref, own_grad, near_grad, far_grads, up_ref,
+        down_ref, bias_ref, proj_bias, gain_ref, shift_ref,
+    ) = refs[:13]
+    (
+        middle_ref, out_ref, down_total, up_total, middle_grad, attended, context_grad, vectors,
+    ) = refs[13:21]
+    entry, gelu_s, pre_s, own_back, near_s, last_s, far_s, got_near, got_last, got_far = refs[21:31]
+    send_sem, recv_sem = refs[31:]
+    wide = jnp.float32
+    low = jnp.bfloat16
+    me = lax.axis_index("fsdp")
+    near = {"fsdp": flip(me, 1)[0]}
+    far = {"fsdp": flip(me, 2)[0]}
+    rows, width = embed_ref.shape
+    hidden = up_ref.shape[1]
+    tile = rows // 2
+    pairs, _, lanes = context_grad.shape
+    meet([near, far])
+
+    def span(t):
+        return pl.ds(t * tile, tile)
+
+    def copy(kind, t, src, dst, device):
+        return pltpu.make_async_remote_copy(
+            src_ref=src.at[span(t), :],
+            dst_ref=dst.at[span(t), :],
+            send_sem=send_sem.at[kind, t],
+            recv_sem=recv_sem.at[kind, t],
+            device_id=device,
+            device_id_type=pl.DeviceIdType.MESH,
+        )
+
+    def rows_near(t):
+        return copy(0, t, entry.at[0], entry.at[1], near)
+
+    def rows_far(t):
+        return copy(1, t, entry.at[0], entry.at[2], far)
+
+    def rows_last(t):
+        return copy(2, t, entry.at[2], entry.at[3], near)
+
+    def back_near(t):
+        return copy(3, t, near_s, got_near, near)
+
+    def back_last(t):
+        return copy(4, t, last_s, got_last, near)
+
+    def back_far(t):
+        return copy(5, t, far_s, got_far, far)
+
+    def grad_rows(s, t):
+        if s == 0:
+            return own_grad[span(t), :]
+        if s == 1:
+            return near_grad[span(t), :]
+        return far_grads[s - 2, span(t), :]
+
+    def feed(s, t, target):
+        rows_in = entry[s, span(t), :]
+        pre_act = jnp.dot(rows_in, up_ref[...], preferred_element_type=wide) + bias_ref[...]
+        cdf = 0.5 * (1.0 + lax.erf(pre_act * 0.7071067811865476))
+        density = jnp.exp(-0.5 * pre_act * pre_act) * 0.3989422804014327
+        gelu = (pre_act * cdf).astype(low)
+        gelu_s[s, span(t), :] = gelu
+        act_grad = lax.dot_general(
+            grad_rows(s, t), down_ref[...], (((1,), (1,)), ((), ())), preferred_element_type=wide
+        )
+        pre_grad = act_grad * (cdf + pre_act * density)
+        pre_low = pre_grad.astype(low)
+        pre_s[s, span(t), :] = pre_low
+        vectors[4:5, :] += jnp.sum(pre_low.astype(wide), axis=0, keepdims=True)
+        out_ref[s, span(t), :] = jnp.dot(
+            gelu, down_ref[...], preferred_element_type=wide
+        ).astype(low)
+        target[span(t), :] = lax.dot_general(
+            pre_low, up_ref[...], (((1,), (1,)), ((), ())), preferred_element_type=wide
+        ).astype(target.dtype)
+
+    vectors[...] = jnp.zeros_like(vectors)
+    for t in range(2):
+        middle = (
+            embed_ref[span(t), :]
+            + jnp.dot(context_ref[span(t), :], proj_ref[...], preferred_element_type=wide)
+            + proj_bias[...]
+        )
+        middle_ref[span(t), :] = middle
+        xhat, inverse = normalise(middle)
+        entry[0, span(t), :] = (xhat * gain_ref[...] + shift_ref[...]).astype(low)
+        rows_far(t).start()
+        rows_near(t).start()
+    for t in range(2):
+        feed(0, t, own_back)
+    for t in range(2):
+        rows_near(t).wait()
+        feed(1, t, near_s)
+        back_near(t).start()
+
+    for t in range(2):
+        rows_far(t).wait()
+        rows_last(t).start()
+        feed(2, t, far_s)
+        rows_last(t).wait()
+        feed(3, t, last_s)
+        back_last(t).start()
+        if t > 0:
+            add_last(t - 1, back_last, back_far, far_s, got_last, span)
+    add_last(1, back_last, back_far, far_s, got_last, span)
+
+    block = min(hidden, 256)
+    grads = [own_grad[...], near_grad[...], far_grads[0], far_grads[1]]
+    for start in range(0, hidden, block):
+        value = 0.0
+        for s in range(4):
+            value = value + lax.dot_general(
+                gelu_s[s, :, start : start + block],
+                grads[s],
+                (((0,), (0,)), ((), ())),
+                preferred_element_type=wide,
+            )
+        down_total[start : start + block, :] = (value * share_ref[0]).astype(low)
+    for start in range(0, width, block):
+        value = 0.0
+        for s in range(4):
+            value = value + lax.dot_general(
+                entry[s, :, start : start + block],
+                pre_s[s],
+                (((0,), (0,)), ((), ())),
+                preferred_element_type=wide,
+            )
+        up_total[start : start + block, :] = (value * share_ref[0]).astype(low)
+
+    for t in range(2):
+        back_near(t).wait()
+        back_far(t).wait()
+        at = span(t)
+        grad = own_back[at, :] + got_near[at, :].astype(wide) + got_far[at, :].astype(wide)
+        xhat, inverse = normalise(middle_ref[at, :])
+        vectors[0:1, :] += jnp.sum(grad * xhat, axis=0, keepdims=True)
+        vectors[1:2, :] += jnp.sum(grad, axis=0, keepdims=True)
+        upstream = own_grad[at, :].astype(wide)
+        vectors[3:4, :] += jnp.sum(upstream, axis=0, keepdims=True)
+        value = upstream + norm_back(grad, xhat, inverse, gain_ref[...])
+        middle_grad[at, :] = value
+        value_low = value.astype(low)
+        attended[at, :] = value_low
+        vectors[2:3, :] += jnp.sum(value_low.astype(wide), axis=0, keepdims=True)
+        back = lax.dot_general(
+            value_low, proj_ref[...], (((1,), (1,)), ((), ())), preferred_element_type=wide
+        ).astype(low)
+        for i in range(pairs):
+            context_grad[i, at, :] = back[:, i * lanes : (i + 1) * lanes]
+
+
+def add_last(t, back_last, back_far, far_s, got_last, span):
+    back_last(t).wait()
+    at = span(t)
+    value = far_s[at, :].astype(jnp.float32) + got_last[at, :].astype(jnp.float32)
+    far_s[at, :] = value.astype(jnp.bfloat16)
+    back_far(t).start()
+
+
+def feed(
+    share, context, proj, embedded, own_grad, near_grad, far_grads, up, down, bias, proj_bias, gain, shift
 ):
-    tile = first_ref.shape[0]
-    entry = jnp.concatenate([first_ref[...], second_ref[...]], axis=0)
-    grad = jnp.concatenate([grad_ref[0], grad_ref[1]], axis=0)
-    pre_act = jnp.dot(entry, up_ref[...], preferred_element_type=jnp.float32) + bias_ref[...]
-    cdf = 0.5 * (1.0 + lax.erf(pre_act * 0.7071067811865476))
-    density = jnp.exp(-0.5 * pre_act * pre_act) * 0.3989422804014327
-    gelu = (pre_act * cdf).astype(jnp.bfloat16)
-    act_grad = lax.dot_general(
-        grad, down_ref[...], (((1,), (1,)), ((), ())), preferred_element_type=jnp.float32
-    )
-    pre_grad = (act_grad * (cdf + pre_act * density)).astype(jnp.bfloat16)
-    out = jnp.dot(gelu, down_ref[...], preferred_element_type=jnp.float32).astype(jnp.bfloat16)
-    back = lax.dot_general(
-        pre_grad, up_ref[...], (((1,), (1,)), ((), ())), preferred_element_type=jnp.float32
-    ).astype(jnp.bfloat16)
-
-    @pl.when(pl.program_id(0) == 0)
-    def _():
-        bias_grad_ref[...] = jnp.zeros_like(bias_grad_ref)
-
-    bias_grad_ref[...] += jnp.sum(pre_grad.astype(jnp.float32), axis=0, keepdims=True)
-    for ref, value in (
-        (rows_ref, entry),
-        (gelu_ref, gelu),
-        (pre_ref, pre_grad),
-        (out_ref, out),
-        (back_ref, back),
-    ):
-        ref[0] = value[:tile]
-        ref[1] = value[tile:]
-
-
-def feed(first, second, grads, up, down, bias):
-    rows, width = first.shape
+    rows, width = embedded.shape
     hidden = up.shape[1]
-    tile = min(rows, 128)
-    one = pl.BlockSpec((tile, width), lambda i: (i, 0))
-    pair = pl.BlockSpec((2, tile, width), lambda i: (0, i, 0))
-    pair_hidden = pl.BlockSpec((2, tile, hidden), lambda i: (0, i, 0))
-
-    def fixed(shape):
-        return pl.BlockSpec(shape, lambda i: (0, 0))
-
-    out = jax.ShapeDtypeStruct((2, rows, width), jnp.bfloat16)
-    out_hidden = jax.ShapeDtypeStruct((2, rows, hidden), jnp.bfloat16)
+    pairs = HEADS // 2
+    low = jnp.bfloat16
+    wide = jnp.float32
+    vmem = pl.BlockSpec(memory_space=pltpu.VMEM)
+    flat = (rows, width)
+
+    def shape(dims, kind):
+        return jax.ShapeDtypeStruct(dims, kind)
+
     return pl.pallas_call(
         feed_kernel,
-        grid=(rows // tile,),
-        in_specs=[
-            one,
-            one,
-            pair,
-            fixed(up.shape),
-            fixed(down.shape),
-            fixed((1, hidden)),
+        in_specs=[pl.BlockSpec(memory_space=pltpu.SMEM)] + [vmem] * 12,
+        out_specs=[vmem] * 8,
+        out_shape=[
+            shape(flat, wide),
+            shape((4,) + flat, low),
+            shape((hidden, width), low),
+            shape((width, hidden), low),
+            shape(flat, wide),
+            shape(flat, low),
+            shape((pairs, rows, width // pairs), low),
+            shape((8, width), wide),
         ],
-        out_specs=[pair, pair_hidden, pair_hidden, pair, pair, fixed((1, hidden))],
-        out_shape=[
-            out,
-            out_hidden,
-            out_hidden,
-            out,
-            out,
-            jax.ShapeDtypeStruct((1, hidden), jnp.float32),
+        scratch_shapes=[
+            pltpu.VMEM((4,) + flat, low),
+            pltpu.VMEM((4, rows, hidden), low),
+            pltpu.VMEM((4, rows, hidden), low),
+            pltpu.VMEM(flat, wide),
+            pltpu.VMEM(flat, low),
+            pltpu.VMEM(flat, low),
+            pltpu.VMEM(flat, low),
+            pltpu.VMEM(flat, low),
+            pltpu.VMEM(flat, low),
+            pltpu.VMEM(flat, low),
+            pltpu.SemaphoreType.DMA((6, 2)),
+            pltpu.SemaphoreType.DMA((6, 2)),
         ],
-        compiler_params=pltpu.CompilerParams(vmem_limit_bytes=VMEM_LIMIT),
+        compiler_params=pltpu.CompilerParams(
+            collective_id=4, has_side_effects=True, vmem_limit_bytes=VMEM_LIMIT
+        ),
         cost_estimate=pl.CostEstimate(
-            flops=16 * rows * width * hidden * 2,
-            bytes_accessed=16 * rows * width,
-            transcendentals=4 * rows * hidden,
+            flops=48 * rows * width * hidden, bytes_accessed=100_000_000, transcendentals=0
         ),
         name="feed",
-    )(first, second, grads, up, down, bias)
+    )(
+        share, context, proj, embedded, own_grad, near_grad, far_grads, up, down, bias,
+        proj_bias, gain, shift,
+    )
 
 
 def total_kernel(group_size, widths, share_ref, *refs):
@@ -836,21 +1300,6 @@
     )(share, *[array for pair in pairs for array in pair], bundle)
 
 
-def normalise(values_in):
-    row_mean = jnp.mean(values_in, axis=-1, keepdims=True)
-    centred = values_in - row_mean
-    spread = jnp.mean(centred * centred, axis=-1, keepdims=True)
-    inverse = lax.rsqrt(spread + 1e-05)
-    return centred * inverse, inverse
-
-
-def norm_back(grad, xhat, inverse, gain_vec):
-    scaled = grad * gain_vec
-    first = jnp.mean(scaled, axis=-1, keepdims=True)
-    second = jnp.mean(scaled * xhat, axis=-1, keepdims=True)
-    return (scaled - first - xhat * second) * inverse
-
-
 def on_device(
     patches,
     patch_counts,
@@ -889,181 +1338,146 @@
     own_vars = patch_weight.shape[0]
     score_scale = head_dim ** (-0.5)
 
-    counts = patch_counts.astype(wide)
-    count_total = counts
-    for bit in group_bits():
-        count_total = count_total + swap(count_total, "grp", bit)
-    count_share = counts[0] / count_total[0]
     item_count = patch_counts[0]
     own_valid = me * rows + jnp.arange(rows, dtype=jnp.int32) < item_count
     shard_valid = jnp.clip(
         item_count - (me ^ jnp.arange(4, dtype=jnp.int32)) * rows, 0, rows
     ).astype(jnp.int32)
-
-    present = var_present[0] > 0
+    down_grad = jnp.where(own_valid[:, None], out_grad, jnp.zeros_like(out_grad))
+
     slot_vars = lax.dynamic_index_in_dim(var_ids, item_dataset[0], 0, keepdims=False)
-    selector = slot_vars[:, None] == jnp.arange(VTOT, dtype=jnp.int32)[None, :]
-    own_rows = jnp.concatenate(
+    part_size = -(-(PIX + 1) * own_vars // 16) * 16
+    size = 4 * part_size
+    slot_row = jnp.arange(size, dtype=jnp.int32)
+    slot_var = jnp.pad(jnp.tile(slot_vars, PIX + 1), (0, size - (PIX + 1) * VTOT))
+    place = (slot_var // own_vars) * part_size + (slot_row // VTOT) * own_vars + slot_var % own_vars
+    select = (
+        (place[:, None] == jnp.arange(size, dtype=jnp.int32)[None, :])
+        & (slot_row < (PIX + 1) * VTOT)[:, None]
+    ).astype(low)
+    own_table = jnp.concatenate(
         [
-            patch_weight.reshape(own_vars * PIX, width),
+            patch_weight.transpose(1, 0, 2).reshape(own_vars * PIX, width),
             var_embed,
+            jnp.zeros((part_size - (PIX + 1) * own_vars, width), low),
         ],
         axis=0,
     )
-    near_rows = swap(own_rows, "fsdp", 1)
-    far_rows = swap(jnp.stack([own_rows, near_rows]), "fsdp", 2)
-    row_sets = [own_rows, near_rows, far_rows[0], far_rows[1]]
-    table_parts = []
-    for part in row_sets:
-        pixels = part[: own_vars * PIX].reshape(own_vars, PIX, width)
-        embeds = part[own_vars * PIX : own_vars * (PIX + 1)][:, None, :]
-        table_parts.append(jnp.concatenate([pixels, embeds], axis=1).transpose(1, 0, 2))
-    stacked = in_order(table_parts, axis=1)
-    stacked_rows = stacked.reshape((PIX + 1) * VTOT, width)
-
     own_query = lax.dynamic_slice_in_dim(agg_query, me * own_width, own_width, 0)
-    query_sum = product(own_query[None, :], query_weight)
-    query_sum = query_sum + swap(query_sum, "fsdp", 1)
-    query_sum = query_sum + swap(query_sum, "fsdp", 2)
-    query_vec = query_sum[0].astype(low)
-    own_key_query = (
-        jnp.einsum(
-            "dhj,hj->hd",
-            key_weight.reshape(own_width, HEADS, head_dim),
-            query_vec.reshape(HEADS, head_dim),
-            preferred_element_type=wide,
-        )
-        * score_scale
-    ).astype(low)
-    near_key_query = swap(own_key_query, "fsdp", 1)
-    far_key_query = swap(jnp.stack([own_key_query, near_key_query]), "fsdp", 2)
-    key_query = in_order(
-        [own_key_query, near_key_query, far_key_query[0], far_key_query[1]], axis=1
-    )
-    coeffs_by_var = right_product(key_query, stacked_rows).reshape(HEADS, PIX + 1, VTOT)
-    coeff_heads = jnp.einsum(
-        "hku,su->hks", coeffs_by_var, selector.astype(wide), precision=exact_mode
-    )[..., None]
-
-    value_shards = four_shards(value_weight, gather_far_half(value_weight))
-    full_value = in_order(value_shards)
-    table_by_var = left_product(full_value, stacked_rows.T).astype(low)
-    table_values = (
-        jnp.einsum(
-            "hku,su->hks",
-            table_by_var.reshape(width, PIX + 1, VTOT),
-            selector.astype(low),
-            preferred_element_type=wide,
-        )
-        .astype(low)
-        .reshape(width, (PIX + 1) * VTOT)
-    )
-    own_table = lax.dynamic_slice_in_dim(stacked_rows, me * own_width, own_width, 1)
-    key_table = product(own_table, key_weight)
+    patch_rows = patches.transpose(1, 0, 2)
+    slot_mask = jnp.where(var_present[0] > 0, 0.0, masked_out).astype(wide)[:, None]
+    (
+        count_rows,
+        tables,
+        query_rows,
+        key_query,
+        full_value,
+        full_agg_proj,
+        full_qkv,
+        full_proj,
+        near_down_grad,
+        far_grads,
+        table_values,
+        coeffs,
+        heads_t,
+        embedded,
+        normed1,
+    ) = prepare(
+        group_count,
+        jnp.full((8, 128), item_count.astype(wide)),
+        jnp.broadcast_to(own_query[None, :], (16, own_width)),
+        query_weight,
+        key_weight,
+        own_table,
+        select,
+        value_weight,
+        agg_proj,
+        qkv_weight,
+        proj_weight,
+        down_grad,
+        patch_rows,
+        slot_mask,
+        agg_bias[None, :],
+        norm1_gain[None, :],
+        norm1_shift[None, :],
+    )
+    count_share = item_count.astype(wide) / count_rows[0, 0]
+    query_vec = query_rows[0].astype(low)
+    table_rows = tables.reshape(size, width)
+    own_columns = lax.dynamic_slice_in_dim(table_rows, me * own_width, own_width, 1)
+    key_table = product(own_columns, key_weight)
     key_table = key_table + swap(key_table.astype(low), "fsdp", 1).astype(wide)
     key_table = key_table + swap(key_table.astype(low), "fsdp", 2).astype(wide)
 
-    agg_proj_shards = four_shards(agg_proj, gather_far_half(agg_proj))
-    full_agg_proj = in_order(agg_proj_shards)
-    qkv_shards = four_shards(qkv_weight, gather_far_half(qkv_weight))
-    full_qkv = in_order(qkv_shards)
-    proj_shards = four_shards(proj_weight, gather_far_half(proj_weight))
-    full_proj = in_order(proj_shards)
-    upstream = out_grad.astype(wide) * own_valid[:, None].astype(wide)
-    down_grad = upstream.astype(low)
-    near_down_grad = swap(down_grad, "fsdp", 1)
-    far_down_grad = swap(down_grad, "fsdp", 2)
-    last_down_grad = swap(far_down_grad, "fsdp", 1)
-    near_grads = jnp.stack([down_grad, near_down_grad])
-    far_grads = jnp.stack([far_down_grad, last_down_grad])
-
-    patch_rows = patches.transpose(1, 0, 2)
-    slot_mask = jnp.where(present, 0.0, masked_out).astype(wide)[:, None]
-    heads_t = aggregate(patch_rows, coeff_heads, slot_mask, table_values)
-    embedded = left_product(heads_t, full_agg_proj) + agg_bias
-    xhat1, inverse1 = normalise(embedded)
-    normed1 = (xhat1 * norm1_gain + norm1_shift).astype(low)
+
     queries, key_values, context_pairs, logs = attend(normed1, full_qkv, shard_valid)
     context = context_pairs.transpose(1, 0, 2).reshape(rows, width)
-    middle = embedded + (product(context, full_proj) + proj_bias)
-    xhat2, inverse2 = normalise(middle)
-    normed2 = (xhat2 * norm2_gain + norm2_shift).astype(low)
-    near_normed2 = swap(normed2, "fsdp", 1)
-    far_normed2 = swap(normed2, "fsdp", 2)
-    last_normed2 = swap(far_normed2, "fsdp", 1)
-    bias_row = up_bias.astype(wide)[None, :]
-    near = feed(normed2, near_normed2, near_grads, up_weight, down_weight, bias_row)
-    far = feed(far_normed2, last_normed2, far_grads, up_weight, down_weight, bias_row)
-    far_got = swap(far[4][1], "fsdp", 1)
-    far_sum = (far[4][0].astype(wide) + far_got.astype(wide)).astype(low)
-    far_back = swap(far_sum, "fsdp", 2)
-    near_back = swap(near[4][1], "fsdp", 1)
-
-    def both_left(left, right):
-        def one(i):
-            return left_product(
-                left[i].reshape(-1, left[i].shape[2]), right[i].reshape(-1, right[i].shape[2])
-            )
-
-        return ((one(0) + one(1)) * count_share).astype(low)
-
-    down_weight_part = both_left([near[1], far[1]], [near_grads, far_grads])
-    up_weight_part = both_left([near[0], far[0]], [near[2], far[2]])
+    (
+        middle,
+        out_parts,
+        down_weight_part,
+        up_weight_part,
+        middle_grad,
+        attended_grad,
+        context_grad,
+        feed_vectors,
+    ) = feed(
+        count_share[None],
+        context,
+        full_proj,
+        embedded,
+        down_grad,
+        near_down_grad,
+        far_grads,
+        up_weight,
+        down_weight,
+        up_bias.astype(wide)[None, :],
+        proj_bias[None, :],
+        norm2_gain[None, :],
+        norm2_shift[None, :],
+    )
     down_weight_grad = lax.psum(down_weight_part, "grp").astype(wide)
     up_weight_grad = lax.psum(up_weight_part, "grp").astype(wide)
-    up_bias_grad = near[5] + far[5]
-    down_bias_grad = column_sums(down_grad)
-    normed2_grad = near[4][0].astype(wide) + near_back.astype(wide) + far_back.astype(wide)
-    out_got = swap(jnp.stack([near[3][1], far[3][1]]), "fsdp", 1)
-    out_far = swap((far[3][0].astype(wide) + out_got[1].astype(wide)).astype(low), "fsdp", 2)
-    down_sum = near[3][0].astype(wide) + out_got[0].astype(wide) + out_far.astype(wide)
+    out_got = swap(jnp.stack([out_parts[1], out_parts[3]]), "fsdp", 1)
+    out_far = swap((out_parts[2].astype(wide) + out_got[1].astype(wide)).astype(low), "fsdp", 2)
+    down_sum = out_parts[0].astype(wide) + out_got[0].astype(wide) + out_far.astype(wide)
     output = (middle + down_sum + down_bias).astype(low)
-    norm2_gain_grad = jnp.sum(normed2_grad * xhat2, axis=0)
-    norm2_shift_grad = jnp.sum(normed2_grad, axis=0)
-    middle_grad = upstream + norm_back(normed2_grad, xhat2, inverse2, norm2_gain)
-    attended_grad = middle_grad.astype(low)
-    proj_bias_grad = column_sums(attended_grad)
-
-    context_grad = right_product(attended_grad, full_proj).astype(low)
-    context_grad = context_grad.reshape(rows, HEADS // 2, 2 * head_dim).transpose(1, 0, 2)
+
     qkv_grad = attend_back(queries, key_values, context_grad, context_pairs, logs, shard_valid)
+    xhat1, inverse1 = normalise(embedded)
     normed1_grad = right_product(qkv_grad, full_qkv)
     norm1_gain_grad = jnp.sum(normed1_grad * xhat1, axis=0)
     norm1_shift_grad = jnp.sum(normed1_grad, axis=0)
     embedded_grad = (middle_grad + norm_back(normed1_grad, xhat1, inverse1, norm1_gain)).astype(low)
     agg_bias_grad = column_sums(embedded_grad)
     heads_grad = right_product(full_agg_proj, embedded_grad).astype(low)
-    input_scale = (group_count * count_share)[None]
-    table_grad, coeff_grad, patch_grad = aggregate_back(
-        patch_rows, coeff_heads, slot_mask, table_values, heads_grad, input_scale
+    scales = jnp.stack([count_share, group_count * count_share])
+    table_sum, coeff_sum, patch_grad = aggregate_back(
+        patch_rows, coeffs, slot_mask, table_values, select, heads_grad, scales
     )
     patches_grad = patch_grad.transpose(1, 0, 2)
 
-    table_sum = jnp.einsum(
-        "hks,su->kuh",
-        table_grad.reshape(width, PIX + 1, VTOT),
-        selector.astype(wide),
-        precision=exact_mode,
-    ).reshape((PIX + 1) * VTOT, width)
-    coeff_sum = jnp.einsum(
-        "hks,su->hku", coeff_grad[..., 0], selector.astype(wide), precision=exact_mode
-    ).reshape(-1)
-    coeff_rows = -(-coeff_sum.shape[0] // width)
-    coeff_flat = jnp.pad(coeff_sum, (0, coeff_rows * width - coeff_sum.shape[0]))
-    vectors = [
-        agg_bias_grad,
-        norm1_gain_grad,
-        norm1_shift_grad,
-        proj_bias_grad,
-        norm2_gain_grad,
-        norm2_shift_grad,
-        down_bias_grad,
-    ]
-    up_bias_rows = lax.dynamic_update_slice_in_dim(jnp.zeros((4, width), wide), up_bias_grad, me, 0)
-    pieces = [table_sum, coeff_flat.reshape(coeff_rows, width), jnp.stack(vectors), up_bias_rows]
-    bundle = jnp.concatenate(pieces, axis=0) * count_share
-    bundle = jnp.pad(bundle, ((0, -bundle.shape[0] % 128), (0, 0))).astype(low)
-    bundle_shape = bundle.shape
+    vectors = [agg_bias_grad, norm1_gain_grad, norm1_shift_grad]
+    up_bias_rows = lax.dynamic_update_slice_in_dim(
+        jnp.zeros((4, width), wide), feed_vectors[4:5], me, 0
+    )
+    coeff_rows = coeff_sum.T.reshape(-1, width)
+    spare = part_size - (PIX + 1) * own_vars
+    extras = jnp.concatenate(
+        [
+            coeff_rows,
+            jnp.concatenate([jnp.stack(vectors), feed_vectors[:4], up_bias_rows]) * count_share,
+        ],
+        axis=0,
+    )
+    extras = jnp.pad(extras, ((0, 4 * spare - extras.shape[0]), (0, 0))).astype(low)
+    bundle = jnp.concatenate(
+        [
+            table_sum.reshape(4, part_size, width)[:, : part_size - spare],
+            extras.reshape(4, spare, width),
+        ],
+        axis=1,
+    ).reshape(size, width)
     qkv_weight_grad, agg_proj_grad, proj_weight_grad, bundle = total(
         group_count,
         count_share[None],
@@ -1072,19 +1486,17 @@
         (context.T, attended_grad),
         bundle.reshape(width, -1),
     )
-    bundle = bundle.reshape(bundle_shape)
-    table_total = bundle[: table_sum.shape[0]]
-    at = table_sum.shape[0]
-    coeff_total = bundle[at : at + coeff_rows].reshape(-1)[: coeff_sum.shape[0]]
-    coeff_total = coeff_total.reshape(HEADS, (PIX + 1) * VTOT)
-    at += coeff_rows
-    vector_total = bundle[at : at + len(vectors)]
-    at += len(vectors)
-    up_bias_total = lax.dynamic_slice_in_dim(bundle, at + me, 1, 0)[0]
+    table_total = bundle.reshape(size, width)
+    extras = table_total.reshape(4, part_size, width)[:, part_size - spare :].reshape(-1, width)
+    at = coeff_rows.shape[0]
+    coeff_total = extras[:at].reshape(HEADS, size)
+    vector_total = extras[at : at + 7]
+    at += 7
+    up_bias_total = lax.dynamic_slice_in_dim(extras, at + me, 1, 0)[0]
     vector_own = lax.dynamic_slice_in_dim(vector_total, me * own_width, own_width, 1)
 
-    value_weight_grad = left_product(own_table, table_total.astype(low))
-    key_query_grad = jnp.dot(coeff_total, own_table.astype(wide), precision=exact_mode)
+    value_weight_grad = left_product(own_columns, table_total.astype(low))
+    key_query_grad = jnp.dot(coeff_total, own_columns.astype(wide), precision=exact_mode)
     key_weight_grad = (
         key_query_grad.T[:, :, None]
         * query_vec.astype(wide).reshape(1, HEADS, head_dim)
@@ -1094,7 +1506,7 @@
         jnp.einsum(
             "hx,xhj->hj",
             coeff_total,
-            key_table.reshape((PIX + 1) * VTOT, HEADS, head_dim),
+            key_table.reshape(size, HEADS, head_dim),
             precision=exact_mode,
         ).reshape(width)
         * score_scale
@@ -1103,16 +1515,12 @@
     agg_query_grad = jnp.dot(
         query_weight.astype(wide), query_grad, precision=exact_mode
     )
-    own_totals = lax.dynamic_slice_in_dim(
-        table_total.reshape(PIX + 1, VTOT, width), me * own_vars, own_vars, 1
-    ).reshape((PIX + 1) * own_vars, width)
-    own_coeffs = lax.dynamic_slice_in_dim(
-        coeff_total.reshape(HEADS, PIX + 1, VTOT), me * own_vars, own_vars, 2
-    ).reshape(HEADS, (PIX + 1) * own_vars)
+    own_totals = lax.dynamic_slice_in_dim(table_total, me * part_size, part_size, 0)
+    own_coeffs = lax.dynamic_slice_in_dim(coeff_total, me * part_size, part_size, 1)
     var_grads = right_product(own_totals.astype(low), full_value) + lax.dot_general(
         own_coeffs, key_query.astype(wide), (((0,), (0,)), ((), ())), precision=exact_mode
     )
-    var_grads = var_grads.reshape(PIX + 1, own_vars, width)
+    var_grads = var_grads[: (PIX + 1) * own_vars].reshape(PIX + 1, own_vars, width)
     patch_weight_grad = var_grads[:PIX].transpose(1, 0, 2)
     var_embed_grad = var_grads[PIX]
     return (
@@ -1130,9 +1538,9 @@
         vector_own[2],
         qkv_weight_grad,
         proj_weight_grad,
+        vector_own[5],
         vector_own[3],
         vector_own[4],
-        vector_own[5],
         up_weight_grad,
         up_bias_total,
         down_weight_grad,

time: 593 us -> 519 us (0.88)
  Pallas kernels: 282 us -> 390 us
  waiting for transfers between devices: 78.3 us -> 19.7 us
  local copies, waits for them, and re-layouts: 86 us -> 29.7 us
  starting transfers between devices: 29.9 us -> 2.26 us
  matrix products: 44 us -> 24.5 us
  other arithmetic: 49 us -> 32.9 us
    pallas_call x4 -> x3, Pallas kernels: 55.9 us -> 150 us  [the longest x1 71.2 us: prepare(): pl.pallas_call(functools.partial(prepare_kernel, group_size, head_dim), i...]
    ppermute x38 -> x4, waiting for transfers between devices: 78.3 us -> 19.7 us  [swap(): return lax.ppermute(value, axis, [(i, i ^ bit) for i in range(size)])]
    ppermute x38 -> x4, starting transfers between devices: 29.9 us -> 2.22 us  [swap(): return lax.ppermute(value, axis, [(i, i ^ bit) for i in range(size)])]
    dynamic_update_slice x19 -> x1, local copies, waits for them, and re-layouts: 20.9 us -> 0.07 us  [on_device(): lax.dynamic_update_slice_in_dim(jnp.zeros((4, width), wide), feed_vectors...]
    dot_general x7 -> x1, matrix products: 18.9 us -> 2.2 us  [left_product(): lax.dot_general(left_side, right_side, (((0,), (0,)), ((), ())), preferre...]
    pallas_call x1, Pallas kernels: 103 us -> 115 us  [total(): pl.pallas_call(functools.partial(total_kernel, group_size, widths), in_sp...]
    unnamed x148 -> x43, local copies, waits for them, and re-layouts: 19.6 us -> 9.98 us
    dynamic_update_slice x5 -> x0, other arithmetic: 8.6 us -> none  [in_order(): whole = lax.dynamic_update_slice_in_dim(whole, shard, (me ^ j) * size, axis)]
  transfers between devices with their start and end apart: 39 -> 5, of which waited for: 13 -> 2; matrix products, arithmetic and copies ran while one was open for 27% -> 12% of each run, Pallas kernels for 48% -> 62%
where the time goes in v4:
time: 519 us; the launch traced here: 515 us
  Pallas kernels  390 us (75%)
  other arithmetic  32.9 us (6%)
  local copies, waits for them, and re-layouts  29.7 us (6%)
  matrix products  24.5 us (5%)
  waiting for transfers between devices  19.7 us (4%)
  between operations  16.7 us (3%)
    pallas_call x1, Pallas kernels, total(): pl.pallas_call(functools.partial(total_kernel, group_size, widths), in_sp...  115 us
    pallas_call x1, Pallas kernels, prepare(): pl.pallas_call(functools.partial(prepare_kernel, group_size, head_dim), i...  71.2 us
    pallas_call x1, Pallas kernels, feed(): pl.pallas_call(feed_kernel, in_specs=[pl.BlockSpec(memory_space=pltpu.SME...  65.9 us
    pallas_call x1, Pallas kernels, attend_back(): pl.pallas_call(functools.partial(attend_back_kernel, head_dim), in_specs=...  64.1 us
    pallas_call x1, Pallas kernels, attend(): pl.pallas_call(functools.partial(attend_kernel, head_dim), in_specs=[pl.B...  59.8 us
    ppermute x4, waiting for transfers between devices, swap(): return lax.ppermute(value, axis, [(i, i ^ bit) for i in range(size)])  19.7 us
    dot_general x3, matrix products, right_product(): lax.dot_general(left_side, right_side, (((1,), (1,)), ((), ())), preferre...  15.8 us
    pallas_call x1, Pallas kernels, aggregate_back(): pl.pallas_call(aggregate_back_kernel, in_specs=[vmem] * 6 + [pl.BlockSpec...  13.3 us
  transfers between devices with their start and end apart: 5, of which 2 were waited for; matrix products, arithmetic and copies ran while one was open for 12% of the time, Pallas kernels for 62%

profile of v4, /device:TPU:0, one launch (start us, length us, event | category | flops | bytes accessed | tf_op | source)
XLA Modules:
  0.0 515.4 jit_solution(12562277823763642474)
XLA Ops:
  8.7 1.6 copy.71
  11.7 0.9 copy.56
  12.7 0.8 fusion.31
  13.4 2.3 broadcast_select_fusion.refs_10_.refs_4_
  15.8 0.8 fusion.9.refs_5_.select_ref
  18.6 71.2 %prepare.1 = (f32[8,128]{1,0:T(8,128)}, bf16[4,64,1024]{2,1,0:T(8,128)(2,1)}, f32[8,1024]{1,0:T(8,128)}, bf16[16,1024]{1,0:T(8,128)(2,1)}, bf16[1024,1024]{1,0:T...) custom-call(f32[8,128]{1,0:T(8,128)} %broadcast_in_dim.75.refs_0_, ...), custom_call_target="tpu_custom_call" | custom-call | flops 1073741824 | bytes 100000000 | tf_op jit(solution)/shard_map/prepare/pallas_call | solution.py:415
  89.8 2.0 fusion.34
  92.4 59.8 %attend.1 = (bf16[8,512,128]{2,1,0:T(8,128)(2,1)}, bf16[4,8,2,512,128]{4,3,2,1,0:T(8,128)(2,1)}, bf16[8,512,128]{2,1,0:T(8,128)(2,1)}, f32[8,512,128]{2,1,0:T(8,128)}) custom-call(s32[4]{0:T(128)} %subtract_clamp_fusion.valid_ref, bf16[512,1024]{1,0:T(8,128)(2,1)} %get-tuple-element.56.rows_ref, bf16[1024,3072]{1,0:T(8,128)(2,1)} %get-tuple-element.57.weight_ref), custom_call_target="tpu_custom_call" | custom-call | flops 17179869184 | bytes 100000000 | tf_op jit(solution)/shard_map/attend/pallas_call | solution.py:684
  152.3 1.5 copy.59
  153.8 1.5 copy.60.refs_1_
  155.3 1.2 slice.79
  157.8 65.9 %feed.1 = (f32[512,1024]{1,0:T(8,128)}, bf16[4,512,1024]{2,1,0:T(8,128)(2,1)}, bf16[1024,1024]{1,0:T(8,128)(2,1)}, bf16[1024,1024]{1,0:T(8,128)(2,1)}, f32[512,1...) custom-call(f32[1]{0:T(128)} %bitcast.10.refs_0_.share_ref, ...), custom_call_target="tpu_custom_call" | custom-call | flops 25769803776 | bytes 100000000 | tf_op jit(solution)/shard_map/feed/pallas_call | solution.py:1044
  223.7 1.7 fusion.32
  225.5 1.5 pad_maximum_fusion
  227.7 2.3 copy.62
  230.6 64.1 %attend_back.1.refs_1_ = bf16[512,3072]{1,0:T(8,128)(2,1)} custom-call(s32[4]{0:T(128)} %subtract_clamp_fusion.valid_ref, bf16[8,512,128]{2,1,0:T(8,128)(2,1)} %get-tuple-element.69.q_ref, bf16[4,8,2,512,128]{4,3,2,1,0:T(8,128)(2,1)} %get-tuple-element.70.kv_ref, bf16[8,512,128]{2,1,0:T(8,128)(2,1)} %get-tuple-element.71.grad_ref, ...), custom_call_target="tpu_custom_call" | custom-call | flops 42949672960 | bytes 100000000 | tf_op jit(solution)/shard_map/attend_back/pallas_call | solution.py:838
  294.7 9.0 %multiply_reduce_fusion = (f32[1024]{0:T(1024)S(1)}, f32[512]{0:T(512)S(1)}, f32[512]{0:T(512)S(1)}, f32[1024]{0:T(1024)S(1)}, f32[512,1024]{1,0:T(8,128)}) fusion(f32[512,1024]{1,0:T(8,128)S(1)} %copy-done.2, f32[512]{0:T(512)S(1)} %add_rsqrt_fusion, f32[512]{0:T(512)S(1)} %broadcast_multiply_fusion.3, f32[1024]{0:T(1024)S(1)} %copy-done.14, ...), kind=kOutput, calls=%fused_computation.5 | convolution fusion | flops 3225940992 | bytes 13651968 | tf_op jit(solution)/shard_map/dot_general | solution.py:35
  303.8 4.0 convert_reduce_fusion
  308.5 4.3 convolution_convert_fusion.heads_ref
  312.8 13.3 %aggregate_back.1 = (bf16[256,1024]{1,0:T(8,128)(2,1)}, f32[256,16]{1,0:T(8,128)}, f32[4,48,512]{2,1,0:T(8,128)}) custom-call(bf16[4,48,512]{2,1,0:T(8,128)(2,1)} %bitcast.88, f32[256,16]{1,0:T(8,128)} %get-tuple-element.65.coeff_ref, f32[48,1]{1,0:T(8,128)} %copy.58.refs_12_.mask_ref, bf16[1024,256]{1,0:T(8,128)(2,1)} %get-tuple-element.66.table_ref, ...), custom_call_target="tpu_custom_call" | custom-call | flops 2147483648 | bytes 4194304 | tf_op jit(solution)/shard_map/aggregate_back/pallas_call | solution.py:526
  326.1 0.9 convert_bitcast_fusion
  327.2 1.1 pad_maximum_fusion.1
  328.3 1.1 reshape_reshape.6.refs_6_
  329.4 115.3 %total.1 = (f32[256,3072]{1,0:T(8,128)}, f32[256,1024]{1,0:T(8,128)}, f32[256,1024]{1,0:T(8,128)}, f32[1024,256]{1,0:T(8,128)}) custom-call(f32[1]{0:T(128)} %bitcast.10.refs_0_.share_ref, bf16[1024,512]{1,0:T(8,128)(2,1)} %bitcast.85, bf16[512,3072]{1,0:T(8,128)(2,1)} %attend_back.1.refs_1_, bf16[1024,512]{1,0:T(8,128)(2,1)} %get-tuple-element.74.refs_2_, ...), custom_call_target="tpu_custom_call" | custom-call | flops 5368709120 | bytes 200000000 | tf_op jit(solution)/shard_map/total/pallas_call | solution.py:1282
  444.7 1.6 reshape.166
  446.3 1.3 reshape_reshape.7
  448.8 2.5 convolution_add_fusion
  451.3 1.0 fusion.11
  453.1 0.9 slice.110
  455.0 1.3 copy.67
  456.3 0.8 copy.66
  457.2 1.0 copy.65
  459.4 1.2 fusion.5
  460.7 2.2 fusion.6
  462.9 2.9 fusion.3
  465.8 2.0 collective-permute-start.1
  467.8 7.7 %collective-permute-done.3 = bf16[256,1024]{1,0:T(8,128)(2,1)S(1)} collective-permute-done((bf16[256,1024]{1,0:T(8,128)(2,1)S(1)}, bf16[256,1024]{1,0:T(8,128)(2,1)S(1)}, u32[]{:S(2)}, u32[]{:S(2)}) %collective-permute-start.3) | collective-permute-done | bytes 524320 | tf_op jit(solution)/shard_map/ppermute | solution.py:21
  475.6 1.3 convert_add_fusion
  477.2 1.0 fusion.35
  478.3 2.1 fusion.36
  480.4 1.1 broadcast_multiply_fusion
  481.5 11.9 %collective-permute-done.1 = bf16[512,1024]{1,0:T(8,128)(2,1)} collective-permute-done((bf16[512,1024]{1,0:T(8,128)(2,1)}, bf16[512,1024]{1,0:T(8,128)(2,1)}, u32[]{:S(2)}, u32[]{:S(2)}) %collective-permute-start.1) | collective-permute-done | bytes 1048608 | tf_op jit(solution)/shard_map/ppermute | solution.py:21
  493.5 3.6 fusion.2
  497.1 4.2 convert_element_type.116
  501.3 2.6 convert_element_type.117
  503.9 1.0 copy.80
  505.4 1.7 copy.81
  507.4 1.0 copy.82
  (93 shorter events, 12.7 us)
Async XLA Ops:
  7.2 1.4 copy-start
  7.2 9.5 %copy-start.13 = (bf16[12,1024]{1,0:T(8,128)(2,1)S(1)}, bf16[12,1024]{1,0:T(8,128)(2,1)}, u32[]{:S(2)}) copy-start(bf16[12,1024]{1,0:T(8,128)(2,1)} %param.31) | copy-start | bytes 73732
  7.2 489.9 %all-reduce.5.cloned.1.call-start = ((), (), s32[]{:S(2)}) async-start(), calls=%async_computation | async-start | bytes 8388608 | tf_op jit(solution)/shard_map/psum | solution.py:1440
  18.6 71.2 %copy-start.8 = (bf16[256,1024]{1,0:T(8,128)(2,1)S(1)}, bf16[256,1024]{1,0:T(8,128)(2,1)}, u32[]{:S(2)}) copy-start(bf16[256,1024]{1,0:T(8,128)(2,1)} %refs_3_.1) | copy-start | bytes 1572868
  91.8 367.6 %collective-permute-start.2 = (bf16[256,1024]{1,0:T(8,128)(2,1)}, bf16[256,1024]{1,0:T(8,128)(2,1)}, u32[]{:S(2)}, u32[]{:S(2)}) collective-permute-start(bf16[256,1024]{1,0:T(8,128)(2,1)} %get-tuple-element.151), channel_id=1, source_target_pairs={{0,1},{1,0},{2,3},{3,2},{4,5},{5,4},{6,7},{7,6},{8,9},{9,8},{10,11... | collective-permute-start | bytes 1572872 | tf_op jit(solution)/shard_map/ppermute | solution.py:21
  152.3 4.9 copy-start.17
  153.8 70.0 %copy-start.3 = (bf16[512,8,128]{0,2,1:T(8,128)(2,1)}, bf16[512,8,128]{0,2,1:T(8,128)(2,1)S(1)}, u32[]{:S(2)}) copy-start(bf16[512,8,128]{0,2,1:T(8,128)(2,1)S(1)} %copy.59) | copy-start | bytes 3145732
  227.0 236.0 %collective-permute-start = (bf16[2,512,1024]{2,1,0:T(8,128)(2,1)}, bf16[2,512,1024]{2,1,0:T(8,128)(2,1)}, u32[]{:S(2)}, u32[]{:S(2)}) collective-permute-start(bf16[2,512,1024]{2,1,0:T(8,128)(2,1)} %pad_maximum_fusion), channel_id=1, source_target_pairs={{0,1},{1,0},{2,3},{3,2},{4,5},{5,4},{6,7},{7,6},{8,9},{9,8},{10,11... | collective-permute-start | bytes 6291464 | tf_op jit(solution)/shard_map/ppermute | solution.py:21
  227.0 0.8 copy-start.15
  227.0 3.0 copy-start.2
  230.6 64.1 %copy-start.14 = (f32[1024]{0:T(1024)S(1)}, f32[1024]{0:T(1024)}, u32[]{:S(2)}) copy-start(f32[1024]{0:T(1024)} %param.38) | copy-start | bytes 12292
  444.7 1.6 copy-start.4
  444.7 3.7 copy-start.12
  454.8 2.4 copy-start.11
  460.6 14.9 %collective-permute-start.3 = (bf16[256,1024]{1,0:T(8,128)(2,1)S(1)}, bf16[256,1024]{1,0:T(8,128)(2,1)S(1)}, u32[]{:S(2)}, u32[]{:S(2)}) collective-permute-start(bf16[256,1024]{1,0:T(8,128)(2,1)S(1)} %fusion.5), channel_id=1, source_target_pairs={{0,2},{1,3},{2,0},{3,1},{4,6},{5,7},{6,4},{7,5},{8,10},{9,11},{10,... | collective-permute-start | bytes 1572872 | tf_op jit(solution)/shard_map/ppermute | solution.py:21
  465.8 27.6 %collective-permute-start.1 = (bf16[512,1024]{1,0:T(8,128)(2,1)}, bf16[512,1024]{1,0:T(8,128)(2,1)}, u32[]{:S(2)}, u32[]{:S(2)}) collective-permute-start(bf16[512,1024]{1,0:T(8,128)(2,1)} %fusion.3), channel_id=1, source_target_pairs={{0,2},{1,3},{2,0},{3,1},{4,6},{5,7},{6,4},{7,5},{8,10},{9,11},{10,... | collective-permute-start | bytes 3145736 | tf_op jit(solution)/shard_map/ppermute | solution.py:21
  476.8 16.7 %copy-start.16 = (f32[1024]{0:T(1024)S(1)}, f32[1024]{0:T(1024)}, u32[]{:S(2)}) copy-start(f32[1024]{0:T(1024)} %param.48) | copy-start | bytes 12292
  477.2 16.3 %copy-start.7 = (f32[512,1024]{1,0:T(8,128)S(1)}, f32[512,1024]{1,0:T(8,128)}, u32[]{:S(2)}) copy-start(f32[512,1024]{1,0:T(8,128)} %get-tuple-element.63) | copy-start | bytes 6291460
  497.1 4.2 copy-start.6
  501.3 2.6 copy-start.10
  501.3 4.1 copy-start.5
  505.4 2.0 copy-start.9
  505.4 2.9 copy-start.1
Sparse Core Ops, SparseCore 0:
  227.1 174.4 all-reduce.4

commit v5 on v4

--- a/solution.py
+++ b/solution.py
@@ -275,19 +275,16 @@
     query_part[...] = jnp.dot(own_query[...], query_w[...], preferred_element_type=wide)[:8]
     for kind in range(3):
         query_copy(kind).start()
+    weight_copy(0, 1).start()
     for n in late:
         weight_copy(n, 1).start()
     table_copy(1).start()
     table_copy(0).start()
+    weight_copy(0, 0).start()
     counts[0] = count_ref[...]
     count_copy(0).start()
-    weight_copy(0, 0).start()
-    weight_copy(1, 0).start()
     tables[me] = own_table[...]
     whole_value[span(me * block, block), :] = own_value[...]
-    whole_agg[span(me * block, block), :] = own_agg[...]
-    whole_qkv[span(me * block, block), :] = own_qkv[...]
-    whole_proj[span(me * block, block), :] = own_proj[...]
     for kind in range(3):
         query_copy(kind).wait()
     query = query_part[...] + query_got[0] + query_got[1] + query_got[2]
@@ -301,20 +298,23 @@
     keys_out[:, pl.ds(pl.multiple_of(me * block, 128), block)] = own_keys.astype(low)
     for kind in range(3):
         key_copy(kind).start()
-    weight_copy(0, 1).start()
     weight_copy(1, 1).start()
-    for p in range(grad_parts):
-        grad_far(p).start()
-    for n in late:
-        weight_copy(n, 0).start()
-    grad_near().start()
+    whole_agg[span(me * block, block), :] = own_agg[...]
+    whole_qkv[span(me * block, block), :] = own_qkv[...]
+    whole_proj[span(me * block, block), :] = own_proj[...]
+    forward(0, 1)
     for n in late:
         forward(n, 1)
+    forward(0, 4)
+    forward(2, 2)
+    forward(3, 2)
     table_copy(0).wait()
     table_copy(1).wait()
     table_copy(2).start()
-    for n in late:
-        forward(n, 2)
+    for p in range(grad_parts):
+        grad_far(p).start()
+    forward(1, 1)
+    weight_copy(1, 0).start()
     table_copy(2).wait()
     stacked = tables[...].reshape(select_ref.shape[1], width)
     table = jnp.dot(select_ref[...], stacked, preferred_element_type=wide).astype(low)
@@ -323,17 +323,11 @@
     coeff_out[...] = lax.dot_general(
         table, keys_out[...], (((1,), (1,)), ((), ())), preferred_element_type=wide
     )
-    forward(0, 1)
-    forward(2, 3)
-    forward(1, 1)
-    forward(0, 4)
-    forward(2, 4)
     weight_copy(0, 0).wait()
     weight_copy(0, 5).wait()
     out_copy(0).start()
     values = jnp.dot(table, whole_value[...], preferred_element_type=wide)
     table_out[...] = jnp.transpose(values).astype(low)
-    forward(3, 3)
 
     def one_head(h, carry):
         weights = slot_softmax(patch_ref, head_columns(coeff_out, h, slots), mask_ref)
@@ -345,13 +339,16 @@
         return carry
 
     half = heads // 2
+    forward(2, 3)
+    forward(4, 2)
+    for n in late:
+        weight_copy(n, 0).start()
     lax.fori_loop(0, half, one_head, 0)
     forward(1, 4)
-    count_step(0)
+    forward(3, 3)
+    forward(5, 2)
+    grad_near().start()
     lax.fori_loop(half, heads, one_head, 0)
-    keep(2)
-    forward(4, 3)
-    forward(3, 4)
     keep(1)
     embedded = (
         lax.dot_general(
@@ -360,27 +357,32 @@
         + bias_ref[...]
     )
     embed_out[...] = embedded
-    count_step(1)
+    count_step(0)
+    forward(2, 4)
     grad_far(0).wait()
     grad_last(0).start()
     xhat, inverse = normalise(embedded)
     norm_out[...] = (xhat * gain_ref[...] + shift_ref[...]).astype(low)
-    forward(5, 3)
-    forward(4, 4)
-    keep(3)
+    forward(4, 3)
+    keep(2)
+    forward(3, 4)
+    count_step(1)
     grad_far(1).wait()
     grad_last(1).start()
-    keep(4)
+    forward(5, 3)
+    keep(3)
+    forward(4, 4)
     for n in range(2, len(bits)):
         count_step(n)
-    forward(5, 4)
     grad_far(2).wait()
     grad_last(2).start()
-    keep(5)
+    keep(4)
+    forward(5, 4)
     grad_near().wait()
     grad_out(0).start()
     grad_far(3).wait()
     grad_last(3).start()
+    keep(5)
     for p in range(grad_parts):
         grad_last(p).wait()
     grad_out(1).start()
@@ -461,98 +463,13 @@
     )
 
 
-def aggregate_back_kernel(
-    patch_ref, coeff_ref, mask_ref, table_ref, select_ref, heads_ref, scale_ref,
-    sum_ref, coeff_sum_ref, patch_grad_ref, table_s, coeff_s,
-):
-    slots = mask_ref.shape[0]
-    head_dim = table_ref.shape[0] // HEADS
-    size = table_ref.shape[1]
-    wide = jnp.float32
-    low = jnp.bfloat16
-    patch_grad_ref[...] = jnp.zeros_like(patch_grad_ref)
-    coeff_s[...] = jnp.zeros_like(coeff_s)
-    lane = lax.broadcasted_iota(jnp.int32, (slots, HEADS), 1)
-
-    def one_head(h, carry):
-        columns = head_columns(coeff_ref, h, slots)
-        weights = slot_softmax(patch_ref, columns, mask_ref)
-        mixed = mixed_of(patch_ref, weights, size)
-        at = pl.ds(pl.multiple_of(h * head_dim, 16), head_dim)
-        heads_grad = heads_ref[at, :]
-        table_s[at, :] = (
-            lax.dot_general(
-                heads_grad, mixed, (((1,), (1,)), ((), ())), preferred_element_type=wide
-            )
-            * scale_ref[0]
-        ).astype(low)
-        mixed_grad = lax.dot_general(
-            table_ref[at, :], heads_grad, (((0,), (0,)), ((), ())), preferred_element_type=wide
-        )
-        parts = [mixed_grad[k * slots : (k + 1) * slots] for k in range(PIX + 1)]
-        values = [patch_ref[k].astype(wide) for k in range(PIX)]
-        weights_grad = parts[PIX]
-        for k in range(PIX):
-            weights_grad = weights_grad + parts[k] * values[k]
-        mean_grad = jnp.sum(weights * weights_grad, axis=0, keepdims=True)
-        scores_grad = weights * (weights_grad - mean_grad)
-        for k in range(PIX + 1):
-            value = scores_grad * values[k] if k < PIX else scores_grad
-            column = jnp.sum(value, axis=1, keepdims=True)
-            rows = slice(k * slots, (k + 1) * slots)
-            coeff_s[rows, :] = coeff_s[rows, :] + jnp.where(lane == h, column, 0.0)
-        for k in range(PIX):
-            patch_grad_ref[k] += scale_ref[1] * (parts[k] * weights + scores_grad * columns[k])
-        return carry
-
-    lax.fori_loop(0, HEADS, one_head, 0)
-    sum_ref[...] = lax.dot_general(
-        select_ref[...], table_s[...], (((0,), (1,)), ((), ())), preferred_element_type=wide
-    ).astype(low)
-    coeff_sum_ref[...] = scale_ref[0] * lax.dot_general(
-        select_ref[...].astype(wide),
-        coeff_s[...],
-        (((0,), (0,)), ((), ())),
-        preferred_element_type=wide,
-        precision=exact_mode,
-    )
-
-
-def aggregate_back(patch_rows, coeffs, slot_mask, table_values, select, heads_grad, scales):
-    rows = patch_rows.shape[2]
-    width, size = table_values.shape
-    slots = slot_mask.shape[0]
-    vmem = pl.BlockSpec(memory_space=pltpu.VMEM)
-    return pl.pallas_call(
-        aggregate_back_kernel,
-        in_specs=[vmem] * 6 + [pl.BlockSpec(memory_space=pltpu.SMEM)],
-        out_specs=[vmem] * 3,
-        out_shape=[
-            jax.ShapeDtypeStruct((select.shape[1], width), jnp.bfloat16),
-            jax.ShapeDtypeStruct((select.shape[1], HEADS), jnp.float32),
-            jax.ShapeDtypeStruct((PIX, slots, rows), jnp.float32),
-        ],
-        scratch_shapes=[
-            pltpu.VMEM((width, size), jnp.bfloat16),
-            pltpu.VMEM((size, HEADS), jnp.float32),
-        ],
-        compiler_params=pltpu.CompilerParams(vmem_limit_bytes=VMEM_LIMIT),
-        cost_estimate=pl.CostEstimate(
-            flops=16 * size * rows * width,
-            bytes_accessed=8 * width * rows,
-            transcendentals=HEADS * slots * rows,
-        ),
-        name="aggregate_back",
-    )(patch_rows, coeffs, slot_mask, table_values, select, heads_grad, scales)
-
-
 def lane_half(rows, pair, head_dim):
     lane = lax.broadcasted_iota(jnp.int32, (rows, 2 * head_dim), 1)
     return (lane // head_dim) == pair
 
 
 def attend_kernel(
-    head_dim, valid_ref, rows_ref, weight_ref, q_ref, kv_ref, out_ref, log_ref, sum_s, top_s, total_s, send_sem, recv_sem
+    head_dim, valid_ref, rows_ref, weight_ref, q_ref, kv_out, out_ref, log_ref, kv_ref, weight_s, sum_s, top_s, total_s, send_sem, recv_sem, fetch_sem, keep_sem
 ):
     me = lax.axis_index("fsdp")
     near = {"fsdp": flip(me, 1)[0]}
@@ -563,6 +480,22 @@
     lanes = 2 * head_dim
     pairs = width // lanes
     scale = head_dim ** (-0.5)
+    groups = pairs // 2
+
+    def fetch(part, g):
+        at = pl.ds(part * width + g * 2 * lanes, 2 * lanes)
+        return pltpu.make_async_copy(
+            weight_ref.at[:, at], weight_s.at[:, at], fetch_sem.at[part, g]
+        )
+
+    def keep(i):
+        return pltpu.make_async_copy(kv_ref.at[:, i], kv_out.at[:, i], keep_sem.at[i])
+
+    for g in range(groups):
+        fetch(1, g).start()
+        fetch(2, g).start()
+    for g in range(groups):
+        fetch(0, g).start()
     meet([near, far])
 
     def copy(kind, i, source, target, device):
@@ -585,21 +518,23 @@
         return copy(2, i, 2, 3, near)
 
     entry = rows_ref[...]
-    for g in range(pairs // 2):
+    for g in range(groups):
         for part in range(2):
             start = (part + 1) * width + g * 2 * lanes
+            fetch(part + 1, g).wait()
             value = jnp.dot(
-                entry, weight_ref[:, start : start + 2 * lanes], preferred_element_type=wide
+                entry, weight_s[:, start : start + 2 * lanes], preferred_element_type=wide
             ).astype(low)
             kv_ref[0, 2 * g, part] = value[:, :lanes]
             kv_ref[0, 2 * g + 1, part] = value[:, lanes:]
         for i in (2 * g, 2 * g + 1):
             far_copy(i).start()
             near_copy(i).start()
-    for g in range(pairs // 2):
+    for g in range(groups):
         start = g * 2 * lanes
+        fetch(0, g).wait()
         value = jnp.dot(
-            entry, weight_ref[:, start : start + 2 * lanes], preferred_element_type=wide
+            entry, weight_s[:, start : start + 2 * lanes], preferred_element_type=wide
         ).astype(low)
         value = value * jnp.asarray(scale, low)
         q_ref[2 * g] = value[:, :lanes]
@@ -658,6 +593,7 @@
         attend(i, (2,), False)
         last_copy(i).wait_recv()
         attend(i, (3,), False)
+        keep(i).start()
         out_ref[i] = (sum_s[...] / total_s[...]).astype(low)
         log_ref[i] = top_s[...] + jnp.log(total_s[...])
         return carry
@@ -668,6 +604,7 @@
         near_copy(i).wait_send()
         far_copy(i).wait_send()
         last_copy(i).wait_send()
+        keep(i).wait()
         return carry
 
     lax.fori_loop(0, pairs, end, 0)
@@ -679,12 +616,13 @@
     lanes = 2 * head_dim
     pairs = HEADS // 2
     whole = pl.BlockSpec(memory_space=pltpu.VMEM)
+    hbm = pl.BlockSpec(memory_space=pl.ANY)
     low = jnp.bfloat16
     wide = jnp.float32
     return pl.pallas_call(
         functools.partial(attend_kernel, head_dim),
-        in_specs=[pl.BlockSpec(memory_space=pltpu.SMEM), whole, whole],
-        out_specs=[whole] * 4,
+        in_specs=[pl.BlockSpec(memory_space=pltpu.SMEM), whole, hbm],
+        out_specs=[whole, hbm, whole, whole],
         out_shape=[
             jax.ShapeDtypeStruct((pairs, rows, lanes), low),
             jax.ShapeDtypeStruct((4, pairs, 2, rows, lanes), low),
@@ -692,11 +630,15 @@
             jax.ShapeDtypeStruct((pairs, rows, lanes), wide),
         ],
         scratch_shapes=[
+            pltpu.VMEM((4, pairs, 2, rows, lanes), low),
+            pltpu.VMEM(weight.shape, low),
             pltpu.VMEM((rows, lanes), wide),
             pltpu.VMEM((rows, lanes), wide),
             pltpu.VMEM((rows, lanes), wide),
             pltpu.SemaphoreType.DMA((3, pairs)),
             pltpu.SemaphoreType.DMA((3, pairs)),
+            pltpu.SemaphoreType.DMA((3, pairs // 2)),
+            pltpu.SemaphoreType.DMA((pairs,)),
         ],
         compiler_params=pltpu.CompilerParams(
             collective_id=1, has_side_effects=True, vmem_limit_bytes=VMEM_LIMIT
@@ -709,16 +651,24 @@
 
 
 def attend_back_kernel(
-    head_dim, valid_ref, q_ref, kv_ref, grad_ref, out_ref, log_ref, *refs
+    head_dim, valid_ref, q_ref, kv_in, grad_ref, out_ref, log_ref, *refs
 ):
     result_ref, q_sum, own_s, far_s, last_s, near_s, got_far, got_last, got_near, log_rows, dot_rows = refs[:11]
-    send_sem, recv_sem = refs[11:]
+    send_sem, recv_sem, kv_ref, fetch_sem = refs[11:]
     me = lax.axis_index("fsdp")
     near = {"fsdp": flip(me, 1)[0]}
     far = {"fsdp": flip(me, 2)[0]}
     wide = jnp.float32
     low = jnp.bfloat16
     pairs, rows, lanes = q_ref.shape
+
+    def fetch(half, i):
+        at = pl.ds(2 * half, 2)
+        return pltpu.make_async_copy(kv_in.at[at, i], kv_ref.at[at, i], fetch_sem.at[half, i])
+
+    for half in (1, 0):
+        for i in range(pairs):
+            fetch(half, i).start()
     width = pairs * lanes
     scale = head_dim ** (-0.5)
     meet([near, far])
@@ -799,6 +749,7 @@
             here = slice(pair * head_dim, (pair + 1) * head_dim)
             log_rows[i, pair : pair + 1, :] = log_t[pair * head_dim : pair * head_dim + 1, :]
             dot_rows[i, pair : pair + 1, :] = jnp.sum(dots[here, :], axis=0, keepdims=True)
+        fetch(1, i).wait()
         q_sum[i] = back(i, (3, 2), (last_s, far_s))
         last_copy(i).start()
 
@@ -812,6 +763,7 @@
     send_far(pairs - 1)
 
     def second_loop(i, carry):
+        fetch(0, i).wait()
         q_sum[i] = (q_sum[i] + back(i, (1, 0), (near_s, own_s))) * scale
         near_copy(i).start()
         return carry
@@ -837,7 +789,14 @@
     slab = (pairs, 2, rows, lanes)
     return pl.pallas_call(
         functools.partial(attend_back_kernel, head_dim),
-        in_specs=[pl.BlockSpec(memory_space=pltpu.SMEM)] + [whole] * 5,
+        in_specs=[
+            pl.BlockSpec(memory_space=pltpu.SMEM),
+            whole,
+            pl.BlockSpec(memory_space=pl.ANY),
+            whole,
+            whole,
+            whole,
+        ],
         out_specs=whole,
         out_shape=jax.ShapeDtypeStruct((rows, 3 * pairs * lanes), low),
         scratch_shapes=[
@@ -853,6 +812,8 @@
             pltpu.VMEM((pairs, 8, rows), wide),
             pltpu.SemaphoreType.DMA((3, pairs)),
             pltpu.SemaphoreType.DMA((3, pairs)),
+            pltpu.VMEM(key_values.shape, low),
+            pltpu.SemaphoreType.DMA((2, pairs)),
         ],
         compiler_params=pltpu.CompilerParams(
             collective_id=2, has_side_effects=True, vmem_limit_bytes=VMEM_LIMIT
@@ -866,14 +827,15 @@
 
 def feed_kernel(*refs):
     (
-        share_ref, context_ref, proj_ref, embed_ref, own_grad, near_grad, far_grads, up_ref,
-        down_ref, bias_ref, proj_bias, gain_ref, shift_ref,
+        share_ref, context_ref, proj_ref, embed_ref, own_in, near_in, far_in, up_in,
+        down_in, bias_ref, proj_bias, gain_ref, shift_ref,
     ) = refs[:13]
     (
-        middle_ref, out_ref, down_total, up_total, middle_grad, attended, context_grad, vectors,
+        middle_out, out_out, down_out, up_out, middle_grad, attended, context_grad, vectors,
     ) = refs[13:21]
     entry, gelu_s, pre_s, own_back, near_s, last_s, far_s, got_near, got_last, got_far = refs[21:31]
-    send_sem, recv_sem = refs[31:]
+    grad_s, up_ref, down_ref, middle_ref, out_ref, down_total, up_total = refs[31:38]
+    send_sem, recv_sem, fetch_sem, keep_sem = refs[38:]
     wide = jnp.float32
     low = jnp.bfloat16
     me = lax.axis_index("fsdp")
@@ -883,10 +845,33 @@
     hidden = up_ref.shape[1]
     tile = rows // 2
     pairs, _, lanes = context_grad.shape
+    fetches = [
+        pltpu.make_async_copy(up_in, up_ref, fetch_sem.at[0]),
+        pltpu.make_async_copy(own_in, grad_s.at[0], fetch_sem.at[1]),
+        pltpu.make_async_copy(down_in, down_ref, fetch_sem.at[2]),
+        pltpu.make_async_copy(near_in, grad_s.at[1], fetch_sem.at[3]),
+        pltpu.make_async_copy(far_in, grad_s.at[pl.ds(2, 2)], fetch_sem.at[4]),
+    ]
+    for fetch in fetches:
+        fetch.start()
     meet([near, far])
 
     def span(t):
         return pl.ds(t * tile, tile)
+
+    def keep_middle(t):
+        return pltpu.make_async_copy(
+            middle_ref.at[span(t), :], middle_out.at[span(t), :], keep_sem.at[0, t]
+        )
+
+    def keep_out(s, t):
+        return pltpu.make_async_copy(
+            out_ref.at[s, span(t), :], out_out.at[s, span(t), :], keep_sem.at[1 + s, t]
+        )
+
+    def keep_total(n):
+        source, target = ((down_total, down_out), (up_total, up_out))[n]
+        return pltpu.make_async_copy(source, target, keep_sem.at[5, n])
 
     def copy(kind, t, src, dst, device):
         return pltpu.make_async_remote_copy(
@@ -916,13 +901,6 @@
     def back_far(t):
         return copy(5, t, far_s, got_far, far)
 
-    def grad_rows(s, t):
-        if s == 0:
-            return own_grad[span(t), :]
-        if s == 1:
-            return near_grad[span(t), :]
-        return far_grads[s - 2, span(t), :]
-
     def feed(s, t, target):
         rows_in = entry[s, span(t), :]
         pre_act = jnp.dot(rows_in, up_ref[...], preferred_element_type=wide) + bias_ref[...]
@@ -931,7 +909,10 @@
         gelu = (pre_act * cdf).astype(low)
         gelu_s[s, span(t), :] = gelu
         act_grad = lax.dot_general(
-            grad_rows(s, t), down_ref[...], (((1,), (1,)), ((), ())), preferred_element_type=wide
+            grad_s[s, span(t), :],
+            down_ref[...],
+            (((1,), (1,)), ((), ())),
+            preferred_element_type=wide,
         )
         pre_grad = act_grad * (cdf + pre_act * density)
         pre_low = pre_grad.astype(low)
@@ -940,6 +921,7 @@
         out_ref[s, span(t), :] = jnp.dot(
             gelu, down_ref[...], preferred_element_type=wide
         ).astype(low)
+        keep_out(s, t).start()
         target[span(t), :] = lax.dot_general(
             pre_low, up_ref[...], (((1,), (1,)), ((), ())), preferred_element_type=wide
         ).astype(target.dtype)
@@ -956,8 +938,13 @@
         entry[0, span(t), :] = (xhat * gain_ref[...] + shift_ref[...]).astype(low)
         rows_far(t).start()
         rows_near(t).start()
+        keep_middle(t).start()
+    for fetch in fetches[:3]:
+        fetch.wait()
     for t in range(2):
         feed(0, t, own_back)
+    for fetch in fetches[3:]:
+        fetch.wait()
     for t in range(2):
         rows_near(t).wait()
         feed(1, t, near_s)
@@ -975,17 +962,17 @@
     add_last(1, back_last, back_far, far_s, got_last, span)
 
     block = min(hidden, 256)
-    grads = [own_grad[...], near_grad[...], far_grads[0], far_grads[1]]
     for start in range(0, hidden, block):
         value = 0.0
         for s in range(4):
             value = value + lax.dot_general(
                 gelu_s[s, :, start : start + block],
-                grads[s],
+                grad_s[s],
                 (((0,), (0,)), ((), ())),
                 preferred_element_type=wide,
             )
         down_total[start : start + block, :] = (value * share_ref[0]).astype(low)
+    keep_total(0).start()
     for start in range(0, width, block):
         value = 0.0
         for s in range(4):
@@ -996,6 +983,7 @@
                 preferred_element_type=wide,
             )
         up_total[start : start + block, :] = (value * share_ref[0]).astype(low)
+    keep_total(1).start()
 
     for t in range(2):
         back_near(t).wait()
@@ -1005,7 +993,7 @@
         xhat, inverse = normalise(middle_ref[at, :])
         vectors[0:1, :] += jnp.sum(grad * xhat, axis=0, keepdims=True)
         vectors[1:2, :] += jnp.sum(grad, axis=0, keepdims=True)
-        upstream = own_grad[at, :].astype(wide)
+        upstream = grad_s[0, at, :].astype(wide)
         vectors[3:4, :] += jnp.sum(upstream, axis=0, keepdims=True)
         value = upstream + norm_back(grad, xhat, inverse, gain_ref[...])
         middle_grad[at, :] = value
@@ -1017,6 +1005,11 @@
         ).astype(low)
         for i in range(pairs):
             context_grad[i, at, :] = back[:, i * lanes : (i + 1) * lanes]
+    for t in range(2):
+        keep_middle(t).wait()
+        keep_total(t).wait()
+        for s in range(4):
+            keep_out(s, t).wait()
 
 
 def add_last(t, back_last, back_far, far_s, got_last, span):
@@ -1036,6 +1029,7 @@
     low = jnp.bfloat16
     wide = jnp.float32
     vmem = pl.BlockSpec(memory_space=pltpu.VMEM)
+    hbm = pl.BlockSpec(memory_space=pl.ANY)
     flat = (rows, width)
 
     def shape(dims, kind):
@@ -1043,8 +1037,8 @@
 
     return pl.pallas_call(
         feed_kernel,
-        in_specs=[pl.BlockSpec(memory_space=pltpu.SMEM)] + [vmem] * 12,
-        out_specs=[vmem] * 8,
+        in_specs=[pl.BlockSpec(memory_space=pltpu.SMEM)] + [vmem] * 3 + [hbm] * 5 + [vmem] * 4,
+        out_specs=[hbm] * 4 + [vmem] * 4,
         out_shape=[
             shape(flat, wide),
             shape((4,) + flat, low),
@@ -1066,7 +1060,16 @@
             pltpu.VMEM(flat, low),
             pltpu.VMEM(flat, low),
             pltpu.VMEM(flat, low),
+            pltpu.VMEM((4,) + flat, low),
+            pltpu.VMEM(up.shape, low),
+            pltpu.VMEM(down.shape, low),
+            pltpu.VMEM(flat, wide),
+            pltpu.VMEM((4,) + flat, low),
+            pltpu.VMEM((hidden, width), low),
+            pltpu.VMEM((width, hidden), low),
             pltpu.SemaphoreType.DMA((6, 2)),
+            pltpu.SemaphoreType.DMA((6, 2)),
+            pltpu.SemaphoreType.DMA((5,)),
             pltpu.SemaphoreType.DMA((6, 2)),
         ],
         compiler_params=pltpu.CompilerParams(
@@ -1082,222 +1085,503 @@
     )
 
 
-def total_kernel(group_size, widths, share_ref, *refs):
-    pairs = [(refs[2 * i], refs[2 * i + 1]) for i in range(3)]
-    bundle_ref = refs[6]
-    outs = refs[7:10]
-    bundle_out = refs[10]
-    send1, recv1, own1, send2, recv2, hold, halves, done, full, send_sem, recv_sem = refs[11:]
-    me = lax.axis_index("fsdp")
-    group = lax.axis_index("grp")
-    core_partner, core = flip(me, 1)
-    far_partner, far = flip(me, 2)
-    quarter = own1.shape[2]
-    wide = jnp.float32
-    low = jnp.bfloat16
-
+def group_steps(group, group_size, size):
     steps = []
-    size, bit, offset = quarter, 1, 0
+    bit, offset = 1, 0
     while bit < group_size:
         partner, bit_set = flip(group, bit)
-        halving = size >= 64
+        halving = size >= 32
         steps.append((partner, bit_set, halving, size, offset))
         if halving:
             size = size // 2
             offset = offset + bit_set * size
         bit *= 2
-    halvings = [i for i, step in enumerate(steps) if step[2]]
-
-    meet([{"fsdp": core_partner}, {"fsdp": far_partner}] + [{"grp": step[0]} for step in steps])
-
-    chunks = [(None, None, None, 0, bundle_ref.shape[1])]
-    for (left, right), out in zip(pairs, outs):
-        for start in range(0, right.shape[1], widths):
-            chunks.append((left, right, out, start, widths))
-
-    def copy(stage, c, src, dst, device):
+    return steps
+
+
+def finish_kernel(group_size, widths, head_dim, *refs):
+    share_ref = refs[0]
+    left_qkv, qkv_grad, left_agg_in, left_proj_in, attended_in = refs[1:6]
+    (
+        full_qkv, full_agg_in, full_value, embed_in, middle_in, gain_ref, vectors_ref, patch_ref,
+        coeff_ref, mask_ref, table_ref, select_ref, own_columns, keys_ref, query_ref, key_w,
+        query_w, own_query, out_sum,
+    ) = refs[6:25]
+    outs = refs[25:28]
+    value_out, key_out, query_out, agg_query_out, var_out, extra_out, patch_grad = refs[28:35]
+    out_far = refs[35]
+    sets = [refs[36:46], refs[46:55]]
+    full, query_part, query_got, var_s, last_send, last_recv = refs[55:61]
+    entry_grad, embed_grad, heads_grad, table_s, coeff_s, extras, bundle = refs[61:68]
+    weight_s, weight_sem, left_agg, left_proj, attended, full_agg, embed_ref, middle_grad = refs[68:76]
+    fetch_sem = refs[76]
+    fetches = [
+        pltpu.make_async_copy(source, target, fetch_sem.at[n])
+        for n, (source, target) in enumerate(
+            [
+                (embed_in, embed_ref),
+                (middle_in, middle_grad),
+                (full_agg_in, full_agg),
+                (left_proj_in, left_proj),
+                (attended_in, attended),
+                (left_agg_in, left_agg),
+            ]
+        )
+    ]
+    me = lax.axis_index("fsdp")
+    group = lax.axis_index("grp")
+    core_partner, core = flip(me, 1)
+    far_partner, far = flip(me, 2)
+    diagonal = flip(far_partner, 1)[0]
+    wide = jnp.float32
+    low = jnp.bfloat16
+    quarters = [buffers[2].shape[2] for buffers in sets]
+    all_steps = [group_steps(group, group_size, quarter) for quarter in quarters]
+    all_halvings = [[i for i, step in enumerate(steps) if step[2]] for steps in all_steps]
+    count = len(all_steps[0])
+    slots = sets[1][0].shape[0]
+    others = [{"fsdp": core_partner}, {"fsdp": far_partner}, {"fsdp": diagonal}]
+    pltpu.make_async_copy(full_qkv.at[:, pl.ds(0, key_w.shape[1])], weight_s, weight_sem.at[0]).start()
+    for fetch in fetches:
+        fetch.start()
+    meet(others + [{"grp": step[0]} for step in all_steps[0]])
+
+    def pieces(left, right, out):
+        return [(left, right, out, start) for start in range(0, right.shape[1], widths)]
+
+    qkv_pieces = pieces(left_qkv, qkv_grad, outs[0])
+    agg_pieces = pieces(left_agg, embed_grad, outs[1])
+    proj_pieces = pieces(left_proj, attended, outs[2])
+    bulk = qkv_pieces + proj_pieces[:1] + [None] + proj_pieces[1:] + agg_pieces
+    chunks = []
+    for piece in bulk:
+        if piece is None:
+            chunks.append((0, 0, None, None, None, 0))
+        else:
+            chunks.append((1, sum(chunk[0] for chunk in chunks)) + piece)
+    small = bulk.index(None)
+
+    def remote(src, dst, send, recv, device):
         return pltpu.make_async_remote_copy(
             src_ref=src,
             dst_ref=dst,
-            send_sem=send_sem.at[stage, c],
-            recv_sem=recv_sem.at[stage, c],
+            send_sem=send,
+            recv_sem=recv,
             device_id=device,
             device_id_type=pl.DeviceIdType.MESH,
         )
 
+    def copy(stage, c, src, dst, device):
+        which, place = chunks[c][:2]
+        send_sem, recv_sem = sets[which][-2:]
+        return remote(src, dst, send_sem.at[stage, place], recv_sem.at[stage, place], device)
+
     def span(start, size):
         return pl.ds(pl.multiple_of(start, 16), size)
 
-    def columns(c):
-        return pl.ds(0, chunks[c][4])
+    def held(c):
+        which, place, left, right, out, start = chunks[c]
+        buffers = sets[which]
+        rest = [
+            buffer.at[place % slots if n in (0, 2) else place]
+            for n, buffer in enumerate(buffers[:6])
+        ]
+        rest.append([part.at[place] for part in buffers[6]])
+        rest.append(buffers[7].at[place] if out is None else out.at[:, start : start + widths])
+        return rest
 
     def core_copy(c):
-        cols = columns(c)
-        return copy(
-            0, c, send1.at[c, :, :, cols], recv1.at[c, :, :, cols], {"fsdp": core_partner}
-        )
+        at = held(c)
+        return copy(0, c, at[0], at[1], others[0])
 
     def far_copy(c):
-        cols = columns(c)
-        return copy(1, c, send2.at[c, :, cols], recv2.at[c, :, cols], {"fsdp": far_partner})
+        at = held(c)
+        return copy(1, c, at[3], at[4], others[1])
 
     def step_copy(i, c):
-        partner, bit_set, halving, size, offset = steps[i]
-        cols = columns(c)
+        partner, bit_set, halving, size, offset = all_steps[chunks[c][0]][i]
         if halving:
             size = size // 2
             offset = offset + (1 - bit_set) * size
-        src = hold.at[c, span(offset, size), cols]
-        dst = halves[i].at[c, :, cols]
-        return copy(2 + i, c, src, dst, {"grp": partner})
+        at = held(c)
+        return copy(2 + i, c, at[5].at[span(offset, size), :], at[6][i], {"grp": partner})
 
     def back_copy(i, c):
-        partner, bit_set, halving, size, offset = steps[i]
+        partner, bit_set, halving, size, offset = all_steps[chunks[c][0]][i]
         size = size // 2
         offset = offset + bit_set * size
-        at = done.at[c, span(offset, size), columns(c)]
-        return copy(2 + len(steps) + i, c, at, at, {"grp": partner})
+        at = held(c)[7].at[span(offset, size), :]
+        return copy(2 + count + i, c, at, at, {"grp": partner})
 
     def begin(c):
-        left, right, out, start, width = chunks[c]
-        cols = columns(c)
+        which, place, left, right, out, start = chunks[c]
+        quarter = quarters[which]
+        send1, recv1, own1 = held(c)[:3]
 
         def part(q):
-            rows = span(q * quarter, quarter)
             if left is None:
-                return bundle_ref[rows, :]
+                return bundle[q]
             value = jnp.dot(
-                left[rows, :], right[:, start : start + width], preferred_element_type=wide
+                left[span(q * quarter, quarter), :],
+                right[:, start : start + widths],
+                preferred_element_type=wide,
             )
             return (value * share_ref[0]).astype(low)
 
         for y in range(2):
-            send1[c, y, :, cols] = part(2 * y + 1 - core)
+            send1[y] = part(2 * y + 1 - core)
         core_copy(c).start()
         for y in range(2):
-            own1[c, y, :, cols] = part(2 * y + core)
+            own1[y] = part(2 * y + core)
 
     def after_core(c):
-        cols = columns(c)
+        send1, recv1, own1, send2 = held(c)[:4]
         core_copy(c).wait()
-        value = own1[c, 1 - far, :, cols].astype(wide) + recv1[c, 1 - far, :, cols].astype(wide)
-        send2[c, :, cols] = value.astype(low)
+        value = own1[1 - far].astype(wide) + recv1[1 - far].astype(wide)
+        send2[...] = value.astype(low)
         far_copy(c).start()
 
     def after_far(c):
-        cols = columns(c)
+        send1, recv1, own1, send2, recv2, hold = held(c)[:6]
         far_copy(c).wait()
-        value = own1[c, far, :, cols].astype(wide) + recv1[c, far, :, cols].astype(wide)
-        hold[c, :, cols] = (value + recv2[c, :, cols].astype(wide)).astype(low)
+        value = own1[far].astype(wide) + recv1[far].astype(wide) + recv2[...].astype(wide)
+        hold[...] = value.astype(low)
         step_copy(0, c).start()
 
     def after_step(i, c):
-        cols = columns(c)
         step_copy(i, c).wait()
+        hold, halves, done = held(c)[5:]
+        steps, halvings = all_steps[chunks[c][0]], all_halvings[chunks[c][0]]
         partner, bit_set, halving, size, offset = steps[i]
         if halving:
             size = size // 2
             offset = offset + bit_set * size
         at = span(offset, size)
-        value = hold[c, at, cols].astype(wide) + halves[i][c, :, cols].astype(wide)
-        if i + 1 < len(steps):
-            hold[c, at, cols] = value.astype(low)
+        value = hold[at, :].astype(wide) + halves[i][...].astype(wide)
+        if i + 1 < count:
+            hold[at, :] = value.astype(low)
             step_copy(i + 1, c).start()
         else:
-            done[c, at, cols] = value.astype(low)
+            done[at, :] = value.astype(low)
             back_copy(halvings[-1], c).start()
 
     def after_back(k, c):
+        halvings = all_halvings[chunks[c][0]]
+        if k >= len(halvings):
+            return
         back_copy(halvings[k], c).wait()
         if k > 0:
             back_copy(halvings[k - 1], c).start()
-        else:
-            left, right, out, start, width = chunks[c]
-            if out is None:
-                full[me] = done[c, :, columns(c)]
-                bundle_core().start()
-            else:
-                out[:, start : start + width] = done[c].astype(wide)
-
-    last = 2 + 2 * len(steps)
+        elif chunks[c][0] == 0:
+            full[me] = held(c)[7][...]
+            bundle_core().start()
 
     def bundle_core():
-        return copy(last, 0, full.at[me], full.at[me], {"fsdp": core_partner})
+        at = full.at[me]
+        return remote(at, at, last_send.at[0], last_recv.at[0], others[0])
 
     def bundle_far():
         at = full.at[pl.ds(me - core, 2)]
-        return copy(last, 1, at, at, {"fsdp": far_partner})
-
-    def finish_core(c):
+        return remote(at, at, last_send.at[1], last_recv.at[1], others[1])
+
+    def query_copy(kind):
+        return remote(
+            query_part,
+            query_got.at[kind],
+            last_send.at[2 + kind],
+            last_recv.at[2 + kind],
+            others[kind],
+        )
+
+    size = own_columns.shape[0]
+    width = key_w.shape[1]
+    part_rows = quarters[0]
+    spare = extra_out.shape[0] // 4
+    per_row = width // size
+    scale = head_dim ** (-0.5)
+
+    def coefficients():
+        rows = []
+        for n in range(HEADS):
+            place, column = n // per_row, (n % per_row) * size
+            shard, row = place // spare, part_rows - spare + place % spare
+            rows.append(full[shard, row : row + 1, column : column + size].astype(wide))
+        return jnp.concatenate(rows, axis=0)
+
+    def own_head(value):
+        lane = lax.broadcasted_iota(jnp.int32, (HEADS, width), 1)
+        head = lax.broadcasted_iota(jnp.int32, (HEADS, width), 0)
+        return jnp.where(lane // head_dim == head, value, 0.0)
+
+    def key_grad(coeffs):
+        return jnp.dot(coeffs.astype(low), own_columns[...], preferred_element_type=wide)
+
+    def finish_core():
         bundle_core().wait()
         bundle_far().start()
 
-    def finish_far(c):
+    def finish_far():
         bundle_far().wait()
+        spread = jnp.dot(
+            key_grad(coefficients()).astype(low), key_w[...], preferred_element_type=wide
+        )
+        partial = jnp.sum(own_head(spread), axis=0, keepdims=True) * scale
+        query_part[...] = jnp.broadcast_to(partial, query_part.shape)
+        for kind in range(3):
+            query_copy(kind).start()
+
+    def finish_table():
+        weights(3).wait()
+        table = full[...].reshape(size, width)
+        value_out[...] = lax.dot_general(
+            own_columns[...], table, (((0,), (0,)), ((), ())), preferred_element_type=wide
+        )
+        coeffs = coefficients()
+        var_s[...] = lax.dot_general(
+            coeffs.astype(low), keys_ref[...], (((0,), (0,)), ((), ())), preferred_element_type=wide
+        )
+        var_out[...] = var_s[span(me * part_rows, part_rows), :] + lax.dot_general(
+            full[me], weight_s[...], (((1,), (1,)), ((), ())), preferred_element_type=wide
+        )
         for q in range(4):
-            bundle_out[q * quarter : (q + 1) * quarter, :] = full[q].astype(wide)
-
+            extra_out[q * spare : (q + 1) * spare, :] = full[q, part_rows - spare :, :].astype(wide)
+
+    def finish_query():
+        for kind in range(3):
+            query_copy(kind).wait()
+        grad = query_part[...] + query_got[0] + query_got[1] + query_got[2]
+        query_out[...] = own_query[...] * grad[:1]
+        agg_query_out[...] = lax.dot_general(
+            grad,
+            query_w[...].astype(wide),
+            (((1,), (1,)), ((), ())),
+            preferred_element_type=wide,
+            precision=exact_mode,
+        )
+        spread = own_head(jnp.broadcast_to(query_ref[:1].astype(low).astype(wide), (HEADS, width)))
+        key_out[...] = scale * lax.dot_general(
+            key_grad(coefficients()),
+            spread,
+            (((0,), (0,)), ((), ())),
+            preferred_element_type=wide,
+            precision=exact_mode,
+        )
+
+    def weights(n):
+        source = full_qkv.at[:, pl.ds(n * width, width)] if n < 3 else full_value
+        return pltpu.make_async_copy(source, weight_s, weight_sem.at[0])
+
+    def entry_part(n):
+        weights(n).wait()
+        value = lax.dot_general(
+            qkv_grad[:, n * width : (n + 1) * width],
+            weight_s[...],
+            (((1,), (1,)), ((), ())),
+            preferred_element_type=wide,
+        )
+        entry_grad[...] = value if n == 0 else entry_grad[...] + value
+        weights(n + 1).start()
+
+    def norm_part():
+        for fetch in fetches:
+            fetch.wait()
+        grad = entry_grad[...]
+        xhat, inverse = normalise(embed_ref[...])
+        extras[...] = jnp.zeros_like(extras)
+        value = middle_grad[...] + norm_back(grad, xhat, inverse, gain_ref[...])
+        value_low = value.astype(low)
+        embed_grad[...] = value_low
+        first = HEADS // per_row
+        extras[first : first + 1, :] = jnp.sum(value_low.astype(wide), axis=0, keepdims=True)
+        extras[first + 1 : first + 2, :] = jnp.sum(grad * xhat, axis=0, keepdims=True)
+        extras[first + 2 : first + 3, :] = jnp.sum(grad, axis=0, keepdims=True)
+        for n in range(4):
+            extras[first + 3 + n : first + 4 + n, :] = vectors_ref[n : n + 1, :]
+        extras[pl.ds(first + 7 + me, 1), :] = vectors_ref[4:5, :]
+
+    def heads_part():
+        heads_grad[...] = lax.dot_general(
+            full_agg[...], embed_grad[...], (((1,), (1,)), ((), ())), preferred_element_type=wide
+        ).astype(low)
+        patch_grad[...] = jnp.zeros_like(patch_grad)
+        coeff_s[...] = jnp.zeros_like(coeff_s)
+
+    slot_count = mask_ref.shape[0]
+
+    def one_head(h, carry):
+        lane = lax.broadcasted_iota(jnp.int32, (slot_count, HEADS), 1)
+        columns = head_columns(coeff_ref, h, slot_count)
+        weights = slot_softmax(patch_ref, columns, mask_ref)
+        mixed = mixed_of(patch_ref, weights, table_ref.shape[1])
+        at = pl.ds(pl.multiple_of(h * head_dim, 16), head_dim)
+        grad = heads_grad[at, :]
+        table_s[at, :] = (
+            lax.dot_general(grad, mixed, (((1,), (1,)), ((), ())), preferred_element_type=wide)
+            * share_ref[0]
+        ).astype(low)
+        mixed_grad = lax.dot_general(
+            table_ref[at, :], grad, (((0,), (0,)), ((), ())), preferred_element_type=wide
+        )
+        parts = [
+            mixed_grad[k * slot_count : (k + 1) * slot_count] for k in range(PIX + 1)
+        ]
+        values = [patch_ref[k].astype(wide) for k in range(PIX)]
+        weights_grad = parts[PIX]
+        for k in range(PIX):
+            weights_grad = weights_grad + parts[k] * values[k]
+        mean_grad = jnp.sum(weights * weights_grad, axis=0, keepdims=True)
+        scores_grad = weights * (weights_grad - mean_grad)
+        for k in range(PIX + 1):
+            value = scores_grad * values[k] if k < PIX else scores_grad
+            column = jnp.sum(value, axis=1, keepdims=True)
+            rows = slice(k * slot_count, (k + 1) * slot_count)
+            coeff_s[rows, :] = coeff_s[rows, :] + jnp.where(lane == h, column, 0.0)
+        for k in range(PIX):
+            patch_grad[k] += share_ref[1] * (parts[k] * weights + scores_grad * columns[k])
+        return carry
+
+    def heads_from(first, last):
+        lax.fori_loop(first, last, one_head, 0)
+
+    def bundle_part():
+        sums = lax.dot_general(
+            select_ref[...], table_s[...], (((0,), (1,)), ((), ())), preferred_element_type=wide
+        )
+        coeff_sum = lax.dot_general(
+            coeff_s[...],
+            select_ref[...].astype(wide),
+            (((0,), (0,)), ((), ())),
+            preferred_element_type=wide,
+            precision=exact_mode,
+        )
+        for n in range(HEADS):
+            place, column = n // per_row, (n % per_row) * size
+            extras[place : place + 1, column : column + size] = coeff_sum[n : n + 1, :]
+        row = lax.broadcasted_iota(jnp.int32, (size, extras.shape[0]), 0)
+        line = lax.broadcasted_iota(jnp.int32, (size, extras.shape[0]), 1)
+        spot = (row // part_rows) * spare + row % part_rows - (part_rows - spare)
+        chosen = (spot == line) & (row % part_rows >= part_rows - spare)
+        placed = jnp.dot(
+            chosen.astype(low),
+            (extras[...] * share_ref[0]).astype(low),
+            preferred_element_type=wide,
+        )
+        bundle[...] = (sums + placed).astype(low).reshape(bundle.shape)
+
+    middle_parts = [[functools.partial(entry_part, n)] for n in range(3)]
+    middle_parts += [[norm_part, heads_part]]
+    third = HEADS // 4
+    middle_parts += [
+        [functools.partial(heads_from, 0, third)],
+        [functools.partial(heads_from, third, 2 * third)],
+        [
+            functools.partial(heads_from, 2 * third, HEADS),
+            bundle_part,
+        ],
+    ]
+
+    out_copy = remote(out_sum, out_far, last_send.at[5], last_recv.at[5], others[1])
     stages = [begin, after_core, after_far]
-    stages += [functools.partial(after_step, i) for i in range(len(steps))]
-    stages += [functools.partial(after_back, k) for k in reversed(range(len(halvings)))]
-    order = [1, 0] + list(range(2, len(stages)))
-    extra = [finish_core, finish_far]
-    for t in range(len(chunks) + len(stages) - 1):
-        for s in order:
+    stages += [functools.partial(after_step, i) for i in range(count)]
+    stages += [functools.partial(after_back, k) for k in reversed(range(count))]
+    extra = [finish_core, finish_far, finish_table, finish_query]
+    steps = max(len(chunks), small + 1 + len(extra)) + len(stages) - 1
+    for t in range(steps):
+        for s in [1, 0]:
             if 0 <= t - s < len(chunks):
                 stages[s](t - s)
-        if 0 <= t - len(stages) < len(extra):
-            extra[t - len(stages)](0)
-
-
-def total(group_size, share, qkv_pair, agg_pair, proj_pair, bundle):
-    pairs = [qkv_pair, agg_pair, proj_pair]
-    width = qkv_pair[0].shape[0]
+        if t < len(middle_parts):
+            for part in middle_parts[t]:
+                part()
+        for s in range(2, len(stages)):
+            if 0 <= t - s < len(chunks):
+                stages[s](t - s)
+        if 0 <= t - small - len(stages) < len(extra):
+            extra[t - small - len(stages)]()
+        if t == len(chunks):
+            out_copy.start()
+    out_copy.wait()
+
+
+def finish(group_size, spare, shares, lefts, rights, others):
+    left_qkv, left_agg, left_proj = lefts
+    qkv_grad, attended = rights
+    width, rows = left_qkv.shape
     quarter = width // 4
     widths = 512
-    count = 1 + sum(right.shape[1] // widths for left, right in pairs)
+    low = jnp.bfloat16
+    wide = jnp.float32
+    size = others["own_columns"].shape[0]
+    part = size // 4
     steps = 0
-    halves = []
-    size = quarter
     while 2**steps < group_size:
-        if size >= 64:
-            size //= 2
-        halves.append(pltpu.VMEM((count, size, widths), jnp.bfloat16))
         steps += 1
-    low = jnp.bfloat16
+
+    def buffers(count, slots, rows, columns, last):
+        halves = []
+        size = rows
+        for _ in range(steps):
+            if size >= 32:
+                size //= 2
+            halves.append(pltpu.VMEM((count, size, columns), low))
+        few = pltpu.VMEM((slots, 2, rows, columns), low)
+        two = pltpu.VMEM((count, 2, rows, columns), low)
+        one = pltpu.VMEM((count, rows, columns), low)
+        semaphores = pltpu.SemaphoreType.DMA((2 + 2 * steps, count))
+        found = [few, two, few, one, one, one, halves]
+        return found + ([one] if last else []) + [semaphores, semaphores]
+
+    shapes = [(quarter, qkv_grad.shape[1]), (quarter, width), (quarter, width)]
+    count = sum(columns for _, columns in shapes) // widths
+    scratch = buffers(1, 1, part, width, True) + buffers(count, 3, quarter, widths, False)
+    scratch += [
+        pltpu.VMEM((4, part, width), low),
+        pltpu.VMEM((8, width), wide),
+        pltpu.VMEM((3, 8, width), wide),
+        pltpu.VMEM((size, width), wide),
+        pltpu.SemaphoreType.DMA((6,)),
+        pltpu.SemaphoreType.DMA((6,)),
+        pltpu.VMEM((rows, width), wide),
+        pltpu.VMEM((rows, width), low),
+        pltpu.VMEM((width, rows), low),
+        pltpu.VMEM((width, size), low),
+        pltpu.VMEM((size, HEADS), wide),
+        pltpu.VMEM((4 * spare, width), wide),
+        pltpu.VMEM((4, part, width), low),
+        pltpu.VMEM((width, width), low),
+        pltpu.SemaphoreType.DMA((1,)),
+        pltpu.VMEM((width, rows), low),
+        pltpu.VMEM((width, rows), low),
+        pltpu.VMEM((rows, width), low),
+        pltpu.VMEM((width, width), low),
+        pltpu.VMEM((rows, width), wide),
+        pltpu.VMEM((rows, width), wide),
+        pltpu.SemaphoreType.DMA((6,)),
+    ]
     whole = pl.BlockSpec(memory_space=pltpu.VMEM)
-    scratch = [
-        pltpu.VMEM((count, 2, quarter, widths), low),
-        pltpu.VMEM((count, 2, quarter, widths), low),
-        pltpu.VMEM((count, 2, quarter, widths), low),
-        pltpu.VMEM((count, quarter, widths), low),
-        pltpu.VMEM((count, quarter, widths), low),
-        pltpu.VMEM((count, quarter, widths), low),
-        halves,
-        pltpu.VMEM((count, quarter, widths), low),
-        pltpu.VMEM((4, quarter, bundle.shape[1]), low),
-        pltpu.SemaphoreType.DMA((3 + 2 * steps, count)),
-        pltpu.SemaphoreType.DMA((3 + 2 * steps, count)),
-    ]
+    out_shape = [jax.ShapeDtypeStruct(dims, low) for dims in shapes]
+    more = [(quarter, width)] * 3 + [(8, quarter), (part, width), (4 * spare, width)]
+    more.append(others["patch_rows"].shape)
+    out_shape += [jax.ShapeDtypeStruct(dims, wide) for dims in more]
+    out_shape.append(jax.ShapeDtypeStruct(others["out_sum"].shape, low))
+    hbm = pl.BlockSpec(memory_space=pl.ANY)
+    far_off = ("full_qkv", "full_agg", "full_value", "embedded", "middle_grad", "out_sum")
+    operands = [shares, left_qkv, qkv_grad, left_agg, left_proj, attended, *others.values()]
     return pl.pallas_call(
-        functools.partial(total_kernel, group_size, widths),
-        in_specs=[pl.BlockSpec(memory_space=pltpu.SMEM)] + [whole] * 7,
-        out_specs=[whole] * 4,
-        out_shape=[
-            jax.ShapeDtypeStruct((quarter, right.shape[1]), jnp.float32) for left, right in pairs
-        ]
-        + [jax.ShapeDtypeStruct(bundle.shape, jnp.float32)],
+        functools.partial(finish_kernel, group_size, widths, width // HEADS),
+        in_specs=[pl.BlockSpec(memory_space=pltpu.SMEM), whole, whole, hbm, hbm, hbm]
+        + [hbm if name in far_off else whole for name in others],
+        out_specs=[whole] * (len(out_shape) - 1) + [hbm],
+        out_shape=out_shape,
         scratch_shapes=scratch,
         compiler_params=pltpu.CompilerParams(
-            collective_id=0, has_side_effects=True, vmem_limit_bytes=VMEM_LIMIT
+            collective_id=0, has_side_effects=True, vmem_limit_bytes=62 * 1024 * 1024
         ),
         cost_estimate=pl.CostEstimate(
-            flops=sum(2 * left.size * right.shape[1] for left, right in pairs),
-            bytes_accessed=200_000_000,
-            transcendentals=0,
+            flops=20 * rows * width * width, bytes_accessed=200_000_000, transcendentals=0
         ),
-        name="total",
-    )(share, *[array for pair in pairs for array in pair], bundle)
+        name="finish",
+    )(*operands)
 
 
 def on_device(
@@ -1336,7 +1620,6 @@
     head_dim = width // HEADS
     own_width = width // 4
     own_vars = patch_weight.shape[0]
-    score_scale = head_dim ** (-0.5)
 
     item_count = patch_counts[0]
     own_valid = me * rows + jnp.arange(rows, dtype=jnp.int32) < item_count
@@ -1402,13 +1685,9 @@
         norm1_shift[None, :],
     )
     count_share = item_count.astype(wide) / count_rows[0, 0]
-    query_vec = query_rows[0].astype(low)
-    table_rows = tables.reshape(size, width)
-    own_columns = lax.dynamic_slice_in_dim(table_rows, me * own_width, own_width, 1)
-    key_table = product(own_columns, key_weight)
-    key_table = key_table + swap(key_table.astype(low), "fsdp", 1).astype(wide)
-    key_table = key_table + swap(key_table.astype(low), "fsdp", 2).astype(wide)
-
+    own_columns = lax.dynamic_slice_in_dim(
+        tables.reshape(size, width), me * own_width, own_width, 1
+    )
 
     queries, key_values, context_pairs, logs = attend(normed1, full_qkv, shard_valid)
     context = context_pairs.transpose(1, 0, 2).reshape(rows, width)
@@ -1439,87 +1718,62 @@
     down_weight_grad = lax.psum(down_weight_part, "grp").astype(wide)
     up_weight_grad = lax.psum(up_weight_part, "grp").astype(wide)
     out_got = swap(jnp.stack([out_parts[1], out_parts[3]]), "fsdp", 1)
-    out_far = swap((out_parts[2].astype(wide) + out_got[1].astype(wide)).astype(low), "fsdp", 2)
+    out_sum = (out_parts[2].astype(wide) + out_got[1].astype(wide)).astype(low)
+
+    qkv_grad = attend_back(queries, key_values, context_grad, context_pairs, logs, shard_valid)
+    spare = part_size - (PIX + 1) * own_vars
+    (
+        qkv_weight_grad,
+        agg_proj_grad,
+        proj_weight_grad,
+        value_weight_grad,
+        key_weight_grad,
+        query_weight_grad,
+        agg_query_grad,
+        var_grads,
+        extras,
+        patch_grad,
+        out_far,
+    ) = finish(
+        group_count,
+        spare,
+        jnp.stack([count_share, group_count * count_share]),
+        (normed1.T, heads_t, context.T),
+        (qkv_grad, attended_grad),
+        dict(
+            full_qkv=full_qkv,
+            full_agg=full_agg_proj,
+            full_value=full_value,
+            embedded=embedded,
+            middle_grad=middle_grad,
+            gain=norm1_gain[None, :],
+            vectors=feed_vectors,
+            patch_rows=patch_rows,
+            coeffs=coeffs,
+            slot_mask=slot_mask,
+            table_values=table_values,
+            select=select,
+            own_columns=own_columns,
+            key_query=key_query,
+            query_rows=query_rows,
+            key_weight=key_weight,
+            query_weight=query_weight,
+            own_query=own_query.astype(wide)[:, None],
+            out_sum=out_sum,
+        ),
+    )
     down_sum = out_parts[0].astype(wide) + out_got[0].astype(wide) + out_far.astype(wide)
     output = (middle + down_sum + down_bias).astype(low)
-
-    qkv_grad = attend_back(queries, key_values, context_grad, context_pairs, logs, shard_valid)
-    xhat1, inverse1 = normalise(embedded)
-    normed1_grad = right_product(qkv_grad, full_qkv)
-    norm1_gain_grad = jnp.sum(normed1_grad * xhat1, axis=0)
-    norm1_shift_grad = jnp.sum(normed1_grad, axis=0)
-    embedded_grad = (middle_grad + norm_back(normed1_grad, xhat1, inverse1, norm1_gain)).astype(low)
-    agg_bias_grad = column_sums(embedded_grad)
-    heads_grad = right_product(full_agg_proj, embedded_grad).astype(low)
-    scales = jnp.stack([count_share, group_count * count_share])
-    table_sum, coeff_sum, patch_grad = aggregate_back(
-        patch_rows, coeffs, slot_mask, table_values, select, heads_grad, scales
-    )
     patches_grad = patch_grad.transpose(1, 0, 2)
-
-    vectors = [agg_bias_grad, norm1_gain_grad, norm1_shift_grad]
-    up_bias_rows = lax.dynamic_update_slice_in_dim(
-        jnp.zeros((4, width), wide), feed_vectors[4:5], me, 0
-    )
-    coeff_rows = coeff_sum.T.reshape(-1, width)
-    spare = part_size - (PIX + 1) * own_vars
-    extras = jnp.concatenate(
-        [
-            coeff_rows,
-            jnp.concatenate([jnp.stack(vectors), feed_vectors[:4], up_bias_rows]) * count_share,
-        ],
-        axis=0,
-    )
-    extras = jnp.pad(extras, ((0, 4 * spare - extras.shape[0]), (0, 0))).astype(low)
-    bundle = jnp.concatenate(
-        [
-            table_sum.reshape(4, part_size, width)[:, : part_size - spare],
-            extras.reshape(4, spare, width),
-        ],
-        axis=1,
-    ).reshape(size, width)
-    qkv_weight_grad, agg_proj_grad, proj_weight_grad, bundle = total(
-        group_count,
-        count_share[None],
-        (normed1.T, qkv_grad),
-        (heads_t, embedded_grad),
-        (context.T, attended_grad),
-        bundle.reshape(width, -1),
-    )
-    table_total = bundle.reshape(size, width)
-    extras = table_total.reshape(4, part_size, width)[:, part_size - spare :].reshape(-1, width)
-    at = coeff_rows.shape[0]
-    coeff_total = extras[:at].reshape(HEADS, size)
+    qkv_weight_grad = qkv_weight_grad.astype(wide)
+    agg_proj_grad = agg_proj_grad.astype(wide)
+    proj_weight_grad = proj_weight_grad.astype(wide)
+    at = HEADS * size // width
     vector_total = extras[at : at + 7]
     at += 7
     up_bias_total = lax.dynamic_slice_in_dim(extras, at + me, 1, 0)[0]
     vector_own = lax.dynamic_slice_in_dim(vector_total, me * own_width, own_width, 1)
-
-    value_weight_grad = left_product(own_columns, table_total.astype(low))
-    key_query_grad = jnp.dot(coeff_total, own_columns.astype(wide), precision=exact_mode)
-    key_weight_grad = (
-        key_query_grad.T[:, :, None]
-        * query_vec.astype(wide).reshape(1, HEADS, head_dim)
-        * score_scale
-    ).reshape(own_width, width)
-    query_grad = (
-        jnp.einsum(
-            "hx,xhj->hj",
-            coeff_total,
-            key_table.reshape(size, HEADS, head_dim),
-            precision=exact_mode,
-        ).reshape(width)
-        * score_scale
-    )
-    query_weight_grad = own_query.astype(wide)[:, None] * query_grad[None, :]
-    agg_query_grad = jnp.dot(
-        query_weight.astype(wide), query_grad, precision=exact_mode
-    )
-    own_totals = lax.dynamic_slice_in_dim(table_total, me * part_size, part_size, 0)
-    own_coeffs = lax.dynamic_slice_in_dim(coeff_total, me * part_size, part_size, 1)
-    var_grads = right_product(own_totals.astype(low), full_value) + lax.dot_general(
-        own_coeffs, key_query.astype(wide), (((0,), (0,)), ((), ())), precision=exact_mode
-    )
+    agg_query_grad = agg_query_grad[0]
     var_grads = var_grads[: (PIX + 1) * own_vars].reshape(PIX + 1, own_vars, width)
     patch_weight_grad = var_grads[:PIX].transpose(1, 0, 2)
     var_embed_grad = var_grads[PIX]

time: 519 us -> 470 us (0.906)
  matrix products: 24.5 us -> 0 us
  waiting for transfers between devices: 19.7 us -> 0.02 us
  other arithmetic: 32.9 us -> 25.6 us
    dot_general x9 -> x0, matrix products: 24.5 us -> none  [the longest x3 15.8 us: right_product(): lax.dot_general(left_side, right_side, (((1,), (1,)), ((), ())), preferre...]
    ppermute x4 -> x1, waiting for transfers between devices: 19.7 us -> 0.01 us  [swap(): return lax.ppermute(value, axis, [(i, i ^ bit) for i in range(size)])]
    pallas_call x2 -> x1, Pallas kernels: 129 us -> 145 us  [finish(): pl.pallas_call(functools.partial(finish_kernel, group_size, widths, width...]
    unnamed x43 -> x40, local copies, waits for them, and re-layouts: 9.98 us -> 10.6 us
  transfers between devices with their start and end apart: 5 -> 2, of which waited for: 2 -> 0; matrix products, arithmetic and copies ran while one was open for 12% -> 5% of each run, Pallas kernels for 62% -> 45%
where the time goes in v5:
time: 470 us; the launch traced here: 467 us
  Pallas kernels  394 us (84%)
  local copies, waits for them, and re-layouts  30.3 us (6%)
  other arithmetic  25.6 us (5%)
  between operations  16.7 us (4%)
    pallas_call x1, Pallas kernels, finish(): pl.pallas_call(functools.partial(finish_kernel, group_size, widths, width...  145 us
    pallas_call x1, Pallas kernels, prepare(): pl.pallas_call(functools.partial(prepare_kernel, group_size, head_dim), i...  66.8 us
    pallas_call x1, Pallas kernels, attend_back(): pl.pallas_call(functools.partial(attend_back_kernel, head_dim), in_specs=...  64.3 us
    pallas_call x1, Pallas kernels, feed(): pl.pallas_call(feed_kernel, in_specs=[pl.BlockSpec(memory_space=pltpu.SME...  61.6 us
    pallas_call x1, Pallas kernels, attend(): pl.pallas_call(functools.partial(attend_kernel, head_dim), in_specs=[pl.B...  56.7 us
    unnamed x40, local copies, waits for them, and re-layouts  10.6 us
  transfers between devices with their start and end apart: 2, of which 0 were waited for; matrix products, arithmetic and copies ran while one was open for 5% of the time, Pallas kernels for 45%

profile of v5, /device:TPU:0, one launch (start us, length us, event | category | flops | bytes accessed | tf_op | source)
XLA Modules:
  0.0 466.6 jit_solution(1459562622559536123)
XLA Ops:
  8.6 0.5 subtract_clamp_fusion.valid_ref
  9.1 0.7 fusion.10
  9.8 0.1 tile.13
  9.9 1.3 broadcast_in_dim.87
  11.2 0.7 copy.57.refs_12_.refs_15_
  11.9 0.9 copy.55
  12.8 1.6 copy.66
  14.5 0.8 fusion.11
  15.3 0.8 fusion.5.refs_5_.refs_17_
  16.1 2.3 broadcast_select_fusion.refs_10_.refs_4_
  18.4 0.7 maximum_maximum_fusion.refs_4_
  19.2 0.6 broadcast_in_dim.69.refs_0_
  19.8 0.6 broadcast_in_dim.70.refs_1_
  20.4 66.8 %prepare.1 = (f32[8,128]{1,0:T(8,128)}, bf16[4,64,1024]{2,1,0:T(8,128)(2,1)}, f32[8,1024]{1,0:T(8,128)}, bf16[16,1024]{1,0:T(8,128)(2,1)}, bf16[1024,1024]{1,0:T...) custom-call(f32[8,128]{1,0:T(8,128)} %broadcast_in_dim.69.refs_0_, ...), custom_call_target="tpu_custom_call" | custom-call | flops 1073741824 | bytes 100000000 | tf_op jit(solution)/shard_map/prepare/pallas_call | solution.py:417
  87.2 1.2 slice.61
  89.0 56.7 %attend.1 = (bf16[8,512,128]{2,1,0:T(8,128)(2,1)}, bf16[4,8,2,512,128]{4,3,2,1,0:T(8,128)(2,1)}, bf16[8,512,128]{2,1,0:T(8,128)(2,1)}, f32[8,512,128]{2,1,0:T(8,128)}) custom-call(s32[4]{0:T(128)} %subtract_clamp_fusion.valid_ref, bf16[512,1024]{1,0:T(8,128)(2,1)} %get-tuple-element.60.rows_ref, bf16[1024,3072]{1,0:T(8,128)(2,1)} %get-tuple-element.61.weight_ref.refs_6_), custom_call_target="tpu_custom_call" | custom-call | flops 17179869184 | bytes 100000000 | tf_op jit(solution)/shard_map/attend/pallas_call | solution.py:622
  145.7 1.5 copy.58
  147.2 1.6 copy.59.refs_1_
  148.8 61.6 %feed.1 = (f32[512,1024]{1,0:T(8,128)}, bf16[4,512,1024]{2,1,0:T(8,128)(2,1)}, bf16[1024,1024]{1,0:T(8,128)(2,1)}, bf16[1024,1024]{1,0:T(8,128)(2,1)}, f32[512,1...) custom-call(f32[1]{0:T(128)} %bitcast.10.refs_0_, ...), custom_call_target="tpu_custom_call" | custom-call | flops 25769803776 | bytes 100000000 | tf_op jit(solution)/shard_map/feed/pallas_call | solution.py:1038
  210.4 1.7 fusion.12
  212.1 1.5 pad_maximum_fusion
  213.7 1.2 copy-done.11
  214.9 1.3 copy.60
  216.2 0.8 copy.62.refs_23_
  217.0 0.6 pad_maximum_fusion.1.refs_0_
  217.6 1.6 constant_dynamic-slice_fusion.2.refs_18_
  219.1 64.3 %attend_back.1.refs_2_ = bf16[512,3072]{1,0:T(8,128)(2,1)} custom-call(s32[4]{0:T(128)} %subtract_clamp_fusion.valid_ref, bf16[8,512,128]{2,1,0:T(8,128)(2,1)} %get-tuple-element.69.q_ref, bf16[4,8,2,512,128]{4,3,2,1,0:T(8,128)(2,1)} %get-tuple-element.70.kv_in, bf16[8,512,128]{2,1,0:T(8,128)(2,1)} %get-tuple-element.71.grad_ref, ...), custom_call_target="tpu_custom_call" | custom-call | flops 42949672960 | bytes 100000000 | tf_op jit(solution)/shard_map/attend_back/pallas_call | solution.py:790
  283.4 1.3 copy-done.4
  284.7 2.6 fusion.3.refs_24_
  287.4 144.7 %finish.1 = (bf16[256,3072]{1,0:T(8,128)(2,1)}, bf16[256,1024]{1,0:T(8,128)(2,1)}, bf16[256,1024]{1,0:T(8,128)(2,1)}, f32[256,1024]{1,0:T(8,128)}, f32[256,1024]...) custom-call(f32[2]{0:T(128)} %pad_maximum_fusion.1.refs_0_, ...), custom_call_target="tpu_custom_call" | custom-call | flops 10737418240 | bytes 200000000 | tf_op jit(solution)/shard_map/finish/pallas_call | solution.py:1570
  432.1 1.6 slice.70
  433.6 0.9 slice.68
  434.6 2.0 copy.63
  436.6 1.4 slice.71
  438.0 0.8 slice.72
  438.8 0.8 copy.64
  439.6 1.1 convert_element_type.61
  440.7 1.1 convert_element_type.63
  441.8 2.0 convert_element_type.62
  443.9 1.7 constant_dynamic-slice_fusion.1
  445.6 0.7 fusion.13
  446.3 2.8 fusion.2
  449.1 4.2 convert_element_type.64
  453.3 2.5 convert_element_type.65
  455.8 1.0 copy.74
  456.8 0.6 copy-done.9
  457.4 1.0 copy.75
  458.4 1.0 copy.76
  (45 shorter events, 0.3 us)
Async XLA Ops:
  7.2 2.6 copy-start
  7.2 11.2 %copy-start.15 = (bf16[12,1024]{1,0:T(8,128)(2,1)S(1)}, bf16[12,1024]{1,0:T(8,128)(2,1)}, u32[]{:S(2)}) copy-start(bf16[12,1024]{1,0:T(8,128)(2,1)} %param.31) | copy-start | bytes 73732
  7.2 441.9 %all-reduce.4.cloned.1.call-start = ((), (), s32[]{:S(2)}) async-start(), calls=%async_computation | async-start | bytes 8388608 | tf_op jit(solution)/shard_map/psum | solution.py:1719
  147.2 63.2 %copy-start.2 = (bf16[512,8,128]{0,2,1:T(8,128)(2,1)}, bf16[512,8,128]{0,2,1:T(8,128)(2,1)S(1)}, u32[]{:S(2)}) copy-start(bf16[512,8,128]{0,2,1:T(8,128)(2,1)S(1)} %copy.58) | copy-start | bytes 3145732
  213.6 69.8 %collective-permute-start = (bf16[2,512,1024]{2,1,0:T(8,128)(2,1)}, bf16[2,512,1024]{2,1,0:T(8,128)(2,1)S(1)}, u32[]{:S(2)}, u32[]{:S(2)}) collective-permute-start(bf16[2,512,1024]{2,1,0:T(8,128)(2,1)} %pad_maximum_fusion), channel_id=1, source_target_pairs={{0,1},{1,0},{2,3},{3,2},{4,5},{5,4},{6,7},{7,6},{8,9},{9,8},{10,11... | collective-permute-start | bytes 6291464 | tf_op jit(solution)/shard_map/ppermute | solution.py:21
  213.6 1.2 copy-start.11
  283.4 1.3 copy-start.4
  432.1 7.6 %copy-start.14 = (bf16[256,1024]{1,0:T(8,128)(2,1)S(1)}, bf16[256,1024]{1,0:T(8,128)(2,1)}, u32[]{:S(2)}) copy-start(bf16[256,1024]{1,0:T(8,128)(2,1)} %get-tuple-element.91) | copy-start | bytes 1572868
  432.1 8.7 %copy-start.13 = (bf16[256,1024]{1,0:T(8,128)(2,1)S(1)}, bf16[256,1024]{1,0:T(8,128)(2,1)}, u32[]{:S(2)}) copy-start(bf16[256,1024]{1,0:T(8,128)(2,1)} %get-tuple-element.94) | copy-start | bytes 1572868
  436.6 5.2 %copy-start.7 = (bf16[256,3072]{1,0:T(8,128)(2,1)S(1)}, bf16[256,3072]{1,0:T(8,128)(2,1)}, u32[]{:S(2)}) copy-start(bf16[256,3072]{1,0:T(8,128)(2,1)} %get-tuple-element.93) | copy-start | bytes 4718596
  440.7 5.5 %copy-start.12 = (bf16[512,1024]{1,0:T(8,128)(2,1)S(1)}, bf16[512,1024]{1,0:T(8,128)(2,1)}, u32[]{:S(2)}) copy-start(bf16[512,1024]{1,0:T(8,128)(2,1)} %get-tuple-element.84) | copy-start | bytes 3145732
  441.8 4.4 copy-start.5
  441.8 4.4 copy-start.6
  441.8 4.4 copy-start.16
  449.1 4.2 copy-start.3
  453.3 2.5 copy-start.10
  455.8 1.6 copy-start.9
  455.8 2.6 copy-start.8
  455.8 3.5 copy-start.1
Sparse Core Ops, SparseCore 0:
  213.8 190.7 all-reduce.3

commit v6 on v5

--- a/solution.py
+++ b/solution.py
@@ -463,6 +463,133 @@
     )
 
 
+def group_steps(group, order, size):
+    steps = []
+    offset = 0
+    for bit in order:
+        partner, bit_set = flip(group, bit)
+        halving = size >= 32
+        steps.append((partner, bit_set, halving, size, offset))
+        if halving:
+            size = size // 2
+            offset = offset + bit_set * size
+    return steps
+
+
+def group_orders(group_size):
+    bits = []
+    while 2 ** len(bits) < group_size:
+        bits.append(2 ** len(bits))
+    return bits, bits[1:] + bits[:1]
+
+
+def group_sum(steps, hold, halves, done, send_sem, recv_sem):
+    count = len(steps)
+    halvings = [i for i, step in enumerate(steps) if step[2]]
+    wide = jnp.float32
+
+    def span(start, size):
+        return pl.ds(pl.multiple_of(start, 16), size)
+
+    def copy(stage, c, src, dst, partner):
+        return pltpu.make_async_remote_copy(
+            src_ref=src,
+            dst_ref=dst,
+            send_sem=send_sem.at[stage, c],
+            recv_sem=recv_sem.at[stage, c],
+            device_id={"grp": partner},
+            device_id_type=pl.DeviceIdType.MESH,
+        )
+
+    def step_copy(i, c):
+        partner, bit_set, halving, size, offset = steps[i]
+        if halving:
+            size = size // 2
+            offset = offset + (1 - bit_set) * size
+        return copy(i, c, hold.at[c, span(offset, size), :], halves[i].at[c], partner)
+
+    def back_copy(i, c):
+        partner, bit_set, halving, size, offset = steps[i]
+        size = size // 2
+        at = done.at[c, span(offset + bit_set * size, size), :]
+        return copy(count + i, c, at, at, partner)
+
+    def begin(c):
+        step_copy(0, c).start()
+
+    def after_step(i, c):
+        step_copy(i, c).wait()
+        partner, bit_set, halving, size, offset = steps[i]
+        if halving:
+            size = size // 2
+            offset = offset + bit_set * size
+        at = span(offset, size)
+        value = hold[c, at, :].astype(wide) + halves[i][c].astype(wide)
+        if i + 1 < count:
+            hold[c, at, :] = value.astype(hold.dtype)
+            step_copy(i + 1, c).start()
+        else:
+            done[c, at, :] = value.astype(done.dtype)
+            back_copy(halvings[-1], c).start()
+
+    def after_back(k, c):
+        back_copy(halvings[k], c).wait()
+        if k > 0:
+            back_copy(halvings[k - 1], c).start()
+
+    stages = [begin] + [functools.partial(after_step, i) for i in range(count)]
+    return stages + [functools.partial(after_back, k) for k in reversed(range(len(halvings)))]
+
+
+def group_buffers(group_size, chunks, rows, columns):
+    low = jnp.bfloat16
+    steps = len(group_orders(group_size)[0])
+    halves = []
+    size = rows
+    for _ in range(steps):
+        if size >= 32:
+            size //= 2
+        halves.append(pltpu.VMEM((chunks, size, columns), low))
+    one = pltpu.VMEM((chunks, rows, columns), low)
+    semaphores = pltpu.SemaphoreType.DMA((2 * steps, chunks))
+    return [one, halves, one, semaphores, semaphores]
+
+
+def sum_beside(group, group_size, first, total_in, total_out, buffers):
+    hold, halves, done, send_sem, recv_sem, in_sem, keep_sem = buffers
+    chunks, rows, columns = hold.shape
+    steps = group_steps(group, group_orders(group_size)[0], rows)
+    stages = group_sum(steps, hold, halves, done, send_sem, recv_sem)
+
+    def at(c):
+        return pl.ds(pl.multiple_of((first + c) * columns, 128), columns)
+
+    def take(c):
+        return pltpu.make_async_copy(total_in.at[:, at(c)], hold.at[c], in_sem.at[c])
+
+    def give(c):
+        place = pl.ds(pl.multiple_of(c * columns, 128), columns)
+        return pltpu.make_async_copy(done.at[c], total_out.at[:, place], keep_sem.at[c])
+
+    def start():
+        for c in range(chunks):
+            take(c).wait()
+            stages[0](c)
+
+    def end(c):
+        stages[-1](c)
+        give(c).start()
+
+    return chunks, take, start, stages[1:-1] + [end], give
+
+
+def beside_buffers(group_size, chunks, rows, columns):
+    return group_buffers(group_size, chunks, rows, columns) + [
+        pltpu.SemaphoreType.DMA((chunks,)),
+        pltpu.SemaphoreType.DMA((chunks,)),
+    ]
+
+
 def lane_half(rows, pair, head_dim):
     lane = lax.broadcasted_iota(jnp.int32, (rows, 2 * head_dim), 1)
     return (lane // head_dim) == pair
@@ -651,10 +778,12 @@
 
 
 def attend_back_kernel(
-    head_dim, valid_ref, q_ref, kv_in, grad_ref, out_ref, log_ref, *refs
+    head_dim, group_size, valid_ref, q_ref, kv_in, grad_ref, out_ref, log_ref, *refs
 ):
-    result_ref, q_sum, own_s, far_s, last_s, near_s, got_far, got_last, got_near, log_rows, dot_rows = refs[:11]
-    send_sem, recv_sem, kv_ref, fetch_sem = refs[11:]
+    total_in, result_ref, total_out = refs[:3]
+    q_sum, own_s, far_s, last_s, near_s, got_far, got_last, got_near, log_rows, dot_rows = refs[3:13]
+    send_sem, recv_sem, kv_ref, fetch_sem = refs[13:17]
+    group = lax.axis_index("grp")
     me = lax.axis_index("fsdp")
     near = {"fsdp": flip(me, 1)[0]}
     far = {"fsdp": flip(me, 2)[0]}
@@ -666,12 +795,29 @@
         at = pl.ds(2 * half, 2)
         return pltpu.make_async_copy(kv_in.at[at, i], kv_ref.at[at, i], fetch_sem.at[half, i])
 
-    for half in (1, 0):
-        for i in range(pairs):
-            fetch(half, i).start()
+    chunks, take, sum_start, sum_stages, give = sum_beside(
+        group, group_size, 0, total_in, total_out, refs[17:]
+    )
+
+    waits = [s + 1 + max(0, s - len(sum_stages) + 3) for s in range(len(sum_stages))]
+
+    def sum_step(t):
+        for wait, stage in zip(waits, sum_stages):
+            c = t - wait
+
+            @pl.when((c >= 0) & (c < chunks))
+            def _(stage=stage, c=c):
+                stage(c)
+
+    for i in range(pairs):
+        fetch(1, i).start()
+    for c in range(chunks):
+        take(c).start()
+    for i in range(pairs):
+        fetch(0, i).start()
     width = pairs * lanes
     scale = head_dim ** (-0.5)
-    meet([near, far])
+    meet([near, far] + [{"grp": flip(group, bit)[0]} for bit in group_orders(group_size)[0]])
 
     def copy(kind, i, source, target, device):
         return pltpu.make_async_remote_copy(
@@ -757,6 +903,11 @@
         def _():
             send_far(i - 1)
 
+        @pl.when(i == 0)
+        def _():
+            sum_start()
+
+        sum_step(i)
         return carry
 
     lax.fori_loop(0, pairs, first_loop, 0)
@@ -766,6 +917,7 @@
         fetch(0, i).wait()
         q_sum[i] = (q_sum[i] + back(i, (1, 0), (near_s, own_s))) * scale
         near_copy(i).start()
+        sum_step(pairs + i)
         return carry
 
     lax.fori_loop(0, pairs, second_loop, 0)
@@ -778,9 +930,15 @@
             value = own_s[i, part] + got_near[i, part].astype(wide) + got_far[i, part].astype(wide)
             start = (part + 1) * width + i * lanes
             result_ref[:, start : start + lanes] = value.astype(low)
-
-
-def attend_back(queries, key_values, grad, out, logs, valid):
+    for t in range(2 * pairs, chunks + waits[-1]):
+        for wait, stage in zip(waits, sum_stages):
+            if 0 <= t - wait < chunks:
+                stage(t - wait)
+    for c in range(chunks):
+        give(c).wait()
+
+
+def attend_back(group_size, queries, key_values, grad, out, logs, valid, totals, columns, chunks):
     pairs, rows, lanes = queries.shape
     head_dim = lanes // 2
     whole = pl.BlockSpec(memory_space=pltpu.VMEM)
@@ -788,7 +946,7 @@
     wide = jnp.float32
     slab = (pairs, 2, rows, lanes)
     return pl.pallas_call(
-        functools.partial(attend_back_kernel, head_dim),
+        functools.partial(attend_back_kernel, head_dim, group_size),
         in_specs=[
             pl.BlockSpec(memory_space=pltpu.SMEM),
             whole,
@@ -796,9 +954,13 @@
             whole,
             whole,
             whole,
+            pl.BlockSpec(memory_space=pl.ANY),
         ],
-        out_specs=whole,
-        out_shape=jax.ShapeDtypeStruct((rows, 3 * pairs * lanes), low),
+        out_specs=[whole, pl.BlockSpec(memory_space=pl.ANY)],
+        out_shape=[
+            jax.ShapeDtypeStruct((rows, 3 * pairs * lanes), low),
+            jax.ShapeDtypeStruct((totals.shape[0], chunks * columns), low),
+        ],
         scratch_shapes=[
             pltpu.VMEM((pairs, rows, lanes), wide),
             pltpu.VMEM(slab, wide),
@@ -814,7 +976,8 @@
             pltpu.SemaphoreType.DMA((3, pairs)),
             pltpu.VMEM(key_values.shape, low),
             pltpu.SemaphoreType.DMA((2, pairs)),
-        ],
+        ]
+        + beside_buffers(group_size, chunks, totals.shape[0], columns),
         compiler_params=pltpu.CompilerParams(
             collective_id=2, has_side_effects=True, vmem_limit_bytes=VMEM_LIMIT
         ),
@@ -822,7 +985,7 @@
             flops=160 * rows * rows * pairs * lanes, bytes_accessed=100_000_000, transcendentals=0
         ),
         name="attend_back",
-    )(valid, queries, key_values, grad, out, logs)
+    )(valid, queries, key_values, grad, out, logs, totals)
 
 
 def feed_kernel(*refs):
@@ -831,11 +994,11 @@
         down_in, bias_ref, proj_bias, gain_ref, shift_ref,
     ) = refs[:13]
     (
-        middle_out, out_out, down_out, up_out, middle_grad, attended, context_grad, vectors,
-    ) = refs[13:21]
-    entry, gelu_s, pre_s, own_back, near_s, last_s, far_s, got_near, got_last, got_far = refs[21:31]
-    grad_s, up_ref, down_ref, middle_ref, out_ref, down_total, up_total = refs[31:38]
-    send_sem, recv_sem, fetch_sem, keep_sem = refs[38:]
+        middle_out, out_out, total_out, middle_grad, attended, context_grad, vectors,
+    ) = refs[13:20]
+    entry, gelu_s, pre_s, own_back, near_s, last_s, far_s, got_near, got_last, got_far = refs[20:30]
+    grad_s, up_ref, down_ref, middle_ref, out_ref, down_total, up_total = refs[30:37]
+    send_sem, recv_sem, fetch_sem, keep_sem = refs[37:]
     wide = jnp.float32
     low = jnp.bfloat16
     me = lax.axis_index("fsdp")
@@ -870,7 +1033,8 @@
         )
 
     def keep_total(n):
-        source, target = ((down_total, down_out), (up_total, up_out))[n]
+        source = (down_total, up_total)[n]
+        target = total_out.at[:, pl.ds(n * width, width)]
         return pltpu.make_async_copy(source, target, keep_sem.at[5, n])
 
     def copy(kind, t, src, dst, device):
@@ -1038,12 +1202,11 @@
     return pl.pallas_call(
         feed_kernel,
         in_specs=[pl.BlockSpec(memory_space=pltpu.SMEM)] + [vmem] * 3 + [hbm] * 5 + [vmem] * 4,
-        out_specs=[hbm] * 4 + [vmem] * 4,
+        out_specs=[hbm] * 3 + [vmem] * 4,
         out_shape=[
             shape(flat, wide),
             shape((4,) + flat, low),
-            shape((hidden, width), low),
-            shape((width, hidden), low),
+            shape((width, width + hidden), low),
             shape(flat, wide),
             shape(flat, low),
             shape((pairs, rows, width // pairs), low),
@@ -1085,36 +1248,25 @@
     )
 
 
-def group_steps(group, group_size, size):
-    steps = []
-    bit, offset = 1, 0
-    while bit < group_size:
-        partner, bit_set = flip(group, bit)
-        halving = size >= 32
-        steps.append((partner, bit_set, halving, size, offset))
-        if halving:
-            size = size // 2
-            offset = offset + bit_set * size
-        bit *= 2
-    return steps
-
-
-def finish_kernel(group_size, widths, head_dim, *refs):
+def finish_kernel(group_size, widths, head_dim, first_chunk, *refs):
     share_ref = refs[0]
     left_qkv, qkv_grad, left_agg_in, left_proj_in, attended_in = refs[1:6]
     (
         full_qkv, full_agg_in, full_value, embed_in, middle_in, gain_ref, vectors_ref, patch_ref,
         coeff_ref, mask_ref, table_ref, select_ref, own_columns, keys_ref, query_ref, key_w,
-        query_w, own_query, out_sum,
-    ) = refs[6:25]
-    outs = refs[25:28]
-    value_out, key_out, query_out, agg_query_out, var_out, extra_out, patch_grad = refs[28:35]
-    out_far = refs[35]
-    sets = [refs[36:46], refs[46:55]]
-    full, query_part, query_got, var_s, last_send, last_recv = refs[55:61]
-    entry_grad, embed_grad, heads_grad, table_s, coeff_s, extras, bundle = refs[61:68]
-    weight_s, weight_sem, left_agg, left_proj, attended, full_agg, embed_ref, middle_grad = refs[68:76]
-    fetch_sem = refs[76]
+        query_w, own_query, out_sum, total_in,
+    ) = refs[6:26]
+    outs = refs[26:29]
+    value_out, key_out, query_out, agg_query_out, var_out, extra_out, patch_grad = refs[29:36]
+    out_far, total_out = refs[36:38]
+    sets = [refs[38:48], refs[48:57]]
+    full, query_part, query_got, var_s, last_send, last_recv = refs[57:63]
+    entry_grad, embed_grad, heads_grad, table_s, coeff_s, extras, bundle = refs[63:70]
+    weight_s, weight_sem, left_agg, left_proj, attended, full_agg, embed_ref, middle_grad = refs[70:78]
+    fetch_sem = refs[78]
+    sum_chunks, sum_take, sum_start, sum_stages, sum_give = sum_beside(
+        lax.axis_index("grp"), group_size, first_chunk, total_in, total_out, refs[79:]
+    )
     fetches = [
         pltpu.make_async_copy(source, target, fetch_sem.at[n])
         for n, (source, target) in enumerate(
@@ -1136,12 +1288,16 @@
     wide = jnp.float32
     low = jnp.bfloat16
     quarters = [buffers[2].shape[2] for buffers in sets]
-    all_steps = [group_steps(group, group_size, quarter) for quarter in quarters]
+    all_steps = [
+        group_steps(group, group_orders(group_size)[0], quarter) for quarter in quarters
+    ]
     all_halvings = [[i for i, step in enumerate(steps) if step[2]] for steps in all_steps]
     count = len(all_steps[0])
     slots = sets[1][0].shape[0]
     others = [{"fsdp": core_partner}, {"fsdp": far_partner}, {"fsdp": diagonal}]
     pltpu.make_async_copy(full_qkv.at[:, pl.ds(0, key_w.shape[1])], weight_s, weight_sem.at[0]).start()
+    for c in range(sum_chunks):
+        sum_take(c).start()
     for fetch in fetches:
         fetch.start()
     meet(others + [{"grp": step[0]} for step in all_steps[0]])
@@ -1490,6 +1646,8 @@
         for s in [1, 0]:
             if 0 <= t - s < len(chunks):
                 stages[s](t - s)
+        if t == 0:
+            sum_start()
         if t < len(middle_parts):
             for part in middle_parts[t]:
                 part()
@@ -1498,12 +1656,18 @@
                 stages[s](t - s)
         if 0 <= t - small - len(stages) < len(extra):
             extra[t - small - len(stages)]()
+        for s, stage in enumerate(sum_stages):
+            for c in range(sum_chunks):
+                if t == 1 + s + c // 2:
+                    stage(c)
         if t == len(chunks):
             out_copy.start()
     out_copy.wait()
-
-
-def finish(group_size, spare, shares, lefts, rights, others):
+    for c in range(sum_chunks):
+        sum_give(c).wait()
+
+
+def finish(group_size, spare, shares, lefts, rights, columns, first_chunk, others):
     left_qkv, left_agg, left_proj = lefts
     qkv_grad, attended = rights
     width, rows = left_qkv.shape
@@ -1558,20 +1722,24 @@
         pltpu.VMEM((rows, width), wide),
         pltpu.SemaphoreType.DMA((6,)),
     ]
+    totals = others["totals"]
+    left_chunks = totals.shape[1] // columns - first_chunk
+    scratch += beside_buffers(group_size, left_chunks, totals.shape[0], columns)
     whole = pl.BlockSpec(memory_space=pltpu.VMEM)
     out_shape = [jax.ShapeDtypeStruct(dims, low) for dims in shapes]
     more = [(quarter, width)] * 3 + [(8, quarter), (part, width), (4 * spare, width)]
     more.append(others["patch_rows"].shape)
     out_shape += [jax.ShapeDtypeStruct(dims, wide) for dims in more]
     out_shape.append(jax.ShapeDtypeStruct(others["out_sum"].shape, low))
+    out_shape.append(jax.ShapeDtypeStruct((totals.shape[0], left_chunks * columns), low))
     hbm = pl.BlockSpec(memory_space=pl.ANY)
-    far_off = ("full_qkv", "full_agg", "full_value", "embedded", "middle_grad", "out_sum")
+    far_off = ("full_qkv", "full_agg", "full_value", "embedded", "middle_grad", "out_sum", "totals")
     operands = [shares, left_qkv, qkv_grad, left_agg, left_proj, attended, *others.values()]
     return pl.pallas_call(
-        functools.partial(finish_kernel, group_size, widths, width // HEADS),
+        functools.partial(finish_kernel, group_size, widths, width // HEADS, first_chunk),
         in_specs=[pl.BlockSpec(memory_space=pltpu.SMEM), whole, whole, hbm, hbm, hbm]
         + [hbm if name in far_off else whole for name in others],
-        out_specs=[whole] * (len(out_shape) - 1) + [hbm],
+        out_specs=[whole] * (len(out_shape) - 2) + [hbm] * 2,
         out_shape=out_shape,
         scratch_shapes=scratch,
         compiler_params=pltpu.CompilerParams(
@@ -1694,8 +1862,7 @@
     (
         middle,
         out_parts,
-        down_weight_part,
-        up_weight_part,
+        totals,
         middle_grad,
         attended_grad,
         context_grad,
@@ -1715,12 +1882,24 @@
         norm2_gain[None, :],
         norm2_shift[None, :],
     )
-    down_weight_grad = lax.psum(down_weight_part, "grp").astype(wide)
-    up_weight_grad = lax.psum(up_weight_part, "grp").astype(wide)
     out_got = swap(jnp.stack([out_parts[1], out_parts[3]]), "fsdp", 1)
     out_sum = (out_parts[2].astype(wide) + out_got[1].astype(wide)).astype(low)
 
-    qkv_grad = attend_back(queries, key_values, context_grad, context_pairs, logs, shard_valid)
+    columns = width // 8
+    chunks = 12
+    qkv_grad, summed = attend_back(
+        group_count,
+        queries,
+        key_values,
+        context_grad,
+        context_pairs,
+        logs,
+        shard_valid,
+        totals,
+        columns,
+        chunks,
+    )
+    down_weight_grad = summed[:, :width].astype(wide)
     spare = part_size - (PIX + 1) * own_vars
     (
         qkv_weight_grad,
@@ -1734,12 +1913,15 @@
         extras,
         patch_grad,
         out_far,
+        rest,
     ) = finish(
         group_count,
         spare,
         jnp.stack([count_share, group_count * count_share]),
         (normed1.T, heads_t, context.T),
         (qkv_grad, attended_grad),
+        columns,
+        chunks,
         dict(
             full_qkv=full_qkv,
             full_agg=full_agg_proj,
@@ -1760,10 +1942,12 @@
             query_weight=query_weight,
             own_query=own_query.astype(wide)[:, None],
             out_sum=out_sum,
+            totals=totals,
         ),
     )
     down_sum = out_parts[0].astype(wide) + out_got[0].astype(wide) + out_far.astype(wide)
     output = (middle + down_sum + down_bias).astype(low)
+    up_weight_grad = jnp.concatenate([summed[:, width:], rest], axis=1).astype(wide)
     patches_grad = patch_grad.transpose(1, 0, 2)
     qkv_weight_grad = qkv_weight_grad.astype(wide)
     agg_proj_grad = agg_proj_grad.astype(wide)

time: 470 us -> 455 us (0.968)
  between operations: 16.7 us -> 3.09 us
    pallas_call x1, Pallas kernels: 145 us -> 116 us  [finish(): pl.pallas_call(functools.partial(finish_kernel, group_size, widths, width...]
    pallas_call x1, Pallas kernels: 64.3 us -> 91.1 us  [attend_back(): pl.pallas_call(functools.partial(attend_back_kernel, head_dim, group_size...]
    unnamed x40 -> x34, local copies, waits for them, and re-layouts: 10.6 us -> 8.03 us
  transfers between devices with their start and end apart: 2 -> 1, of which waited for: 0 -> 0; matrix products, arithmetic and copies ran while one was open for 5% -> 2% of each run, Pallas kernels for 45% -> 20%
where the time goes in v6:
time: 455 us; the launch traced here: 451 us
  Pallas kernels  392 us (86%)
  local copies, waits for them, and re-layouts  28.6 us (6%)
  other arithmetic  27.7 us (6%)
    pallas_call x1, Pallas kernels, finish(): pl.pallas_call(functools.partial(finish_kernel, group_size, widths, width...  116 us
    pallas_call x1, Pallas kernels, attend_back(): pl.pallas_call(functools.partial(attend_back_kernel, head_dim, group_size...  91.1 us
    pallas_call x1, Pallas kernels, prepare(): pl.pallas_call(functools.partial(prepare_kernel, group_size, head_dim), i...  66.7 us
    pallas_call x1, Pallas kernels, feed(): pl.pallas_call(feed_kernel, in_specs=[pl.BlockSpec(memory_space=pltpu.SME...  61.7 us
    pallas_call x1, Pallas kernels, attend(): pl.pallas_call(functools.partial(attend_kernel, head_dim), in_specs=[pl.B...  56.7 us
  transfers between devices with their start and end apart: 1, of which 0 were waited for; matrix products, arithmetic and copies ran while one was open for 2% of the time, Pallas kernels for 20%

profile of v6, /device:TPU:0, one launch (start us, length us, event | category | flops | bytes accessed | tf_op | source)
XLA Modules:
  0.0 451.5 jit_solution(8157032597725248829)
XLA Ops:
  2.0 0.5 subtract_clamp_fusion.valid_ref
  2.5 0.7 fusion.10
  3.2 0.1 tile.13
  3.3 1.3 broadcast_in_dim.87
  4.6 0.7 copy.57.refs_12_.refs_15_
  5.3 0.9 copy.55
  6.2 1.6 copy.66
  7.9 0.1 pad.13.clone
  8.0 0.8 fusion.11
  8.7 0.8 fusion.5.refs_5_.refs_17_
  9.5 2.3 broadcast_select_fusion.refs_10_.refs_4_
  11.9 0.7 maximum_maximum_fusion.refs_4_
  12.6 0.6 broadcast_in_dim.69.refs_0_
  13.2 0.6 broadcast_in_dim.70.refs_1_
  13.8 66.7 %prepare.1 = (f32[8,128]{1,0:T(8,128)}, bf16[4,64,1024]{2,1,0:T(8,128)(2,1)}, f32[8,1024]{1,0:T(8,128)}, bf16[16,1024]{1,0:T(8,128)(2,1)}, bf16[1024,1024]{1,0:T...) custom-call(f32[8,128]{1,0:T(8,128)} %broadcast_in_dim.69.refs_0_, ...), custom_call_target="tpu_custom_call" | custom-call | flops 1073741824 | bytes 100000000 | tf_op jit(solution)/shard_map/prepare/pallas_call | solution.py:417
  80.5 1.2 slice.67
  82.4 56.7 %attend.1 = (bf16[8,512,128]{2,1,0:T(8,128)(2,1)}, bf16[4,8,2,512,128]{4,3,2,1,0:T(8,128)(2,1)}, bf16[8,512,128]{2,1,0:T(8,128)(2,1)}, f32[8,512,128]{2,1,0:T(8,128)}) custom-call(s32[4]{0:T(128)} %subtract_clamp_fusion.valid_ref, bf16[512,1024]{1,0:T(8,128)(2,1)} %get-tuple-element.62.rows_ref, bf16[1024,3072]{1,0:T(8,128)(2,1)} %get-tuple-element.63.weight_ref.refs_6_), custom_call_target="tpu_custom_call" | custom-call | flops 17179869184 | bytes 100000000 | tf_op jit(solution)/shard_map/attend/pallas_call | solution.py:749
  139.1 1.5 copy.58
  140.6 1.5 copy.59.refs_1_
  142.1 61.7 %feed.1 = (f32[512,1024]{1,0:T(8,128)}, bf16[4,512,1024]{2,1,0:T(8,128)(2,1)}, bf16[1024,2048]{1,0:T(8,128)(2,1)}, f32[512,1024]{1,0:T(8,128)}, bf16[512,1024]{1...) custom-call(f32[1]{0:T(128)} %bitcast.10.refs_0_, bf16[512,1024]{1,0:T(8,128)(2,1)} %copy.59.refs_1_, ...), custom_call_target="tpu_custom_call" | custom-call | flops 25769803776 | bytes 100000000 | tf_op jit(solution)/shard_map/feed/pallas_call | solution.py:1202
  203.8 1.7 fusion.12
  205.5 1.5 pad_maximum_fusion
  207.0 91.1 %attend_back.1 = (bf16[512,3072]{1,0:T(8,128)(2,1)}, bf16[1024,1536]{1,0:T(8,128)(2,1)}) custom-call(s32[4]{0:T(128)} %subtract_clamp_fusion.valid_ref, bf16[8,512,128]{2,1,0:T(8,128)(2,1)} %get-tuple-element.71.q_ref, bf16[4,8,2,512,128]{4,3,2,1,0:T(8,128)(2,1)} %get-tuple-element.72.kv_in, bf16[8,512,128]{2,1,0:T(8,128)(2,1)} %get-tuple-element.73.grad_ref, ...), custom_call_target="tpu_custom_call" | custom-call | flops 42949672960 | bytes 100000000 | tf_op jit(solution)/shard_map/attend_back/pallas_call | solution.py:948
  298.2 1.3 copy.60
  299.5 0.8 copy.62.refs_23_
  300.3 1.3 slice.85
  301.6 0.6 pad_maximum_fusion.1.refs_0_
  302.2 1.6 constant_dynamic-slice_fusion.2.refs_18_
  303.7 4.1 slice_convert_fusion
  307.8 2.9 fusion.3.refs_24_
  310.7 115.9 %finish.1 = (bf16[256,3072]{1,0:T(8,128)(2,1)}, bf16[256,1024]{1,0:T(8,128)(2,1)}, bf16[256,1024]{1,0:T(8,128)(2,1)}, f32[256,1024]{1,0:T(8,128)}, f32[256,1024]...) custom-call(f32[2]{0:T(128)} %pad_maximum_fusion.1.refs_0_, ...), custom_call_target="tpu_custom_call" | custom-call | flops 10737418240 | bytes 200000000 | tf_op jit(solution)/shard_map/finish/pallas_call | solution.py:1738
  426.7 1.6 slice.76
  428.2 0.9 slice.74
  429.2 2.0 copy.63
  431.2 1.3 slice.77
  432.4 0.8 slice.78
  433.3 1.4 constant_dynamic-slice_fusion.1
  434.7 0.8 copy.64
  435.5 1.1 convert_element_type.61
  436.6 1.1 convert_element_type.63
  437.6 3.5 convert_element_type.62
  441.2 2.6 maximum_convert_fusion
  443.8 0.7 fusion.13
  444.5 3.2 fusion.2
  447.7 1.0 copy.72
  448.7 0.6 copy-done.5
  449.3 1.0 copy.73
  450.3 1.0 copy.74
  (37 shorter events, 0.2 us)
Async XLA Ops:
  0.7 2.5 copy-start
  0.7 11.2 %copy-start.12 = (bf16[12,1024]{1,0:T(8,128)(2,1)S(1)}, bf16[12,1024]{1,0:T(8,128)(2,1)}, u32[]{:S(2)}) copy-start(bf16[12,1024]{1,0:T(8,128)(2,1)} %param.31) | copy-start | bytes 73732
  140.6 63.2 %copy-start.2 = (bf16[512,8,128]{0,2,1:T(8,128)(2,1)}, bf16[512,8,128]{0,2,1:T(8,128)(2,1)S(1)}, u32[]{:S(2)}) copy-start(bf16[512,8,128]{0,2,1:T(8,128)(2,1)S(1)} %copy.58) | copy-start | bytes 3145732
  207.0 100.8 %collective-permute-start = (bf16[2,512,1024]{2,1,0:T(8,128)(2,1)}, bf16[2,512,1024]{2,1,0:T(8,128)(2,1)}, u32[]{:S(2)}, u32[]{:S(2)}) collective-permute-start(bf16[2,512,1024]{2,1,0:T(8,128)(2,1)} %pad_maximum_fusion), channel_id=1, source_target_pairs={{0,1},{1,0},{2,3},{3,2},{4,5},{5,4},{6,7},{7,6},{8,9},{9,8},{10,11... | collective-permute-start | bytes 6291464 | tf_op jit(solution)/shard_map/ppermute | solution.py:21
  207.0 91.1 %copy-start.7 = (bf16[512,1024]{1,0:T(8,128)(2,1)S(1)}, bf16[512,1024]{1,0:T(8,128)(2,1)}, u32[]{:S(2)}) copy-start(bf16[512,1024]{1,0:T(8,128)(2,1)} %get-tuple-element.62.rows_ref) | copy-start | bytes 3145732
  426.7 8.8 %copy-start.11 = (bf16[256,1024]{1,0:T(8,128)(2,1)S(1)}, bf16[256,1024]{1,0:T(8,128)(2,1)}, u32[]{:S(2)}) copy-start(bf16[256,1024]{1,0:T(8,128)(2,1)} %get-tuple-element.95) | copy-start | bytes 1572868
  426.7 9.9 %copy-start.10 = (bf16[256,1024]{1,0:T(8,128)(2,1)S(1)}, bf16[256,1024]{1,0:T(8,128)(2,1)}, u32[]{:S(2)}) copy-start(bf16[256,1024]{1,0:T(8,128)(2,1)} %get-tuple-element.98) | copy-start | bytes 1572868
  437.6 3.5 copy-start.9
  441.2 3.3 copy-start.3
  441.2 3.3 copy-start.8
  441.2 3.3 copy-start.13
  444.5 3.3 copy-start.6
  447.7 1.6 copy-start.5
  447.7 2.6 copy-start.4
  447.7 3.5 copy-start.1

commit v7 on v6

--- a/solution.py
+++ b/solution.py
@@ -596,7 +596,7 @@
 
 
 def attend_kernel(
-    head_dim, valid_ref, rows_ref, weight_ref, q_ref, kv_out, out_ref, log_ref, kv_ref, weight_s, sum_s, top_s, total_s, send_sem, recv_sem, fetch_sem, keep_sem
+    head_dim, valid_ref, rows_ref, weight_ref, q_ref, kv_out, out_ref, flat_ref, log_ref, kv_ref, weight_s, sum_s, top_s, total_s, send_sem, recv_sem, fetch_sem, keep_sem
 ):
     me = lax.axis_index("fsdp")
     near = {"fsdp": flip(me, 1)[0]}
@@ -721,8 +721,12 @@
         last_copy(i).wait_recv()
         attend(i, (3,), False)
         keep(i).start()
-        out_ref[i] = (sum_s[...] / total_s[...]).astype(low)
-        log_ref[i] = top_s[...] + jnp.log(total_s[...])
+        context = (sum_s[...] / total_s[...]).astype(low)
+        out_ref[i] = context
+        flat_ref[:, pl.ds(pl.multiple_of(i * lanes, lanes), lanes)] = context
+        logs = jnp.transpose(top_s[...] + jnp.log(total_s[...]))
+        for pair in range(2):
+            log_ref[i, pair : pair + 1, :] = logs[pair * head_dim : pair * head_dim + 1, :]
         return carry
 
     lax.fori_loop(0, pairs, one_pair, 0)
@@ -749,12 +753,13 @@
     return pl.pallas_call(
         functools.partial(attend_kernel, head_dim),
         in_specs=[pl.BlockSpec(memory_space=pltpu.SMEM), whole, hbm],
-        out_specs=[whole, hbm, whole, whole],
+        out_specs=[whole, hbm, whole, whole, whole],
         out_shape=[
             jax.ShapeDtypeStruct((pairs, rows, lanes), low),
             jax.ShapeDtypeStruct((4, pairs, 2, rows, lanes), low),
             jax.ShapeDtypeStruct((pairs, rows, lanes), low),
-            jax.ShapeDtypeStruct((pairs, rows, lanes), wide),
+            jax.ShapeDtypeStruct((rows, width), low),
+            jax.ShapeDtypeStruct((pairs, 8, rows), wide),
         ],
         scratch_shapes=[
             pltpu.VMEM((4, pairs, 2, rows, lanes), low),
@@ -781,8 +786,8 @@
     head_dim, group_size, valid_ref, q_ref, kv_in, grad_ref, out_ref, log_ref, *refs
 ):
     total_in, result_ref, total_out = refs[:3]
-    q_sum, own_s, far_s, last_s, near_s, got_far, got_last, got_near, log_rows, dot_rows = refs[3:13]
-    send_sem, recv_sem, kv_ref, fetch_sem = refs[13:17]
+    q_sum, own_s, far_s, last_s, near_s, got_far, got_last, got_near, dot_rows = refs[3:12]
+    send_sem, recv_sem, kv_ref, fetch_sem = refs[12:16]
     group = lax.axis_index("grp")
     me = lax.axis_index("fsdp")
     near = {"fsdp": flip(me, 1)[0]}
@@ -796,7 +801,7 @@
         return pltpu.make_async_copy(kv_in.at[at, i], kv_ref.at[at, i], fetch_sem.at[half, i])
 
     chunks, take, sum_start, sum_stages, give = sum_beside(
-        group, group_size, 0, total_in, total_out, refs[17:]
+        group, group_size, 0, total_in, total_out, refs[16:]
     )
 
     waits = [s + 1 + max(0, s - len(sum_stages) + 3) for s in range(len(sum_stages))]
@@ -850,7 +855,7 @@
 
         for pair in range(2):
             side = lane_half(rows, pair, head_dim)
-            log_row = log_rows[i, pair : pair + 1, :]
+            log_row = log_ref[i, pair : pair + 1, :]
             dot_row = dot_rows[i, pair : pair + 1, :]
             one_query = jnp.where(side, query, jnp.zeros_like(query))
             one_grad = jnp.where(side, grad, jnp.zeros_like(grad))
@@ -889,11 +894,9 @@
         far_copy(i).start()
 
     def first_loop(i, carry):
-        log_t = jnp.transpose(log_ref[i])
         dots = jnp.transpose(grad_ref[i].astype(wide) * out_ref[i].astype(wide))
         for pair in range(2):
             here = slice(pair * head_dim, (pair + 1) * head_dim)
-            log_rows[i, pair : pair + 1, :] = log_t[pair * head_dim : pair * head_dim + 1, :]
             dot_rows[i, pair : pair + 1, :] = jnp.sum(dots[here, :], axis=0, keepdims=True)
         fetch(1, i).wait()
         q_sum[i] = back(i, (3, 2), (last_s, far_s))
@@ -971,7 +974,6 @@
             pltpu.VMEM(slab, low),
             pltpu.VMEM(slab, low),
             pltpu.VMEM((pairs, 8, rows), wide),
-            pltpu.VMEM((pairs, 8, rows), wide),
             pltpu.SemaphoreType.DMA((3, pairs)),
             pltpu.SemaphoreType.DMA((3, pairs)),
             pltpu.VMEM(key_values.shape, low),
@@ -1115,14 +1117,14 @@
         back_near(t).start()
 
     for t in range(2):
+        if t > 0:
+            add_last(t - 1, back_last, back_far, far_s, got_last, span)
         rows_far(t).wait()
         rows_last(t).start()
         feed(2, t, far_s)
         rows_last(t).wait()
         feed(3, t, last_s)
         back_last(t).start()
-        if t > 0:
-            add_last(t - 1, back_last, back_far, far_s, got_last, span)
     add_last(1, back_last, back_far, far_s, got_last, span)
 
     block = min(hidden, 256)
@@ -1626,14 +1628,11 @@
 
     middle_parts = [[functools.partial(entry_part, n)] for n in range(3)]
     middle_parts += [[norm_part, heads_part]]
-    third = HEADS // 4
+    some = HEADS // 4
     middle_parts += [
-        [functools.partial(heads_from, 0, third)],
-        [functools.partial(heads_from, third, 2 * third)],
-        [
-            functools.partial(heads_from, 2 * third, HEADS),
-            bundle_part,
-        ],
+        [functools.partial(heads_from, 0, some)],
+        [functools.partial(heads_from, some, 2 * some)],
+        [functools.partial(heads_from, 2 * some, HEADS), bundle_part],
     ]
 
     out_copy = remote(out_sum, out_far, last_send.at[5], last_recv.at[5], others[1])
@@ -1857,8 +1856,7 @@
         tables.reshape(size, width), me * own_width, own_width, 1
     )
 
-    queries, key_values, context_pairs, logs = attend(normed1, full_qkv, shard_valid)
-    context = context_pairs.transpose(1, 0, 2).reshape(rows, width)
+    queries, key_values, context_pairs, context, logs = attend(normed1, full_qkv, shard_valid)
     (
         middle,
         out_parts,

time: 455 us -> 441 us (0.969)
  Pallas kernels: 392 us -> 384 us
    pallas_call x1, Pallas kernels: 61.7 us -> 55.2 us  [feed(): pl.pallas_call(feed_kernel, in_specs=[pl.BlockSpec(memory_space=pltpu.SME...]
  transfers between devices with their start and end apart: 1 -> 1, of which waited for: 0 -> 0; matrix products, arithmetic and copies ran while one was open for 2% -> 3% of each run, Pallas kernels for 20% -> 21%
where the time goes in v7:
time: 441 us; the launch traced here: 438 us
  Pallas kernels  384 us (87%)
  other arithmetic  25.5 us (6%)
  local copies, waits for them, and re-layouts  25.3 us (6%)
    pallas_call x1, Pallas kernels, finish(): pl.pallas_call(functools.partial(finish_kernel, group_size, widths, width...  116 us
    pallas_call x1, Pallas kernels, attend_back(): pl.pallas_call(functools.partial(attend_back_kernel, head_dim, group_size...  90.3 us
    pallas_call x1, Pallas kernels, prepare(): pl.pallas_call(functools.partial(prepare_kernel, group_size, head_dim), i...  66.7 us
    pallas_call x1, Pallas kernels, attend(): pl.pallas_call(functools.partial(attend_kernel, head_dim), in_specs=[pl.B...  56.1 us
    pallas_call x1, Pallas kernels, feed(): pl.pallas_call(feed_kernel, in_specs=[pl.BlockSpec(memory_space=pltpu.SME...  55.2 us
  transfers between devices with their start and end apart: 1, of which 0 were waited for; matrix products, arithmetic and copies ran while one was open for 3% of the time, Pallas kernels for 21%

profile of v7, /device:TPU:0, one launch (start us, length us, event | category | flops | bytes accessed | tf_op | source)
XLA Modules:
  0.0 437.8 jit_solution(13881707042704144195)
XLA Ops:
  0.7 0.0 copy-start
  1.4 0.9 copy.54
  3.0 0.1 tile.13
  3.1 1.6 copy.64
  4.7 0.7 fusion.10
  5.4 0.7 copy.56.refs_12_.refs_15_
  6.1 0.8 fusion.11
  6.9 0.1 pad.13.clone
  6.9 0.8 fusion.5.refs_5_.refs_17_
  7.7 2.3 broadcast_select_fusion.refs_10_.refs_4_
  10.1 0.7 maximum_maximum_fusion.refs_4_
  10.8 0.6 broadcast_in_dim.69.refs_0_
  11.4 0.6 broadcast_in_dim.70.refs_1_
  12.0 66.7 %prepare.1 = (f32[8,128]{1,0:T(8,128)}, bf16[4,64,1024]{2,1,0:T(8,128)(2,1)}, f32[8,1024]{1,0:T(8,128)}, bf16[16,1024]{1,0:T(8,128)(2,1)}, bf16[1024,1024]{1,0:T...) custom-call(f32[8,128]{1,0:T(8,128)} %broadcast_in_dim.69.refs_0_, ...), custom_call_target="tpu_custom_call" | custom-call | flops 1073741824 | bytes 100000000 | tf_op jit(solution)/shard_map/prepare/pallas_call | solution.py:417
  78.7 1.2 slice.67
  80.6 0.5 subtract_clamp_fusion.valid_ref
  81.1 0.6 broadcast_in_dim.87
  81.7 56.1 %attend.1 = (bf16[8,512,128]{2,1,0:T(8,128)(2,1)}, bf16[4,8,2,512,128]{4,3,2,1,0:T(8,128)(2,1)}, bf16[8,512,128]{2,1,0:T(8,128)(2,1)}, bf16[512,1024]{1,0:T(8,128)(2,1)}, f32[8,8,512]{2,1,0:T(8,128)}) custom-call(s32[4]{0:T(128)} %subtract_clamp_fusion.valid_ref, bf16[512,1024]{1,0:T(8,128)(2,1)} %get-tuple-element.63.rows_ref, ...), custom_call_target="tpu_custom_call" | custom-call | flops 17179869184 | bytes 100000000 | tf_op jit(solution)/shard_map/attend/pallas_call | solution.py:753
  137.8 55.2 %feed.1 = (f32[512,1024]{1,0:T(8,128)}, bf16[4,512,1024]{2,1,0:T(8,128)(2,1)}, bf16[1024,2048]{1,0:T(8,128)(2,1)}, f32[512,1024]{1,0:T(8,128)}, bf16[512,1024]{1...) custom-call(f32[1]{0:T(128)} %bitcast.10.refs_0_, bf16[512,1024]{1,0:T(8,128)(2,1)} %get-tuple-element.65.refs_1_, ...), custom_call_target="tpu_custom_call" | custom-call | flops 25769803776 | bytes 100000000 | tf_op jit(solution)/shard_map/feed/pallas_call | solution.py:1204
  193.1 1.7 fusion.12
  194.8 1.5 pad_maximum_fusion
  196.3 0.0 collective-permute-start
  196.3 90.3 %attend_back.1 = (bf16[512,3072]{1,0:T(8,128)(2,1)}, bf16[1024,1536]{1,0:T(8,128)(2,1)}) custom-call(s32[4]{0:T(128)} %subtract_clamp_fusion.valid_ref, bf16[8,512,128]{2,1,0:T(8,128)(2,1)} %get-tuple-element.72.q_ref, bf16[4,8,2,512,128]{4,3,2,1,0:T(8,128)(2,1)} %get-tuple-element.73.kv_in, bf16[8,512,128]{2,1,0:T(8,128)(2,1)} %get-tuple-element.74.grad_ref, ...), custom_call_target="tpu_custom_call" | custom-call | flops 42949672960 | bytes 100000000 | tf_op jit(solution)/shard_map/attend_back/pallas_call | solution.py:951
  286.6 1.3 copy.57
  288.0 1.3 copy.58
  289.3 0.8 copy.60.refs_23_
  290.1 1.3 slice.85
  291.4 0.6 pad_maximum_fusion.1.refs_0_
  292.0 1.6 constant_dynamic-slice_fusion.2.refs_18_
  293.5 4.1 slice_convert_fusion
  297.6 2.9 fusion.3.refs_24_
  300.5 115.5 %finish.1 = (bf16[256,3072]{1,0:T(8,128)(2,1)}, bf16[256,1024]{1,0:T(8,128)(2,1)}, bf16[256,1024]{1,0:T(8,128)(2,1)}, f32[256,1024]{1,0:T(8,128)}, f32[256,1024]...) custom-call(f32[2]{0:T(128)} %pad_maximum_fusion.1.refs_0_, ...), custom_call_target="tpu_custom_call" | custom-call | flops 10737418240 | bytes 200000000 | tf_op jit(solution)/shard_map/finish/pallas_call | solution.py:1737
  416.1 1.0 slice.74
  417.1 1.5 slice.76
  418.5 2.0 copy.61
  420.6 0.8 copy.62
  421.4 1.3 slice.77
  422.6 1.1 convert_element_type.61
  423.8 2.0 convert_element_type.62
  425.8 1.1 convert_element_type.63
  426.9 0.6 constant_dynamic-slice_fusion.1
  427.5 2.6 maximum_convert_fusion
  430.1 0.7 fusion.13
  430.8 3.2 fusion.2
  434.0 1.0 copy.70
  435.0 0.6 copy-done.5
  435.6 1.0 copy.71
  436.6 1.0 copy.72
  (42 shorter events, 0.2 us)
Async XLA Ops:
  0.7 2.3 copy-start
  0.7 9.4 %copy-start.13 = (bf16[12,1024]{1,0:T(8,128)(2,1)S(1)}, bf16[12,1024]{1,0:T(8,128)(2,1)}, u32[]{:S(2)}) copy-start(bf16[12,1024]{1,0:T(8,128)(2,1)} %param.31) | copy-start | bytes 73732
  12.0 69.1 %copy-start.16 = (bf16[1024]{0:T(1024)(128)(2,1)S(1)}, bf16[1024]{0:T(1024)(128)(2,1)}, u32[]{:S(2)}) copy-start(bf16[1024]{0:T(1024)(128)(2,1)} %param.46) | copy-start | bytes 6148
  196.3 101.3 %collective-permute-start = (bf16[2,512,1024]{2,1,0:T(8,128)(2,1)}, bf16[2,512,1024]{2,1,0:T(8,128)(2,1)}, u32[]{:S(2)}, u32[]{:S(2)}) collective-permute-start(bf16[2,512,1024]{2,1,0:T(8,128)(2,1)} %pad_maximum_fusion), channel_id=1, source_target_pairs={{0,1},{1,0},{2,3},{3,2},{4,5},{5,4},{6,7},{7,6},{8,9},{9,8},{10,11... | collective-permute-start | bytes 6291464 | tf_op jit(solution)/shard_map/ppermute | solution.py:21
  196.3 90.3 %copy-start.7 = (bf16[512,1024]{1,0:T(8,128)(2,1)S(1)}, bf16[512,1024]{1,0:T(8,128)(2,1)}, u32[]{:S(2)}) copy-start(bf16[512,1024]{1,0:T(8,128)(2,1)} %get-tuple-element.63.rows_ref) | copy-start | bytes 3145732
  286.6 1.3 copy-start.8
  416.0 6.6 %copy-start.12 = (bf16[256,1024]{1,0:T(8,128)(2,1)S(1)}, bf16[256,1024]{1,0:T(8,128)(2,1)}, u32[]{:S(2)}) copy-start(bf16[256,1024]{1,0:T(8,128)(2,1)} %get-tuple-element.97) | copy-start | bytes 1572868
  416.1 7.7 %copy-start.14 = (f32[16,1024]{1,0:T(8,128)S(1)}, f32[16,1024]{1,0:T(8,128)}, u32[]{:S(2)}) copy-start(f32[16,1024]{1,0:T(8,128)} %get-tuple-element.98) | copy-start | bytes 196612
  420.6 3.2 copy-start.3
  423.8 2.0 copy-start.11
  423.8 3.7 copy-start.10
  427.5 3.3 copy-start.2
  427.5 3.3 copy-start.9
  427.5 3.3 copy-start.15
  430.8 3.3 copy-start.6
  434.0 1.6 copy-start.5
  434.0 2.6 copy-start.4
  434.0 3.5 copy-start.1

commit v8 on v7

--- a/solution.py
+++ b/solution.py
@@ -1884,7 +1884,7 @@
     out_sum = (out_parts[2].astype(wide) + out_got[1].astype(wide)).astype(low)
 
     columns = width // 8
-    chunks = 12
+    chunks = 11
     qkv_grad, summed = attend_back(
         group_count,
         queries,

time: 441 us -> 438 us (level)
    pallas_call x1, Pallas kernels: 90.3 us -> 82.9 us  [attend_back(): pl.pallas_call(functools.partial(attend_back_kernel, head_dim, group_size...]
    pallas_call x1, Pallas kernels: 116 us -> 120 us  [finish(): pl.pallas_call(functools.partial(finish_kernel, group_size, widths, width...]
  transfers between devices with their start and end apart: 1 -> 1, of which waited for: 0 -> 0; matrix products, arithmetic and copies ran while one was open for 3% -> 3% of each run, Pallas kernels for 21% -> 19%
where the time goes in v8:
time: 438 us; the launch traced here: 435 us
  Pallas kernels  381 us (87%)
  other arithmetic  25.5 us (6%)
  local copies, waits for them, and re-layouts  25.2 us (6%)
    pallas_call x1, Pallas kernels, finish(): pl.pallas_call(functools.partial(finish_kernel, group_size, widths, width...  120 us
    pallas_call x1, Pallas kernels, attend_back(): pl.pallas_call(functools.partial(attend_back_kernel, head_dim, group_size...  82.9 us
    pallas_call x1, Pallas kernels, prepare(): pl.pallas_call(functools.partial(prepare_kernel, group_size, head_dim), i...  66.7 us
    pallas_call x1, Pallas kernels, attend(): pl.pallas_call(functools.partial(attend_kernel, head_dim), in_specs=[pl.B...  56.1 us
    pallas_call x1, Pallas kernels, feed(): pl.pallas_call(feed_kernel, in_specs=[pl.BlockSpec(memory_space=pltpu.SME...  55.3 us
  transfers between devices with their start and end apart: 1, of which 0 were waited for; matrix products, arithmetic and copies ran while one was open for 3% of the time, Pallas kernels for 19%

profile of v8, /device:TPU:0, one launch (start us, length us, event | category | flops | bytes accessed | tf_op | source)
XLA Modules:
  0.0 434.9 jit_solution(11600590364306521141)
XLA Ops:
  0.7 0.0 copy-start
  1.4 0.9 copy.54
  3.0 0.1 tile.13
  3.1 1.6 copy.64
  4.7 0.7 fusion.10
  5.4 0.7 copy.56.refs_12_.refs_15_
  6.1 0.8 fusion.11
  6.9 0.1 pad.13.clone
  6.9 0.8 fusion.5.refs_5_.refs_17_
  7.7 2.3 broadcast_select_fusion.refs_10_.refs_4_
  10.1 0.7 maximum_maximum_fusion.refs_4_
  10.8 0.6 broadcast_in_dim.69.refs_0_
  11.4 0.6 broadcast_in_dim.70.refs_1_
  12.0 66.7 %prepare.1 = (f32[8,128]{1,0:T(8,128)}, bf16[4,64,1024]{2,1,0:T(8,128)(2,1)}, f32[8,1024]{1,0:T(8,128)}, bf16[16,1024]{1,0:T(8,128)(2,1)}, bf16[1024,1024]{1,0:T...) custom-call(f32[8,128]{1,0:T(8,128)} %broadcast_in_dim.69.refs_0_, ...), custom_call_target="tpu_custom_call" | custom-call | flops 1073741824 | bytes 100000000 | tf_op jit(solution)/shard_map/prepare/pallas_call | solution.py:417
  78.7 1.2 slice.67
  80.6 0.5 subtract_clamp_fusion.valid_ref
  81.1 0.6 broadcast_in_dim.87
  81.7 56.1 %attend.1 = (bf16[8,512,128]{2,1,0:T(8,128)(2,1)}, bf16[4,8,2,512,128]{4,3,2,1,0:T(8,128)(2,1)}, bf16[8,512,128]{2,1,0:T(8,128)(2,1)}, bf16[512,1024]{1,0:T(8,128)(2,1)}, f32[8,8,512]{2,1,0:T(8,128)}) custom-call(s32[4]{0:T(128)} %subtract_clamp_fusion.valid_ref, bf16[512,1024]{1,0:T(8,128)(2,1)} %get-tuple-element.63.rows_ref, ...), custom_call_target="tpu_custom_call" | custom-call | flops 17179869184 | bytes 100000000 | tf_op jit(solution)/shard_map/attend/pallas_call | solution.py:753
  137.8 55.3 %feed.1 = (f32[512,1024]{1,0:T(8,128)}, bf16[4,512,1024]{2,1,0:T(8,128)(2,1)}, bf16[1024,2048]{1,0:T(8,128)(2,1)}, f32[512,1024]{1,0:T(8,128)}, bf16[512,1024]{1...) custom-call(f32[1]{0:T(128)} %bitcast.10.refs_0_, bf16[512,1024]{1,0:T(8,128)(2,1)} %get-tuple-element.65.refs_1_, ...), custom_call_target="tpu_custom_call" | custom-call | flops 25769803776 | bytes 100000000 | tf_op jit(solution)/shard_map/feed/pallas_call | solution.py:1204
  193.1 1.7 fusion.12
  194.8 1.5 pad_maximum_fusion
  196.3 82.9 %attend_back.1 = (bf16[512,3072]{1,0:T(8,128)(2,1)}, bf16[1024,1408]{1,0:T(8,128)(2,1)}) custom-call(s32[4]{0:T(128)} %subtract_clamp_fusion.valid_ref, bf16[8,512,128]{2,1,0:T(8,128)(2,1)} %get-tuple-element.72.q_ref, bf16[4,8,2,512,128]{4,3,2,1,0:T(8,128)(2,1)} %get-tuple-element.73.kv_in, bf16[8,512,128]{2,1,0:T(8,128)(2,1)} %get-tuple-element.74.grad_ref, ...), custom_call_target="tpu_custom_call" | custom-call | flops 42949672960 | bytes 100000000 | tf_op jit(solution)/shard_map/attend_back/pallas_call | solution.py:951
  279.2 1.3 copy.57
  280.6 1.3 copy.58
  281.9 0.8 copy.60.refs_23_
  282.7 1.2 slice.85
  283.9 0.6 pad_maximum_fusion.1.refs_0_
  284.5 1.6 constant_dynamic-slice_fusion.2.refs_18_
  286.1 4.1 slice_convert_fusion
  290.1 0.0 collective-permute-done
  290.1 2.9 fusion.3.refs_24_
  293.0 120.1 %finish.1 = (bf16[256,3072]{1,0:T(8,128)(2,1)}, bf16[256,1024]{1,0:T(8,128)(2,1)}, bf16[256,1024]{1,0:T(8,128)(2,1)}, f32[256,1024]{1,0:T(8,128)}, f32[256,1024]...) custom-call(f32[2]{0:T(128)} %pad_maximum_fusion.1.refs_0_, ...), custom_call_target="tpu_custom_call" | custom-call | flops 10737418240 | bytes 200000000 | tf_op jit(solution)/shard_map/finish/pallas_call | solution.py:1737
  413.2 1.0 slice.74
  414.2 1.5 slice.76
  415.7 2.0 copy.61
  417.7 0.8 copy.62
  418.5 1.3 slice.77
  419.8 1.1 convert_element_type.61
  420.9 2.0 convert_element_type.62
  422.9 1.1 convert_element_type.63
  424.0 0.6 constant_dynamic-slice_fusion.1
  424.6 2.6 maximum_convert_fusion
  427.2 0.7 fusion.13
  427.9 3.2 fusion.2
  431.1 1.0 copy.70
  432.1 0.6 copy-done.6
  432.7 1.0 copy.71
  433.7 1.0 copy.72
  (42 shorter events, 0.2 us)
Async XLA Ops:
  0.7 2.3 copy-start
  0.7 9.4 %copy-start.13 = (bf16[12,1024]{1,0:T(8,128)(2,1)S(1)}, bf16[12,1024]{1,0:T(8,128)(2,1)}, u32[]{:S(2)}) copy-start(bf16[12,1024]{1,0:T(8,128)(2,1)} %param.31) | copy-start | bytes 73732
  12.0 69.1 %copy-start.16 = (bf16[1024]{0:T(1024)(128)(2,1)S(1)}, bf16[1024]{0:T(1024)(128)(2,1)}, u32[]{:S(2)}) copy-start(bf16[1024]{0:T(1024)(128)(2,1)} %param.46) | copy-start | bytes 6148
  196.3 93.8 %collective-permute-start = (bf16[2,512,1024]{2,1,0:T(8,128)(2,1)}, bf16[2,512,1024]{2,1,0:T(8,128)(2,1)}, u32[]{:S(2)}, u32[]{:S(2)}) collective-permute-start(bf16[2,512,1024]{2,1,0:T(8,128)(2,1)} %pad_maximum_fusion), channel_id=1, source_target_pairs={{0,1},{1,0},{2,3},{3,2},{4,5},{5,4},{6,7},{7,6},{8,9},{9,8},{10,11... | collective-permute-start | bytes 6291464 | tf_op jit(solution)/shard_map/ppermute | solution.py:21
  196.3 82.9 %copy-start.8 = (bf16[512,1024]{1,0:T(8,128)(2,1)S(1)}, bf16[512,1024]{1,0:T(8,128)(2,1)}, u32[]{:S(2)}) copy-start(bf16[512,1024]{1,0:T(8,128)(2,1)} %get-tuple-element.63.rows_ref) | copy-start | bytes 3145732
  279.2 1.3 copy-start.9
  413.2 6.6 %copy-start.12 = (bf16[256,1024]{1,0:T(8,128)(2,1)S(1)}, bf16[256,1024]{1,0:T(8,128)(2,1)}, u32[]{:S(2)}) copy-start(bf16[256,1024]{1,0:T(8,128)(2,1)} %get-tuple-element.97) | copy-start | bytes 1572868
  413.2 7.7 %copy-start.14 = (f32[16,1024]{1,0:T(8,128)S(1)}, f32[16,1024]{1,0:T(8,128)}, u32[]{:S(2)}) copy-start(f32[16,1024]{1,0:T(8,128)} %get-tuple-element.98) | copy-start | bytes 196612
  417.7 3.2 copy-start.3
  420.9 2.0 copy-start.11
  420.9 3.7 copy-start.4
  424.6 3.2 copy-start.2
  424.6 3.2 copy-start.10
  424.6 3.2 copy-start.15
  427.9 3.3 copy-start.7
  431.1 1.6 copy-start.6
  431.1 2.6 copy-start.5
  431.1 3.5 copy-start.1
